TPU v7x, 32 devices: a whole 2x2x4 slice. The times are simulated.
32 devices in a mesh: dp: 16 (over z, x, core), blk: 2 (over y).
Axes of the slice: x: 2, y: 2, z: 4, core: 2. Of those that a mesh axis runs over, the one named last changes fastest.
Arguments:
- tokens: bfloat16 [16, 768, 768], P('dp', 'blk'), may hold values from -6 to 6
- visible: int32 [16, 768], P('dp', 'blk'), may hold values from 0 to 1535, as said below
- ln1_gain: float32 [768], replicated, may hold values from 0.1 to 1.9
- w_qkv: bfloat16 [768, 2304], replicated, may hold values from -0.21875 to 0.21875
- w_proj: bfloat16 [768, 768], replicated, may hold values from -3.5 to 3.5
- ln2_gain: float32 [768], replicated, may hold values from 0.1 to 1.9
- w_up: bfloat16 [768, 3072], replicated, may hold values from -0.21875 to 0.21875
- w_down: bfloat16 [3072, 768], replicated, may hold values from -0.109375 to 0.109375
- d_out: bfloat16 [16, 768, 768], P('dp', 'blk'), may hold values from -6 to 6
Outputs:
- out: bfloat16 [16, 768, 768], P('dp', 'blk')
- d_tokens: float32 [16, 768, 768], P('dp', 'blk')
- d_ln1_gain: float32 [768], replicated
- d_w_qkv: float32 [768, 2304], replicated
- d_w_proj: float32 [768, 768], replicated
- d_ln2_gain: float32 [768], replicated
- d_w_up: float32 [768, 3072], replicated
- d_w_down: float32 [3072, 768], replicated
Inputs may be any that keep to these rules, and one draw needn't show every extreme that they name: `visible`: each row is strictly increasing, starts at 0 and ends at 1535.
All inputs are finite; a program needn't handle non-finite values.
Results may differ from a plain program's by a relative error of at most 0.015.
Values may be sent and summed in bfloat16 or wider, within the bound.
No kernel may reach another device: no remote copies, remote signals or barrier semaphores. Data moves between devices by JAX's collectives and lax.ppermute only.
A program may use at most 192 MiB of HBM per device.

v0:
```python
import math

import jax
import jax.numpy as jnp
from jax import lax
from jax.sharding import PartitionSpec as P

HEADS = 12
HD = 64


epsilon = 1e-06


def layer_norm(values, gain):
    center = values - jnp.mean(values, -1, keepdims=True)
    spread = jnp.mean(center * center, -1, keepdims=True)
    return center * lax.rsqrt(spread + epsilon) * gain


def position_table(visible, width):
    half = width // 2
    column = jnp.arange(half, dtype=jnp.float32)
    freqs = jnp.exp(column * (-math.log(10000.0) / half))
    angles = visible.astype(jnp.float32)[..., None] * freqs
    return jnp.concatenate([jnp.sin(angles), jnp.cos(angles)], -1)


def outer_product(left, right):
    return lax.dot_general(
        left, right, (((0,), (0,)), ((), ())), preferred_element_type=jnp.float32
    )


def times_transposed(left, weight):
    return lax.dot_general(
        left, weight, (((1,), (1,)), ((), ())), preferred_element_type=jnp.float32
    )


def split_blocks(keys, values):
    count = keys.shape[0]
    size = math.gcd(count, 512)
    shape = (count // size, size, HEADS, HD)
    return (keys.reshape(shape), values.reshape(shape))


def local(tokens, visible, ln1_gain, w_qkv, w_proj, ln2_gain, w_up, w_down, d_out):
    rows = tokens.shape[1]
    width = tokens.shape[2]
    factor = HD ** (-0.5)
    resid = tokens[0].astype(jnp.float32) + position_table(visible[0], width)
    normed1, back_one = jax.vjp(layer_norm, resid, ln1_gain)
    normed1 = normed1.astype(jnp.bfloat16)
    qkv = jnp.dot(normed1, w_qkv, preferred_element_type=jnp.float32).astype(jnp.bfloat16)
    query = qkv[:, :width]
    keys = qkv[:, width : 2 * width]
    values = qkv[:, 2 * width :]
    query_heads = query.reshape(rows, HEADS, HD)
    initial = (
        jnp.full((HEADS, rows), -1e30, jnp.float32),
        jnp.zeros((HEADS, rows), jnp.float32),
        jnp.zeros((HEADS, rows, HD), jnp.float32),
    )
    key_blocks, value_blocks = split_blocks(
        lax.all_gather(keys, "blk", axis=0, tiled=True),
        lax.all_gather(values, "blk", axis=0, tiled=True),
    )

    def one_block(state, block):
        running, total, accum = state
        block_keys, block_values = block
        scores = (
            jnp.einsum("qhd,khd->hqk", query_heads, block_keys, preferred_element_type=jnp.float32)
            * factor
        )
        top = jnp.maximum(running, jnp.max(scores, -1))
        weights = jnp.exp(scores - top[..., None])
        shrink = jnp.exp(running - top)
        total = total * shrink + jnp.sum(weights, -1)
        accum = accum * shrink[..., None] + jnp.einsum(
            "hqk,khd->hqd",
            weights.astype(jnp.bfloat16),
            block_values,
            preferred_element_type=jnp.float32,
        )
        return ((top, total, accum), None)

    running, total, accum = lax.scan(one_block, initial, (key_blocks, value_blocks))[0]
    log_total = running + jnp.log(total)
    attended = (accum / total[..., None]).transpose(1, 0, 2).reshape(rows, width)
    attended_low = attended.astype(jnp.bfloat16)
    resid2 = resid + jnp.dot(attended_low, w_proj, preferred_element_type=jnp.float32)
    normed2, back_two = jax.vjp(layer_norm, resid2, ln2_gain)
    normed2 = normed2.astype(jnp.bfloat16)
    hidden = jnp.dot(normed2, w_up, preferred_element_type=jnp.float32)
    activated, back_gelu = jax.vjp(jax.nn.gelu, hidden)
    activated = activated.astype(jnp.bfloat16)
    result = resid2 + jnp.dot(activated, w_down, preferred_element_type=jnp.float32)
    cotangent = d_out[0]
    grad_down = outer_product(activated, cotangent)
    (grad_hidden,) = back_gelu(times_transposed(cotangent, w_down))
    grad_hidden = grad_hidden.astype(jnp.bfloat16)
    grad_up = outer_product(normed2, grad_hidden)
    grad_resid2, grad_gain2 = back_two(times_transposed(grad_hidden, w_up))
    grad_resid2 = grad_resid2 + cotangent.astype(jnp.float32)
    grad_branch = grad_resid2.astype(jnp.bfloat16)
    grad_proj = outer_product(attended_low, grad_branch)
    grad_attended = times_transposed(grad_branch, w_proj).astype(jnp.bfloat16)
    correction = (grad_attended.astype(jnp.float32) * attended).reshape(rows, HEADS, HD)
    correction = jnp.sum(correction, -1).T
    grad_heads = grad_attended.reshape(rows, HEADS, HD)
    all_keys, all_values = (
        lax.all_gather(keys, "blk", axis=0, tiled=True),
        lax.all_gather(values, "blk", axis=0, tiled=True),
    )
    full_rows = all_keys.shape[0]
    key_blocks, value_blocks = split_blocks(all_keys, all_values)

    def back_block(grad_query, block):
        block_keys, block_values = block
        scores = (
            jnp.einsum("qhd,khd->hqk", query_heads, block_keys, preferred_element_type=jnp.float32)
            * factor
        )
        probs = jnp.exp(scores - log_total[..., None])
        grad_value = jnp.einsum(
            "hqk,qhd->khd",
            probs.astype(jnp.bfloat16),
            grad_heads,
            preferred_element_type=jnp.float32,
        )
        grad_probs = jnp.einsum(
            "qhd,khd->hqk", grad_heads, block_values, preferred_element_type=jnp.float32
        )
        grad_scores = (probs * (grad_probs - correction[..., None])).astype(jnp.bfloat16)
        grad_query = grad_query + jnp.einsum(
            "hqk,khd->qhd", grad_scores, block_keys, preferred_element_type=jnp.float32
        )
        grad_key = (
            jnp.einsum("hqk,qhd->khd", grad_scores, query_heads, preferred_element_type=jnp.float32)
            * factor
        )
        return (grad_query, (grad_key, grad_value))

    grad_query, (key_parts, value_parts) = lax.scan(
        back_block, jnp.zeros((rows, HEADS, HD), jnp.float32), (key_blocks, value_blocks)
    )
    grad_query = (grad_query * factor).reshape(rows, width)
    grad_keys, grad_values = (
        lax.psum_scatter(
            key_parts.reshape(full_rows, width).astype(jnp.bfloat16),
            "blk",
            scatter_dimension=0,
            tiled=True,
        ).astype(jnp.float32),
        lax.psum_scatter(
            value_parts.reshape(full_rows, width).astype(jnp.bfloat16),
            "blk",
            scatter_dimension=0,
            tiled=True,
        ).astype(jnp.float32),
    )
    grad_qkv = jnp.concatenate([grad_query, grad_keys, grad_values], 1).astype(jnp.bfloat16)
    grad_joint = outer_product(normed1, grad_qkv)
    grad_resid, grad_gain1 = back_one(times_transposed(grad_qkv, w_qkv))
    input_grad = grad_resid2 + grad_resid
    flats = (
        grad_joint.reshape(-1),
        grad_proj.reshape(-1),
        grad_up.reshape(-1),
        grad_down.reshape(-1),
    )
    shares = (
        lax.psum_scatter(flats[0], ("dp", "blk"), scatter_dimension=0, tiled=True),
        lax.psum_scatter(flats[1], ("dp", "blk"), scatter_dimension=0, tiled=True),
        lax.psum_scatter(flats[2], ("dp", "blk"), scatter_dimension=0, tiled=True),
        lax.psum_scatter(flats[3], ("dp", "blk"), scatter_dimension=0, tiled=True),
    )
    summed = (
        lax.all_gather(shares[0].astype(jnp.bfloat16), ("dp", "blk"), axis=0, tiled=True).astype(
            jnp.float32
        ),
        lax.all_gather(shares[1].astype(jnp.bfloat16), ("dp", "blk"), axis=0, tiled=True).astype(
            jnp.float32
        ),
        lax.all_gather(shares[2].astype(jnp.bfloat16), ("dp", "blk"), axis=0, tiled=True).astype(
            jnp.float32
        ),
        lax.all_gather(shares[3].astype(jnp.bfloat16), ("dp", "blk"), axis=0, tiled=True).astype(
            jnp.float32
        ),
    )
    gain_one, gain_two = lax.psum((grad_gain1, grad_gain2), ("dp", "blk"))
    return (
        result.astype(jnp.bfloat16)[None],
        input_grad[None],
        gain_one,
        summed[0].reshape(w_qkv.shape),
        summed[1].reshape(w_proj.shape),
        gain_two,
        summed[2].reshape(w_up.shape),
        summed[3].reshape(w_down.shape),
    )


def solution(mesh):
    return jax.shard_map(
        local,
        mesh=mesh,
        in_specs=(
            P("dp", "blk", None),
            P("dp", "blk"),
            P(),
            P(),
            P(),
            P(),
            P(),
            P(),
            P("dp", "blk", None),
        ),
        out_specs=(P("dp", "blk", None), P("dp", "blk", None), P(), P(), P(), P(), P(), P()),
        check_vma=False,
    )
```

profile of v0, /device:TPU:0, one launch (start us, length us, event | category | flops | bytes accessed | tf_op | source)
XLA Modules:
  0.0 994.5 jit_solution(17611237664140996087)
XLA Ops:
  17.9 22.1 %all-gather.7.cloned.1.call-done = bf16[768,768]{1,0:T(8,128)(2,1)} async-done(((bf16[384,768]{1,0:T(8,128)(2,1)}), bf16[768,768]{1,0:T(8,128)(2,1)}) %all-gather.7.cloned.1.call-update) | async-done | bytes 1179664 | tf_op jit(solution)/shard_map/all_gather | solution.py:66
  40.0 4.7 reshape.186
  44.7 4.6 copy.43
  49.2 15.7 %all-gather.9.cloned.1.call-done = bf16[768,768]{1,0:T(8,128)(2,1)} async-done(((bf16[384,768]{1,0:T(8,128)(2,1)}), bf16[768,768]{1,0:T(8,128)(2,1)}) %all-gather.9.cloned.1.call-update) | async-done | bytes 1179664 | tf_op jit(solution)/shard_map/all_gather | solution.py:67
  64.9 4.7 reshape.187
  69.6 4.6 copy.44
  74.2 38.5 %while.30 = (s32[]{:T(128)}, f32[12,384]{1,0:T(8,128)}, f32[12,384]{1,0:T(8,128)}, f32[12,384,64]{1,2,0:T(8,128)}, bf16[3,256,12,64]{1,3,2,0:T(8,128)(2,1)}, /*i...) while((s32[]{:T(128)}, f32[12,384]{1,0:T(8,128)}, ...), condition=%wide.region_5.6_spmd.clone, body=%wide.region_2.5_spmd.clone.sunk | while | flops 312334848 | bytes 37282024 | solution.py:89
  74.2 4.8 bitcast_reduce_fusion.2
  86.7 4.8 bitcast_reduce_fusion.2
  92.3 3.3 fusion.117
  96.3 3.4 fusion.119
  99.7 4.8 bitcast_reduce_fusion.2
  105.3 3.3 fusion.117
  109.3 3.4 fusion.119
  124.2 9.2 fusion.50
  147.6 45.9 %while.31 = (s32[]{:T(128)}, f32[384,12,64]{0,2,1:T(8,128)}, bf16[3,256,12,64]{1,3,2,0:T(8,128)(2,1)}, bf16[3,256,12,64]{1,3,2,0:T(8,128)(2,1)}, bf16[3,256,12,6...) while((s32[]{:T(128)}, f32[384,12,64]{0,2,1:T(8,128)}, ...), condition=%wide.region_12.13_spmd.clone, body=%wide.region_11.12_spmd.clone.sunk | while | flops 765198336 | bytes 80892304 | solution.py:146
  149.7 4.0 multiply_convert_fusion.12
  153.7 3.4 fusion.131
  157.2 3.5 fusion.132
  164.8 4.0 multiply_convert_fusion.12
  168.8 3.7 fusion.131
  172.6 3.5 fusion.132
  180.2 4.0 multiply_convert_fusion.12
  184.2 3.7 fusion.131
  188.0 3.5 fusion.132
  193.5 5.0 copy.62
  198.5 4.7 reshape.184
  203.3 5.0 copy.61
  208.3 4.8 reshape.182
  213.2 3.6 fusion.62
  216.8 3.4 reshape.164
  220.3 5.0 convolution_bitcast_fusion.1
  225.3 5.9 copy.65
  231.2 5.4 fusion.56
  236.6 10.8 %reshape.170 = f32[2359296]{0:T(1024)} reshape(f32[3072,768]{1,0:T(8,128)} %fusion.56) | data formatting | bytes 18874368 | tf_op jit(solution)/shard_map/reshape | solution.py:172
  253.8 5.3 multiply_reduce_fusion.1
  259.2 5.2 fusion.54
  264.4 7.9 reshape.161
  272.3 456.8 %all-reduce.6 = (f32[768]{0:T(1024)}, bf16[1769472]{0:T(1024)(128)(2,1)}, bf16[589824]{0:T(1024)(128)(2,1)}, f32[768]{0:T(1024)}, bf16[2359296]{0:T(1024)(128)(2,1)}, /*index=5*/bf16[2359296]{0:T(1024)(128)(2,1)}) all-reduce(f32[768]{0:T(1024)} %get-tuple-element.217, ...), channel_id=1, replica_groups=mesh['dp'=16,'blk'=2] {'dp','blk'}, use_global_device_ids=true, to_apply=%region_18.19 | all-reduce | flops 7079424 | bytes 42479616 | tf_op jit(solution)/shard_map/psum | solution.py:194
  735.5 7.9 fusion.52
  746.1 37.2 %all-gather.13.cloned.1.call-done = bf16[589824]{0:T(1024)(128)(2,1)} async-done(((bf16[18432]{0:T(1024)(128)(2,1)}), bf16[589824]{0:T(1024)(128)(2,1)}) %all-gather.13.cloned.1.call-update) | async-done | bytes 1179664 | tf_op jit(solution)/shard_map/all_gather | solution.py:184
  783.3 3.6 reshape.177
  786.9 58.9 %all-gather.11.cloned.1.call-done = bf16[1769472]{0:T(1024)(128)(2,1)} async-done(((bf16[55296]{0:T(1024)(128)(2,1)}), bf16[1769472]{0:T(1024)(128)(2,1)}) %all-gather.11.cloned.1.call-update) | async-done | bytes 3538960 | tf_op jit(solution)/shard_map/all_gather | solution.py:181
  845.8 7.9 reshape.175
  853.7 58.0 %all-gather.15.cloned.1.call-done = bf16[2359296]{0:T(1024)(128)(2,1)} async-done(((bf16[73728]{0:T(1024)(128)(2,1)}), bf16[2359296]{0:T(1024)(128)(2,1)}) %all-gather.15.cloned.1.call-update) | async-done | bytes 4718608 | tf_op jit(solution)/shard_map/all_gather | solution.py:187
  911.8 8.7 reshape.179
  920.5 56.7 %all-gather.17.cloned.1.call-done = bf16[2359296]{0:T(1024)(128)(2,1)} async-done(((bf16[73728]{0:T(1024)(128)(2,1)}), bf16[2359296]{0:T(1024)(128)(2,1)}) %all-gather.17.cloned.1.call-update) | async-done | bytes 4718608 | tf_op jit(solution)/shard_map/all_gather | solution.py:190
  977.2 10.0 %reshape.181 = f32[3072,768]{1,0:T(8,128)} reshape(bf16[2359296]{0:T(1024)(128)(2,1)} %all-gather.17.cloned.1.call-done) | data formatting | bytes 14155776 | tf_op jit(solution)/shard_map/reshape | solution.py:203
  (230 shorter events, 74.4 us)
Async XLA Ops:
  7.2 4.3 copy-start
  7.2 32.8 %all-gather.7.cloned.1.call-start = ((), (), s32[]{:S(2)}) async-start(), calls=%async_computation.2 | async-start | bytes 1769472 | tf_op jit(solution)/shard_map/all_gather | solution.py:66
  14.4 50.6 %all-gather.9.cloned.1.call-start = ((), (), s32[]{:S(2)}) async-start(), calls=%async_computation.3 | async-start | bytes 1769472 | tf_op jit(solution)/shard_map/all_gather | solution.py:67
  15.1 234.4 %reduce-scatter.9.cloned.1.call-start = ((), (), s32[]{:S(2)}) async-start(), calls=%async_computation.9 | async-start | bytes 1769472
  79.7 3.3 copy-start.26
  79.7 4.0 copy-start.1
  83.1 3.7 copy-start.27
  92.3 4.0 copy-start.1
  95.7 4.1 copy-start.27
  105.3 4.0 copy-start.1
  108.7 4.1 copy-start.27
  117.8 4.4 copy-start.45
  120.7 15.6 %copy-start.9 = (f32[384,768]{1,0:T(8,128)}, f32[384,768]{1,0:T(8,128)S(1)}, u32[]{:S(2)}) copy-start(f32[384,768]{1,0:T(8,128)S(1)} %get-tuple-element.275) | copy-start | bytes 3538948
  121.0 15.3 %copy-start.38 = (f32[384]{0:T(512)}, f32[384]{0:T(512)S(1)}, u32[]{:S(2)}) copy-start(f32[384]{0:T(512)S(1)} %fusion.66) | copy-start | bytes 4612
  124.2 9.2 copy-start.46
  149.7 4.1 copy-start.2
  153.7 7.0 copy-start.3
  157.2 3.5 copy-start.5
  157.2 3.5 copy-start.18
  157.2 3.5 copy-start.29
  164.8 4.1 copy-start.2
  168.8 7.3 copy-start.3
  172.6 3.5 copy-start.5
  172.6 3.5 copy-start.18
  172.6 3.5 copy-start.29
  180.2 4.1 copy-start.2
  184.2 7.3 copy-start.3
  188.0 3.5 copy-start.5
  188.0 3.5 copy-start.18
  188.0 3.6 copy-start.29
  203.3 48.4 %reduce-scatter.7.cloned.1.call-start = ((), (), s32[]{:S(2)}) async-start(), calls=%async_computation.8 | async-start | bytes 1769472
  213.2 570.1 %all-gather.13.cloned.1.call-start = ((), (), s32[]{:S(2)}) async-start(), calls=%async_computation.5 | async-start | bytes 1216512 | tf_op jit(solution)/shard_map/all_gather | solution.py:184
  220.3 10.9 %slice-start = ((s8[4718592]{0:T(1024)(128)(4,1)}), s8[4194304]{0:T(1024)(128)(4,1)S(1)}, s32[]{:S(2)}) async-start(s8[4718592]{0:T(1024)(128)(4,1)} %bitcast.139), calls=%async_computation.10 | async-start | bytes 8388608
  225.2 6.0 copy-start.23
  225.2 6.0 slice-start.1
  249.5 4.3 copy-start.37
  253.8 5.4 copy-start.7
  253.8 5.4 copy-start.19
  253.8 5.4 copy-start.20
  253.8 5.4 copy-start.21
  264.4 7.9 copy-start.43
  730.5 115.3 %all-gather.11.cloned.1.call-start = ((), (), s32[]{:S(2)}) async-start(), calls=%async_computation.4 | async-start | bytes 3649536 | tf_op jit(solution)/shard_map/all_gather | solution.py:181
  732.2 179.6 %all-gather.15.cloned.1.call-start = ((), (), s32[]{:S(2)}) async-start(), calls=%async_computation.6 | async-start | bytes 4866048 | tf_op jit(solution)/shard_map/all_gather | solution.py:187
  733.8 243.3 %all-gather.17.cloned.1.call-start = ((), (), s32[]{:S(2)}) async-start(), calls=%async_computation.7 | async-start | bytes 4866048 | tf_op jit(solution)/shard_map/all_gather | solution.py:190
  735.5 7.9 copy-start.40
  735.5 7.9 copy-start.44
  735.5 7.9 copy-start.8
  735.5 7.9 copy-start.31
  (35 other events, 65.8 us)
Sparse Core Ops, SparseCore 0:
  14.5 25.4 all-gather.6
  42.1 22.7 all-gather.8
  203.4 21.7 reduce-scatter.8
  227.4 21.7 reduce-scatter.6
  730.6 52.6 all-gather.12
  786.6 59.1 all-gather.10
  849.3 62.4 all-gather.14
  914.7 62.4 all-gather.16
where the time goes:
time: 1000 us; the launch traced here: 994 us
  blocking collectives  457 us (46%)
  waiting for transfers between devices  249 us (25%)
  local copies, waits for them, and re-layouts  127 us (13%)
  matrix products  120 us (12%)
  other arithmetic  25.6 us (3%)
  between operations  15.1 us (2%)
    psum x1, blocking collectives, local(): gain_one, gain_two = lax.psum((grad_gain1, grad_gain2), ('dp', 'blk'))  457 us
    all_gather x1, waiting for transfers between devices, local(): lax.all_gather(shares[0].astype(jnp.bfloat16), ('dp', 'blk'), axis=0, til...  58.9 us
    all_gather x1, waiting for transfers between devices, local(): lax.all_gather(shares[2].astype(jnp.bfloat16), ('dp', 'blk'), axis=0, til...  58 us
    all_gather x1, waiting for transfers between devices, local(): lax.all_gather(shares[3].astype(jnp.bfloat16), ('dp', 'blk'), axis=0, til...  56.7 us
    unnamed x85, local copies, waits for them, and re-layouts  49.2 us
    all_gather x1, waiting for transfers between devices, local(): lax.all_gather(shares[1].astype(jnp.bfloat16), ('dp', 'blk'), axis=0, til...  37.2 us
    all_gather x1, waiting for transfers between devices, local(): lax.all_gather(keys, 'blk', axis=0, tiled=True)  22.1 us
  transfers between devices with their start and end apart: 8, of which 6 were waited for; matrix products, arithmetic and copies ran while one was open for 9% of the time, Pallas kernels for 0%

commit v1 on v0

--- a/solution.py
+++ b/solution.py
@@ -1,29 +1,654 @@
+import functools
 import math
 
 import jax
 import jax.numpy as jnp
 from jax import lax
+from jax.experimental import pallas as pl
+from jax.experimental.pallas import tpu as pltpu
 from jax.sharding import PartitionSpec as P
 
 HEADS = 12
 HD = 64
-
-
+PAIR = 2 * HD
 epsilon = 1e-06
+f32 = jnp.float32
+bf16 = jnp.bfloat16
+NN = ((1,), (0,))
+NT = ((1,), (1,))
+TN = ((0,), (0,))
+AXES = ("dp", "blk")
+MIB = 1 << 20
+
+
+def dot(left, right, dims=NN):
+    return lax.dot_general(left, right, (dims, ((), ())), preferred_element_type=f32)
+
+
+def position_table(visible, width):
+    half = width // 2
+    column = jnp.arange(half, dtype=f32)
+    freqs = jnp.exp(column * (-math.log(10000.0) / half))
+    angles = visible.astype(f32)[..., None] * freqs
+    return jnp.concatenate([jnp.sin(angles), jnp.cos(angles)], -1)
+
+
+def normalize(values):
+    center = values - jnp.mean(values, -1, keepdims=True)
+    spread = jnp.mean(center * center, -1, keepdims=True)
+    scale = lax.rsqrt(spread + epsilon)
+    return center * scale, scale
+
+
+def norm_backward(grad, gain, xhat, scale):
+    e = grad * gain
+    return scale * (
+        e - jnp.mean(e, -1, keepdims=True) - xhat * jnp.mean(e * xhat, -1, keepdims=True)
+    )
+
+
+def call(kernel, grid, in_specs, out_specs, out_shape, args, scalars, vmem, scratch=(), aliases=None):
+    return pl.pallas_call(
+        kernel,
+        grid_spec=pltpu.PrefetchScalarGridSpec(
+            num_scalar_prefetch=1,
+            grid=grid,
+            in_specs=in_specs,
+            out_specs=out_specs,
+            scratch_shapes=list(scratch),
+        ),
+        out_shape=out_shape,
+        input_output_aliases=aliases or {},
+        compiler_params=pltpu.CompilerParams(vmem_limit_bytes=vmem * MIB),
+    )(scalars, *args)
+
+
+def spec(shape, index):
+    return pl.BlockSpec(shape, index)
+
+
+def whole(array):
+    zeros = (0,) * array.ndim
+    return pl.BlockSpec(array.shape, lambda i, s: zeros)
+
+
+def shape(dims, dtype):
+    return jax.ShapeDtypeStruct(dims, dtype)
+
+
+FF_ORDERS = (
+    (("x", "y", "z0", "z1"), ("z0", "x", "y", "z1")),
+    (("y", "z0", "x", "z1"), ("x", "y", "z0", "z1")),
+    (("z0", "x", "y", "z1"), ("y", "z0", "x", "z1")),
+)
+QKV_ORDER = (("x", "z0", "z1"), ("z0", "x", "z1"))
+DP_BIT = {"c": 1, "x": 2, "z0": 4, "z1": 8}
+
+
+def swap(array, first, second=None):
+    second = second or first
+    pairs = []
+    for d in range(16):
+        for b in range(2):
+            bit = second if d & 1 else first
+            to = (d, b ^ 1) if bit == "y" else (d ^ DP_BIT[bit], b)
+            pairs.append((d * 2 + b, to[0] * 2 + to[1]))
+    return lax.ppermute(array, AXES, pairs)
+
+
+def place(order):
+    d, b = lax.axis_index("dp"), lax.axis_index("blk")
+    code = jnp.int32(0)
+    for bit in order:
+        value = b & 1 if bit == "y" else (d // DP_BIT[bit]) & 1
+        code = code * 2 + value
+    return code
+
+
+def places(orders):
+    core = lax.axis_index("dp") & 1
+    first, second = place(orders[0]), place(orders[1])
+    return jnp.where(core == 0, first, second), jnp.where(core == 0, second, first)
+
+
+def add(a, b):
+    return (a.astype(f32) + b.astype(f32)).astype(bf16)
+
+
+def reduce_halves(keep, send, orders):
+    received = swap(send, "c")
+    count = len(orders[0])
+    for step in range(count - 1):
+        half = keep.shape[0] // 2
+        send = add(keep[half:], received[half:])
+        keep = add(keep[:half], received[:half])
+        received = swap(send, orders[0][step], orders[1][step])
+    keep = add(keep, received)
+    received = swap(keep, orders[0][-1], orders[1][-1])
+    return add(keep, received[::-1])
+
+
+def spread_halves(block, orders):
+    for step in range(len(orders[0]) - 2, 0, -1):
+        block = jnp.concatenate([block, swap(block, orders[0][step], orders[1][step])], 0)
+    other = swap(block, "c")
+    far = swap(block, orders[0][0], orders[1][0])
+    return block, far, other, swap(far, "c")
+
+
+def ln_qkv_kernel(s, tok, pos, gain, w, normed, qkv):
+    @pl.when(pl.program_id(0) == 0)
+    def _():
+        xhat, _ = normalize(tok[...].astype(f32) + pos[...])
+        normed[...] = (xhat * gain[...]).astype(bf16)
+
+    qkv[...] = dot(normed[...], w[...]).astype(bf16)
+
+
+def ln_qkv(scalars, tok, pos, gain, w):
+    rows, width = tok.shape
+    return call(
+        ln_qkv_kernel,
+        (3,),
+        [whole(tok), whole(pos), whole(gain), spec((width, width), lambda i, s: (0, i))],
+        [spec((rows, width), lambda i, s: (0, 0)), spec((rows, width), lambda i, s: (0, i))],
+        [shape((rows, width), bf16), shape((rows, 3 * width), bf16)],
+        (tok, pos, gain, w),
+        scalars,
+        24,
+    )
+
+
+def head_masks(x):
+    lane = lax.broadcasted_iota(jnp.int32, x.shape, 1)
+    return jnp.where(lane < HD, x, 0.0).astype(bf16), jnp.where(lane >= HD, x, 0.0).astype(bf16)
+
+
+def attn_kernel(s, q, k_own, v_own, k_far, v_far, out):
+    rows = q.shape[0]
+    k = jnp.concatenate([k_own[...], k_far[...]], 0)
+    vt = jnp.concatenate([v_own[...], v_far[...]], 0).T
+    parts = []
+    for h, qh in enumerate(head_masks(q[...].astype(f32) * HD**-0.5)):
+        scores = dot(k, qh, NT)
+        e = jnp.exp(scores - jnp.max(scores, 0, keepdims=True))
+        total = jnp.sum(e, 0, keepdims=True)
+        part = dot(vt[h * HD : (h + 1) * HD], e.astype(bf16))
+        parts.append(part * (1.0 / total))
+    out[...] = jnp.concatenate(parts, 0).T.astype(bf16)
+
+
+def attention(scalars, qkv, qkv_far):
+    rows, width = qkv.shape[0], qkv.shape[1] // 3
+    pairs = width // PAIR
+
+    def column(part):
+        return spec((rows, PAIR), lambda i, s: (0, part * pairs + i))
+
+    return call(
+        attn_kernel,
+        (pairs,),
+        [column(0), column(1), column(2), column(1), column(2)],
+        spec((rows, PAIR), lambda i, s: (0, i)),
+        shape((rows, width), bf16),
+        (qkv, qkv, qkv, qkv_far, qkv_far),
+        scalars,
+        32,
+    )
+
+
+def proj_kernel(s, att, w, tok, pos, gain, resid2, normed2, normed2_t):
+    value = tok[...].astype(f32) + pos[...] + dot(att[...], w[...])
+    resid2[...] = value
+    xhat, _ = normalize(value)
+    low = (xhat * gain[...]).astype(bf16)
+    normed2[...] = low
+    normed2_t[...] = low.T
+
+
+def project(scalars, att, w, tok, pos, gain):
+    rows, width = att.shape
+    args = (att, w, tok, pos, gain)
+    full = spec((rows, width), lambda i, s: (0, 0))
+    return call(
+        proj_kernel,
+        (1,),
+        [whole(a) for a in args],
+        [full, full, spec((width, rows), lambda i, s: (0, 0))],
+        [shape((rows, width), f32), shape((rows, width), bf16), shape((width, rows), bf16)],
+        args,
+        scalars,
+        24,
+    )
+
+
+def gelu_and_slope(v):
+    c = math.sqrt(2.0 / math.pi)
+    square = v * v
+    t = jnp.tanh(v * (c + (c * 0.044715) * square))
+    act = 0.5 * v * (1.0 + t)
+    slope = 0.5 * (1.0 + t) + (0.5 * v) * (1.0 - t * t) * (c + (3.0 * c * 0.044715) * square)
+    return act, slope
+
+
+def ff_kernel(s, normed, normed_t, cot, up, down, out_in, back_in, keep, send, out, back):
+    step = pl.program_id(0)
+    hidden = dot(normed[...], up[...])
+    act, slope = gelu_and_slope(hidden)
+    act = act.astype(bf16)
+    grad = (dot(cot[...], down[...], NT) * slope).astype(bf16)
+    out_part = dot(act, down[...])
+    back_part = dot(grad, up[...], NT)
+
+    @pl.when(step == 0)
+    def _():
+        out[...] = out_in[...] + out_part
+        back[...] = back_in[...] + back_part
+
+    @pl.when(step == 1)
+    def _():
+        out[...] += out_part
+        back[...] += back_part
+
+    g_down = dot(act, cot[...], TN).astype(bf16)
+    g_up = dot(normed_t[...], grad).astype(bf16)
+
+    def store(target, code):
+        rows_d = g_down.shape[0] // 16
+        rows_u = g_up.shape[0] // 16
+        half = g_up.shape[1] // 2
+        for block in range(16):
+            at = block ^ code
+            target[at, :rows_d, :] = g_down[block * rows_d : (block + 1) * rows_d]
+            part = g_up[block * rows_u : (block + 1) * rows_u]
+            target[at, rows_d:, : 2 * half] = part[:rows_d]
+            target[at, rows_d : rows_d + 16, 2 * half :] = part[rows_d:, :half]
+            target[at, rows_d + 16 :, 2 * half :] = part[rows_d:, half:]
+
+    @pl.when(step == 0)
+    def _():
+        store(send, s[2])
+
+    @pl.when(step == 1)
+    def _():
+        store(keep, s[1])
+
+
+def ff_chunk(scalars, chunk, normed, normed_t, cot, up, down, out_in, back_in):
+    rows, width = normed.shape
+    wide = 512
+
+    def half(i, s):
+        return 2 * chunk + (s[0] ^ (1 - i))
+
+    full = spec((rows, width), lambda i, s: (0, 0))
+    piece = spec((16, 64, width), lambda i, s: (0, 0, 0))
+    return call(
+        ff_kernel,
+        (2,),
+        [
+            whole(normed),
+            whole(normed_t),
+            whole(cot),
+            spec((width, wide), lambda i, s: (0, half(i, s))),
+            spec((wide, width), lambda i, s: (half(i, s), 0)),
+            full,
+            full,
+        ],
+        [piece, piece, full, full],
+        [shape((16, 64, width), bf16)] * 2 + [shape((rows, width), f32)] * 2,
+        (normed, normed_t, cot, up, down, out_in, back_in),
+        scalars,
+        40,
+    )
+
+
+def mid_kernel(s, back, resid2, out_acc, cot, gain, w_own, w_other, out, grad2, branch, g_own, g_other):
+    value = resid2[...]
+    out[...] = (value + out_acc[...]).astype(bf16)
+    xhat, scale = normalize(value)
+    grad = cot[...].astype(f32) + norm_backward(back[...], gain[...], xhat, scale)
+    grad2[...] = grad
+    low = grad.astype(bf16)
+    branch[...] = low
+    g_other[...] = dot(low, w_other[...], NT).astype(bf16)
+    g_own[...] = dot(low, w_own[...], NT).astype(bf16)
+
+
+def middle(scalars, back, resid2, out_acc, cot, gain, w):
+    rows, width = resid2.shape
+    half = width // 2
+    full = spec((rows, width), lambda i, s: (0, 0))
+    part = spec((rows, half), lambda i, s: (0, 0))
+    return call(
+        mid_kernel,
+        (1,),
+        [
+            full,
+            full,
+            full,
+            full,
+            whole(gain),
+            spec((half, width), lambda i, s: (s[0], 0)),
+            spec((half, width), lambda i, s: (1 - s[0], 0)),
+        ],
+        [full, full, full, part, part],
+        [
+            shape((rows, width), bf16),
+            shape((rows, width), f32),
+            shape((rows, width), bf16),
+            shape((rows, half), bf16),
+            shape((rows, half), bf16),
+        ],
+        (back, resid2, out_acc, cot, gain, w, w),
+        scalars,
+        32,
+    )
+
+
+def attn_back_kernel(s, q_o, k_o, v_o, q_f, k_f, v_f, g_o, g_f, gq, gk, gv):
+    k = jnp.concatenate([k_o[...], k_f[...]], 0)
+    v = jnp.concatenate([v_o[...], v_f[...]], 0)
+    q = jnp.concatenate([q_o[...], q_f[...]], 0).astype(f32) * HD**-0.5
+    g = jnp.concatenate([g_o[...], g_f[...]], 0).astype(f32)
+    kt = (k.astype(f32) * HD**-0.5).astype(bf16).T
+    grad_q, grad_k, grad_v = [], 0.0, 0.0
+    for h, (qh, gh) in enumerate(zip(head_masks(q), head_masks(g))):
+        scores = dot(k, qh, NT)
+        e = jnp.exp(scores - jnp.max(scores, 0, keepdims=True))
+        probs = e * (1.0 / jnp.sum(e, 0, keepdims=True))
+        grad_v = grad_v + dot(probs.astype(bf16), gh)
+        grad_p = dot(v, gh, NT)
+        row = jnp.sum(probs * grad_p, 0, keepdims=True)
+        grad_s = (probs * (grad_p - row)).astype(bf16)
+        grad_k = grad_k + dot(grad_s, qh)
+        grad_q.append(dot(kt[h * HD : (h + 1) * HD], grad_s))
+    gq[...] = jnp.concatenate(grad_q, 0).T.astype(bf16)
+    gk[...] = grad_k.astype(bf16)
+    gv[...] = grad_v.astype(bf16)
+
+
+def attention_back(scalars, qkv, qkv_far, g_own, g_far):
+    rows, width = qkv.shape[0], qkv.shape[1] // 3
+    pairs = width // PAIR
+    mine = pairs // 2
+
+    def column(part):
+        return spec((rows, PAIR), lambda i, s: (0, part * pairs + mine * s[0] + i))
+
+    block = spec((rows, PAIR), lambda i, s: (0, i))
+    out = spec((2 * rows, PAIR), lambda i, s: (0, i))
+    return call(
+        attn_back_kernel,
+        (mine,),
+        [column(0), column(1), column(2)] * 2 + [block, block],
+        [out] * 3,
+        [shape((2 * rows, width // 2), bf16)] * 3,
+        (qkv, qkv, qkv, qkv_far, qkv_far, qkv_far, g_own, g_far),
+        scalars,
+        48,
+    )
+
+
+def joint_kernel(s, n_own, n_far, gq, gk, gv, att, branch, keep, send):
+    step = pl.program_id(0)
+    n = jnp.concatenate([n_own[...], n_far[...]], 0)
+    cols = gq.shape[1]
+
+    def fill(target, code):
+        tiles = [dot(n, g[...], TN).astype(bf16) for g in (gq, gk, gv)]
+        tiles.append(dot(att[...], branch[...], TN).astype(bf16))
+        rows = tiles[0].shape[0] // 8
+        for block in range(8):
+            at = block ^ code
+            for i, tile in enumerate(tiles):
+                part = tile[block * rows : (block + 1) * rows]
+                target[at, :, i * cols : i * cols + part.shape[1]] = part
+
+    @pl.when(step == 0)
+    def _():
+        fill(send, s[2])
+
+    @pl.when(step == 1)
+    def _():
+        fill(keep, s[1])
+
+
+def joint_grads(scalars, n_own, n_far, gq, gk, gv, att, branch):
+    rows, width = n_own.shape
+    half = width // 2
+    feature = spec((rows, half), lambda i, s: (0, s[0] ^ (1 - i)))
+    cols = 3 * half + width
+    piece = spec((8, half // 8, cols), lambda i, s: (0, 0, 0))
+    return call(
+        joint_kernel,
+        (2,),
+        [feature, feature, whole(gq), whole(gk), whole(gv), feature, whole(branch)],
+        [piece, piece],
+        [shape((8, half // 8, cols), bf16)] * 2,
+        (n_own, n_far, gq, gk, gv, att, branch),
+        scalars,
+        32,
+    )
+
+
+def back_qkv_kernel(s, gq, gk, gv, wq, wk, wv, own, far):
+    rows = own.shape[0]
+
+    def part(at):
+        total = dot(gq[pl.ds(at, rows)], wq[...], NT)
+        total += dot(gk[pl.ds(at, rows)], wk[...], NT)
+        return total + dot(gv[pl.ds(at, rows)], wv[...], NT)
+
+    far[...] = part(rows).astype(bf16)
+    own[...] = part(0)
+
+
+def back_qkv(scalars, gq, gk, gv, w):
+    rows, half = gq.shape[0] // 2, gq.shape[1]
+    width = 2 * half
+
+    def column(part):
+        return spec((width, half), lambda i, s: (0, 2 * part + s[0]))
+
+    full = spec((rows, width), lambda i, s: (0, 0))
+    return call(
+        back_qkv_kernel,
+        (1,),
+        [whole(gq), whole(gk), whole(gv), column(0), column(1), column(2)],
+        [full, full],
+        [shape((rows, width), f32), shape((rows, width), bf16)],
+        (gq, gk, gv, w, w, w),
+        scalars,
+        32,
+    )
+
+
+def last_kernel(s, own, far, tok, pos, gain, grad2, out):
+    xhat, scale = normalize(tok[...].astype(f32) + pos[...])
+    grad = own[...] + far[...].astype(f32)
+    out[...] = grad2[...] + norm_backward(grad, gain[...], xhat, scale)
+
+
+def token_grad(scalars, own, far, tok, pos, gain, grad2):
+    args = (own, far, tok, pos, gain, grad2)
+    return call(
+        last_kernel,
+        (1,),
+        [whole(a) for a in args],
+        whole(own),
+        shape(own.shape, f32),
+        args,
+        scalars,
+        24,
+    )
+
+
+def unpack_ff_kernel(s, near, far, *refs):
+    down, up = refs[-2:]
+    step = pl.program_id(0)
+    low = s[1] & 7
+
+    def unpack(source):
+        for block in range(8):
+            at = block ^ low
+            down[pl.ds(pl.multiple_of(at * 32, 32), 32), :] = source[block, :32, :].astype(f32)
+            row = pl.multiple_of(at * 48, 16)
+            up[pl.ds(row, 32), :] = source[block, 32:, :512].astype(f32)
+            up[pl.ds(row + 32, 16), :256] = source[block, 32:48, 512:].astype(f32)
+            up[pl.ds(row + 32, 16), 256:] = source[block, 48:, 512:].astype(f32)
+
+    @pl.when(step == 0)
+    def _():
+        unpack(near)
+
+    @pl.when(step == 1)
+    def _():
+        unpack(far)
+
+
+def unpack_ff(scalars, chunk, near, far, width, hidden, so_far):
+    def side(i, s):
+        return i ^ (s[1] // 8)
+
+    any_spec = pl.BlockSpec(memory_space=pl.ANY)
+    return call(
+        unpack_ff_kernel,
+        (2,),
+        [whole(near), whole(far)] + [any_spec] * len(so_far),
+        [
+            spec((256, width), lambda i, s: (2 * (2 * chunk + s[0]) + side(i, s), 0)),
+            spec((width // 2, 512), lambda i, s: (side(i, s), 2 * chunk + s[0])),
+        ],
+        [shape((hidden, width), f32), shape((width, hidden), f32)],
+        (near, far) + tuple(so_far),
+        scalars,
+        32,
+        aliases={3: 0, 4: 1} if so_far else None,
+    )
+
+
+def unpack_qkv_kernel(s, near, far, *refs):
+    joint, proj = refs[-2:]
+    step = pl.program_id(0)
+    low = s[1] & 3
+    mine = s[2]
+
+    def unpack(source):
+        half = source.shape[2] // 8
+        for block in range(4):
+            at = pl.multiple_of((block ^ low) * 48, 16)
+            rows = pl.ds(at, 48)
+            for part in range(3):
+                for side in range(2):
+                    column = pl.multiple_of(2 * half * part + half * (mine ^ side), 128)
+                    value = source[block, :, (3 * side + part) * half : (3 * side + part + 1) * half]
+                    joint[rows, pl.ds(column, half)] = value.astype(f32)
+            proj[rows, :] = source[block, :, 6 * half :].astype(f32)
+
+    @pl.when(step == 0)
+    def _():
+        unpack(near)
+
+    @pl.when(step == 1)
+    def _():
+        unpack(far)
+
+
+def unpack_qkv(scalars, near, far, width, so_far):
+    def row(i, s):
+        return 2 * s[0] + (i ^ (s[1] // 4))
+
+    any_spec = pl.BlockSpec(memory_space=pl.ANY)
+    return call(
+        unpack_qkv_kernel,
+        (2,),
+        [whole(near), whole(far)] + [any_spec] * len(so_far),
+        [
+            spec((width // 4, 3 * width), lambda i, s: (row(i, s), 0)),
+            spec((width // 4, width), lambda i, s: (row(i, s), 0)),
+        ],
+        [shape((width, 3 * width), f32), shape((width, width), f32)],
+        (near, far) + tuple(so_far),
+        scalars,
+        32,
+        aliases={3: 0, 4: 1} if so_far else None,
+    )
+
+
+def fast(tokens, visible, ln1_gain, w_qkv, w_proj, ln2_gain, w_up, w_down, d_out):
+    tok, cot = tokens[0], d_out[0]
+    rows, width = tok.shape
+    hidden = w_up.shape[1]
+    gain1, gain2 = ln1_gain[None], ln2_gain[None]
+    core = lax.axis_index("dp") & 1
+    head_half = lax.axis_index("blk")
+    ints = lambda *values: jnp.stack([jnp.int32(v) for v in values])
+    none = ints(0)
+    heads = ints(head_half)
+
+    vis_far = swap(visible, "y")[0]
+    tok_far = swap(tok, "y")
+    pos = position_table(visible[0], width)
+    pos_far = position_table(vis_far, width)
+    normed1, qkv = ln_qkv(none, tok, pos, gain1, w_qkv)
+    normed1_far, qkv_far = ln_qkv(none, tok_far, pos_far, gain1, w_qkv)
+    attended = attention(none, qkv, qkv_far)
+    resid2, normed2, normed2_t = project(none, attended, w_proj, tok, pos, gain2)
+
+    out_acc = jnp.zeros((rows, width), f32)
+    back = jnp.zeros((rows, width), f32)
+    pieces = []
+    for chunk, orders in enumerate(FF_ORDERS):
+        own_code, other_code = places(orders)
+        keep, send, out_acc, back = ff_chunk(
+            ints(core, own_code, other_code), chunk, normed2, normed2_t, cot, w_up, w_down, out_acc, back
+        )
+        pieces.append((keep, send))
+    out, grad2, branch, g_own, g_other = middle(heads, back, resid2, out_acc, cot, gain2, w_proj)
+    g_far = swap(g_other, "y")
+
+    summed = [reduce_halves(*pair, orders) for pair, orders in zip(pieces, FF_ORDERS)]
+    gathered = [spread_halves(block, orders) for block, orders in zip(summed, FF_ORDERS)]
+
+    gq, gk, gv = attention_back(heads, qkv, qkv_far, g_own, g_far)
+    own_code, other_code = places(QKV_ORDER)
+    keep, send = joint_grads(
+        ints(core, own_code, other_code), normed1, normed1_far, gq, gk, gv, attended, branch
+    )
+    back_own, back_far = back_qkv(heads, gq, gk, gv, w_qkv)
+    back_far = swap(back_far, "y")
+    block = reduce_halves(keep, send, QKV_ORDER)
+    other = swap(block, "y")
+    cut = 3 * (width // 2)
+    block = jnp.concatenate(
+        [block[..., :cut], other[..., :cut], add(block[..., cut:], other[..., cut:])], -1
+    )
+    joint_pieces = spread_halves(block, QKV_ORDER)
+
+    d_tokens = token_grad(none, back_own, back_far, tok, pos, gain1, grad2)
+
+    ff = ()
+    for chunk, orders in enumerate(FF_ORDERS):
+        own_code, other_code = places(orders)
+        near, far, near_other, far_other = gathered[chunk]
+        ff = unpack_ff(ints(core, own_code), chunk, near, far, width, hidden, ff)
+        ff = unpack_ff(ints(1 - core, other_code), chunk, near_other, far_other, width, hidden, ff)
+    own_code, other_code = places(QKV_ORDER)
+    near, far, near_other, far_other = joint_pieces
+    qkvp = unpack_qkv(ints(core, own_code, head_half), near, far, width, ())
+    qkvp = unpack_qkv(ints(1 - core, other_code, head_half), near_other, far_other, width, qkvp)
+    d_down, d_up = ff
+    d_qkv, d_proj = qkvp
+    d_gain1 = jnp.sum(w_qkv.astype(f32) * d_qkv, 1) / ln1_gain
+    d_gain2 = jnp.sum(w_up.astype(f32) * d_up, 1) / ln2_gain
+    return out[None], d_tokens[None], d_gain1, d_qkv, d_proj, d_gain2, d_up, d_down
 
 
 def layer_norm(values, gain):
     center = values - jnp.mean(values, -1, keepdims=True)
     spread = jnp.mean(center * center, -1, keepdims=True)
     return center * lax.rsqrt(spread + epsilon) * gain
-
-
-def position_table(visible, width):
-    half = width // 2
-    column = jnp.arange(half, dtype=jnp.float32)
-    freqs = jnp.exp(column * (-math.log(10000.0) / half))
-    angles = visible.astype(jnp.float32)[..., None] * freqs
-    return jnp.concatenate([jnp.sin(angles), jnp.cos(angles)], -1)
 
 
 def outer_product(left, right):
@@ -45,7 +670,7 @@
     return (keys.reshape(shape), values.reshape(shape))
 
 
-def local(tokens, visible, ln1_gain, w_qkv, w_proj, ln2_gain, w_up, w_down, d_out):
+def general(tokens, visible, ln1_gain, w_qkv, w_proj, ln2_gain, w_up, w_down, d_out):
     rows = tokens.shape[1]
     width = tokens.shape[2]
     factor = HD ** (-0.5)
@@ -205,8 +830,9 @@
 
 
 def solution(mesh):
+    split = mesh.shape["dp"] == 16 and mesh.shape["blk"] == 2
     return jax.shard_map(
-        local,
+        fast if split else general,
         mesh=mesh,
         in_specs=(
             P("dp", "blk", None),

time: 1000 us -> 305 us (0.30)
  blocking collectives: 457 us -> 0 us
  waiting for transfers between devices: 249 us -> 104 us
  matrix products: 120 us -> 0 us
  Pallas kernels: 0 us -> 97.1 us
  local copies, waits for them, and re-layouts: 127 us -> 31.9 us
  starting transfers between devices: 0.85 us -> 39.6 us
  between operations: 15.1 us -> 1.86 us
    psum x1 -> x0, blocking collectives: 457 us -> none  [local(): gain_one, gain_two = lax.psum((grad_gain1, grad_gain2), ('dp', 'blk'))]
    all_gather x6 -> x0, waiting for transfers between devices: 249 us -> none  [the longest x1 58.9 us: local(): lax.all_gather(shares[0].astype(jnp.bfloat16), ('dp', 'blk'), axis=0, til...]
    dot_general x33 -> x0, matrix products: 120 us -> none  [the longest x4 19.2 us: times_transposed(): lax.dot_general(left, weight, (((1,), (1,)), ((), ())), preferred_element...]
    ppermute x0 -> x43, waiting for transfers between devices: none -> 104 us  [swap(): return lax.ppermute(array, AXES, pairs)]
    pallas_call x0 -> x20, Pallas kernels: none -> 97.1 us  [call(): pl.pallas_call(kernel, grid_spec=pltpu.PrefetchScalarGridSpec(num_scalar_...]
    reshape x10 -> x0, local copies, waits for them, and re-layouts: 64.3 us -> none  [the longest x1 10.8 us: local(): grad_down.reshape(-1)]
    ppermute x0 -> x43, starting transfers between devices: none -> 39.6 us  [swap(): return lax.ppermute(array, AXES, pairs)]
    unnamed x85 -> x120, local copies, waits for them, and re-layouts: 49.2 us -> 30.4 us
  transfers between devices with their start and end apart: 8 -> 43, of which waited for: 6 -> 17; matrix products, arithmetic and copies ran while one was open for 9% -> 8% of each run, Pallas kernels for 0% -> 24%
where the time goes in v1:
time: 305 us; the launch traced here: 301 us
  waiting for transfers between devices  104 us (34%)
  Pallas kernels  97.1 us (32%)
  starting transfers between devices  39.6 us (13%)
  local copies, waits for them, and re-layouts  31.9 us (10%)
  other arithmetic  25.7 us (8%)
    ppermute x43, waiting for transfers between devices, swap(): return lax.ppermute(array, AXES, pairs)  104 us
    pallas_call x20, Pallas kernels, call(): pl.pallas_call(kernel, grid_spec=pltpu.PrefetchScalarGridSpec(num_scalar_...  97.1 us
    ppermute x43, starting transfers between devices, swap(): return lax.ppermute(array, AXES, pairs)  39.6 us
    unnamed x120, local copies, waits for them, and re-layouts  30.4 us
    convert_element_type x20, other arithmetic, add(): return (a.astype(f32) + b.astype(f32)).astype(bf16)  7.54 us
  transfers between devices with their start and end apart: 43, of which 17 were waited for; matrix products, arithmetic and copies ran while one was open for 8% of the time, Pallas kernels for 24%

profile of v1, /device:TPU:0, one launch (start us, length us, event | category | flops | bytes accessed | tf_op | source)
XLA Modules:
  0.0 300.5 jit_solution(4280940258668990362)
XLA Ops:
  0.6 3.0 %collective-permute-start.1 = (s32[1,384]{1,0:T(1,128)}, s32[1,384]{1,0:T(1,128)S(1)}, u32[]{:S(2)}, u32[]{:S(2)}) collective-permute-start(s32[1,384]{1,0:T(1,128)} %param.10), channel_id=1, source_target_pairs={{0,1},{1,0},{2,3},{3,2},{4,5},{5,4},{6,7},{7,6},{8,9},{9,8},{10,11... | collective-permute-start | bytes 4616 | tf_op jit(solution)/shard_map/ppermute | solution.py:96
  5.9 4.2 %multiply_sine_fusion = (f32[384,384]{1,0:T(8,128)S(1)}, f32[384,384]{1,0:T(8,128)S(1)}, f32[384,384]{1,0:T(8,128)S(1)}, f32[384,384]{1,0:T(8,128)S(1)}) fusion(f32[384]{0:T(512)S(1)} %convert_reduce_fusion, f32[384]{0:T(512)S(1)} %multiply_exponential_fusion, f32[384]{0:T(512)S(1)} %convert_reduce_fusion.1), kind=kLoop, calls=%fused_computation.14 | loop fusion | flops 294912 | bytes 2363904 | tf_op jit(solution)/shard_map/sin | solution.py:33
  11.2 2.8 shard_map.152
  14.1 4.6 %collective-permute-done.tok = bf16[384,768]{1,0:T(8,128)(2,1)} collective-permute-done((bf16[384,768]{1,0:T(8,128)(2,1)}, bf16[384,768]{1,0:T(8,128)(2,1)}, u32[]{:S(2)}, u32[]{:S(2)}) %collective-permute-start) | collective-permute-done | bytes 589856 | tf_op jit(solution)/shard_map/ppermute | solution.py:96
  18.8 3.7 %shard_map.153 = (bf16[384,768]{1,0:T(8,128)(2,1)S(1)}, bf16[384,2304]{1,0:T(8,128)(2,1)S(1)}) custom-call(s32[1]{0:T(128)} %constant.139.clone.1.s, bf16[384,768]{1,0:T(8,128)(2,1)} %collective-permute-done.tok, f32[384,768]{1,0:T(8,128)S(1)} %pad_maximum_fusion.1.pos, f32[1,768]{1,0:T(1,128)S(1)} %broadcast_in_dim.16.gain, bf16[768,2304]{1,0:T(8,128)(2,1)S(1)} %copy-done), custom_call_target="tpu_custom_call" | custom-call | tf_op jit(solution)/shard_map/pallas_call | solution.py:51
  23.3 8.0 %shard_map.154.att = bf16[384,768]{1,0:T(8,128)(2,1)S(1)} custom-call(s32[1]{0:T(128)} %constant.139.clone.1.s, bf16[384,2304]{1,0:T(8,128)(2,1)S(1)} %get-tuple-element.55.q.k_own.v_own.q_o.k_o.v_o, bf16[384,2304]{1,0:T(8,128)(2,1)S(1)} %get-tuple-element.55.q.k_own.v_own.q_o.k_o.v_o, bf16[384,2304]{1,0:T(8,128)(2,1)S(1)} %get-tuple-element.55.q.k_own.v_own.q_o.k_o.v_o, ...), custom_call_target="tpu_custom_call" | custom-call | tf_op jit(solution)/shard_map/pallas_call | solution.py:51
  33.6 8.9 %shard_map.156 = (bf16[16,64,768]{2,1,0:T(8,128)(2,1)S(1)}, bf16[16,64,768]{2,1,0:T(8,128)(2,1)}, f32[384,768]{1,0:T(8,128)S(1)}, f32[384,768]{1,0:T(8,128)S(1)}) custom-call(s32[3]{0:T(128)S(1)} %pad_add_fusion.2.s, bf16[384,768]{1,0:T(8,128)(2,1)S(1)} %get-tuple-element.57.normed, bf16[768,384]{1,0:T(8,128)(2,1)S(1)} %get-tuple-element.58.normed_t, ...), custom_call_target="tpu_custom_call" | custom-call | tf_op jit(solution)/shard_map/pallas_call | solution.py:51
  45.8 2.3 copy-done.1
  53.9 8.8 %shard_map.157 = (bf16[16,64,768]{2,1,0:T(8,128)(2,1)S(1)}, bf16[16,64,768]{2,1,0:T(8,128)(2,1)}, f32[384,768]{1,0:T(8,128)S(1)}, f32[384,768]{1,0:T(8,128)S(1)}) custom-call(s32[3]{0:T(128)S(1)} %get-tuple-element.123.s, bf16[384,768]{1,0:T(8,128)(2,1)S(1)} %copy-done.17, bf16[768,384]{1,0:T(8,128)(2,1)S(1)} %copy-done.19, bf16[384,768]{1,0:T(8,128)(2,1)S(1)} %bitcast.20, ...), custom_call_target="tpu_custom_call" | custom-call | tf_op jit(solution)/shard_map/pallas_call | solution.py:51
  64.4 9.2 %shard_map.158 = (bf16[16,64,768]{2,1,0:T(8,128)(2,1)S(1)}, bf16[16,64,768]{2,1,0:T(8,128)(2,1)}, f32[384,768]{1,0:T(8,128)S(1)}, f32[384,768]{1,0:T(8,128)S(1)}) custom-call(s32[3]{0:T(128)S(1)} %get-tuple-element.122.s, bf16[384,768]{1,0:T(8,128)(2,1)S(1)} %copy-done.17, bf16[768,384]{1,0:T(8,128)(2,1)S(1)} %copy-done.19, bf16[384,768]{1,0:T(8,128)(2,1)S(1)} %bitcast.21, ...), custom_call_target="tpu_custom_call" | custom-call | tf_op jit(solution)/shard_map/pallas_call | solution.py:51
  73.6 2.1 shard_map.159
  78.7 9.3 %collective-permute-done.2.g_f = bf16[384,384]{1,0:T(8,128)(2,1)} collective-permute-done((bf16[384,384]{1,0:T(8,128)(2,1)}, bf16[384,384]{1,0:T(8,128)(2,1)}, u32[]{:S(2)}, u32[]{:S(2)}) %collective-permute-start.2) | collective-permute-done | bytes 294944 | tf_op jit(solution)/shard_map/ppermute | solution.py:96
  91.9 14.8 %shard_map.160 = (bf16[768,384]{1,0:T(8,128)(2,1)S(1)}, bf16[768,384]{1,0:T(8,128)(2,1)S(1)}, bf16[768,384]{1,0:T(8,128)(2,1)S(1)}) custom-call(s32[1]{0:T(128)} %bitcast.s, bf16[384,2304]{1,0:T(8,128)(2,1)S(1)} %copy-done.3, bf16[384,2304]{1,0:T(8,128)(2,1)S(1)} %copy-done.3, bf16[384,2304]{1,0:T(8,128)(2,1)S(1)} %copy-done.3, ...), custom_call_target="tpu_custom_call" | custom-call | tf_op jit(solution)/shard_map/pallas_call | solution.py:51
  106.8 4.1 %shard_map.163 = (bf16[8,48,1920]{2,1,0:T(8,128)(2,1)S(1)}, bf16[8,48,1920]{2,1,0:T(8,128)(2,1)S(1)}) custom-call(s32[3]{0:T(128)S(1)} %pad_add_fusion.3.s, bf16[384,768]{1,0:T(8,128)(2,1)S(1)} %copy-done.45, bf16[384,768]{1,0:T(8,128)(2,1)S(1)} %copy-done.49, bf16[768,384]{1,0:T(8,128)(2,1)S(1)} %get-tuple-element.69.gq, ...), custom_call_target="tpu_custom_call" | custom-call | tf_op jit(solution)/shard_map/pallas_call | solution.py:51
  111.0 1.9 add_convert_fusion.1
  114.5 1.9 add_convert_fusion.3
  121.5 9.0 %collective-permute-done.34 = bf16[8,64,768]{2,1,0:T(8,128)(2,1)S(1)} collective-permute-done((bf16[8,64,768]{2,1,0:T(8,128)(2,1)S(1)}, bf16[8,64,768]{2,1,0:T(8,128)(2,1)S(1)}, u32[]{:S(2)}, u32[]{:S(2)}) %collective-permute-start.34) | collective-permute-done | bytes 786464 | tf_op jit(solution)/shard_map/ppermute | solution.py:96
  131.1 3.4 %collective-permute-done.24 = bf16[8,64,768]{2,1,0:T(8,128)(2,1)S(1)} collective-permute-done((bf16[8,64,768]{2,1,0:T(8,128)(2,1)S(1)}, bf16[8,64,768]{2,1,0:T(8,128)(2,1)S(1)}, u32[]{:S(2)}, u32[]{:S(2)}) %collective-permute-start.24) | collective-permute-done | bytes 786464 | tf_op jit(solution)/shard_map/ppermute | solution.py:96
  134.6 2.9 collective-permute-start.25
  137.5 1.9 collective-permute-done.14
  140.1 5.5 %collective-permute-done.5 = bf16[4,48,1920]{2,1,0:T(8,128)(2,1)S(1)} collective-permute-done((bf16[4,48,1920]{2,1,0:T(8,128)(2,1)S(1)}, bf16[4,48,1920]{2,1,0:T(8,128)(2,1)S(1)}, u32[]{:S(2)}, u32[]{:S(2)}) %collective-permute-start.5) | collective-permute-done | bytes 737312 | tf_op jit(solution)/shard_map/ppermute | solution.py:96
  149.5 4.1 %collective-permute-done.15 = bf16[4,64,768]{2,1,0:T(8,128)(2,1)S(1)} collective-permute-done((bf16[4,64,768]{2,1,0:T(8,128)(2,1)S(1)}, bf16[4,64,768]{2,1,0:T(8,128)(2,1)S(1)}, u32[]{:S(2)}, u32[]{:S(2)}) %collective-permute-start.15) | collective-permute-done | bytes 393248 | tf_op jit(solution)/shard_map/ppermute | solution.py:96
  155.5 2.7 collective-permute-start.7
  158.2 2.7 collective-permute-start.37
  161.4 26.5 %collective-permute-done.37 = bf16[2,64,768]{2,1,0:T(8,128)(2,1)S(1)} collective-permute-done((bf16[2,64,768]{2,1,0:T(8,128)(2,1)S(1)}, bf16[2,64,768]{2,1,0:T(8,128)(2,1)S(1)}, u32[]{:S(2)}, u32[]{:S(2)}) %collective-permute-start.37) | collective-permute-done | bytes 196640 | tf_op jit(solution)/shard_map/ppermute | solution.py:96
  188.0 2.4 collective-permute-done.27
  192.6 4.4 %collective-permute-done.38 = bf16[2,64,768]{2,1,0:T(8,128)(2,1)S(1)} collective-permute-done((bf16[2,64,768]{2,1,0:T(8,128)(2,1)S(1)}, bf16[2,64,768]{2,1,0:T(8,128)(2,1)S(1)}, u32[]{:S(2)}, u32[]{:S(2)}) %collective-permute-start.38) | collective-permute-done | bytes 196640 | tf_op jit(solution)/shard_map/ppermute | solution.py:96
  198.8 3.9 %collective-permute-done.8 = bf16[2,48,1920]{2,1,0:T(8,128)(2,1)S(1)} collective-permute-done((bf16[2,48,1920]{2,1,0:T(8,128)(2,1)S(1)}, bf16[2,48,1920]{2,1,0:T(8,128)(2,1)S(1)}, u32[]{:S(2)}, u32[]{:S(2)}) %collective-permute-start.8) | collective-permute-done | bytes 368672 | tf_op jit(solution)/shard_map/ppermute | solution.py:96
  205.5 4.4 %collective-permute-done.39 = bf16[4,64,768]{2,1,0:T(8,128)(2,1)S(1)} collective-permute-done((bf16[4,64,768]{2,1,0:T(8,128)(2,1)S(1)}, bf16[4,64,768]{2,1,0:T(8,128)(2,1)S(1)}, u32[]{:S(2)}, u32[]{:S(2)}) %collective-permute-start.39) | collective-permute-done | bytes 393248 | tf_op jit(solution)/shard_map/ppermute | solution.py:96
  210.0 2.8 collective-permute-start.41
  212.7 2.1 shard_map.161
  215.0 1.9 collective-permute-start.19
  217.0 2.9 collective-permute-done.9
  219.9 1.8 collective-permute-start.31
  223.0 11.9 %collective-permute-done.19 = bf16[4,64,768]{2,1,0:T(8,128)(2,1)S(1)} collective-permute-done((bf16[4,64,768]{2,1,0:T(8,128)(2,1)S(1)}, bf16[4,64,768]{2,1,0:T(8,128)(2,1)S(1)}, u32[]{:S(2)}, u32[]{:S(2)}) %collective-permute-start.19) | collective-permute-done | bytes 393248 | tf_op jit(solution)/shard_map/ppermute | solution.py:96
  234.9 2.5 collective-permute-start.11
  242.4 9.0 %collective-permute-done.21.far = bf16[8,64,768]{2,1,0:T(8,128)(2,1)} collective-permute-done((bf16[8,64,768]{2,1,0:T(8,128)(2,1)}, bf16[8,64,768]{2,1,0:T(8,128)(2,1)}, u32[]{:S(2)}, u32[]{:S(2)}) %collective-permute-start.21) | collective-permute-done | bytes 786464 | tf_op jit(solution)/shard_map/ppermute | solution.py:96
  258.6 1.9 shard_map.162
  260.5 3.5 %shard_map.166 = (f32[3072,768]{1,0:T(8,128)}, f32[768,3072]{1,0:T(8,128)}) custom-call(s32[2]{0:T(128)S(1)} %pad_add_fusion.10.s, bf16[8,64,768]{2,1,0:T(8,128)(2,1)S(1)} %copy-done.23, bf16[8,64,768]{2,1,0:T(8,128)(2,1)} %collective-permute-done.41.far), custom_call_target="tpu_custom_call" | custom-call | tf_op jit(solution)/shard_map/pallas_call | solution.py:51
  264.0 3.5 %shard_map.167 = (f32[3072,768]{1,0:T(8,128)}, f32[768,3072]{1,0:T(8,128)}) custom-call(s32[2]{0:T(128)S(1)} %pad_add_fusion.9.s, bf16[8,64,768]{2,1,0:T(8,128)(2,1)S(1)} %copy-done.41, bf16[8,64,768]{2,1,0:T(8,128)(2,1)} %collective-permute-done.42.far, f32[3072,768]{1,0:T(8,128)} %get-tuple-element.90.refs_0_, ...), custom_call_target="tpu_custom_call", output_to_operand_aliasing={{0}: (3, {}), {1}: (4, {})} | custom-call | tf_op jit(solution)/shard_map/pallas_call | solution.py:51
  267.5 3.5 %shard_map.168 = (f32[3072,768]{1,0:T(8,128)}, f32[768,3072]{1,0:T(8,128)}) custom-call(s32[2]{0:T(128)S(1)} %pad_add_fusion.8.s, bf16[8,64,768]{2,1,0:T(8,128)(2,1)S(1)} %copy-done.21, bf16[8,64,768]{2,1,0:T(8,128)(2,1)} %collective-permute-done.31.far, f32[3072,768]{1,0:T(8,128)} %get-tuple-element.92.refs_0_, ...), custom_call_target="tpu_custom_call", output_to_operand_aliasing={{0}: (3, {}), {1}: (4, {})} | custom-call | tf_op jit(solution)/shard_map/pallas_call | solution.py:51
  271.0 3.5 %shard_map.169 = (f32[3072,768]{1,0:T(8,128)}, f32[768,3072]{1,0:T(8,128)}) custom-call(s32[2]{0:T(128)S(1)} %pad_add_fusion.7.s, bf16[8,64,768]{2,1,0:T(8,128)(2,1)S(1)} %copy-done.43, bf16[8,64,768]{2,1,0:T(8,128)(2,1)} %collective-permute-done.32.far, f32[3072,768]{1,0:T(8,128)} %get-tuple-element.94.refs_0_, ...), custom_call_target="tpu_custom_call", output_to_operand_aliasing={{0}: (3, {}), {1}: (4, {})} | custom-call | tf_op jit(solution)/shard_map/pallas_call | solution.py:51
  274.5 4.0 %shard_map.170 = (f32[3072,768]{1,0:T(8,128)}, f32[768,3072]{1,0:T(8,128)}) custom-call(s32[2]{0:T(128)S(1)} %pad_add_fusion.6.s, bf16[8,64,768]{2,1,0:T(8,128)(2,1)} %pad_maximum_fusion.3.near, bf16[8,64,768]{2,1,0:T(8,128)(2,1)} %collective-permute-done.21.far, ...), custom_call_target="tpu_custom_call", output_to_operand_aliasing={{0}: (3, {}), {1}: (4, {})} | custom-call | tf_op jit(solution)/shard_map/pallas_call | solution.py:51
  278.6 4.0 %shard_map.171 = (f32[3072,768]{1,0:T(8,128)}, f32[768,3072]{1,0:T(8,128)}) custom-call(s32[2]{0:T(128)S(1)} %pad_add_fusion.5.s, bf16[8,64,768]{2,1,0:T(8,128)(2,1)} %collective-permute-done.20.near, bf16[8,64,768]{2,1,0:T(8,128)(2,1)} %collective-permute-done.22.far, ...), custom_call_target="tpu_custom_call", output_to_operand_aliasing={{0}: (3, {}), {1}: (4, {})} | custom-call | tf_op jit(solution)/shard_map/pallas_call | solution.py:51
  282.7 4.8 %multiply_reduce_fusion = f32[768]{0:T(1024)S(1)} fusion(f32[768,3072]{1,0:T(8,128)} %get-tuple-element.53, bf16[768,3072]{1,0:T(8,128)(2,1)S(1)} %bitcast.18), kind=kLoop, calls=%fused_computation | loop fusion | flops 7077120 | bytes 14158848 | tf_op jit(solution)/shard_map/reduce_sum | solution.py:644
  288.1 4.6 %shard_map.164 = (f32[768,2304]{1,0:T(8,128)}, f32[768,768]{1,0:T(8,128)}) custom-call(s32[3]{0:T(128)S(1)} %pad_add_fusion.11.s, bf16[4,48,3072]{2,1,0:T(8,128)(2,1)} %pad_maximum_fusion.2.near, bf16[4,48,3072]{2,1,0:T(8,128)(2,1)} %collective-permute-done.11.far), custom_call_target="tpu_custom_call" | custom-call | tf_op jit(solution)/shard_map/pallas_call | solution.py:51
  292.7 3.0 shard_map.165
  295.6 3.8 %multiply_reduce_fusion.1 = f32[768]{0:T(1024)S(1)} fusion(f32[768,2304]{1,0:T(8,128)} %get-tuple-element.50, bf16[768,2304]{1,0:T(8,128)(2,1)S(1)} %copy-done), kind=kLoop, calls=%fused_computation.1 | loop fusion | flops 5307648 | bytes 10619904 | tf_op jit(solution)/shard_map/reduce_sum | solution.py:643
  (234 shorter events, 60.2 us)
Async XLA Ops:
  0.6 5.3 %collective-permute-start.1 = (s32[1,384]{1,0:T(1,128)}, s32[1,384]{1,0:T(1,128)S(1)}, u32[]{:S(2)}, u32[]{:S(2)}) collective-permute-start(s32[1,384]{1,0:T(1,128)} %param.10), channel_id=1, source_target_pairs={{0,1},{1,0},{2,3},{3,2},{4,5},{5,4},{6,7},{7,6},{8,9},{9,8},{10,11... | collective-permute-start | bytes 4616 | tf_op jit(solution)/shard_map/ppermute | solution.py:96
  3.7 15.1 %collective-permute-start = (bf16[384,768]{1,0:T(8,128)(2,1)}, bf16[384,768]{1,0:T(8,128)(2,1)}, u32[]{:S(2)}, u32[]{:S(2)}) collective-permute-start(bf16[384,768]{1,0:T(8,128)(2,1)} %bitcast.23), channel_id=1, source_target_pairs={{0,1},{1,0},{2,3},{3,2},{4,5},{5,4},{6,7},{7,6},{8,9},{9,8},{10,11... | collective-permute-start | bytes 1769480 | tf_op jit(solution)/shard_map/ppermute | solution.py:96
  11.2 20.1 %copy-start.6 = (f32[384,768]{1,0:T(8,128)}, f32[384,768]{1,0:T(8,128)S(1)}, u32[]{:S(2)}) copy-start(f32[384,768]{1,0:T(8,128)S(1)} %pad_maximum_fusion.pos) | copy-start | bytes 3538948
  45.7 65.3 %collective-permute-start.33 = (bf16[16,64,768]{2,1,0:T(8,128)(2,1)}, bf16[16,64,768]{2,1,0:T(8,128)(2,1)}, u32[]{:S(2)}, u32[]{:S(2)}) collective-permute-start(bf16[16,64,768]{2,1,0:T(8,128)(2,1)} %get-tuple-element.89), channel_id=1, source_target_pairs={{0,2},{1,3},{2,0},{3,1},{4,6},{5,7},{6,4},{7,5},{8,10},{9,11},{10,... | collective-permute-start | bytes 4718600 | tf_op jit(solution)/shard_map/ppermute | solution.py:96
  63.9 50.7 %collective-permute-start.23 = (bf16[16,64,768]{2,1,0:T(8,128)(2,1)}, bf16[16,64,768]{2,1,0:T(8,128)(2,1)}, u32[]{:S(2)}, u32[]{:S(2)}) collective-permute-start(bf16[16,64,768]{2,1,0:T(8,128)(2,1)} %get-tuple-element.87), channel_id=1, source_target_pairs={{0,2},{1,3},{2,0},{3,1},{4,6},{5,7},{6,4},{7,5},{8,10},{9,11},{10,... | collective-permute-start | bytes 4718600 | tf_op jit(solution)/shard_map/ppermute | solution.py:96
  73.5 43.5 %collective-permute-start.13 = (bf16[16,64,768]{2,1,0:T(8,128)(2,1)}, bf16[16,64,768]{2,1,0:T(8,128)(2,1)}, u32[]{:S(2)}, u32[]{:S(2)}) collective-permute-start(bf16[16,64,768]{2,1,0:T(8,128)(2,1)} %get-tuple-element.85), channel_id=1, source_target_pairs={{0,2},{1,3},{2,0},{3,1},{4,6},{5,7},{6,4},{7,5},{8,10},{9,11},{10,... | collective-permute-start | bytes 4718600 | tf_op jit(solution)/shard_map/ppermute | solution.py:96
  78.3 9.7 %collective-permute-start.2 = (bf16[384,384]{1,0:T(8,128)(2,1)}, bf16[384,384]{1,0:T(8,128)(2,1)}, u32[]{:S(2)}, u32[]{:S(2)}) collective-permute-start(bf16[384,384]{1,0:T(8,128)(2,1)} %get-tuple-element.68), channel_id=1, source_target_pairs={{0,1},{1,0},{2,3},{3,2},{4,5},{5,4},{6,7},{7,6},{8,9},{9,8},{10,11... | collective-permute-start | bytes 884744 | tf_op jit(solution)/shard_map/ppermute | solution.py:96
  91.9 14.9 %copy-start.45 = (bf16[384,768]{1,0:T(8,128)(2,1)S(1)}, bf16[384,768]{1,0:T(8,128)(2,1)}, u32[]{:S(2)}) copy-start(bf16[384,768]{1,0:T(8,128)(2,1)} %copy-done.44) | copy-start | bytes 1769476
  91.9 14.9 %copy-start.49 = (bf16[384,768]{1,0:T(8,128)(2,1)S(1)}, bf16[384,768]{1,0:T(8,128)(2,1)}, u32[]{:S(2)}) copy-start(bf16[384,768]{1,0:T(8,128)(2,1)} %copy-done.48) | copy-start | bytes 1769476
  91.9 14.9 %copy-start.51 = (bf16[384,768]{1,0:T(8,128)(2,1)S(1)}, bf16[384,768]{1,0:T(8,128)(2,1)}, u32[]{:S(2)}) copy-start(bf16[384,768]{1,0:T(8,128)(2,1)} %copy-done.50) | copy-start | bytes 1769476
  110.9 9.6 %collective-permute-start.4 = (bf16[8,48,1920]{2,1,0:T(8,128)(2,1)S(1)}, bf16[8,48,1920]{2,1,0:T(8,128)(2,1)S(1)}, u32[]{:S(2)}, u32[]{:S(2)}) collective-permute-start(bf16[8,48,1920]{2,1,0:T(8,128)(2,1)S(1)} %get-tuple-element.79), channel_id=1, source_target_pairs={{0,2},{1,3},{2,0},{3,1},{4,6},{5,7},{6,4},{7,5},{8,10},{9,11},{10,... | collective-permute-start | bytes 4423688 | tf_op jit(solution)/shard_map/ppermute | solution.py:96
  113.0 17.6 %collective-permute-start.34 = (bf16[8,64,768]{2,1,0:T(8,128)(2,1)S(1)}, bf16[8,64,768]{2,1,0:T(8,128)(2,1)S(1)}, u32[]{:S(2)}, u32[]{:S(2)}) collective-permute-start(bf16[8,64,768]{2,1,0:T(8,128)(2,1)S(1)} %get-tuple-element.103), channel_id=1, source_target_pairs={{0,4},{1,5},{2,10},{3,11},{4,0},{5,1},{6,14},{7,15},{8,12},{9,13},... | collective-permute-start | bytes 2359304 | tf_op jit(solution)/shard_map/ppermute | solution.py:96
  116.5 18.0 %collective-permute-start.24 = (bf16[8,64,768]{2,1,0:T(8,128)(2,1)S(1)}, bf16[8,64,768]{2,1,0:T(8,128)(2,1)S(1)}, u32[]{:S(2)}, u32[]{:S(2)}) collective-permute-start(bf16[8,64,768]{2,1,0:T(8,128)(2,1)S(1)} %get-tuple-element.105), channel_id=1, source_target_pairs={{0,1},{1,0},{2,6},{3,7},{4,5},{5,4},{6,2},{7,3},{8,9},{9,8},{10,14... | collective-permute-start | bytes 2359304 | tf_op jit(solution)/shard_map/ppermute | solution.py:96
  118.9 20.5 %collective-permute-start.14 = (bf16[8,64,768]{2,1,0:T(8,128)(2,1)S(1)}, bf16[8,64,768]{2,1,0:T(8,128)(2,1)S(1)}, u32[]{:S(2)}, u32[]{:S(2)}) collective-permute-start(bf16[8,64,768]{2,1,0:T(8,128)(2,1)S(1)} %get-tuple-element.107), channel_id=1, source_target_pairs={{0,8},{1,9},{2,3},{3,2},{4,12},{5,13},{6,7},{7,6},{8,0},{9,1},{10,... | collective-permute-start | bytes 2359304 | tf_op jit(solution)/shard_map/ppermute | solution.py:96
  120.9 24.7 %collective-permute-start.5 = (bf16[4,48,1920]{2,1,0:T(8,128)(2,1)S(1)}, bf16[4,48,1920]{2,1,0:T(8,128)(2,1)S(1)}, u32[]{:S(2)}, u32[]{:S(2)}) collective-permute-start(bf16[4,48,1920]{2,1,0:T(8,128)(2,1)S(1)} %get-tuple-element.109), channel_id=1, source_target_pairs={{0,4},{1,5},{2,10},{3,11},{4,0},{5,1},{6,14},{7,15},{8,12},{9,13},... | collective-permute-start | bytes 2211848 | tf_op jit(solution)/shard_map/ppermute | solution.py:96
  130.8 16.5 %collective-permute-start.35 = (bf16[4,64,768]{2,1,0:T(8,128)(2,1)S(1)}, bf16[4,64,768]{2,1,0:T(8,128)(2,1)S(1)}, u32[]{:S(2)}, u32[]{:S(2)}) collective-permute-start(bf16[4,64,768]{2,1,0:T(8,128)(2,1)S(1)} %get-tuple-element.111), channel_id=1, source_target_pairs={{0,1},{1,0},{2,6},{3,7},{4,5},{5,4},{6,2},{7,3},{8,9},{9,8},{10,14... | collective-permute-start | bytes 1179656 | tf_op jit(solution)/shard_map/ppermute | solution.py:96
  134.6 13.2 %collective-permute-start.25 = (bf16[4,64,768]{2,1,0:T(8,128)(2,1)S(1)}, bf16[4,64,768]{2,1,0:T(8,128)(2,1)S(1)}, u32[]{:S(2)}, u32[]{:S(2)}) collective-permute-start(bf16[4,64,768]{2,1,0:T(8,128)(2,1)S(1)} %get-tuple-element.113), channel_id=1, source_target_pairs={{0,8},{1,9},{2,3},{3,2},{4,12},{5,13},{6,7},{7,6},{8,0},{9,1},{10,... | collective-permute-start | bytes 1179656 | tf_op jit(solution)/shard_map/ppermute | solution.py:96
  139.6 13.9 %collective-permute-start.15 = (bf16[4,64,768]{2,1,0:T(8,128)(2,1)S(1)}, bf16[4,64,768]{2,1,0:T(8,128)(2,1)S(1)}, u32[]{:S(2)}, u32[]{:S(2)}) collective-permute-start(bf16[4,64,768]{2,1,0:T(8,128)(2,1)S(1)} %get-tuple-element.115), channel_id=1, source_target_pairs={{0,4},{1,5},{2,10},{3,11},{4,0},{5,1},{6,14},{7,15},{8,12},{9,13},... | collective-permute-start | bytes 1179656 | tf_op jit(solution)/shard_map/ppermute | solution.py:96
  145.7 9.7 %collective-permute-start.6 = (bf16[2,48,1920]{2,1,0:T(8,128)(2,1)S(1)}, bf16[2,48,1920]{2,1,0:T(8,128)(2,1)S(1)}, u32[]{:S(2)}, u32[]{:S(2)}) collective-permute-start(bf16[2,48,1920]{2,1,0:T(8,128)(2,1)S(1)} %add_convert_fusion.16), channel_id=1, source_target_pairs={{0,8},{1,9},{2,6},{3,7},{4,12},{5,13},{6,2},{7,3},{8,0},{9,1},{10,... | collective-permute-start | bytes 1105928 | tf_op jit(solution)/shard_map/ppermute | solution.py:96
  147.3 10.8 %collective-permute-start.36 = (bf16[2,64,768]{2,1,0:T(8,128)(2,1)S(1)}, bf16[2,64,768]{2,1,0:T(8,128)(2,1)S(1)}, u32[]{:S(2)}, u32[]{:S(2)}) collective-permute-start(bf16[2,64,768]{2,1,0:T(8,128)(2,1)S(1)} %add_convert_fusion.20), channel_id=1, source_target_pairs={{0,8},{1,9},{2,3},{3,2},{4,12},{5,13},{6,7},{7,6},{8,0},{9,1},{10,... | collective-permute-start | bytes 589832 | tf_op jit(solution)/shard_map/ppermute | solution.py:96
  147.9 13.1 %collective-permute-start.26 = (bf16[2,64,768]{2,1,0:T(8,128)(2,1)S(1)}, bf16[2,64,768]{2,1,0:T(8,128)(2,1)S(1)}, u32[]{:S(2)}, u32[]{:S(2)}) collective-permute-start(bf16[2,64,768]{2,1,0:T(8,128)(2,1)S(1)} %add_convert_fusion.24), channel_id=1, source_target_pairs={{0,4},{1,5},{2,10},{3,11},{4,0},{5,1},{6,14},{7,15},{8,12},{9,13},... | collective-permute-start | bytes 589832 | tf_op jit(solution)/shard_map/ppermute | solution.py:96
  153.6 38.9 %collective-permute-start.16 = (bf16[2,64,768]{2,1,0:T(8,128)(2,1)S(1)}, bf16[2,64,768]{2,1,0:T(8,128)(2,1)S(1)}, u32[]{:S(2)}, u32[]{:S(2)}) collective-permute-start(bf16[2,64,768]{2,1,0:T(8,128)(2,1)S(1)} %add_convert_fusion.28), channel_id=1, source_target_pairs={{0,1},{1,0},{2,6},{3,7},{4,5},{5,4},{6,2},{7,3},{8,9},{9,8},{10,14... | collective-permute-start | bytes 589832 | tf_op jit(solution)/shard_map/ppermute | solution.py:96
  155.5 36.8 %collective-permute-start.7 = (bf16[2,48,1920]{2,1,0:T(8,128)(2,1)S(1)}, bf16[2,48,1920]{2,1,0:T(8,128)(2,1)S(1)}, u32[]{:S(2)}, u32[]{:S(2)}) collective-permute-start(bf16[2,48,1920]{2,1,0:T(8,128)(2,1)S(1)} %add_convert_fusion.15), channel_id=1, source_target_pairs={{0,16},{1,17},{2,18},{3,19},{4,20},{5,21},{6,22},{7,23},{8,24},{9,... | collective-permute-start | bytes 1105928 | tf_op jit(solution)/shard_map/ppermute | solution.py:96
  158.2 29.6 %collective-permute-start.37 = (bf16[2,64,768]{2,1,0:T(8,128)(2,1)S(1)}, bf16[2,64,768]{2,1,0:T(8,128)(2,1)S(1)}, u32[]{:S(2)}, u32[]{:S(2)}) collective-permute-start(bf16[2,64,768]{2,1,0:T(8,128)(2,1)S(1)} %add_convert_fusion.19), channel_id=1, source_target_pairs={{0,16},{1,17},{2,18},{3,19},{4,20},{5,21},{6,22},{7,23},{8,24},{9,... | collective-permute-start | bytes 589832 | tf_op jit(solution)/shard_map/ppermute | solution.py:96
  161.1 29.3 %collective-permute-start.27 = (bf16[2,64,768]{2,1,0:T(8,128)(2,1)S(1)}, bf16[2,64,768]{2,1,0:T(8,128)(2,1)S(1)}, u32[]{:S(2)}, u32[]{:S(2)}) collective-permute-start(bf16[2,64,768]{2,1,0:T(8,128)(2,1)S(1)} %add_convert_fusion.23), channel_id=1, source_target_pairs={{0,16},{1,17},{2,18},{3,19},{4,20},{5,21},{6,22},{7,23},{8,24},{9,... | collective-permute-start | bytes 589832 | tf_op jit(solution)/shard_map/ppermute | solution.py:96
  187.9 9.1 %collective-permute-start.38 = (bf16[2,64,768]{2,1,0:T(8,128)(2,1)S(1)}, bf16[2,64,768]{2,1,0:T(8,128)(2,1)S(1)}, u32[]{:S(2)}, u32[]{:S(2)}) collective-permute-start(bf16[2,64,768]{2,1,0:T(8,128)(2,1)S(1)} %add_convert_fusion.18), channel_id=1, source_target_pairs={{0,8},{1,9},{2,3},{3,2},{4,12},{5,13},{6,7},{7,6},{8,0},{9,1},{10,... | collective-permute-start | bytes 589832 | tf_op jit(solution)/shard_map/ppermute | solution.py:96
  190.4 6.7 %collective-permute-start.28 = (bf16[2,64,768]{2,1,0:T(8,128)(2,1)S(1)}, bf16[2,64,768]{2,1,0:T(8,128)(2,1)S(1)}, u32[]{:S(2)}, u32[]{:S(2)}) collective-permute-start(bf16[2,64,768]{2,1,0:T(8,128)(2,1)S(1)} %add_convert_fusion.22), channel_id=1, source_target_pairs={{0,4},{1,5},{2,10},{3,11},{4,0},{5,1},{6,14},{7,15},{8,12},{9,13},... | collective-permute-start | bytes 589832 | tf_op jit(solution)/shard_map/ppermute | solution.py:96
  192.4 10.4 %collective-permute-start.8 = (bf16[2,48,1920]{2,1,0:T(8,128)(2,1)S(1)}, bf16[2,48,1920]{2,1,0:T(8,128)(2,1)S(1)}, u32[]{:S(2)}, u32[]{:S(2)}) collective-permute-start(bf16[2,48,1920]{2,1,0:T(8,128)(2,1)S(1)} %add_convert_fusion.14), channel_id=1, source_target_pairs={{0,1},{1,0},{2,3},{3,2},{4,5},{5,4},{6,7},{7,6},{8,9},{9,8},{10,11... | collective-permute-start | bytes 1105928 | tf_op jit(solution)/shard_map/ppermute | solution.py:96
  192.5 11.4 %collective-permute-start.17 = (bf16[2,64,768]{2,1,0:T(8,128)(2,1)S(1)}, bf16[2,64,768]{2,1,0:T(8,128)(2,1)S(1)}, u32[]{:S(2)}, u32[]{:S(2)}) collective-permute-start(bf16[2,64,768]{2,1,0:T(8,128)(2,1)S(1)} %add_convert_fusion.27), channel_id=1, source_target_pairs={{0,16},{1,17},{2,18},{3,19},{4,20},{5,21},{6,22},{7,23},{8,24},{9,... | collective-permute-start | bytes 589832 | tf_op jit(solution)/shard_map/ppermute | solution.py:96
  197.0 12.8 %collective-permute-start.39 = (bf16[4,64,768]{2,1,0:T(8,128)(2,1)S(1)}, bf16[4,64,768]{2,1,0:T(8,128)(2,1)S(1)}, u32[]{:S(2)}, u32[]{:S(2)}) collective-permute-start(bf16[4,64,768]{2,1,0:T(8,128)(2,1)S(1)} %pad_maximum_fusion.9), channel_id=1, source_target_pairs={{0,1},{1,0},{2,6},{3,7},{4,5},{5,4},{6,2},{7,3},{8,9},{9,8},{10,14... | collective-permute-start | bytes 1179656 | tf_op jit(solution)/shard_map/ppermute | solution.py:96
  197.2 19.7 %collective-permute-start.29 = (bf16[4,64,768]{2,1,0:T(8,128)(2,1)S(1)}, bf16[4,64,768]{2,1,0:T(8,128)(2,1)S(1)}, u32[]{:S(2)}, u32[]{:S(2)}) collective-permute-start(bf16[4,64,768]{2,1,0:T(8,128)(2,1)S(1)} %pad_maximum_fusion.8), channel_id=1, source_target_pairs={{0,8},{1,9},{2,3},{3,2},{4,12},{5,13},{6,7},{7,6},{8,0},{9,1},{10,... | collective-permute-start | bytes 1179656 | tf_op jit(solution)/shard_map/ppermute | solution.py:96
  202.8 17.1 %collective-permute-start.9 = (bf16[2,48,3072]{2,1,0:T(8,128)(2,1)S(1)}, bf16[2,48,3072]{2,1,0:T(8,128)(2,1)S(1)}, u32[]{:S(2)}, u32[]{:S(2)}) collective-permute-start(bf16[2,48,3072]{2,1,0:T(8,128)(2,1)S(1)} %pad_maximum_fusion.6), channel_id=1, source_target_pairs={{0,8},{1,9},{2,6},{3,7},{4,12},{5,13},{6,2},{7,3},{8,0},{9,1},{10,... | collective-permute-start | bytes 1769480 | tf_op jit(solution)/shard_map/ppermute | solution.py:96
  204.0 10.9 %collective-permute-start.18 = (bf16[2,64,768]{2,1,0:T(8,128)(2,1)S(1)}, bf16[2,64,768]{2,1,0:T(8,128)(2,1)S(1)}, u32[]{:S(2)}, u32[]{:S(2)}) collective-permute-start(bf16[2,64,768]{2,1,0:T(8,128)(2,1)S(1)} %add_convert_fusion.26), channel_id=1, source_target_pairs={{0,1},{1,0},{2,6},{3,7},{4,5},{5,4},{6,2},{7,3},{8,9},{9,8},{10,14... | collective-permute-start | bytes 589832 | tf_op jit(solution)/shard_map/ppermute | solution.py:96
  210.0 29.2 %collective-permute-start.41 = (bf16[8,64,768]{2,1,0:T(8,128)(2,1)S(1)}, bf16[8,64,768]{2,1,0:T(8,128)(2,1)}, u32[]{:S(2)}, u32[]{:S(2)}) collective-permute-start(bf16[8,64,768]{2,1,0:T(8,128)(2,1)S(1)} %pad_maximum_fusion.5.near), channel_id=1, source_target_pairs={{0,4},{1,5},{2,10},{3,11},{4,0},{5,1},{6,14},{7,15},{8,12},{9,13},... | collective-permute-start | bytes 2359304 | tf_op jit(solution)/shard_map/ppermute | solution.py:96
  214.8 23.5 %collective-permute-start.3 = (bf16[384,768]{1,0:T(8,128)(2,1)S(1)}, bf16[384,768]{1,0:T(8,128)(2,1)S(1)}, u32[]{:S(2)}, u32[]{:S(2)}) collective-permute-start(bf16[384,768]{1,0:T(8,128)(2,1)S(1)} %get-tuple-element.73), channel_id=1, source_target_pairs={{0,1},{1,0},{2,3},{3,2},{4,5},{5,4},{6,7},{7,6},{8,9},{9,8},{10,11... | collective-permute-start | bytes 1769480 | tf_op jit(solution)/shard_map/ppermute | solution.py:96
  215.0 19.9 %collective-permute-start.19 = (bf16[4,64,768]{2,1,0:T(8,128)(2,1)S(1)}, bf16[4,64,768]{2,1,0:T(8,128)(2,1)S(1)}, u32[]{:S(2)}, u32[]{:S(2)}) collective-permute-start(bf16[4,64,768]{2,1,0:T(8,128)(2,1)S(1)} %pad_maximum_fusion.7), channel_id=1, source_target_pairs={{0,4},{1,5},{2,10},{3,11},{4,0},{5,1},{6,14},{7,15},{8,12},{9,13},... | collective-permute-start | bytes 1179656 | tf_op jit(solution)/shard_map/ppermute | solution.py:96
  216.9 22.2 %collective-permute-start.40 = (bf16[8,64,768]{2,1,0:T(8,128)(2,1)S(1)}, bf16[8,64,768]{2,1,0:T(8,128)(2,1)S(1)}, u32[]{:S(2)}, u32[]{:S(2)}) collective-permute-start(bf16[8,64,768]{2,1,0:T(8,128)(2,1)S(1)} %pad_maximum_fusion.5.near), channel_id=1, source_target_pairs={{0,2},{1,3},{2,0},{3,1},{4,6},{5,7},{6,4},{7,5},{8,10},{9,11},{10,... | collective-permute-start | bytes 2359304 | tf_op jit(solution)/shard_map/ppermute | solution.py:96
  217.0 21.3 %copy-start.20 = (bf16[8,64,768]{2,1,0:T(8,128)(2,1)}, bf16[8,64,768]{2,1,0:T(8,128)(2,1)S(1)}, u32[]{:S(2)}) copy-start(bf16[8,64,768]{2,1,0:T(8,128)(2,1)S(1)} %pad_maximum_fusion.4.near) | copy-start | bytes 2359300
  219.9 20.6 %collective-permute-start.31 = (bf16[8,64,768]{2,1,0:T(8,128)(2,1)S(1)}, bf16[8,64,768]{2,1,0:T(8,128)(2,1)}, u32[]{:S(2)}, u32[]{:S(2)}) collective-permute-start(bf16[8,64,768]{2,1,0:T(8,128)(2,1)S(1)} %pad_maximum_fusion.4.near), channel_id=1, source_target_pairs={{0,1},{1,0},{2,6},{3,7},{4,5},{5,4},{6,2},{7,3},{8,9},{9,8},{10,14... | collective-permute-start | bytes 2359304 | tf_op jit(solution)/shard_map/ppermute | solution.py:96
  234.9 17.3 %collective-permute-start.11 = (bf16[4,48,3072]{2,1,0:T(8,128)(2,1)}, bf16[4,48,3072]{2,1,0:T(8,128)(2,1)}, u32[]{:S(2)}, u32[]{:S(2)}) collective-permute-start(bf16[4,48,3072]{2,1,0:T(8,128)(2,1)} %pad_maximum_fusion.2.near), channel_id=1, source_target_pairs={{0,4},{1,5},{2,10},{3,11},{4,0},{5,1},{6,14},{7,15},{8,12},{9,13},... | collective-permute-start | bytes 3538952 | tf_op jit(solution)/shard_map/ppermute | solution.py:96
  239.1 2.3 collective-permute-start.30
  239.1 12.3 %collective-permute-start.21 = (bf16[8,64,768]{2,1,0:T(8,128)(2,1)}, bf16[8,64,768]{2,1,0:T(8,128)(2,1)}, u32[]{:S(2)}, u32[]{:S(2)}) collective-permute-start(bf16[8,64,768]{2,1,0:T(8,128)(2,1)} %pad_maximum_fusion.3.near), channel_id=1, source_target_pairs={{0,8},{1,9},{2,3},{3,2},{4,12},{5,13},{6,7},{7,6},{8,0},{9,1},{10,... | collective-permute-start | bytes 2359304 | tf_op jit(solution)/shard_map/ppermute | solution.py:96
  240.0 11.6 %collective-permute-start.42 = (bf16[8,64,768]{2,1,0:T(8,128)(2,1)}, bf16[8,64,768]{2,1,0:T(8,128)(2,1)}, u32[]{:S(2)}, u32[]{:S(2)}) collective-permute-start(bf16[8,64,768]{2,1,0:T(8,128)(2,1)} %collective-permute-done.41.far), channel_id=1, source_target_pairs={{0,2},{1,3},{2,0},{3,1},{4,6},{5,7},{6,4},{7,5},{8,10},{9,11},{10,... | collective-permute-start | bytes 2359304 | tf_op jit(solution)/shard_map/ppermute | solution.py:96
  240.5 38.0 %collective-permute-start.20 = (bf16[8,64,768]{2,1,0:T(8,128)(2,1)}, bf16[8,64,768]{2,1,0:T(8,128)(2,1)}, u32[]{:S(2)}, u32[]{:S(2)}) collective-permute-start(bf16[8,64,768]{2,1,0:T(8,128)(2,1)} %pad_maximum_fusion.3.near), channel_id=1, source_target_pairs={{0,2},{1,3},{2,0},{3,1},{4,6},{5,7},{6,4},{7,5},{8,10},{9,11},{10,... | collective-permute-start | bytes 2359304 | tf_op jit(solution)/shard_map/ppermute | solution.py:96
  242.3 28.7 %collective-permute-start.32 = (bf16[8,64,768]{2,1,0:T(8,128)(2,1)}, bf16[8,64,768]{2,1,0:T(8,128)(2,1)}, u32[]{:S(2)}, u32[]{:S(2)}) collective-permute-start(bf16[8,64,768]{2,1,0:T(8,128)(2,1)} %collective-permute-done.31.far), channel_id=1, source_target_pairs={{0,2},{1,3},{2,0},{3,1},{4,6},{5,7},{6,4},{7,5},{8,10},{9,11},{10,... | collective-permute-start | bytes 2359304 | tf_op jit(solution)/shard_map/ppermute | solution.py:96
  251.5 27.1 %collective-permute-start.22 = (bf16[8,64,768]{2,1,0:T(8,128)(2,1)}, bf16[8,64,768]{2,1,0:T(8,128)(2,1)}, u32[]{:S(2)}, u32[]{:S(2)}) collective-permute-start(bf16[8,64,768]{2,1,0:T(8,128)(2,1)} %collective-permute-done.21.far), channel_id=1, source_target_pairs={{0,2},{1,3},{2,0},{3,1},{4,6},{5,7},{6,4},{7,5},{8,10},{9,11},{10,... | collective-permute-start | bytes 2359304 | tf_op jit(solution)/shard_map/ppermute | solution.py:96
  251.7 41.0 %collective-permute-start.10 = (bf16[4,48,3072]{2,1,0:T(8,128)(2,1)}, bf16[4,48,3072]{2,1,0:T(8,128)(2,1)S(1)}, u32[]{:S(2)}, u32[]{:S(2)}) collective-permute-start(bf16[4,48,3072]{2,1,0:T(8,128)(2,1)} %pad_maximum_fusion.2.near), channel_id=1, source_target_pairs={{0,2},{1,3},{2,0},{3,1},{4,6},{5,7},{6,4},{7,5},{8,10},{9,11},{10,... | collective-permute-start | bytes 3538952 | tf_op jit(solution)/shard_map/ppermute | solution.py:96
  252.2 40.5 %collective-permute-start.12 = (bf16[4,48,3072]{2,1,0:T(8,128)(2,1)}, bf16[4,48,3072]{2,1,0:T(8,128)(2,1)S(1)}, u32[]{:S(2)}, u32[]{:S(2)}) collective-permute-start(bf16[4,48,3072]{2,1,0:T(8,128)(2,1)} %collective-permute-done.11.far), channel_id=1, source_target_pairs={{0,2},{1,3},{2,0},{3,1},{4,6},{5,7},{6,4},{7,5},{8,10},{9,11},{10,... | collective-permute-start | bytes 3538952 | tf_op jit(solution)/shard_map/ppermute | solution.py:96
  (55 other events, 204.3 us)

commit v2 on v1

--- a/solution.py
+++ b/solution.py
@@ -59,7 +59,8 @@
         ),
         out_shape=out_shape,
         input_output_aliases=aliases or {},
-        compiler_params=pltpu.CompilerParams(vmem_limit_bytes=vmem * MIB),
+        compiler_params=pltpu.CompilerParams(vmem_limit_bytes=28 * MIB),
+        cost_estimate=pl.CostEstimate(flops=1, bytes_accessed=1, transcendentals=0),
     )(scalars, *args)
 
 
@@ -77,9 +78,9 @@
 
 
 FF_ORDERS = (
-    (("x", "y", "z0", "z1"), ("z0", "x", "y", "z1")),
-    (("y", "z0", "x", "z1"), ("x", "y", "z0", "z1")),
-    (("z0", "x", "y", "z1"), ("y", "z0", "x", "z1")),
+    (("z0", "y", "x", "z1"), ("y", "x", "z0", "z1")),
+    (("x", "z0", "y", "z1"), ("z0", "y", "x", "z1")),
+    (("y", "x", "z0", "z1"), ("x", "z0", "y", "z1")),
 )
 QKV_ORDER = (("x", "z0", "z1"), ("z0", "x", "z1"))
 DP_BIT = {"c": 1, "x": 2, "z0": 4, "z1": 8}
@@ -115,25 +116,52 @@
     return (a.astype(f32) + b.astype(f32)).astype(bf16)
 
 
-def reduce_halves(keep, send, orders):
-    received = swap(send, "c")
+class Order:
+    def __init__(self):
+        self.last = None
+
+    def pin(self, *arrays):
+        if self.last is None:
+            return arrays
+        return lax.optimization_barrier((*arrays, self.last))[:-1]
+
+    def run(self, function, *arrays):
+        result = function(*self.pin(*arrays))
+        self.last = result[0] if isinstance(result, (tuple, list)) else result
+        return result
+
+    def swap(self, array, first, second=None):
+        return swap(self.pin(array)[0], first, second)
+
+
+def total(order, keep, send, orders, widen=None):
+    received = order.swap(send, "c")
+    yield
     count = len(orders[0])
     for step in range(count - 1):
         half = keep.shape[0] // 2
-        send = add(keep[half:], received[half:])
-        keep = add(keep[:half], received[:half])
-        received = swap(send, orders[0][step], orders[1][step])
-    keep = add(keep, received)
-    received = swap(keep, orders[0][-1], orders[1][-1])
-    return add(keep, received[::-1])
-
-
-def spread_halves(block, orders):
-    for step in range(len(orders[0]) - 2, 0, -1):
-        block = jnp.concatenate([block, swap(block, orders[0][step], orders[1][step])], 0)
-    other = swap(block, "c")
-    far = swap(block, orders[0][0], orders[1][0])
-    return block, far, other, swap(far, "c")
+        send = order.run(lambda k, r: add(k[half:], r[half:]), keep, received)
+        coming = order.swap(send, orders[0][step], orders[1][step])
+        keep = order.run(lambda k, r: add(k[:half], r[:half]), keep, received)
+        received = coming
+        yield
+    keep = order.run(add, keep, received)
+    received = order.swap(keep, orders[0][-1], orders[1][-1])
+    yield
+    block = order.run(lambda k, r: add(k, r[::-1]), keep, received)
+    if widen is not None:
+        received = order.swap(block, "y")
+        yield
+        block = order.run(widen, block, received)
+    for step in range(count - 2, 0, -1):
+        received = order.swap(block, orders[0][step], orders[1][step])
+        yield
+        block = order.run(lambda k, r: jnp.concatenate([k, r], 0), block, received)
+    far = order.swap(block, orders[0][0], orders[1][0])
+    other = order.swap(block, "c")
+    yield
+    far_other = order.swap(far, "c")
+    yield block, far, other, far_other
 
 
 def ln_qkv_kernel(s, tok, pos, gain, w, normed, qkv):
@@ -231,8 +259,15 @@
     return act, slope
 
 
-def ff_kernel(s, normed, normed_t, cot, up, down, out_in, back_in, keep, send, out, back):
+def ff_kernel(at, first, last, s, normed, normed_t, cot, up, down, *refs):
     step = pl.program_id(0)
+    if not first:
+        out_in, back_in, *refs = refs
+    if last:
+        resid2, gain, w_own, w_other, *refs = refs
+        keep, send, out_low, grad2, branch, g_own, g_other, out, back = refs
+    else:
+        keep, send, out, back = refs
     hidden = dot(normed[...], up[...])
     act, slope = gelu_and_slope(hidden)
     act = act.astype(bf16)
@@ -242,8 +277,8 @@
 
     @pl.when(step == 0)
     def _():
-        out[...] = out_in[...] + out_part
-        back[...] = back_in[...] + back_part
+        out[...] = out_part if first else out_in[...] + out_part
+        back[...] = back_part if first else back_in[...] + back_part
 
     @pl.when(step == 1)
     def _():
@@ -258,102 +293,94 @@
         rows_u = g_up.shape[0] // 16
         half = g_up.shape[1] // 2
         for block in range(16):
-            at = block ^ code
-            target[at, :rows_d, :] = g_down[block * rows_d : (block + 1) * rows_d]
+            to = block ^ code
+            target[to, :rows_d, :] = g_down[block * rows_d : (block + 1) * rows_d]
             part = g_up[block * rows_u : (block + 1) * rows_u]
-            target[at, rows_d:, : 2 * half] = part[:rows_d]
-            target[at, rows_d : rows_d + 16, 2 * half :] = part[rows_d:, :half]
-            target[at, rows_d + 16 :, 2 * half :] = part[rows_d:, half:]
+            target[to, rows_d:, : 2 * half] = part[:rows_d]
+            target[to, rows_d : rows_d + 16, 2 * half :] = part[rows_d:, :half]
+            target[to, rows_d + 16 :, 2 * half :] = part[rows_d:, half:]
 
     @pl.when(step == 0)
     def _():
-        store(send, s[2])
+        store(send, s[at + 1])
 
     @pl.when(step == 1)
     def _():
-        store(keep, s[1])
-
-
-def ff_chunk(scalars, chunk, normed, normed_t, cot, up, down, out_in, back_in):
+        store(keep, s[at])
+        if last:
+            value = resid2[...]
+            out_low[...] = (value + out[...]).astype(bf16)
+            xhat, scale = normalize(value)
+            g = cot[...].astype(f32) + norm_backward(back[...], gain[...], xhat, scale)
+            grad2[...] = g
+            low = g.astype(bf16)
+            branch[...] = low
+            g_other[...] = dot(low, w_other[...], NT).astype(bf16)
+            g_own[...] = dot(low, w_own[...], NT).astype(bf16)
+
+
+def ff_chunk(scalars, chunk, last, normed, normed_t, cot, up, down, *more):
     rows, width = normed.shape
+    half = width // 2
     wide = 512
-
-    def half(i, s):
+    first = chunk == 0
+
+    def column(i, s):
         return 2 * chunk + (s[0] ^ (1 - i))
 
     full = spec((rows, width), lambda i, s: (0, 0))
+    part = spec((rows, half), lambda i, s: (0, 0))
     piece = spec((16, 64, width), lambda i, s: (0, 0, 0))
+    in_specs = [
+        whole(normed),
+        whole(normed_t),
+        whole(cot),
+        spec((width, wide), lambda i, s: (0, column(i, s))),
+        spec((wide, width), lambda i, s: (column(i, s), 0)),
+    ]
+    out_specs = [piece, piece]
+    out_shape = [shape((16, 64, width), bf16)] * 2
+    scratch = []
+    if not first:
+        in_specs += [full, full]
+    if last:
+        in_specs += [
+            full,
+            spec((1, width), lambda i, s: (0, 0)),
+            spec((half, width), lambda i, s: (s[1], 0)),
+            spec((half, width), lambda i, s: (1 - s[1], 0)),
+        ]
+        out_specs += [full, full, full, part, part]
+        out_shape += [shape((rows, width), t) for t in (bf16, f32, bf16)]
+        out_shape += [shape((rows, half), bf16)] * 2
+        scratch = [pltpu.VMEM((rows, width), f32)] * 2
+    else:
+        out_specs += [full, full]
+        out_shape += [shape((rows, width), f32)] * 2
     return call(
-        ff_kernel,
+        functools.partial(ff_kernel, 2 + 2 * chunk, first, last),
         (2,),
-        [
-            whole(normed),
-            whole(normed_t),
-            whole(cot),
-            spec((width, wide), lambda i, s: (0, half(i, s))),
-            spec((wide, width), lambda i, s: (half(i, s), 0)),
-            full,
-            full,
-        ],
-        [piece, piece, full, full],
-        [shape((16, 64, width), bf16)] * 2 + [shape((rows, width), f32)] * 2,
-        (normed, normed_t, cot, up, down, out_in, back_in),
+        in_specs,
+        out_specs,
+        out_shape,
+        (normed, normed_t, cot, up, down) + more,
         scalars,
         40,
-    )
-
-
-def mid_kernel(s, back, resid2, out_acc, cot, gain, w_own, w_other, out, grad2, branch, g_own, g_other):
-    value = resid2[...]
-    out[...] = (value + out_acc[...]).astype(bf16)
-    xhat, scale = normalize(value)
-    grad = cot[...].astype(f32) + norm_backward(back[...], gain[...], xhat, scale)
-    grad2[...] = grad
-    low = grad.astype(bf16)
-    branch[...] = low
-    g_other[...] = dot(low, w_other[...], NT).astype(bf16)
-    g_own[...] = dot(low, w_own[...], NT).astype(bf16)
-
-
-def middle(scalars, back, resid2, out_acc, cot, gain, w):
-    rows, width = resid2.shape
-    half = width // 2
-    full = spec((rows, width), lambda i, s: (0, 0))
-    part = spec((rows, half), lambda i, s: (0, 0))
-    return call(
-        mid_kernel,
-        (1,),
-        [
-            full,
-            full,
-            full,
-            full,
-            whole(gain),
-            spec((half, width), lambda i, s: (s[0], 0)),
-            spec((half, width), lambda i, s: (1 - s[0], 0)),
-        ],
-        [full, full, full, part, part],
-        [
-            shape((rows, width), bf16),
-            shape((rows, width), f32),
-            shape((rows, width), bf16),
-            shape((rows, half), bf16),
-            shape((rows, half), bf16),
-        ],
-        (back, resid2, out_acc, cot, gain, w, w),
-        scalars,
-        32,
-    )
-
-
-def attn_back_kernel(s, q_o, k_o, v_o, q_f, k_f, v_f, g_o, g_f, gq, gk, gv):
+        scratch,
+    )
+
+
+def attn_back_kernel(s, q, g, k_o, k_f, v_o, v_f, *refs):
+    gk_in, gv_in = refs[:2] if len(refs) == 5 else (None, None)
+    gq, gk, gv = refs[-3:]
     k = jnp.concatenate([k_o[...], k_f[...]], 0)
     v = jnp.concatenate([v_o[...], v_f[...]], 0)
-    q = jnp.concatenate([q_o[...], q_f[...]], 0).astype(f32) * HD**-0.5
-    g = jnp.concatenate([g_o[...], g_f[...]], 0).astype(f32)
     kt = (k.astype(f32) * HD**-0.5).astype(bf16).T
-    grad_q, grad_k, grad_v = [], 0.0, 0.0
-    for h, (qh, gh) in enumerate(zip(head_masks(q), head_masks(g))):
+    grad_q = []
+    grad_k, grad_v = (gk_in[...], gv_in[...]) if gk_in is not None else (0.0, 0.0)
+    q_heads = head_masks(q[...].astype(f32) * HD**-0.5)
+    g_heads = head_masks(g[...].astype(f32))
+    for h, (qh, gh) in enumerate(zip(q_heads, g_heads)):
         scores = dot(k, qh, NT)
         e = jnp.exp(scores - jnp.max(scores, 0, keepdims=True))
         probs = e * (1.0 / jnp.sum(e, 0, keepdims=True))
@@ -364,39 +391,41 @@
         grad_k = grad_k + dot(grad_s, qh)
         grad_q.append(dot(kt[h * HD : (h + 1) * HD], grad_s))
     gq[...] = jnp.concatenate(grad_q, 0).T.astype(bf16)
-    gk[...] = grad_k.astype(bf16)
-    gv[...] = grad_v.astype(bf16)
-
-
-def attention_back(scalars, qkv, qkv_far, g_own, g_far):
+    gk[...] = grad_k.astype(gk.dtype)
+    gv[...] = grad_v.astype(gv.dtype)
+
+
+def attention_back(scalars, far, qkv, qkv_far, grad, *so_far):
     rows, width = qkv.shape[0], qkv.shape[1] // 3
     pairs = width // PAIR
     mine = pairs // 2
 
     def column(part):
-        return spec((rows, PAIR), lambda i, s: (0, part * pairs + mine * s[0] + i))
+        return spec((rows, PAIR), lambda i, s: (0, part * pairs + mine * s[1] + i))
 
     block = spec((rows, PAIR), lambda i, s: (0, i))
-    out = spec((2 * rows, PAIR), lambda i, s: (0, i))
+    both = spec((2 * rows, PAIR), lambda i, s: (0, i))
+    dtype = bf16 if so_far else f32
     return call(
         attn_back_kernel,
         (mine,),
-        [column(0), column(1), column(2)] * 2 + [block, block],
-        [out] * 3,
-        [shape((2 * rows, width // 2), bf16)] * 3,
-        (qkv, qkv, qkv, qkv_far, qkv_far, qkv_far, g_own, g_far),
+        [column(0), block, column(1), column(1), column(2), column(2)] + [both] * len(so_far),
+        [block, both, both],
+        [shape((rows, width // 2), bf16)] + [shape((2 * rows, width // 2), dtype)] * 2,
+        (qkv_far if far else qkv, grad, qkv, qkv_far, qkv, qkv_far) + so_far,
         scalars,
         48,
     )
 
 
-def joint_kernel(s, n_own, n_far, gq, gk, gv, att, branch, keep, send):
+def joint_kernel(s, n_own, n_far, gq_o, gq_f, gk, gv, att, branch, keep, send):
     step = pl.program_id(0)
+    gq = jnp.concatenate([gq_o[...], gq_f[...]], 0)
     n = jnp.concatenate([n_own[...], n_far[...]], 0)
-    cols = gq.shape[1]
+    cols = gk.shape[1]
 
     def fill(target, code):
-        tiles = [dot(n, g[...], TN).astype(bf16) for g in (gq, gk, gv)]
+        tiles = [dot(n, g, TN).astype(bf16) for g in (gq, gk[...], gv[...])]
         tiles.append(dot(att[...], branch[...], TN).astype(bf16))
         rows = tiles[0].shape[0] // 8
         for block in range(8):
@@ -407,14 +436,14 @@
 
     @pl.when(step == 0)
     def _():
-        fill(send, s[2])
+        fill(send, s[9])
 
     @pl.when(step == 1)
     def _():
-        fill(keep, s[1])
-
-
-def joint_grads(scalars, n_own, n_far, gq, gk, gv, att, branch):
+        fill(keep, s[8])
+
+
+def joint_grads(scalars, n_own, n_far, gq, gq_far, gk, gv, att, branch):
     rows, width = n_own.shape
     half = width // 2
     feature = spec((rows, half), lambda i, s: (0, s[0] ^ (1 - i)))
@@ -423,42 +452,42 @@
     return call(
         joint_kernel,
         (2,),
-        [feature, feature, whole(gq), whole(gk), whole(gv), feature, whole(branch)],
+        [feature, feature, whole(gq), whole(gq), whole(gk), whole(gv), feature, whole(branch)],
         [piece, piece],
         [shape((8, half // 8, cols), bf16)] * 2,
-        (n_own, n_far, gq, gk, gv, att, branch),
+        (n_own, n_far, gq, gq_far, gk, gv, att, branch),
         scalars,
         32,
     )
 
 
-def back_qkv_kernel(s, gq, gk, gv, wq, wk, wv, own, far):
+def back_qkv_kernel(s, gq_o, gq_f, gk, gv, wq, wk, wv, own, far):
     rows = own.shape[0]
 
-    def part(at):
-        total = dot(gq[pl.ds(at, rows)], wq[...], NT)
+    def part(gq, at):
+        total = dot(gq[...], wq[...], NT)
         total += dot(gk[pl.ds(at, rows)], wk[...], NT)
         return total + dot(gv[pl.ds(at, rows)], wv[...], NT)
 
-    far[...] = part(rows).astype(bf16)
-    own[...] = part(0)
-
-
-def back_qkv(scalars, gq, gk, gv, w):
-    rows, half = gq.shape[0] // 2, gq.shape[1]
+    far[...] = part(gq_f, rows).astype(bf16)
+    own[...] = part(gq_o, 0)
+
+
+def back_qkv(scalars, gq, gq_far, gk, gv, w):
+    rows, half = gq.shape
     width = 2 * half
 
     def column(part):
-        return spec((width, half), lambda i, s: (0, 2 * part + s[0]))
+        return spec((width, half), lambda i, s: (0, 2 * part + s[1]))
 
     full = spec((rows, width), lambda i, s: (0, 0))
     return call(
         back_qkv_kernel,
         (1,),
-        [whole(gq), whole(gk), whole(gv), column(0), column(1), column(2)],
+        [whole(gq), whole(gq), whole(gk), whole(gv), column(0), column(1), column(2)],
         [full, full],
         [shape((rows, width), f32), shape((rows, width), bf16)],
-        (gq, gk, gv, w, w, w),
+        (gq, gq_far, gk, gv, w, w, w),
         scalars,
         32,
     )
@@ -484,10 +513,10 @@
     )
 
 
-def unpack_ff_kernel(s, near, far, *refs):
+def unpack_ff_kernel(at, s, near, far, *refs):
     down, up = refs[-2:]
     step = pl.program_id(0)
-    low = s[1] & 7
+    low = s[at] & 7
 
     def unpack(source):
         for block in range(8):
@@ -507,18 +536,23 @@
         unpack(far)
 
 
-def unpack_ff(scalars, chunk, near, far, width, hidden, so_far):
+def unpack_ff(scalars, chunk, other, near, far, width, hidden, so_far):
+    at = 2 + 2 * chunk + other
+
     def side(i, s):
-        return i ^ (s[1] // 8)
+        return i ^ (s[at] // 8)
+
+    def half(s):
+        return 2 * chunk + (s[0] ^ other)
 
     any_spec = pl.BlockSpec(memory_space=pl.ANY)
     return call(
-        unpack_ff_kernel,
+        functools.partial(unpack_ff_kernel, at),
         (2,),
         [whole(near), whole(far)] + [any_spec] * len(so_far),
         [
-            spec((256, width), lambda i, s: (2 * (2 * chunk + s[0]) + side(i, s), 0)),
-            spec((width // 2, 512), lambda i, s: (side(i, s), 2 * chunk + s[0])),
+            spec((256, width), lambda i, s: (2 * half(s) + side(i, s), 0)),
+            spec((width // 2, 512), lambda i, s: (side(i, s), half(s))),
         ],
         [shape((hidden, width), f32), shape((width, hidden), f32)],
         (near, far) + tuple(so_far),
@@ -528,11 +562,11 @@
     )
 
 
-def unpack_qkv_kernel(s, near, far, *refs):
+def unpack_qkv_kernel(at, s, near, far, *refs):
     joint, proj = refs[-2:]
     step = pl.program_id(0)
-    low = s[1] & 3
-    mine = s[2]
+    low = s[at] & 3
+    mine = s[1]
 
     def unpack(source):
         half = source.shape[2] // 8
@@ -555,13 +589,15 @@
         unpack(far)
 
 
-def unpack_qkv(scalars, near, far, width, so_far):
+def unpack_qkv(scalars, other, near, far, width, so_far):
+    at = 8 + other
+
     def row(i, s):
-        return 2 * s[0] + (i ^ (s[1] // 4))
+        return 2 * (s[0] ^ other) + (i ^ (s[at] // 4))
 
     any_spec = pl.BlockSpec(memory_space=pl.ANY)
     return call(
-        unpack_qkv_kernel,
+        functools.partial(unpack_qkv_kernel, at),
         (2,),
         [whole(near), whole(far)] + [any_spec] * len(so_far),
         [
@@ -581,63 +617,91 @@
     rows, width = tok.shape
     hidden = w_up.shape[1]
     gain1, gain2 = ln1_gain[None], ln2_gain[None]
-    core = lax.axis_index("dp") & 1
-    head_half = lax.axis_index("blk")
-    ints = lambda *values: jnp.stack([jnp.int32(v) for v in values])
-    none = ints(0)
-    heads = ints(head_half)
-
+    scalars = [lax.axis_index("dp") & 1, lax.axis_index("blk")]
+    for orders in FF_ORDERS + (QKV_ORDER,):
+        scalars.extend(places(orders))
+    scalars = jnp.stack([jnp.int32(v) for v in scalars])
+
+    order = Order()
+    run = order.run
     vis_far = swap(visible, "y")[0]
     tok_far = swap(tok, "y")
     pos = position_table(visible[0], width)
     pos_far = position_table(vis_far, width)
-    normed1, qkv = ln_qkv(none, tok, pos, gain1, w_qkv)
-    normed1_far, qkv_far = ln_qkv(none, tok_far, pos_far, gain1, w_qkv)
-    attended = attention(none, qkv, qkv_far)
-    resid2, normed2, normed2_t = project(none, attended, w_proj, tok, pos, gain2)
-
-    out_acc = jnp.zeros((rows, width), f32)
-    back = jnp.zeros((rows, width), f32)
-    pieces = []
-    for chunk, orders in enumerate(FF_ORDERS):
-        own_code, other_code = places(orders)
-        keep, send, out_acc, back = ff_chunk(
-            ints(core, own_code, other_code), chunk, normed2, normed2_t, cot, w_up, w_down, out_acc, back
+    normed1, qkv = run(functools.partial(ln_qkv, scalars), tok, pos, gain1, w_qkv)
+    normed1_far, qkv_far = run(functools.partial(ln_qkv, scalars), tok_far, pos_far, gain1, w_qkv)
+    attended = run(functools.partial(attention, scalars), qkv, qkv_far)
+    resid2, normed2, normed2_t = run(functools.partial(project, scalars), attended, w_proj, tok, pos, gain2)
+
+    streams, near = [], [None] * 4
+
+    def go(*which):
+        for i in which:
+            near[i] = next(streams[i], near[i])
+
+    def feed_forward(chunk, *more):
+        keep, send, *rest = run(
+            functools.partial(ff_chunk, scalars, chunk, chunk == 2),
+            normed2, normed2_t, cot, w_up, w_down, *more,
         )
-        pieces.append((keep, send))
-    out, grad2, branch, g_own, g_other = middle(heads, back, resid2, out_acc, cot, gain2, w_proj)
-    g_far = swap(g_other, "y")
-
-    summed = [reduce_halves(*pair, orders) for pair, orders in zip(pieces, FF_ORDERS)]
-    gathered = [spread_halves(block, orders) for block, orders in zip(summed, FF_ORDERS)]
-
-    gq, gk, gv = attention_back(heads, qkv, qkv_far, g_own, g_far)
-    own_code, other_code = places(QKV_ORDER)
-    keep, send = joint_grads(
-        ints(core, own_code, other_code), normed1, normed1_far, gq, gk, gv, attended, branch
-    )
-    back_own, back_far = back_qkv(heads, gq, gk, gv, w_qkv)
-    back_far = swap(back_far, "y")
-    block = reduce_halves(keep, send, QKV_ORDER)
-    other = swap(block, "y")
+        streams.append(total(order, keep, send, FF_ORDERS[chunk]))
+        return rest
+
+    sums = feed_forward(0)
+    go(0)
+    sums = feed_forward(1, *sums)
+    go(0, 1)
+    out, grad2, branch, g_own, g_other = feed_forward(2, *sums, resid2, gain2, w_proj, w_proj)
+    g_far = order.swap(g_other, "y")
+    go(0, 1, 2)
+    gq, *sums = run(functools.partial(attention_back, scalars, False), qkv, qkv_far, g_own)
+    go(0, 1, 2)
+    gq_far, gk, gv = run(functools.partial(attention_back, scalars, True), qkv, qkv_far, g_far, *sums)
+    go(0, 1, 2)
+    keep, send = run(
+        functools.partial(joint_grads, scalars),
+        normed1, normed1_far, gq, gq_far, gk, gv, attended, branch,
+    )
     cut = 3 * (width // 2)
-    block = jnp.concatenate(
-        [block[..., :cut], other[..., :cut], add(block[..., cut:], other[..., cut:])], -1
-    )
-    joint_pieces = spread_halves(block, QKV_ORDER)
-
-    d_tokens = token_grad(none, back_own, back_far, tok, pos, gain1, grad2)
+
+    def widen(mine, theirs):
+        proj = add(mine[..., cut:], theirs[..., cut:])
+        return jnp.concatenate([mine[..., :cut], theirs[..., :cut], proj], -1)
+
+    streams.append(total(order, keep, send, QKV_ORDER, widen))
+    go(3, 0, 1, 2)
+    back_own, back_far = run(functools.partial(back_qkv, scalars), gq, gq_far, gk, gv, w_qkv)
+    back_far = order.swap(back_far, "y")
+    go(3, 0, 1, 2)
+    go(3, 0, 1, 2)
+    go(3, 0, 1, 2)
+    d_tokens = run(functools.partial(token_grad, scalars), back_own, back_far, tok, pos, gain1, grad2)
+    go(3, 0, 1, 2)
 
     ff = ()
-    for chunk, orders in enumerate(FF_ORDERS):
-        own_code, other_code = places(orders)
-        near, far, near_other, far_other = gathered[chunk]
-        ff = unpack_ff(ints(core, own_code), chunk, near, far, width, hidden, ff)
-        ff = unpack_ff(ints(1 - core, other_code), chunk, near_other, far_other, width, hidden, ff)
-    own_code, other_code = places(QKV_ORDER)
-    near, far, near_other, far_other = joint_pieces
-    qkvp = unpack_qkv(ints(core, own_code, head_half), near, far, width, ())
-    qkvp = unpack_qkv(ints(1 - core, other_code, head_half), near_other, far_other, width, qkvp)
+
+    def finish(chunk, other):
+        nonlocal ff
+        ff = run(
+            lambda a, b, *f: unpack_ff(scalars, chunk, other, a, b, width, hidden, f),
+            near[chunk][2 * other], near[chunk][2 * other + 1], *ff,
+        )
+
+    go(3, 0, 1, 2)
+    finish(0, 0)
+    go(3, 1, 2)
+    finish(0, 1)
+    finish(1, 0)
+    finish(2, 0)
+    finish(1, 1)
+    finish(2, 1)
+    go(3)
+    qkvp = ()
+    for other in range(2):
+        qkvp = run(
+            lambda a, b, *f: unpack_qkv(scalars, other, a, b, width, f),
+            near[3][2 * other], near[3][2 * other + 1], *qkvp,
+        )
     d_down, d_up = ff
     d_qkv, d_proj = qkvp
     d_gain1 = jnp.sum(w_qkv.astype(f32) * d_qkv, 1) / ln1_gain

time: 305 us -> 242 us (0.79)
  local copies, waits for them, and re-layouts: 31.9 us -> 3.88 us
  waiting for transfers between devices: 104 us -> 86.7 us
  Pallas kernels: 97.1 us -> 89.7 us
  starting transfers between devices: 39.6 us -> 33.4 us
  other arithmetic: 25.7 us -> 22.4 us
    unnamed x120 -> x39, local copies, waits for them, and re-layouts: 30.4 us -> 2.2 us
    ppermute x43, waiting for transfers between devices: 104 us -> 86.7 us  [swap(): return lax.ppermute(array, AXES, pairs)]
    pallas_call x20, Pallas kernels: 97.1 us -> 89.7 us  [call(): pl.pallas_call(kernel, grid_spec=pltpu.PrefetchScalarGridSpec(num_scalar_...]
    ppermute x43, starting transfers between devices: 39.6 us -> 33.4 us  [swap(): return lax.ppermute(array, AXES, pairs)]
    convert_element_type x20 -> x31, other arithmetic: 7.54 us -> 7.38 us  [add(): return (a.astype(f32) + b.astype(f32)).astype(bf16)]
  transfers between devices with their start and end apart: 43 -> 43, of which waited for: 17 -> 18; matrix products, arithmetic and copies ran while one was open for 8% -> 7% of each run, Pallas kernels for 24% -> 26%
where the time goes in v2:
time: 242 us; the launch traced here: 238 us
  Pallas kernels  89.7 us (37%)
  waiting for transfers between devices  86.7 us (36%)
  starting transfers between devices  33.4 us (14%)
  other arithmetic  22.4 us (9%)
  local copies, waits for them, and re-layouts  3.88 us (2%)
    pallas_call x20, Pallas kernels, call(): pl.pallas_call(kernel, grid_spec=pltpu.PrefetchScalarGridSpec(num_scalar_...  89.7 us
    ppermute x43, waiting for transfers between devices, swap(): return lax.ppermute(array, AXES, pairs)  86.7 us
    ppermute x43, starting transfers between devices, swap(): return lax.ppermute(array, AXES, pairs)  33.4 us
    convert_element_type x31, other arithmetic, add(): return (a.astype(f32) + b.astype(f32)).astype(bf16)  7.38 us
    reduce_sum x1, other arithmetic, fast(): d_gain2 = jnp.sum(w_up.astype(f32) * d_up, 1) / ln2_gain  4.84 us
  transfers between devices with their start and end apart: 43, of which 18 were waited for; matrix products, arithmetic and copies ran while one was open for 7% of the time, Pallas kernels for 26%

profile of v2, /device:TPU:0, one launch (start us, length us, event | category | flops | bytes accessed | tf_op | source)
XLA Modules:
  0.0 238.0 jit_solution(13079518619783252804)
XLA Ops:
  0.6 3.0 %collective-permute-start.1 = (s32[1,384]{1,0:T(1,128)}, s32[1,384]{1,0:T(1,128)S(1)}, u32[]{:S(2)}, u32[]{:S(2)}) collective-permute-start(s32[1,384]{1,0:T(1,128)} %param.10), channel_id=1, source_target_pairs={{0,1},{1,0},{2,3},{3,2},{4,5},{5,4},{6,7},{7,6},{8,9},{9,8},{10,11... | collective-permute-start | bytes 4616 | tf_op jit(solution)/shard_map/ppermute | solution.py:97
  6.0 4.2 %multiply_sine_fusion = (f32[384,384]{1,0:T(8,128)S(1)}, f32[384,384]{1,0:T(8,128)S(1)}, f32[384,384]{1,0:T(8,128)S(1)}, f32[384,384]{1,0:T(8,128)S(1)}) fusion(f32[384]{0:T(512)S(1)} %convert_reduce_fusion, f32[384]{0:T(512)S(1)} %multiply_exponential_fusion, f32[384]{0:T(512)S(1)} %convert_reduce_fusion.1), kind=kLoop, calls=%fused_computation.13 | loop fusion | flops 294912 | bytes 2363904 | tf_op jit(solution)/shard_map/sin | solution.py:33
  11.2 3.4 %shard_map.152 = (bf16[384,768]{1,0:T(8,128)(2,1)S(1)}, bf16[384,2304]{1,0:T(8,128)(2,1)S(1)}) custom-call(s32[10]{0:T(128)S(1)} %stack.43.s, bf16[384,768]{1,0:T(8,128)(2,1)S(1)} %bitcast.24, f32[384,768]{1,0:T(8,128)S(1)} %pad_maximum_fusion.pos, f32[1,768]{1,0:T(1,128)S(1)} %broadcast_in_dim.16.gain, bf16[768,2304]{1,0:T(8,128)(2,1)S(1)} %copy-done), custom_call_target="tpu_custom_call" | custom-call | flops 1 | bytes 1 | tf_op jit(solution)/shard_map/pallas_call | solution.py:51
  14.7 3.9 %collective-permute-done.tok = bf16[384,768]{1,0:T(8,128)(2,1)S(1)} collective-permute-done((bf16[384,768]{1,0:T(8,128)(2,1)}, bf16[384,768]{1,0:T(8,128)(2,1)S(1)}, u32[]{:S(2)}, u32[]{:S(2)}) %collective-permute-start) | collective-permute-done | bytes 589856 | tf_op jit(solution)/shard_map/ppermute | solution.py:97
  18.7 3.2 %shard_map.153 = (bf16[384,768]{1,0:T(8,128)(2,1)S(1)}, bf16[384,2304]{1,0:T(8,128)(2,1)S(1)}) custom-call(s32[10]{0:T(128)S(1)} %stack.43.s, bf16[384,768]{1,0:T(8,128)(2,1)S(1)} %collective-permute-done.tok, f32[384,768]{1,0:T(8,128)S(1)} %pad_maximum_fusion.1.pos, f32[1,768]{1,0:T(1,128)S(1)} %broadcast_in_dim.16.gain, bf16[768,2304]{1,0:T(8,128)(2,1)S(1)} %copy-done), custom_call_target="tpu_custom_call" | custom-call | flops 1 | bytes 1 | tf_op jit(solution)/shard_map/pallas_call | solution.py:51
  22.0 8.5 %shard_map.154.att = bf16[384,768]{1,0:T(8,128)(2,1)S(1)} custom-call(s32[10]{0:T(128)S(1)} %stack.43.s, bf16[384,2304]{1,0:T(8,128)(2,1)S(1)} %get-tuple-element.351.q.k_own.v_own.k_o.v_o, bf16[384,2304]{1,0:T(8,128)(2,1)S(1)} %get-tuple-element.351.q.k_own.v_own.k_o.v_o, bf16[384,2304]{1,0:T(8,128)(2,1)S(1)} %get-tuple-element.351.q.k_own.v_own.k_o.v_o, ...), custom_call_target="tpu_custom_call" | custom-call | flops 1 | bytes 1 | tf_op jit(solution)/shard_map/pallas_call | solution.py:51
  30.5 1.6 shard_map.155
  33.2 7.6 %shard_map.156 = (bf16[16,64,768]{2,1,0:T(8,128)(2,1)S(1)}, bf16[16,64,768]{2,1,0:T(8,128)(2,1)}, f32[384,768]{1,0:T(8,128)S(1)}, f32[384,768]{1,0:T(8,128)S(1)}) custom-call(s32[10]{0:T(128)S(1)} %stack.43.s, bf16[384,768]{1,0:T(8,128)(2,1)S(1)} %get-tuple-element.300.normed, bf16[768,384]{1,0:T(8,128)(2,1)S(1)} %get-tuple-element.301.normed_t, ...), custom_call_target="tpu_custom_call" | custom-call | flops 1 | bytes 1 | tf_op jit(solution)/shard_map/pallas_call | solution.py:51
  40.8 7.7 %shard_map.157 = (bf16[16,64,768]{2,1,0:T(8,128)(2,1)S(1)}, bf16[16,64,768]{2,1,0:T(8,128)(2,1)}, f32[384,768]{1,0:T(8,128)S(1)}, f32[384,768]{1,0:T(8,128)S(1)}) custom-call(s32[10]{0:T(128)S(1)} %stack.43.s, bf16[384,768]{1,0:T(8,128)(2,1)S(1)} %get-tuple-element.300.normed, bf16[768,384]{1,0:T(8,128)(2,1)S(1)} %get-tuple-element.301.normed_t, ...), custom_call_target="tpu_custom_call" | custom-call | flops 1 | bytes 1 | tf_op jit(solution)/shard_map/pallas_call | solution.py:51
  51.9 1.6 collective-permute-start.4
  53.5 9.0 %shard_map.158 = (bf16[16,64,768]{2,1,0:T(8,128)(2,1)S(1)}, bf16[16,64,768]{2,1,0:T(8,128)(2,1)S(1)}, bf16[384,768]{1,0:T(8,128)(2,1)}, f32[384,768]{1,0:T(8,128...) custom-call(s32[10]{0:T(128)S(1)} %stack.43.s, ...), custom_call_target="tpu_custom_call" | custom-call | flops 1 | bytes 1 | tf_op jit(solution)/shard_map/pallas_call | solution.py:51
  62.4 1.5 collective-permute-done.4
  67.1 1.6 collective-permute-start.7
  68.7 1.5 collective-permute-start.5
  70.3 9.6 %shard_map.159 = (bf16[384,384]{1,0:T(8,128)(2,1)S(1)}, f32[768,384]{1,0:T(8,128)S(1)}, f32[768,384]{1,0:T(8,128)S(1)}) custom-call(s32[10]{0:T(128)S(1)} %stack.43.s, bf16[384,2304]{1,0:T(8,128)(2,1)S(1)} %get-tuple-element.351.q.k_own.v_own.k_o.v_o, bf16[384,384]{1,0:T(8,128)(2,1)S(1)} %get-tuple-element.326.g, ...), custom_call_target="tpu_custom_call" | custom-call | flops 1 | bytes 1 | tf_op jit(solution)/shard_map/pallas_call | solution.py:51
  80.5 1.8 collective-permute-done.7
  82.5 1.7 collective-permute-start.10
  85.2 9.8 %shard_map.160 = (bf16[384,384]{1,0:T(8,128)(2,1)S(1)}, bf16[768,384]{1,0:T(8,128)(2,1)S(1)}, bf16[768,384]{1,0:T(8,128)(2,1)S(1)}) custom-call(s32[10]{0:T(128)S(1)} %stack.43.s, bf16[384,2304]{1,0:T(8,128)(2,1)S(1)} %get-tuple-element.349.k_far.v_far.k_f.v_f.q, bf16[384,384]{1,0:T(8,128)(2,1)S(1)} %collective-permute-done.5.g, ...), custom_call_target="tpu_custom_call" | custom-call | flops 1 | bytes 1 | tf_op jit(solution)/shard_map/pallas_call | solution.py:51
  96.7 4.2 %shard_map.161 = (bf16[8,48,1920]{2,1,0:T(8,128)(2,1)S(1)}, bf16[8,48,1920]{2,1,0:T(8,128)(2,1)S(1)}) custom-call(s32[10]{0:T(128)S(1)} %stack.43.s, bf16[384,768]{1,0:T(8,128)(2,1)S(1)} %get-tuple-element.374.n_own, bf16[384,768]{1,0:T(8,128)(2,1)S(1)} %copy-done.7, bf16[384,384]{1,0:T(8,128)(2,1)S(1)} %get-tuple-element.391.gq_o, ...), custom_call_target="tpu_custom_call" | custom-call | flops 1 | bytes 1 | tf_op jit(solution)/shard_map/pallas_call | solution.py:51
  101.0 2.7 %collective-permute-start.14 = (bf16[2,64,768]{2,1,0:T(8,128)(2,1)S(1)}, bf16[2,64,768]{2,1,0:T(8,128)(2,1)S(1)}, u32[]{:S(2)}, u32[]{:S(2)}) collective-permute-start(bf16[2,64,768]{2,1,0:T(8,128)(2,1)S(1)} %add_convert_fusion.27), channel_id=1, source_target_pairs={{0,16},{1,17},{2,18},{3,19},{4,20},{5,21},{6,22},{7,23},{8,24},{9,... | collective-permute-start | bytes 589832 | tf_op jit(solution)/shard_map/ppermute | solution.py:97
  104.7 8.6 %collective-permute-done.14 = bf16[2,64,768]{2,1,0:T(8,128)(2,1)S(1)} collective-permute-done((bf16[2,64,768]{2,1,0:T(8,128)(2,1)S(1)}, bf16[2,64,768]{2,1,0:T(8,128)(2,1)S(1)}, u32[]{:S(2)}, u32[]{:S(2)}) %collective-permute-start.14) | collective-permute-done | bytes 196640 | tf_op jit(solution)/shard_map/ppermute | solution.py:97
  113.3 1.5 collective-permute-start.12
  115.5 5.5 %collective-permute-done.12 = bf16[4,64,768]{2,1,0:T(8,128)(2,1)S(1)} collective-permute-done((bf16[4,64,768]{2,1,0:T(8,128)(2,1)S(1)}, bf16[4,64,768]{2,1,0:T(8,128)(2,1)S(1)}, u32[]{:S(2)}, u32[]{:S(2)}) %collective-permute-start.12) | collective-permute-done | bytes 393248 | tf_op jit(solution)/shard_map/ppermute | solution.py:97
  121.2 2.6 %shard_map.162 = (f32[384,768]{1,0:T(8,128)S(1)}, bf16[384,768]{1,0:T(8,128)(2,1)S(1)}) custom-call(s32[10]{0:T(128)S(1)} %stack.43.s, bf16[384,384]{1,0:T(8,128)(2,1)S(1)} %get-tuple-element.391.gq_o, bf16[384,384]{1,0:T(8,128)(2,1)S(1)} %get-tuple-element.392.gq_f, bf16[768,384]{1,0:T(8,128)(2,1)S(1)} %get-tuple-element.393.gk, ...), custom_call_target="tpu_custom_call" | custom-call | flops 1 | bytes 1 | tf_op jit(solution)/shard_map/pallas_call | solution.py:51
  127.0 1.5 collective-permute-done.16
  130.6 1.7 collective-permute-start.20
  132.3 10.2 %collective-permute-done.23 = bf16[4,48,1920]{2,1,0:T(8,128)(2,1)S(1)} collective-permute-done((bf16[4,48,1920]{2,1,0:T(8,128)(2,1)S(1)}, bf16[4,48,1920]{2,1,0:T(8,128)(2,1)S(1)}, u32[]{:S(2)}, u32[]{:S(2)}) %collective-permute-start.23) | collective-permute-done | bytes 737312 | tf_op jit(solution)/shard_map/ppermute | solution.py:97
  142.8 2.0 collective-permute-done.22
  144.8 2.0 collective-permute-done.21
  150.1 7.3 %collective-permute-done.26 = bf16[2,48,1920]{2,1,0:T(8,128)(2,1)S(1)} collective-permute-done((bf16[2,48,1920]{2,1,0:T(8,128)(2,1)S(1)}, bf16[2,48,1920]{2,1,0:T(8,128)(2,1)S(1)}, u32[]{:S(2)}, u32[]{:S(2)}) %collective-permute-start.26) | collective-permute-done | bytes 368672 | tf_op jit(solution)/shard_map/ppermute | solution.py:97
  157.6 13.0 %collective-permute-done.25 = bf16[4,64,768]{2,1,0:T(8,128)(2,1)S(1)} collective-permute-done((bf16[4,64,768]{2,1,0:T(8,128)(2,1)S(1)}, bf16[4,64,768]{2,1,0:T(8,128)(2,1)S(1)}, u32[]{:S(2)}, u32[]{:S(2)}) %collective-permute-start.25) | collective-permute-done | bytes 393248 | tf_op jit(solution)/shard_map/ppermute | solution.py:97
  170.7 2.0 collective-permute-done.24
  172.8 2.1 collective-permute-start.29
  174.9 2.4 %shard_map.163 = f32[384,768]{1,0:T(8,128)} custom-call(s32[10]{0:T(128)S(1)} %stack.43.s, f32[384,768]{1,0:T(8,128)S(1)} %get-tuple-element.438.own, bf16[384,768]{1,0:T(8,128)(2,1)S(1)} %collective-permute-done.15.far, bf16[384,768]{1,0:T(8,128)(2,1)S(1)} %bitcast.26, f32[384,768]{1,0:T(8,128)S(1)} %pad_maximum_fusion.pos, ...), custom_call_target="tpu_custom_call" | custom-call | flops 1 | bytes 1 | tf_op jit(solution)/shard_map/pallas_call | solution.py:51
  178.7 5.2 %collective-permute-done.29 = bf16[4,64,768]{2,1,0:T(8,128)(2,1)S(1)} collective-permute-done((bf16[4,64,768]{2,1,0:T(8,128)(2,1)S(1)}, bf16[4,64,768]{2,1,0:T(8,128)(2,1)S(1)}, u32[]{:S(2)}, u32[]{:S(2)}) %collective-permute-start.29) | collective-permute-done | bytes 393248 | tf_op jit(solution)/shard_map/ppermute | solution.py:97
  185.7 7.0 %collective-permute-done.31.far = bf16[8,64,768]{2,1,0:T(8,128)(2,1)S(1)} collective-permute-done((bf16[8,64,768]{2,1,0:T(8,128)(2,1)S(1)}, bf16[8,64,768]{2,1,0:T(8,128)(2,1)S(1)}, u32[]{:S(2)}, u32[]{:S(2)}) %collective-permute-start.31) | collective-permute-done | bytes 786464 | tf_op jit(solution)/shard_map/ppermute | solution.py:97
  193.1 2.4 shard_map.164
  195.5 9.9 %collective-permute-done.30 = bf16[2,48,3072]{2,1,0:T(8,128)(2,1)S(1)} collective-permute-done((bf16[2,48,3072]{2,1,0:T(8,128)(2,1)S(1)}, bf16[2,48,3072]{2,1,0:T(8,128)(2,1)S(1)}, u32[]{:S(2)}, u32[]{:S(2)}) %collective-permute-start.30) | collective-permute-done | bytes 589856 | tf_op jit(solution)/shard_map/ppermute | solution.py:97
  207.0 2.4 shard_map.165
  209.4 2.4 shard_map.166
  211.7 2.4 shard_map.167
  214.2 2.4 shard_map.168
  216.6 2.4 shard_map.169
  218.9 2.8 %collective-permute-done.33.far = bf16[4,48,3072]{2,1,0:T(8,128)(2,1)S(1)} collective-permute-done((bf16[4,48,3072]{2,1,0:T(8,128)(2,1)S(1)}, bf16[4,48,3072]{2,1,0:T(8,128)(2,1)S(1)}, u32[]{:S(2)}, u32[]{:S(2)}) %collective-permute-start.33) | collective-permute-done | bytes 1179680 | tf_op jit(solution)/shard_map/ppermute | solution.py:97
  221.7 4.8 %multiply_reduce_fusion = f32[768]{0:T(1024)S(1)} fusion(f32[768,3072]{1,0:T(8,128)} %get-tuple-element.256, bf16[768,3072]{1,0:T(8,128)(2,1)S(1)} %bitcast.15), kind=kLoop, calls=%fused_computation | loop fusion | flops 7077120 | bytes 14158848 | tf_op jit(solution)/shard_map/reduce_sum | solution.py:708
  227.2 3.0 %shard_map.170 = (f32[768,2304]{1,0:T(8,128)}, f32[768,768]{1,0:T(8,128)}) custom-call(s32[10]{0:T(128)S(1)} %stack.43.s, bf16[4,48,3072]{2,1,0:T(8,128)(2,1)S(1)} %constant_dynamic-update-slice_fusion.12.near, bf16[4,48,3072]{2,1,0:T(8,128)(2,1)S(1)} %collective-permute-done.33.far), custom_call_target="tpu_custom_call" | custom-call | flops 1 | bytes 1 | tf_op jit(solution)/shard_map/pallas_call | solution.py:51
  230.1 3.0 %shard_map.171 = (f32[768,2304]{1,0:T(8,128)}, f32[768,768]{1,0:T(8,128)}) custom-call(s32[10]{0:T(128)S(1)} %stack.43.s, bf16[4,48,3072]{2,1,0:T(8,128)(2,1)S(1)} %collective-permute-done.32.near, bf16[4,48,3072]{2,1,0:T(8,128)(2,1)S(1)} %collective-permute-done.42.far, ...), custom_call_target="tpu_custom_call", output_to_operand_aliasing={{0}: (3, {}), {1}: (4, {})} | custom-call | flops 1 | bytes 1 | tf_op jit(solution)/shard_map/pallas_call | solution.py:51
  233.1 3.9 %multiply_reduce_fusion.1 = f32[768]{0:T(1024)S(1)} fusion(f32[768,2304]{1,0:T(8,128)} %get-tuple-element.253, bf16[768,2304]{1,0:T(8,128)(2,1)S(1)} %copy-done), kind=kLoop, calls=%fused_computation.1 | loop fusion | flops 5307648 | bytes 10619904 | tf_op jit(solution)/shard_map/reduce_sum | solution.py:707
  (154 shorter events, 31.7 us)
Async XLA Ops:
  0.6 5.3 %collective-permute-start.1 = (s32[1,384]{1,0:T(1,128)}, s32[1,384]{1,0:T(1,128)S(1)}, u32[]{:S(2)}, u32[]{:S(2)}) collective-permute-start(s32[1,384]{1,0:T(1,128)} %param.10), channel_id=1, source_target_pairs={{0,1},{1,0},{2,3},{3,2},{4,5},{5,4},{6,7},{7,6},{8,9},{9,8},{10,11... | collective-permute-start | bytes 4616 | tf_op jit(solution)/shard_map/ppermute | solution.py:97
  3.7 15.0 %collective-permute-start = (bf16[384,768]{1,0:T(8,128)(2,1)}, bf16[384,768]{1,0:T(8,128)(2,1)S(1)}, u32[]{:S(2)}, u32[]{:S(2)}) collective-permute-start(bf16[384,768]{1,0:T(8,128)(2,1)} %bitcast.23), channel_id=1, source_target_pairs={{0,1},{1,0},{2,3},{3,2},{4,5},{5,4},{6,7},{7,6},{8,9},{9,8},{10,11... | collective-permute-start | bytes 1769480 | tf_op jit(solution)/shard_map/ppermute | solution.py:97
  18.7 14.5 %slice-start.2 = ((s8[4718592]{0:T(1024)(128)(4,1)}), s8[4194304]{0:T(1024)(128)(4,1)S(1)}, s32[]{:S(2)}) async-start(s8[4718592]{0:T(1024)(128)(4,1)} %bitcast.16), calls=%async_computation.2 | async-start | bytes 8388608
  21.9 8.6 %copy-start.6 = (bf16[384,768]{1,0:T(8,128)(2,1)}, bf16[384,768]{1,0:T(8,128)(2,1)S(1)}, u32[]{:S(2)}) copy-start(bf16[384,768]{1,0:T(8,128)(2,1)S(1)} %get-tuple-element.375.n_far) | copy-start | bytes 1769476
  21.9 11.2 %slice-start = ((s8[4718592]{0:T(1024)(128)(4,1)}), s8[4194304]{0:T(1024)(128)(4,1)S(1)}, s32[]{:S(2)}) async-start(s8[4718592]{0:T(1024)(128)(4,1)} %bitcast.14), calls=%async_computation | async-start | bytes 8388608
  21.9 11.2 %slice-start.1 = ((s8[4718592]{0:T(1024)(128)(4,1)}), s8[524288]{0:T(1024)(128)(4,1)S(1)}, s32[]{:S(2)}) async-start(s8[4718592]{0:T(1024)(128)(4,1)} %bitcast.14), calls=%async_computation.1 | async-start | bytes 1048576
  22.0 11.2 %slice-start.3 = ((s8[4718592]{0:T(1024)(128)(4,1)}), s8[524288]{0:T(1024)(128)(4,1)S(1)}, s32[]{:S(2)}) async-start(s8[4718592]{0:T(1024)(128)(4,1)} %bitcast.16), calls=%async_computation.3 | async-start | bytes 1048576
  40.8 7.7 %collective-permute-start.2 = (bf16[16,64,768]{2,1,0:T(8,128)(2,1)}, bf16[16,64,768]{2,1,0:T(8,128)(2,1)}, u32[]{:S(2)}, u32[]{:S(2)}) collective-permute-start(bf16[16,64,768]{2,1,0:T(8,128)(2,1)} %get-tuple-element.294), channel_id=1, source_target_pairs={{0,2},{1,3},{2,0},{3,1},{4,6},{5,7},{6,4},{7,5},{8,10},{9,11},{10,... | collective-permute-start | bytes 4718600 | tf_op jit(solution)/shard_map/ppermute | solution.py:97
  51.3 14.9 %collective-permute-start.3 = (bf16[16,64,768]{2,1,0:T(8,128)(2,1)}, bf16[16,64,768]{2,1,0:T(8,128)(2,1)S(1)}, u32[]{:S(2)}, u32[]{:S(2)}) collective-permute-start(bf16[16,64,768]{2,1,0:T(8,128)(2,1)} %get-tuple-element.314), channel_id=1, source_target_pairs={{0,2},{1,3},{2,0},{3,1},{4,6},{5,7},{6,4},{7,5},{8,10},{9,11},{10,... | collective-permute-start | bytes 4718600 | tf_op jit(solution)/shard_map/ppermute | solution.py:97
  51.9 12.1 %collective-permute-start.4 = (bf16[8,64,768]{2,1,0:T(8,128)(2,1)S(1)}, bf16[8,64,768]{2,1,0:T(8,128)(2,1)}, u32[]{:S(2)}, u32[]{:S(2)}) collective-permute-start(bf16[8,64,768]{2,1,0:T(8,128)(2,1)S(1)} %add_convert_fusion.5), channel_id=1, source_target_pairs={{0,8},{1,9},{2,3},{3,2},{4,12},{5,13},{6,7},{7,6},{8,0},{9,1},{10,... | collective-permute-start | bytes 2359304 | tf_op jit(solution)/shard_map/ppermute | solution.py:97
  66.6 17.7 %collective-permute-start.6 = (bf16[16,64,768]{2,1,0:T(8,128)(2,1)S(1)}, bf16[16,64,768]{2,1,0:T(8,128)(2,1)S(1)}, u32[]{:S(2)}, u32[]{:S(2)}) collective-permute-start(bf16[16,64,768]{2,1,0:T(8,128)(2,1)S(1)} %get-tuple-element.334), channel_id=1, source_target_pairs={{0,2},{1,3},{2,0},{3,1},{4,6},{5,7},{6,4},{7,5},{8,10},{9,11},{10,... | collective-permute-start | bytes 4718600 | tf_op jit(solution)/shard_map/ppermute | solution.py:97
  66.6 13.2 %collective-permute-start.8 = (bf16[4,64,768]{2,1,0:T(8,128)(2,1)S(1)}, bf16[4,64,768]{2,1,0:T(8,128)(2,1)S(1)}, u32[]{:S(2)}, u32[]{:S(2)}) collective-permute-start(bf16[4,64,768]{2,1,0:T(8,128)(2,1)S(1)} %add_convert_fusion.13), channel_id=1, source_target_pairs={{0,1},{1,0},{2,6},{3,7},{4,5},{5,4},{6,2},{7,3},{8,9},{9,8},{10,14... | collective-permute-start | bytes 1179656 | tf_op jit(solution)/shard_map/ppermute | solution.py:97
  67.1 15.3 %collective-permute-start.7 = (bf16[8,64,768]{2,1,0:T(8,128)(2,1)S(1)}, bf16[8,64,768]{2,1,0:T(8,128)(2,1)S(1)}, u32[]{:S(2)}, u32[]{:S(2)}) collective-permute-start(bf16[8,64,768]{2,1,0:T(8,128)(2,1)S(1)} %add_convert_fusion.3), channel_id=1, source_target_pairs={{0,4},{1,5},{2,10},{3,11},{4,0},{5,1},{6,14},{7,15},{8,12},{9,13},... | collective-permute-start | bytes 2359304 | tf_op jit(solution)/shard_map/ppermute | solution.py:97
  68.7 16.5 %collective-permute-start.5 = (bf16[384,384]{1,0:T(8,128)(2,1)S(1)}, bf16[384,384]{1,0:T(8,128)(2,1)S(1)}, u32[]{:S(2)}, u32[]{:S(2)}) collective-permute-start(bf16[384,384]{1,0:T(8,128)(2,1)S(1)} %get-tuple-element.330), channel_id=1, source_target_pairs={{0,1},{1,0},{2,3},{3,2},{4,5},{5,4},{6,7},{7,6},{8,9},{9,8},{10,11... | collective-permute-start | bytes 884744 | tf_op jit(solution)/shard_map/ppermute | solution.py:97
  79.9 15.2 %collective-permute-start.11 = (bf16[2,64,768]{2,1,0:T(8,128)(2,1)S(1)}, bf16[2,64,768]{2,1,0:T(8,128)(2,1)S(1)}, u32[]{:S(2)}, u32[]{:S(2)}) collective-permute-start(bf16[2,64,768]{2,1,0:T(8,128)(2,1)S(1)} %add_convert_fusion.29), channel_id=1, source_target_pairs={{0,4},{1,5},{2,10},{3,11},{4,0},{5,1},{6,14},{7,15},{8,12},{9,13},... | collective-permute-start | bytes 589832 | tf_op jit(solution)/shard_map/ppermute | solution.py:97
  82.5 12.7 %collective-permute-start.10 = (bf16[4,64,768]{2,1,0:T(8,128)(2,1)S(1)}, bf16[4,64,768]{2,1,0:T(8,128)(2,1)S(1)}, u32[]{:S(2)}, u32[]{:S(2)}) collective-permute-start(bf16[4,64,768]{2,1,0:T(8,128)(2,1)S(1)} %add_convert_fusion.11), channel_id=1, source_target_pairs={{0,8},{1,9},{2,3},{3,2},{4,12},{5,13},{6,7},{7,6},{8,0},{9,1},{10,... | collective-permute-start | bytes 1179656 | tf_op jit(solution)/shard_map/ppermute | solution.py:97
  84.4 12.1 %collective-permute-start.9 = (bf16[8,64,768]{2,1,0:T(8,128)(2,1)S(1)}, bf16[8,64,768]{2,1,0:T(8,128)(2,1)S(1)}, u32[]{:S(2)}, u32[]{:S(2)}) collective-permute-start(bf16[8,64,768]{2,1,0:T(8,128)(2,1)S(1)} %add_convert_fusion.1), channel_id=1, source_target_pairs={{0,1},{1,0},{2,6},{3,7},{4,5},{5,4},{6,2},{7,3},{8,9},{9,8},{10,14... | collective-permute-start | bytes 2359304 | tf_op jit(solution)/shard_map/ppermute | solution.py:97
  100.9 24.2 %collective-permute-start.19 = (bf16[8,48,1920]{2,1,0:T(8,128)(2,1)S(1)}, bf16[8,48,1920]{2,1,0:T(8,128)(2,1)S(1)}, u32[]{:S(2)}, u32[]{:S(2)}) collective-permute-start(bf16[8,48,1920]{2,1,0:T(8,128)(2,1)S(1)} %get-tuple-element.404), channel_id=1, source_target_pairs={{0,2},{1,3},{2,0},{3,1},{4,6},{5,7},{6,4},{7,5},{8,10},{9,11},{10,... | collective-permute-start | bytes 4423688 | tf_op jit(solution)/shard_map/ppermute | solution.py:97
  101.0 12.3 %collective-permute-start.14 = (bf16[2,64,768]{2,1,0:T(8,128)(2,1)S(1)}, bf16[2,64,768]{2,1,0:T(8,128)(2,1)S(1)}, u32[]{:S(2)}, u32[]{:S(2)}) collective-permute-start(bf16[2,64,768]{2,1,0:T(8,128)(2,1)S(1)} %add_convert_fusion.27), channel_id=1, source_target_pairs={{0,16},{1,17},{2,18},{3,19},{4,20},{5,21},{6,22},{7,23},{8,24},{9,... | collective-permute-start | bytes 589832 | tf_op jit(solution)/shard_map/ppermute | solution.py:97
  103.6 11.2 %collective-permute-start.13 = (bf16[2,64,768]{2,1,0:T(8,128)(2,1)S(1)}, bf16[2,64,768]{2,1,0:T(8,128)(2,1)S(1)}, u32[]{:S(2)}, u32[]{:S(2)}) collective-permute-start(bf16[2,64,768]{2,1,0:T(8,128)(2,1)S(1)} %add_convert_fusion.26), channel_id=1, source_target_pairs={{0,1},{1,0},{2,6},{3,7},{4,5},{5,4},{6,2},{7,3},{8,9},{9,8},{10,14... | collective-permute-start | bytes 589832 | tf_op jit(solution)/shard_map/ppermute | solution.py:97
  113.3 7.8 %collective-permute-start.12 = (bf16[4,64,768]{2,1,0:T(8,128)(2,1)S(1)}, bf16[4,64,768]{2,1,0:T(8,128)(2,1)S(1)}, u32[]{:S(2)}, u32[]{:S(2)}) collective-permute-start(bf16[4,64,768]{2,1,0:T(8,128)(2,1)S(1)} %add_convert_fusion.9), channel_id=1, source_target_pairs={{0,4},{1,5},{2,10},{3,11},{4,0},{5,1},{6,14},{7,15},{8,12},{9,13},... | collective-permute-start | bytes 1179656 | tf_op jit(solution)/shard_map/ppermute | solution.py:97
  114.8 12.1 %collective-permute-start.18 = (bf16[2,64,768]{2,1,0:T(8,128)(2,1)S(1)}, bf16[2,64,768]{2,1,0:T(8,128)(2,1)S(1)}, u32[]{:S(2)}, u32[]{:S(2)}) collective-permute-start(bf16[2,64,768]{2,1,0:T(8,128)(2,1)S(1)} %add_convert_fusion.24), channel_id=1, source_target_pairs={{0,4},{1,5},{2,10},{3,11},{4,0},{5,1},{6,14},{7,15},{8,12},{9,13},... | collective-permute-start | bytes 589832 | tf_op jit(solution)/shard_map/ppermute | solution.py:97
  115.5 11.5 %collective-permute-start.17 = (bf16[2,64,768]{2,1,0:T(8,128)(2,1)S(1)}, bf16[2,64,768]{2,1,0:T(8,128)(2,1)S(1)}, u32[]{:S(2)}, u32[]{:S(2)}) collective-permute-start(bf16[2,64,768]{2,1,0:T(8,128)(2,1)S(1)} %add_convert_fusion.23), channel_id=1, source_target_pairs={{0,16},{1,17},{2,18},{3,19},{4,20},{5,21},{6,22},{7,23},{8,24},{9,... | collective-permute-start | bytes 589832 | tf_op jit(solution)/shard_map/ppermute | solution.py:97
  121.1 7.4 %collective-permute-start.16 = (bf16[2,64,768]{2,1,0:T(8,128)(2,1)S(1)}, bf16[2,64,768]{2,1,0:T(8,128)(2,1)S(1)}, u32[]{:S(2)}, u32[]{:S(2)}) collective-permute-start(bf16[2,64,768]{2,1,0:T(8,128)(2,1)S(1)} %add_convert_fusion.22), channel_id=1, source_target_pairs={{0,8},{1,9},{2,3},{3,2},{4,12},{5,13},{6,7},{7,6},{8,0},{9,1},{10,... | collective-permute-start | bytes 589832 | tf_op jit(solution)/shard_map/ppermute | solution.py:97
  123.8 49.0 %collective-permute-start.15 = (bf16[384,768]{1,0:T(8,128)(2,1)S(1)}, bf16[384,768]{1,0:T(8,128)(2,1)S(1)}, u32[]{:S(2)}, u32[]{:S(2)}) collective-permute-start(bf16[384,768]{1,0:T(8,128)(2,1)S(1)} %get-tuple-element.398), channel_id=1, source_target_pairs={{0,1},{1,0},{2,3},{3,2},{4,5},{5,4},{6,7},{7,6},{8,9},{9,8},{10,11... | collective-permute-start | bytes 1769480 | tf_op jit(solution)/shard_map/ppermute | solution.py:97
  125.2 17.3 %collective-permute-start.23 = (bf16[4,48,1920]{2,1,0:T(8,128)(2,1)S(1)}, bf16[4,48,1920]{2,1,0:T(8,128)(2,1)S(1)}, u32[]{:S(2)}, u32[]{:S(2)}) collective-permute-start(bf16[4,48,1920]{2,1,0:T(8,128)(2,1)S(1)} %add_convert_fusion.7), channel_id=1, source_target_pairs={{0,4},{1,5},{2,10},{3,11},{4,0},{5,1},{6,14},{7,15},{8,12},{9,13},... | collective-permute-start | bytes 2211848 | tf_op jit(solution)/shard_map/ppermute | solution.py:97
  128.6 16.2 %collective-permute-start.22 = (bf16[4,64,768]{2,1,0:T(8,128)(2,1)S(1)}, bf16[4,64,768]{2,1,0:T(8,128)(2,1)S(1)}, u32[]{:S(2)}, u32[]{:S(2)}) collective-permute-start(bf16[4,64,768]{2,1,0:T(8,128)(2,1)S(1)} %constant_dynamic-update-slice_fusion), channel_id=1, source_target_pairs={{0,1},{1,0},{2,6},{3,7},{4,5},{5,4},{6,2},{7,3},{8,9},{9,8},{10,14... | collective-permute-start | bytes 1179656 | tf_op jit(solution)/shard_map/ppermute | solution.py:97
  129.5 17.3 %collective-permute-start.21 = (bf16[2,64,768]{2,1,0:T(8,128)(2,1)S(1)}, bf16[2,64,768]{2,1,0:T(8,128)(2,1)S(1)}, u32[]{:S(2)}, u32[]{:S(2)}) collective-permute-start(bf16[2,64,768]{2,1,0:T(8,128)(2,1)S(1)} %add_convert_fusion.20), channel_id=1, source_target_pairs={{0,1},{1,0},{2,6},{3,7},{4,5},{5,4},{6,2},{7,3},{8,9},{9,8},{10,14... | collective-permute-start | bytes 589832 | tf_op jit(solution)/shard_map/ppermute | solution.py:97
  130.6 17.3 %collective-permute-start.20 = (bf16[2,64,768]{2,1,0:T(8,128)(2,1)S(1)}, bf16[2,64,768]{2,1,0:T(8,128)(2,1)S(1)}, u32[]{:S(2)}, u32[]{:S(2)}) collective-permute-start(bf16[2,64,768]{2,1,0:T(8,128)(2,1)S(1)} %add_convert_fusion.19), channel_id=1, source_target_pairs={{0,16},{1,17},{2,18},{3,19},{4,20},{5,21},{6,22},{7,23},{8,24},{9,... | collective-permute-start | bytes 589832 | tf_op jit(solution)/shard_map/ppermute | solution.py:97
  146.8 10.6 %collective-permute-start.26 = (bf16[2,48,1920]{2,1,0:T(8,128)(2,1)S(1)}, bf16[2,48,1920]{2,1,0:T(8,128)(2,1)S(1)}, u32[]{:S(2)}, u32[]{:S(2)}) collective-permute-start(bf16[2,48,1920]{2,1,0:T(8,128)(2,1)S(1)} %add_convert_fusion.17), channel_id=1, source_target_pairs={{0,8},{1,9},{2,6},{3,7},{4,12},{5,13},{6,2},{7,3},{8,0},{9,1},{10,... | collective-permute-start | bytes 1105928 | tf_op jit(solution)/shard_map/ppermute | solution.py:97
  147.9 22.7 %collective-permute-start.25 = (bf16[4,64,768]{2,1,0:T(8,128)(2,1)S(1)}, bf16[4,64,768]{2,1,0:T(8,128)(2,1)S(1)}, u32[]{:S(2)}, u32[]{:S(2)}) collective-permute-start(bf16[4,64,768]{2,1,0:T(8,128)(2,1)S(1)} %constant_dynamic-update-slice_fusion.4), channel_id=1, source_target_pairs={{0,8},{1,9},{2,3},{3,2},{4,12},{5,13},{6,7},{7,6},{8,0},{9,1},{10,... | collective-permute-start | bytes 1179656 | tf_op jit(solution)/shard_map/ppermute | solution.py:97
  149.0 23.8 %collective-permute-start.24 = (bf16[2,64,768]{2,1,0:T(8,128)(2,1)S(1)}, bf16[2,64,768]{2,1,0:T(8,128)(2,1)S(1)}, u32[]{:S(2)}, u32[]{:S(2)}) collective-permute-start(bf16[2,64,768]{2,1,0:T(8,128)(2,1)S(1)} %add_convert_fusion.18), channel_id=1, source_target_pairs={{0,8},{1,9},{2,3},{3,2},{4,12},{5,13},{6,7},{7,6},{8,0},{9,1},{10,... | collective-permute-start | bytes 589832 | tf_op jit(solution)/shard_map/ppermute | solution.py:97
  157.6 19.8 %collective-permute-start.27 = (bf16[2,48,1920]{2,1,0:T(8,128)(2,1)S(1)}, bf16[2,48,1920]{2,1,0:T(8,128)(2,1)S(1)}, u32[]{:S(2)}, u32[]{:S(2)}) collective-permute-start(bf16[2,48,1920]{2,1,0:T(8,128)(2,1)S(1)} %add_convert_fusion.15), channel_id=1, source_target_pairs={{0,16},{1,17},{2,18},{3,19},{4,20},{5,21},{6,22},{7,23},{8,24},{9,... | collective-permute-start | bytes 1105928 | tf_op jit(solution)/shard_map/ppermute | solution.py:97
  172.8 11.1 %collective-permute-start.29 = (bf16[4,64,768]{2,1,0:T(8,128)(2,1)S(1)}, bf16[4,64,768]{2,1,0:T(8,128)(2,1)S(1)}, u32[]{:S(2)}, u32[]{:S(2)}) collective-permute-start(bf16[4,64,768]{2,1,0:T(8,128)(2,1)S(1)} %constant_dynamic-update-slice_fusion.8), channel_id=1, source_target_pairs={{0,4},{1,5},{2,10},{3,11},{4,0},{5,1},{6,14},{7,15},{8,12},{9,13},... | collective-permute-start | bytes 1179656 | tf_op jit(solution)/shard_map/ppermute | solution.py:97
  177.4 7.6 %collective-permute-start.28 = (bf16[2,48,1920]{2,1,0:T(8,128)(2,1)S(1)}, bf16[2,48,1920]{2,1,0:T(8,128)(2,1)S(1)}, u32[]{:S(2)}, u32[]{:S(2)}) collective-permute-start(bf16[2,48,1920]{2,1,0:T(8,128)(2,1)S(1)} %add_convert_fusion.14), channel_id=1, source_target_pairs={{0,1},{1,0},{2,3},{3,2},{4,5},{5,4},{6,7},{7,6},{8,9},{9,8},{10,11... | collective-permute-start | bytes 1105928 | tf_op jit(solution)/shard_map/ppermute | solution.py:97
  178.7 14.0 %collective-permute-start.31 = (bf16[8,64,768]{2,1,0:T(8,128)(2,1)S(1)}, bf16[8,64,768]{2,1,0:T(8,128)(2,1)S(1)}, u32[]{:S(2)}, u32[]{:S(2)}) collective-permute-start(bf16[8,64,768]{2,1,0:T(8,128)(2,1)S(1)} %constant_dynamic-update-slice_fusion.2.near), channel_id=1, source_target_pairs={{0,8},{1,9},{2,3},{3,2},{4,12},{5,13},{6,7},{7,6},{8,0},{9,1},{10,... | collective-permute-start | bytes 2359304 | tf_op jit(solution)/shard_map/ppermute | solution.py:97
  185.1 20.2 %collective-permute-start.30 = (bf16[2,48,3072]{2,1,0:T(8,128)(2,1)S(1)}, bf16[2,48,3072]{2,1,0:T(8,128)(2,1)S(1)}, u32[]{:S(2)}, u32[]{:S(2)}) collective-permute-start(bf16[2,48,3072]{2,1,0:T(8,128)(2,1)S(1)} %pad_maximum_fusion.2), channel_id=1, source_target_pairs={{0,8},{1,9},{2,6},{3,7},{4,12},{5,13},{6,2},{7,3},{8,0},{9,1},{10,... | collective-permute-start | bytes 1769480 | tf_op jit(solution)/shard_map/ppermute | solution.py:97
  185.2 21.2 %collective-permute-start.40 = (bf16[8,64,768]{2,1,0:T(8,128)(2,1)S(1)}, bf16[8,64,768]{2,1,0:T(8,128)(2,1)S(1)}, u32[]{:S(2)}, u32[]{:S(2)}) collective-permute-start(bf16[8,64,768]{2,1,0:T(8,128)(2,1)S(1)} %constant_dynamic-update-slice_fusion.2.near), channel_id=1, source_target_pairs={{0,2},{1,3},{2,0},{3,1},{4,6},{5,7},{6,4},{7,5},{8,10},{9,11},{10,... | collective-permute-start | bytes 2359304 | tf_op jit(solution)/shard_map/ppermute | solution.py:97
  185.3 20.6 %collective-permute-start.38 = (bf16[8,64,768]{2,1,0:T(8,128)(2,1)S(1)}, bf16[8,64,768]{2,1,0:T(8,128)(2,1)S(1)}, u32[]{:S(2)}, u32[]{:S(2)}) collective-permute-start(bf16[8,64,768]{2,1,0:T(8,128)(2,1)S(1)} %constant_dynamic-update-slice_fusion.6.near), channel_id=1, source_target_pairs={{0,4},{1,5},{2,10},{3,11},{4,0},{5,1},{6,14},{7,15},{8,12},{9,13},... | collective-permute-start | bytes 2359304 | tf_op jit(solution)/shard_map/ppermute | solution.py:97
  192.7 13.8 %collective-permute-start.41 = (bf16[8,64,768]{2,1,0:T(8,128)(2,1)S(1)}, bf16[8,64,768]{2,1,0:T(8,128)(2,1)S(1)}, u32[]{:S(2)}, u32[]{:S(2)}) collective-permute-start(bf16[8,64,768]{2,1,0:T(8,128)(2,1)S(1)} %collective-permute-done.31.far), channel_id=1, source_target_pairs={{0,2},{1,3},{2,0},{3,1},{4,6},{5,7},{6,4},{7,5},{8,10},{9,11},{10,... | collective-permute-start | bytes 2359304 | tf_op jit(solution)/shard_map/ppermute | solution.py:97
  192.7 13.2 %collective-permute-start.35 = (bf16[8,64,768]{2,1,0:T(8,128)(2,1)S(1)}, bf16[8,64,768]{2,1,0:T(8,128)(2,1)S(1)}, u32[]{:S(2)}, u32[]{:S(2)}) collective-permute-start(bf16[8,64,768]{2,1,0:T(8,128)(2,1)S(1)} %constant_dynamic-update-slice_fusion.10.near), channel_id=1, source_target_pairs={{0,1},{1,0},{2,6},{3,7},{4,5},{5,4},{6,2},{7,3},{8,9},{9,8},{10,14... | collective-permute-start | bytes 2359304 | tf_op jit(solution)/shard_map/ppermute | solution.py:97
  205.4 16.3 %collective-permute-start.33 = (bf16[4,48,3072]{2,1,0:T(8,128)(2,1)S(1)}, bf16[4,48,3072]{2,1,0:T(8,128)(2,1)S(1)}, u32[]{:S(2)}, u32[]{:S(2)}) collective-permute-start(bf16[4,48,3072]{2,1,0:T(8,128)(2,1)S(1)} %constant_dynamic-update-slice_fusion.12.near), channel_id=1, source_target_pairs={{0,4},{1,5},{2,10},{3,11},{4,0},{5,1},{6,14},{7,15},{8,12},{9,13},... | collective-permute-start | bytes 3538952 | tf_op jit(solution)/shard_map/ppermute | solution.py:97
  206.0 8.2 %collective-permute-start.37 = (bf16[8,64,768]{2,1,0:T(8,128)(2,1)S(1)}, bf16[8,64,768]{2,1,0:T(8,128)(2,1)S(1)}, u32[]{:S(2)}, u32[]{:S(2)}) collective-permute-start(bf16[8,64,768]{2,1,0:T(8,128)(2,1)S(1)} %constant_dynamic-update-slice_fusion.6.near), channel_id=1, source_target_pairs={{0,2},{1,3},{2,0},{3,1},{4,6},{5,7},{6,4},{7,5},{8,10},{9,11},{10,... | collective-permute-start | bytes 2359304 | tf_op jit(solution)/shard_map/ppermute | solution.py:97
  206.0 8.2 %collective-permute-start.39 = (bf16[8,64,768]{2,1,0:T(8,128)(2,1)S(1)}, bf16[8,64,768]{2,1,0:T(8,128)(2,1)S(1)}, u32[]{:S(2)}, u32[]{:S(2)}) collective-permute-start(bf16[8,64,768]{2,1,0:T(8,128)(2,1)S(1)} %collective-permute-done.38.far), channel_id=1, source_target_pairs={{0,2},{1,3},{2,0},{3,1},{4,6},{5,7},{6,4},{7,5},{8,10},{9,11},{10,... | collective-permute-start | bytes 2359304 | tf_op jit(solution)/shard_map/ppermute | solution.py:97
  206.5 10.1 %collective-permute-start.34 = (bf16[8,64,768]{2,1,0:T(8,128)(2,1)S(1)}, bf16[8,64,768]{2,1,0:T(8,128)(2,1)S(1)}, u32[]{:S(2)}, u32[]{:S(2)}) collective-permute-start(bf16[8,64,768]{2,1,0:T(8,128)(2,1)S(1)} %constant_dynamic-update-slice_fusion.10.near), channel_id=1, source_target_pairs={{0,2},{1,3},{2,0},{3,1},{4,6},{5,7},{6,4},{7,5},{8,10},{9,11},{10,... | collective-permute-start | bytes 2359304 | tf_op jit(solution)/shard_map/ppermute | solution.py:97
  206.5 10.0 %collective-permute-start.36 = (bf16[8,64,768]{2,1,0:T(8,128)(2,1)S(1)}, bf16[8,64,768]{2,1,0:T(8,128)(2,1)S(1)}, u32[]{:S(2)}, u32[]{:S(2)}) collective-permute-start(bf16[8,64,768]{2,1,0:T(8,128)(2,1)S(1)} %collective-permute-done.35.far), channel_id=1, source_target_pairs={{0,2},{1,3},{2,0},{3,1},{4,6},{5,7},{6,4},{7,5},{8,10},{9,11},{10,... | collective-permute-start | bytes 2359304 | tf_op jit(solution)/shard_map/ppermute | solution.py:97
  214.1 16.0 %collective-permute-start.32 = (bf16[4,48,3072]{2,1,0:T(8,128)(2,1)S(1)}, bf16[4,48,3072]{2,1,0:T(8,128)(2,1)S(1)}, u32[]{:S(2)}, u32[]{:S(2)}) collective-permute-start(bf16[4,48,3072]{2,1,0:T(8,128)(2,1)S(1)} %constant_dynamic-update-slice_fusion.12.near), channel_id=1, source_target_pairs={{0,2},{1,3},{2,0},{3,1},{4,6},{5,7},{6,4},{7,5},{8,10},{9,11},{10,... | collective-permute-start | bytes 3538952 | tf_op jit(solution)/shard_map/ppermute | solution.py:97
  221.7 8.4 %collective-permute-start.42 = (bf16[4,48,3072]{2,1,0:T(8,128)(2,1)S(1)}, bf16[4,48,3072]{2,1,0:T(8,128)(2,1)S(1)}, u32[]{:S(2)}, u32[]{:S(2)}) collective-permute-start(bf16[4,48,3072]{2,1,0:T(8,128)(2,1)S(1)} %collective-permute-done.33.far), channel_id=1, source_target_pairs={{0,2},{1,3},{2,0},{3,1},{4,6},{5,7},{6,4},{7,5},{8,10},{9,11},{10,... | collective-permute-start | bytes 3538952 | tf_op jit(solution)/shard_map/ppermute | solution.py:97
  (11 other events, 46.8 us)

commit v3 on v2

--- a/solution.py
+++ b/solution.py
@@ -78,11 +78,21 @@
 
 
 FF_ORDERS = (
-    (("z0", "y", "x", "z1"), ("y", "x", "z0", "z1")),
-    (("x", "z0", "y", "z1"), ("z0", "y", "x", "z1")),
     (("y", "x", "z0", "z1"), ("x", "z0", "y", "z1")),
+    (("z0", "x", "y", "z1"), ("x", "y", "z0", "z1")),
+    (("x", "y", "z0", "z1"), ("z0", "x", "y", "z1")),
 )
 QKV_ORDER = (("x", "z0", "z1"), ("z0", "x", "z1"))
+PLAN = (
+    ("ff", 0), ("ff", 1), ("wait", "e0"), ("wait", "early"), ("ff", 2), ("dw", 0),
+    ("wait", "branch_other"), ("wait", "e1"), ("dw", 1), ("own",), ("wait", "g"), ("go", 0),
+    ("wait", "e2"), ("dw", 2), ("far",), ("go", 0), ("go", 1), ("joint",), ("go", 0), ("go", 2),
+    ("go", 1), ("go", 3), ("back",), ("go", 0), ("go", 1), ("go", 2), ("go", 0), ("go", 2),
+    ("go", 3), ("go", 1), ("go", 0), ("go", 3), ("wait", "bf"), ("go", 2), ("go", 1), ("go", 2),
+    ("go", 0), ("tokens",), ("go", 1), ("unpack", 0, 0), ("go", 3), ("go", 2), ("unpack", 1, 0),
+    ("unpack", 0, 1), ("go", 3), ("go", 1), ("go", 3), ("go", 2), ("unpack", 1, 1),
+    ("unpack", 2, 0), ("unpack", 3, 0), ("go", 3), ("unpack", 2, 1), ("unpack", 3, 1),
+)
 DP_BIT = {"c": 1, "x": 2, "z0": 4, "z1": 8}
 
 
@@ -134,34 +144,34 @@
         return swap(self.pin(array)[0], first, second)
 
 
-def total(order, keep, send, orders, widen=None):
-    received = order.swap(send, "c")
+def total(order, keep, send, links, widen=None):
+    received = order.swap(send, *links[0])
     yield
-    count = len(orders[0])
-    for step in range(count - 1):
+    for link in links[1:-1]:
         half = keep.shape[0] // 2
         send = order.run(lambda k, r: add(k[half:], r[half:]), keep, received)
-        coming = order.swap(send, orders[0][step], orders[1][step])
+        coming = order.swap(send, *link)
         keep = order.run(lambda k, r: add(k[:half], r[:half]), keep, received)
         received = coming
         yield
     keep = order.run(add, keep, received)
-    received = order.swap(keep, orders[0][-1], orders[1][-1])
+    received = order.swap(keep, *links[-1])
     yield
     block = order.run(lambda k, r: add(k, r[::-1]), keep, received)
     if widen is not None:
         received = order.swap(block, "y")
         yield
         block = order.run(widen, block, received)
-    for step in range(count - 2, 0, -1):
-        received = order.swap(block, orders[0][step], orders[1][step])
+    back = [link for link in links[:-1] if link[0] != "c"][::-1]
+    for link in back[:-1]:
+        received = order.swap(block, *link)
         yield
         block = order.run(lambda k, r: jnp.concatenate([k, r], 0), block, received)
-    far = order.swap(block, orders[0][0], orders[1][0])
+    far = order.swap(block, *back[-1])
     other = order.swap(block, "c")
-    yield
-    far_other = order.swap(far, "c")
-    yield block, far, other, far_other
+    yield block, other
+    far = order.run(lambda value: value, far)
+    yield far, order.swap(far, "c")
 
 
 def ln_qkv_kernel(s, tok, pos, gain, w, normed, qkv):
@@ -225,7 +235,8 @@
     )
 
 
-def proj_kernel(s, att, w, tok, pos, gain, resid2, normed2, normed2_t):
+def proj_kernel(s, att, att_half, w, tok, pos, gain, resid2, normed2, normed2_t, att_send):
+    att_send[...] = att_half[...]
     value = tok[...].astype(f32) + pos[...] + dot(att[...], w[...])
     resid2[...] = value
     xhat, _ = normalize(value)
@@ -236,15 +247,25 @@
 
 def project(scalars, att, w, tok, pos, gain):
     rows, width = att.shape
-    args = (att, w, tok, pos, gain)
     full = spec((rows, width), lambda i, s: (0, 0))
+    half = spec((rows, width // 2), lambda i, s: (0, 1 - s[0]))
     return call(
         proj_kernel,
         (1,),
-        [whole(a) for a in args],
-        [full, full, spec((width, rows), lambda i, s: (0, 0))],
-        [shape((rows, width), f32), shape((rows, width), bf16), shape((width, rows), bf16)],
-        args,
+        [full, half, whole(w), full, full, whole(gain)],
+        [
+            full,
+            full,
+            spec((width, rows), lambda i, s: (0, 0)),
+            spec((rows, width // 2), lambda i, s: (0, 0)),
+        ],
+        [
+            shape((rows, width), f32),
+            shape((rows, width), bf16),
+            shape((width, rows), bf16),
+            shape((rows, width // 2), bf16),
+        ],
+        (att, att, w, tok, pos, gain),
         scalars,
         24,
     )
@@ -259,7 +280,7 @@
     return act, slope
 
 
-def ff_kernel(at, first, last, s, normed, normed_t, cot, up, down, *refs):
+def ff_kernel(first, last, s, normed, cot, up, down, *refs):
     step = pl.program_id(0)
     if not first:
         out_in, back_in, *refs = refs
@@ -277,36 +298,17 @@
 
     @pl.when(step == 0)
     def _():
+        send[0] = act
+        send[1] = grad
         out[...] = out_part if first else out_in[...] + out_part
         back[...] = back_part if first else back_in[...] + back_part
 
     @pl.when(step == 1)
     def _():
+        keep[0] = act
+        keep[1] = grad
         out[...] += out_part
         back[...] += back_part
-
-    g_down = dot(act, cot[...], TN).astype(bf16)
-    g_up = dot(normed_t[...], grad).astype(bf16)
-
-    def store(target, code):
-        rows_d = g_down.shape[0] // 16
-        rows_u = g_up.shape[0] // 16
-        half = g_up.shape[1] // 2
-        for block in range(16):
-            to = block ^ code
-            target[to, :rows_d, :] = g_down[block * rows_d : (block + 1) * rows_d]
-            part = g_up[block * rows_u : (block + 1) * rows_u]
-            target[to, rows_d:, : 2 * half] = part[:rows_d]
-            target[to, rows_d : rows_d + 16, 2 * half :] = part[rows_d:, :half]
-            target[to, rows_d + 16 :, 2 * half :] = part[rows_d:, half:]
-
-    @pl.when(step == 0)
-    def _():
-        store(send, s[at + 1])
-
-    @pl.when(step == 1)
-    def _():
-        store(keep, s[at])
         if last:
             value = resid2[...]
             out_low[...] = (value + out[...]).astype(bf16)
@@ -319,7 +321,7 @@
             g_own[...] = dot(low, w_own[...], NT).astype(bf16)
 
 
-def ff_chunk(scalars, chunk, last, normed, normed_t, cot, up, down, *more):
+def ff_chunk(scalars, chunk, last, normed, cot, up, down, *more):
     rows, width = normed.shape
     half = width // 2
     wide = 512
@@ -330,16 +332,15 @@
 
     full = spec((rows, width), lambda i, s: (0, 0))
     part = spec((rows, half), lambda i, s: (0, 0))
-    piece = spec((16, 64, width), lambda i, s: (0, 0, 0))
+    piece = spec((2, rows, wide), lambda i, s: (0, 0, 0))
     in_specs = [
         whole(normed),
-        whole(normed_t),
         whole(cot),
         spec((width, wide), lambda i, s: (0, column(i, s))),
         spec((wide, width), lambda i, s: (column(i, s), 0)),
     ]
     out_specs = [piece, piece]
-    out_shape = [shape((16, 64, width), bf16)] * 2
+    out_shape = [shape((2, rows, wide), bf16)] * 2
     scratch = []
     if not first:
         in_specs += [full, full]
@@ -358,15 +359,87 @@
         out_specs += [full, full]
         out_shape += [shape((rows, width), f32)] * 2
     return call(
-        functools.partial(ff_kernel, 2 + 2 * chunk, first, last),
+        functools.partial(ff_kernel, first, last),
         (2,),
         in_specs,
         out_specs,
         out_shape,
-        (normed, normed_t, cot, up, down) + more,
+        (normed, cot, up, down) + more,
         scalars,
         40,
         scratch,
+    )
+
+
+def ff_grads_kernel(at, s, act, act_o, grad, grad_o, cot, cot_o, nt, nt_o, *refs):
+    keep, send = refs[-2:]
+    step = pl.program_id(0)
+    rows_both = jnp.concatenate([cot[...], cot_o[...]], 0)
+    g_down = dot(jnp.concatenate([act[0], act_o[0]], 0), rows_both, TN).astype(bf16)
+    grads = jnp.concatenate([grad[0], grad_o[0]], 0)
+    g_up = dot(jnp.concatenate([nt[...], nt_o[...]], 1), grads).astype(bf16)
+    g_proj = None
+    if len(refs) > 2:
+        att, att_o, branch, branch_o = refs[:4]
+        both = jnp.concatenate([branch[...], branch_o[...]], 0)
+        g_proj = dot(jnp.concatenate([att[...], att_o[...]], 0), both, TN).astype(bf16)
+    code = s[at] & 7
+
+    def store(target):
+        rows_d = g_down.shape[0] // 8
+        rows_u = g_up.shape[0] // 8
+        half = g_up.shape[1] // 2
+        for block in range(8):
+            to = block ^ code
+            target[to, :rows_d, :] = g_down[block * rows_d : (block + 1) * rows_d]
+            part = g_up[block * rows_u : (block + 1) * rows_u]
+            target[to, 32:64, : 2 * half] = part[:32]
+            target[to, 32:48, 2 * half :] = part[32:, :half]
+            target[to, 48:64, 2 * half :] = part[32:, half:]
+            if g_proj is not None:
+                part = g_proj[block * rows_u : (block + 1) * rows_u]
+                wide = part.shape[1]
+                target[to, 64:80, :wide] = part[:16]
+                target[to, 64:80, wide:] = part[16:32]
+                target[to, 80:, :wide] = part[32:]
+                target[to, 80:, wide:] = jnp.zeros_like(part[32:])
+
+    @pl.when(step == 0)
+    def _():
+        store(send)
+
+    @pl.when(step == 1)
+    def _():
+        store(keep)
+
+
+def ff_grads(scalars, chunk, mine, theirs, cot, cot_other, normed_t_other, normed_t, *proj):
+    rows, width = cot.shape
+    wide = mine.shape[2]
+    at = 2 + 2 * chunk
+
+    def side(i, s):
+        return (1 - i) ^ (s[at] // 8)
+
+    act = spec((1, rows, wide // 2), lambda i, s: (0, 0, side(i, s)))
+    grad = spec((1, rows, wide), lambda i, s: (1, 0, 0))
+    feature = spec((width // 2, rows), lambda i, s: (side(i, s), 0))
+    in_specs = [act, act, grad, grad, whole(cot), whole(cot), feature, feature]
+    if proj:
+        half = width // 2
+        column = spec((rows, half), lambda i, s: (0, side(i, s)))
+        in_specs += [spec((rows, half), lambda i, s: (0, s[0])), whole(proj[1]), column, column]
+    deep = 96 if proj else 64
+    piece = spec((8, deep, width), lambda i, s: (0, 0, 0))
+    return call(
+        functools.partial(ff_grads_kernel, at),
+        (2,),
+        in_specs,
+        [piece, piece],
+        [shape((8, deep, width), bf16)] * 2,
+        (mine, theirs, mine, theirs, cot, cot_other, normed_t, normed_t_other) + proj,
+        scalars,
+        32,
     )
 
 
@@ -418,7 +491,7 @@
     )
 
 
-def joint_kernel(s, n_own, n_far, gq_o, gq_f, gk, gv, att, branch, keep, send):
+def joint_kernel(s, n_own, n_far, gq_o, gq_f, gk, gv, keep, send):
     step = pl.program_id(0)
     gq = jnp.concatenate([gq_o[...], gq_f[...]], 0)
     n = jnp.concatenate([n_own[...], n_far[...]], 0)
@@ -426,7 +499,6 @@
 
     def fill(target, code):
         tiles = [dot(n, g, TN).astype(bf16) for g in (gq, gk[...], gv[...])]
-        tiles.append(dot(att[...], branch[...], TN).astype(bf16))
         rows = tiles[0].shape[0] // 8
         for block in range(8):
             at = block ^ code
@@ -443,19 +515,19 @@
         fill(keep, s[8])
 
 
-def joint_grads(scalars, n_own, n_far, gq, gq_far, gk, gv, att, branch):
+def joint_grads(scalars, n_own, n_far, gq, gq_far, gk, gv):
     rows, width = n_own.shape
     half = width // 2
     feature = spec((rows, half), lambda i, s: (0, s[0] ^ (1 - i)))
-    cols = 3 * half + width
+    cols = 3 * half
     piece = spec((8, half // 8, cols), lambda i, s: (0, 0, 0))
     return call(
         joint_kernel,
         (2,),
-        [feature, feature, whole(gq), whole(gq), whole(gk), whole(gv), feature, whole(branch)],
+        [feature, feature, whole(gq), whole(gq), whole(gk), whole(gv)],
         [piece, piece],
         [shape((8, half // 8, cols), bf16)] * 2,
-        (n_own, n_far, gq, gq_far, gk, gv, att, branch),
+        (n_own, n_far, gq, gq_far, gk, gv),
         scalars,
         32,
     )
@@ -513,109 +585,123 @@
     )
 
 
-def unpack_ff_kernel(at, s, near, far, *refs):
-    down, up = refs[-2:]
+def lane_sums(values):
+    return sum(values[:, at : at + 128] for at in range(0, values.shape[1], 128))
+
+
+def unpack_ff_kernel(at, last, s, own, other, w, gain_in, *refs):
+    gain, down, up, *proj = refs[-4:] if last else refs[-3:]
     step = pl.program_id(0)
-    low = s[at] & 7
-
-    def unpack(source):
+
+    def unpack(source, code):
         for block in range(8):
-            at = block ^ low
-            down[pl.ds(pl.multiple_of(at * 32, 32), 32), :] = source[block, :32, :].astype(f32)
-            row = pl.multiple_of(at * 48, 16)
-            up[pl.ds(row, 32), :] = source[block, 32:, :512].astype(f32)
+            to = block ^ (code & 7)
+            down[pl.ds(pl.multiple_of(to * 32, 32), 32), :] = source[block, :32, :].astype(f32)
+            row = pl.multiple_of(to * 48, 16)
+            up[pl.ds(row, 32), :] = source[block, 32:64, :512].astype(f32)
             up[pl.ds(row + 32, 16), :256] = source[block, 32:48, 512:].astype(f32)
-            up[pl.ds(row + 32, 16), 256:] = source[block, 48:, 512:].astype(f32)
+            up[pl.ds(row + 32, 16), 256:] = source[block, 48:64, 512:].astype(f32)
+            if last:
+                wide = source.shape[2] // 2
+                proj[0][pl.ds(row, 16), :] = source[block, 64:80, :wide].astype(f32)
+                proj[0][pl.ds(row + 16, 16), :] = source[block, 64:80, wide:].astype(f32)
+                proj[0][pl.ds(row + 32, 16), :] = source[block, 80:, :wide].astype(f32)
 
     @pl.when(step == 0)
     def _():
-        unpack(near)
+        unpack(own, s[at])
 
     @pl.when(step == 1)
     def _():
-        unpack(far)
-
-
-def unpack_ff(scalars, chunk, other, near, far, width, hidden, so_far):
-    at = 2 + 2 * chunk + other
+        unpack(other, s[at + 1])
+
+    sums = lane_sums(up[...] * w[...].astype(f32))
+    gain[...] = gain_in[...] + sums
+
+
+def unpack_ff(scalars, chunk, far, own, other, w, so_far):
+    width, hidden = w.shape
+    at = 2 + 2 * chunk
+    last = own.shape[1] > 64
 
     def side(i, s):
-        return i ^ (s[at] // 8)
-
-    def half(s):
-        return 2 * chunk + (s[0] ^ other)
+        return (s[at + i] // 8) ^ far
+
+    def half(i, s):
+        return 2 * chunk + (s[0] ^ i)
 
     any_spec = pl.BlockSpec(memory_space=pl.ANY)
+    column = spec((width // 2, 512), lambda i, s: (side(i, s), half(i, s)))
+    gain = spec((None, width // 2, 128), lambda i, s: (i, side(i, s), 0))
+    out_specs = [gain, spec((256, width), lambda i, s: (2 * half(i, s) + side(i, s), 0)), column]
+    out_shape = [shape((2, width, 128), f32), shape((hidden, width), f32), shape((width, hidden), f32)]
+    if last:
+        out_specs.append(spec((width // 2, width // 2), lambda i, s: (s[0] ^ i, side(i, s))))
+        out_shape.append(shape((width, width), f32))
+    in_specs = [whole(own), whole(other), column]
+    in_specs += [gain, any_spec, any_spec, any_spec][: len(so_far)]
     return call(
-        functools.partial(unpack_ff_kernel, at),
+        functools.partial(unpack_ff_kernel, at, last),
         (2,),
-        [whole(near), whole(far)] + [any_spec] * len(so_far),
-        [
-            spec((256, width), lambda i, s: (2 * half(s) + side(i, s), 0)),
-            spec((width // 2, 512), lambda i, s: (side(i, s), half(s))),
-        ],
-        [shape((hidden, width), f32), shape((width, hidden), f32)],
-        (near, far) + tuple(so_far),
+        in_specs,
+        out_specs,
+        out_shape,
+        (own, other, w) + tuple(so_far),
         scalars,
         32,
-        aliases={3: 0, 4: 1} if so_far else None,
-    )
-
-
-def unpack_qkv_kernel(at, s, near, far, *refs):
-    joint, proj = refs[-2:]
+        aliases={4 + i: i for i in range(len(so_far))},
+    )
+
+
+def unpack_qkv_kernel(s, own, other, w, *refs):
+    joint, gain = refs[-2:]
     step = pl.program_id(0)
-    low = s[at] & 3
     mine = s[1]
 
-    def unpack(source):
-        half = source.shape[2] // 8
+    def unpack(source, code):
+        half = source.shape[2] // 6
         for block in range(4):
-            at = pl.multiple_of((block ^ low) * 48, 16)
-            rows = pl.ds(at, 48)
+            rows = pl.ds(pl.multiple_of((block ^ (code & 3)) * 48, 16), 48)
             for part in range(3):
                 for side in range(2):
                     column = pl.multiple_of(2 * half * part + half * (mine ^ side), 128)
                     value = source[block, :, (3 * side + part) * half : (3 * side + part + 1) * half]
                     joint[rows, pl.ds(column, half)] = value.astype(f32)
-            proj[rows, :] = source[block, :, 6 * half :].astype(f32)
 
     @pl.when(step == 0)
     def _():
-        unpack(near)
+        unpack(own, s[8])
 
     @pl.when(step == 1)
     def _():
-        unpack(far)
-
-
-def unpack_qkv(scalars, other, near, far, width, so_far):
-    at = 8 + other
-
-    def row(i, s):
-        return 2 * (s[0] ^ other) + (i ^ (s[at] // 4))
+        unpack(other, s[9])
+
+    gain[...] = lane_sums(joint[...] * w[...].astype(f32))
+
+
+def unpack_qkv(scalars, far, own, other, w, so_far):
+    width = w.shape[0]
+
+    def rows(columns):
+        return spec((width // 4, columns), lambda i, s: (2 * (s[0] ^ i) + ((s[8 + i] // 4) ^ far), 0))
 
     any_spec = pl.BlockSpec(memory_space=pl.ANY)
     return call(
-        functools.partial(unpack_qkv_kernel, at),
+        unpack_qkv_kernel,
         (2,),
-        [whole(near), whole(far)] + [any_spec] * len(so_far),
-        [
-            spec((width // 4, 3 * width), lambda i, s: (row(i, s), 0)),
-            spec((width // 4, width), lambda i, s: (row(i, s), 0)),
-        ],
-        [shape((width, 3 * width), f32), shape((width, width), f32)],
-        (near, far) + tuple(so_far),
+        [whole(own), whole(other), rows(3 * width)] + [any_spec] * len(so_far),
+        [rows(3 * width), rows(128)],
+        [shape((width, 3 * width), f32), shape((width, 128), f32)],
+        (own, other, w) + tuple(so_far),
         scalars,
         32,
-        aliases={3: 0, 4: 1} if so_far else None,
+        aliases={4 + i: i for i in range(len(so_far))},
     )
 
 
 def fast(tokens, visible, ln1_gain, w_qkv, w_proj, ln2_gain, w_up, w_down, d_out):
     tok, cot = tokens[0], d_out[0]
     rows, width = tok.shape
-    hidden = w_up.shape[1]
     gain1, gain2 = ln1_gain[None], ln2_gain[None]
     scalars = [lax.axis_index("dp") & 1, lax.axis_index("blk")]
     for orders in FF_ORDERS + (QKV_ORDER,):
@@ -626,86 +712,110 @@
     run = order.run
     vis_far = swap(visible, "y")[0]
     tok_far = swap(tok, "y")
+    cot_other = swap(cot, "c")
     pos = position_table(visible[0], width)
     pos_far = position_table(vis_far, width)
     normed1, qkv = run(functools.partial(ln_qkv, scalars), tok, pos, gain1, w_qkv)
     normed1_far, qkv_far = run(functools.partial(ln_qkv, scalars), tok_far, pos_far, gain1, w_qkv)
     attended = run(functools.partial(attention, scalars), qkv, qkv_far)
-    resid2, normed2, normed2_t = run(functools.partial(project, scalars), attended, w_proj, tok, pos, gain2)
-
-    streams, near = [], [None] * 4
-
-    def go(*which):
-        for i in which:
-            near[i] = next(streams[i], near[i])
-
-    def feed_forward(chunk, *more):
+    resid2, normed2, normed2_t, att_half = run(
+        functools.partial(project, scalars), attended, w_proj, tok, pos, gain2
+    )
+    early = cot_other, order.swap(normed2_t, "c"), order.swap(att_half, "c")
+
+    streams, blocks, values = {}, {}, {"early": early}
+    ff, proj, joint = (jnp.zeros((2, width, 128), f32),), (), ()
+
+    def feed_forward(chunk):
+        more = values.pop("sums", ())
+        if chunk == 2:
+            more += (resid2, gain2, w_proj, w_proj)
         keep, send, *rest = run(
-            functools.partial(ff_chunk, scalars, chunk, chunk == 2),
-            normed2, normed2_t, cot, w_up, w_down, *more,
+            functools.partial(ff_chunk, scalars, chunk, chunk == 2), normed2, cot, w_up, w_down, *more
         )
-        streams.append(total(order, keep, send, FF_ORDERS[chunk]))
-        return rest
-
-    sums = feed_forward(0)
-    go(0)
-    sums = feed_forward(1, *sums)
-    go(0, 1)
-    out, grad2, branch, g_own, g_other = feed_forward(2, *sums, resid2, gain2, w_proj, w_proj)
-    g_far = order.swap(g_other, "y")
-    go(0, 1, 2)
-    gq, *sums = run(functools.partial(attention_back, scalars, False), qkv, qkv_far, g_own)
-    go(0, 1, 2)
-    gq_far, gk, gv = run(functools.partial(attention_back, scalars, True), qkv, qkv_far, g_far, *sums)
-    go(0, 1, 2)
-    keep, send = run(
-        functools.partial(joint_grads, scalars),
-        normed1, normed1_far, gq, gq_far, gk, gv, attended, branch,
-    )
-    cut = 3 * (width // 2)
-
-    def widen(mine, theirs):
-        proj = add(mine[..., cut:], theirs[..., cut:])
-        return jnp.concatenate([mine[..., :cut], theirs[..., :cut], proj], -1)
-
-    streams.append(total(order, keep, send, QKV_ORDER, widen))
-    go(3, 0, 1, 2)
-    back_own, back_far = run(functools.partial(back_qkv, scalars), gq, gq_far, gk, gv, w_qkv)
-    back_far = order.swap(back_far, "y")
-    go(3, 0, 1, 2)
-    go(3, 0, 1, 2)
-    go(3, 0, 1, 2)
-    d_tokens = run(functools.partial(token_grad, scalars), back_own, back_far, tok, pos, gain1, grad2)
-    go(3, 0, 1, 2)
-
-    ff = ()
-
-    def finish(chunk, other):
-        nonlocal ff
-        ff = run(
-            lambda a, b, *f: unpack_ff(scalars, chunk, other, a, b, width, hidden, f),
-            near[chunk][2 * other], near[chunk][2 * other + 1], *ff,
+        values["act", chunk], values["e%d" % chunk] = keep, order.swap(send, "c")
+        if chunk == 2:
+            out, grad2, branch, g_own, g_other = rest
+            values["branch"], values["branch_other"] = branch, order.swap(branch, "c")
+            values["g"] = order.swap(g_other, "y")
+            values.update(out=out, grad2=grad2, own=g_own)
+        else:
+            values["sums"] = tuple(rest)
+
+    def weight_grads(chunk):
+        early = (*values["early"][:2], normed2_t)
+        more = ()
+        if chunk == 2:
+            more = (attended, values["early"][2], values["branch"], values["branch_other"])
+        keep, send = run(
+            functools.partial(ff_grads, scalars, chunk),
+            values["act", chunk], values["e%d" % chunk], cot, *early, *more,
         )
-
-    go(3, 0, 1, 2)
-    finish(0, 0)
-    go(3, 1, 2)
-    finish(0, 1)
-    finish(1, 0)
-    finish(2, 0)
-    finish(1, 1)
-    finish(2, 1)
-    go(3)
-    qkvp = ()
-    for other in range(2):
-        qkvp = run(
-            lambda a, b, *f: unpack_qkv(scalars, other, a, b, width, f),
-            near[3][2 * other], near[3][2 * other + 1], *qkvp,
+        streams[chunk] = total(order, keep, send, list(zip(*FF_ORDERS[chunk])))
+        advance(chunk)
+
+    def advance(chunk):
+        pair = next(streams[chunk])
+        if pair is not None:
+            blocks.setdefault(chunk, []).append(pair)
+
+    def wait(key):
+        value = values[key]
+        values[key] = run(lambda *v: v if isinstance(value, tuple) else v[0], *(value if isinstance(value, tuple) else (value,)))
+
+    def own_queries():
+        values["attn"] = run(functools.partial(attention_back, scalars, False), qkv, qkv_far, values["own"])
+
+    def far_queries():
+        gq, *sums = values["attn"]
+        back = run(functools.partial(attention_back, scalars, True), qkv, qkv_far, values["g"], *sums)
+        values["attn"] = (gq, *back)
+
+    def joint_weights():
+        keep, send = run(functools.partial(joint_grads, scalars), normed1, normed1_far, *values["attn"])
+        links = [("c", "c")] + list(zip(*QKV_ORDER))
+        streams[3] = total(order, keep, send, links, lambda a, b: jnp.concatenate([a, b], -1))
+        advance(3)
+
+    def back_joint():
+        own, far = run(functools.partial(back_qkv, scalars), *values["attn"], w_qkv)
+        values["norm"], values["bf"] = own, order.swap(far, "y")
+
+    def finish_tokens():
+        args = (values["norm"], values["bf"], tok, pos, gain1, values["grad2"])
+        values["tokens"] = run(functools.partial(token_grad, scalars), *args)
+
+    def unpack(chunk, far):
+        nonlocal ff, proj, joint
+        own, other = blocks[chunk][far]
+        if chunk == 3:
+            joint = run(lambda a, b, *f: unpack_qkv(scalars, far, a, b, w_qkv, f), own, other, *joint)
+            return
+        so_far = ff + proj if chunk == 2 else ff
+        result = tuple(
+            run(lambda a, b, *f: unpack_ff(scalars, chunk, far, a, b, w_up, f), own, other, *so_far)
         )
-    d_down, d_up = ff
-    d_qkv, d_proj = qkvp
-    d_gain1 = jnp.sum(w_qkv.astype(f32) * d_qkv, 1) / ln1_gain
-    d_gain2 = jnp.sum(w_up.astype(f32) * d_up, 1) / ln2_gain
+        ff, proj = result[:3], result[3:] or proj
+
+    steps = {
+        "ff": feed_forward,
+        "dw": weight_grads,
+        "go": advance,
+        "wait": wait,
+        "own": own_queries,
+        "far": far_queries,
+        "joint": joint_weights,
+        "back": back_joint,
+        "tokens": finish_tokens,
+        "unpack": unpack,
+    }
+    for name, *args in PLAN:
+        steps[name](*args)
+    sums2, d_down, d_up = ff
+    d_qkv, sums1 = joint
+    out, d_tokens, d_proj = values["out"], values["tokens"], proj[0]
+    d_gain1 = jnp.sum(sums1, 1) / ln1_gain
+    d_gain2 = jnp.sum(sums2, (0, 2)) / ln2_gain
     return out[None], d_tokens[None], d_gain1, d_qkv, d_proj, d_gain2, d_up, d_down
 
 

time: 242 us -> 222 us (0.917)
  waiting for transfers between devices: 86.7 us -> 48.1 us
  starting transfers between devices: 33.4 us -> 57.1 us
  other arithmetic: 22.4 us -> 11.9 us
  local copies, waits for them, and re-layouts: 3.88 us -> 6.32 us
    ppermute x43 -> x47, waiting for transfers between devices: 86.7 us -> 48.1 us  [swap(): return lax.ppermute(array, AXES, pairs)]
    ppermute x43 -> x47, starting transfers between devices: 33.4 us -> 57.1 us  [swap(): return lax.ppermute(array, AXES, pairs)]
    reduce_sum x2, other arithmetic: 8.76 us -> 2.48 us  [the longest x1 1.31 us: fast(): d_gain2 = jnp.sum(sums2, (0, 2)) / ln2_gain]
    convert_element_type x31 -> x24, other arithmetic: 7.38 us -> 1.75 us  [add(): return (a.astype(f32) + b.astype(f32)).astype(bf16)]
    pallas_call x20 -> x23, Pallas kernels: 89.7 us -> 92.1 us  [call(): pl.pallas_call(kernel, grid_spec=pltpu.PrefetchScalarGridSpec(num_scalar_...]
  transfers between devices with their start and end apart: 43 -> 47, of which waited for: 18 -> 15; matrix products, arithmetic and copies ran while one was open for 7% -> 6% of each run, Pallas kernels for 26% -> 32%
where the time goes in v3:
time: 222 us; the launch traced here: 217 us
  Pallas kernels  92.1 us (41%)
  starting transfers between devices  57.1 us (26%)
  waiting for transfers between devices  48.1 us (22%)
  other arithmetic  11.9 us (5%)
  local copies, waits for them, and re-layouts  6.32 us (3%)
    pallas_call x23, Pallas kernels, call(): pl.pallas_call(kernel, grid_spec=pltpu.PrefetchScalarGridSpec(num_scalar_...  92.1 us
    ppermute x47, starting transfers between devices, swap(): return lax.ppermute(array, AXES, pairs)  57.1 us
    ppermute x47, waiting for transfers between devices, swap(): return lax.ppermute(array, AXES, pairs)  48.1 us
    sin x1, other arithmetic, position_table(): return jnp.concatenate([jnp.sin(angles), jnp.cos(angles)], -1)  4.99 us
    unnamed x40, local copies, waits for them, and re-layouts  4.6 us
  transfers between devices with their start and end apart: 47, of which 15 were waited for; matrix products, arithmetic and copies ran while one was open for 6% of the time, Pallas kernels for 32%

profile of v3, /device:TPU:0, one launch (start us, length us, event | category | flops | bytes accessed | tf_op | source)
XLA Modules:
  0.0 217.3 jit_solution(13330314806481918407)
XLA Ops:
  0.6 3.0 %collective-permute-start.1 = (s32[1,384]{1,0:T(1,128)}, s32[1,384]{1,0:T(1,128)S(1)}, u32[]{:S(2)}, u32[]{:S(2)}) collective-permute-start(s32[1,384]{1,0:T(1,128)} %param.10), channel_id=1, source_target_pairs={{0,1},{1,0},{2,3},{3,2},{4,5},{5,4},{6,7},{7,6},{8,9},{9,8},{10,11... | collective-permute-start | bytes 4616 | tf_op jit(solution)/shard_map/ppermute | solution.py:107
  6.5 5.0 %multiply_sine_fusion = (f32[384,384]{1,0:T(8,128)S(1)}, f32[384,384]{1,0:T(8,128)S(1)}, f32[384,384]{1,0:T(8,128)S(1)}, f32[384,384]{1,0:T(8,128)S(1)}) fusion(f32[384]{0:T(512)S(1)} %convert_reduce_fusion, f32[384]{0:T(512)} %multiply_exponential_fusion, f32[384]{0:T(512)S(1)} %convert_reduce_fusion.1), kind=kLoop, calls=%fused_computation.7 | loop fusion | flops 294912 | bytes 2363904 | tf_op jit(solution)/shard_map/sin | solution.py:33
  12.6 3.4 %shard_map.152 = (bf16[384,768]{1,0:T(8,128)(2,1)S(1)}, bf16[384,2304]{1,0:T(8,128)(2,1)S(1)}) custom-call(s32[10]{0:T(128)S(1)} %stack.37.s, bf16[384,768]{1,0:T(8,128)(2,1)S(1)} %bitcast.24, f32[384,768]{1,0:T(8,128)S(1)} %pad_maximum_fusion.pos, f32[1,768]{1,0:T(1,128)S(1)} %broadcast_in_dim.19.gain, bf16[768,2304]{1,0:T(8,128)(2,1)S(1)} %copy-done), custom_call_target="tpu_custom_call" | custom-call | flops 1 | bytes 1 | tf_op jit(solution)/shard_map/pallas_call | solution.py:51
  16.1 2.7 %collective-permute-done.tok = bf16[384,768]{1,0:T(8,128)(2,1)} collective-permute-done((bf16[384,768]{1,0:T(8,128)(2,1)}, bf16[384,768]{1,0:T(8,128)(2,1)}, u32[]{:S(2)}, u32[]{:S(2)}) %collective-permute-start) | collective-permute-done | bytes 589856 | tf_op jit(solution)/shard_map/ppermute | solution.py:107
  18.8 4.2 %shard_map.153 = (bf16[384,768]{1,0:T(8,128)(2,1)S(1)}, bf16[384,2304]{1,0:T(8,128)(2,1)S(1)}) custom-call(s32[10]{0:T(128)S(1)} %stack.37.s, bf16[384,768]{1,0:T(8,128)(2,1)} %collective-permute-done.tok, f32[384,768]{1,0:T(8,128)S(1)} %pad_maximum_fusion.1.pos, f32[1,768]{1,0:T(1,128)S(1)} %broadcast_in_dim.19.gain, bf16[768,2304]{1,0:T(8,128)(2,1)S(1)} %copy-done), custom_call_target="tpu_custom_call" | custom-call | flops 1 | bytes 1 | tf_op jit(solution)/shard_map/pallas_call | solution.py:51
  23.0 8.5 %shard_map.154.att.att_half.refs_0_ = bf16[384,768]{1,0:T(8,128)(2,1)S(1)} custom-call(s32[10]{0:T(128)S(1)} %stack.37.s, bf16[384,2304]{1,0:T(8,128)(2,1)S(1)} %get-tuple-element.408.q.k_own.v_own.k_o.v_o, bf16[384,2304]{1,0:T(8,128)(2,1)S(1)} %get-tuple-element.408.q.k_own.v_own.k_o.v_o, bf16[384,2304]{1,0:T(8,128)(2,1)S(1)} %get-tuple-element.408.q.k_own.v_own.k_o.v_o, ...), custom_call_target="tpu_custom_call" | custom-call | flops 1 | bytes 1 | tf_op jit(solution)/shard_map/pallas_call | solution.py:51
  31.6 1.6 shard_map.155
  33.3 4.3 %shard_map.156 = (bf16[2,384,512]{2,1,0:T(8,128)(2,1)S(1)}, bf16[2,384,512]{2,1,0:T(8,128)(2,1)S(1)}, f32[384,768]{1,0:T(8,128)S(1)}, f32[384,768]{1,0:T(8,128)S(1)}) custom-call(s32[10]{0:T(128)S(1)} %stack.37.s, bf16[384,768]{1,0:T(8,128)(2,1)S(1)} %get-tuple-element.342.normed, bf16[384,768]{1,0:T(8,128)(2,1)S(1)} %bitcast.16, ...), custom_call_target="tpu_custom_call" | custom-call | flops 1 | bytes 1 | tf_op jit(solution)/shard_map/pallas_call | solution.py:51
  38.6 4.4 %shard_map.157 = (bf16[2,384,512]{2,1,0:T(8,128)(2,1)S(1)}, bf16[2,384,512]{2,1,0:T(8,128)(2,1)S(1)}, f32[384,768]{1,0:T(8,128)S(1)}, f32[384,768]{1,0:T(8,128)S(1)}) custom-call(s32[10]{0:T(128)S(1)} %stack.37.s, bf16[384,768]{1,0:T(8,128)(2,1)S(1)} %get-tuple-element.342.normed, bf16[384,768]{1,0:T(8,128)(2,1)S(1)} %bitcast.18, ...), custom_call_target="tpu_custom_call" | custom-call | flops 1 | bytes 1 | tf_op jit(solution)/shard_map/pallas_call | solution.py:51
  43.2 6.5 %shard_map.158 = (bf16[2,384,512]{2,1,0:T(8,128)(2,1)S(1)}, bf16[2,384,512]{2,1,0:T(8,128)(2,1)S(1)}, bf16[384,768]{1,0:T(8,128)(2,1)}, f32[384,768]{1,0:T(8,128...) custom-call(s32[10]{0:T(128)S(1)} %stack.37.s, ...), custom_call_target="tpu_custom_call" | custom-call | flops 1 | bytes 1 | tf_op jit(solution)/shard_map/pallas_call | solution.py:51
  49.7 2.7 %shard_map.159 = (bf16[8,64,768]{2,1,0:T(8,128)(2,1)S(1)}, bf16[8,64,768]{2,1,0:T(8,128)(2,1)S(1)}) custom-call(s32[10]{0:T(128)S(1)} %stack.37.s, bf16[2,384,512]{2,1,0:T(8,128)(2,1)S(1)} %get-tuple-element.360.act.grad, bf16[2,384,512]{2,1,0:T(8,128)(2,1)S(1)} %collective-permute-done.5.act_o.grad_o, bf16[2,384,512]{2,1,0:T(8,128)(2,1)S(1)} %get-tuple-element.360.act.grad, ...), custom_call_target="tpu_custom_call" | custom-call | flops 1 | bytes 1 | tf_op jit(solution)/shard_map/pallas_call | solution.py:51
  55.8 2.5 %shard_map.160 = (bf16[8,64,768]{2,1,0:T(8,128)(2,1)S(1)}, bf16[8,64,768]{2,1,0:T(8,128)(2,1)S(1)}) custom-call(s32[10]{0:T(128)S(1)} %stack.37.s, bf16[2,384,512]{2,1,0:T(8,128)(2,1)S(1)} %get-tuple-element.369.act.grad, bf16[2,384,512]{2,1,0:T(8,128)(2,1)S(1)} %collective-permute-done.6.act_o.grad_o, bf16[2,384,512]{2,1,0:T(8,128)(2,1)S(1)} %get-tuple-element.369.act.grad, ...), custom_call_target="tpu_custom_call" | custom-call | flops 1 | bytes 1 | tf_op jit(solution)/shard_map/pallas_call | solution.py:51
  58.3 9.6 %shard_map.161 = (bf16[384,384]{1,0:T(8,128)(2,1)S(1)}, f32[768,384]{1,0:T(8,128)S(1)}, f32[768,384]{1,0:T(8,128)S(1)}) custom-call(s32[10]{0:T(128)S(1)} %stack.37.s, bf16[384,2304]{1,0:T(8,128)(2,1)S(1)} %get-tuple-element.408.q.k_own.v_own.k_o.v_o, bf16[384,384]{1,0:T(8,128)(2,1)S(1)} %get-tuple-element.377.g, ...), custom_call_target="tpu_custom_call" | custom-call | flops 1 | bytes 1 | tf_op jit(solution)/shard_map/pallas_call | solution.py:51
  67.9 3.0 %collective-permute-done.8.g = bf16[384,384]{1,0:T(8,128)(2,1)S(1)} collective-permute-done((bf16[384,384]{1,0:T(8,128)(2,1)S(1)}, bf16[384,384]{1,0:T(8,128)(2,1)S(1)}, u32[]{:S(2)}, u32[]{:S(2)}) %collective-permute-start.8) | collective-permute-done | bytes 294944 | tf_op jit(solution)/shard_map/ppermute | solution.py:107
  70.9 1.5 collective-permute-start.12
  72.5 1.6 collective-permute-start.11
  74.2 3.4 %shard_map.162 = (bf16[8,96,768]{2,1,0:T(8,128)(2,1)S(1)}, bf16[8,96,768]{2,1,0:T(8,128)(2,1)S(1)}) custom-call(s32[10]{0:T(128)S(1)} %stack.37.s, bf16[2,384,512]{2,1,0:T(8,128)(2,1)S(1)} %get-tuple-element.395.act.grad, bf16[2,384,512]{2,1,0:T(8,128)(2,1)S(1)} %collective-permute-done.9.act_o.grad_o, bf16[2,384,512]{2,1,0:T(8,128)(2,1)S(1)} %get-tuple-element.395.act.grad, ...), custom_call_target="tpu_custom_call" | custom-call | flops 1 | bytes 1 | tf_op jit(solution)/shard_map/pallas_call | solution.py:51
  78.2 9.8 %shard_map.163 = (bf16[384,384]{1,0:T(8,128)(2,1)S(1)}, bf16[768,384]{1,0:T(8,128)(2,1)S(1)}, bf16[768,384]{1,0:T(8,128)(2,1)S(1)}) custom-call(s32[10]{0:T(128)S(1)} %stack.37.s, bf16[384,2304]{1,0:T(8,128)(2,1)S(1)} %get-tuple-element.406.k_far.v_far.k_f.v_f.q, bf16[384,384]{1,0:T(8,128)(2,1)S(1)} %collective-permute-done.8.g, ...), custom_call_target="tpu_custom_call" | custom-call | flops 1 | bytes 1 | tf_op jit(solution)/shard_map/pallas_call | solution.py:51
  88.7 4.1 %collective-permute-done.11 = bf16[8,64,768]{2,1,0:T(8,128)(2,1)S(1)} collective-permute-done((bf16[8,64,768]{2,1,0:T(8,128)(2,1)S(1)}, bf16[8,64,768]{2,1,0:T(8,128)(2,1)S(1)}, u32[]{:S(2)}, u32[]{:S(2)}) %collective-permute-start.11) | collective-permute-done | bytes 786464 | tf_op jit(solution)/shard_map/ppermute | solution.py:107
  93.0 3.4 %shard_map.164 = (bf16[8,48,1152]{2,1,0:T(8,128)(2,1)S(1)}, bf16[8,48,1152]{2,1,0:T(8,128)(2,1)S(1)}) custom-call(s32[10]{0:T(128)S(1)} %stack.37.s, bf16[384,768]{1,0:T(8,128)(2,1)S(1)} %get-tuple-element.425.n_own, bf16[384,768]{1,0:T(8,128)(2,1)S(1)} %get-tuple-element.426.n_far, bf16[384,384]{1,0:T(8,128)(2,1)S(1)} %get-tuple-element.452.gq_o, ...), custom_call_target="tpu_custom_call" | custom-call | flops 1 | bytes 1 | tf_op jit(solution)/shard_map/pallas_call | solution.py:51
  96.4 2.6 %collective-permute-done.16 = bf16[2,64,768]{2,1,0:T(8,128)(2,1)S(1)} collective-permute-done((bf16[2,64,768]{2,1,0:T(8,128)(2,1)S(1)}, bf16[2,64,768]{2,1,0:T(8,128)(2,1)S(1)}, u32[]{:S(2)}, u32[]{:S(2)}) %collective-permute-start.16) | collective-permute-done | bytes 196640 | tf_op jit(solution)/shard_map/ppermute | solution.py:107
  99.1 1.9 collective-permute-start.21
  104.3 2.6 %shard_map.165 = (f32[384,768]{1,0:T(8,128)S(1)}, bf16[384,768]{1,0:T(8,128)(2,1)S(1)}) custom-call(s32[10]{0:T(128)S(1)} %stack.37.s, bf16[384,384]{1,0:T(8,128)(2,1)S(1)} %get-tuple-element.452.gq_o, bf16[384,384]{1,0:T(8,128)(2,1)S(1)} %get-tuple-element.453.gq_f, bf16[768,384]{1,0:T(8,128)(2,1)S(1)} %get-tuple-element.454.gk, ...), custom_call_target="tpu_custom_call" | custom-call | flops 1 | bytes 1 | tf_op jit(solution)/shard_map/pallas_call | solution.py:51
  108.1 2.2 %collective-permute-start.26 = (bf16[2,64,768]{2,1,0:T(8,128)(2,1)S(1)}, bf16[2,64,768]{2,1,0:T(8,128)(2,1)S(1)}, u32[]{:S(2)}, u32[]{:S(2)}) collective-permute-start(bf16[2,64,768]{2,1,0:T(8,128)(2,1)S(1)} %add_convert_fusion.17), channel_id=1, source_target_pairs={{0,16},{1,17},{2,18},{3,19},{4,20},{5,21},{6,22},{7,23},{8,24},{9,... | collective-permute-start | bytes 589832 | tf_op jit(solution)/shard_map/ppermute | solution.py:107
  110.3 2.8 %collective-permute-start.23 = (bf16[2,64,768]{2,1,0:T(8,128)(2,1)S(1)}, bf16[2,64,768]{2,1,0:T(8,128)(2,1)S(1)}, u32[]{:S(2)}, u32[]{:S(2)}) collective-permute-start(bf16[2,64,768]{2,1,0:T(8,128)(2,1)S(1)} %add_convert_fusion.18), channel_id=1, source_target_pairs={{0,8},{1,9},{2,3},{3,2},{4,12},{5,13},{6,7},{7,6},{8,0},{9,1},{10,... | collective-permute-start | bytes 589832 | tf_op jit(solution)/shard_map/ppermute | solution.py:107
  113.1 2.6 %collective-permute-done.19 = bf16[4,96,768]{2,1,0:T(8,128)(2,1)S(1)} collective-permute-done((bf16[4,96,768]{2,1,0:T(8,128)(2,1)S(1)}, bf16[4,96,768]{2,1,0:T(8,128)(2,1)S(1)}, u32[]{:S(2)}, u32[]{:S(2)}) %collective-permute-start.19) | collective-permute-done | bytes 589856 | tf_op jit(solution)/shard_map/ppermute | solution.py:107
  117.3 5.4 %collective-permute-done.23 = bf16[2,64,768]{2,1,0:T(8,128)(2,1)S(1)} collective-permute-done((bf16[2,64,768]{2,1,0:T(8,128)(2,1)S(1)}, bf16[2,64,768]{2,1,0:T(8,128)(2,1)S(1)}, u32[]{:S(2)}, u32[]{:S(2)}) %collective-permute-start.23) | collective-permute-done | bytes 196640 | tf_op jit(solution)/shard_map/ppermute | solution.py:107
  122.7 6.2 %collective-permute-done.22 = bf16[2,96,768]{2,1,0:T(8,128)(2,1)S(1)} collective-permute-done((bf16[2,96,768]{2,1,0:T(8,128)(2,1)S(1)}, bf16[2,96,768]{2,1,0:T(8,128)(2,1)S(1)}, u32[]{:S(2)}, u32[]{:S(2)}) %collective-permute-start.22) | collective-permute-done | bytes 294944 | tf_op jit(solution)/shard_map/ppermute | solution.py:107
  129.5 4.5 %collective-permute-start.28 = (bf16[2,96,768]{2,1,0:T(8,128)(2,1)S(1)}, bf16[2,96,768]{2,1,0:T(8,128)(2,1)S(1)}, u32[]{:S(2)}, u32[]{:S(2)}) collective-permute-start(bf16[2,96,768]{2,1,0:T(8,128)(2,1)S(1)} %add_convert_fusion.9), channel_id=1, source_target_pairs={{0,16},{1,17},{2,18},{3,19},{4,20},{5,21},{6,22},{7,23},{8,24},{9,... | collective-permute-start | bytes 884744 | tf_op jit(solution)/shard_map/ppermute | solution.py:107
  134.1 3.7 %collective-permute-start.32 = (bf16[8,64,768]{2,1,0:T(8,128)(2,1)S(1)}, bf16[8,64,768]{2,1,0:T(8,128)(2,1)S(1)}, u32[]{:S(2)}, u32[]{:S(2)}) collective-permute-start(bf16[8,64,768]{2,1,0:T(8,128)(2,1)S(1)} %constant_dynamic-update-slice_fusion.2.own), channel_id=1, source_target_pairs={{0,2},{1,3},{2,0},{3,1},{4,6},{5,7},{6,4},{7,5},{8,10},{9,11},{10,... | collective-permute-start | bytes 2359304 | tf_op jit(solution)/shard_map/ppermute | solution.py:107
  137.8 3.3 %collective-permute-start.27 = (bf16[8,64,768]{2,1,0:T(8,128)(2,1)S(1)}, bf16[8,64,768]{2,1,0:T(8,128)(2,1)S(1)}, u32[]{:S(2)}, u32[]{:S(2)}) collective-permute-start(bf16[8,64,768]{2,1,0:T(8,128)(2,1)S(1)} %constant_dynamic-update-slice_fusion.2.own), channel_id=1, source_target_pairs={{0,1},{1,0},{2,6},{3,7},{4,5},{5,4},{6,2},{7,3},{8,9},{9,8},{10,14... | collective-permute-start | bytes 2359304 | tf_op jit(solution)/shard_map/ppermute | solution.py:107
  141.3 4.4 %collective-permute-start.29 = (bf16[2,96,768]{2,1,0:T(8,128)(2,1)S(1)}, bf16[2,96,768]{2,1,0:T(8,128)(2,1)S(1)}, u32[]{:S(2)}, u32[]{:S(2)}) collective-permute-start(bf16[2,96,768]{2,1,0:T(8,128)(2,1)S(1)} %add_convert_fusion.8), channel_id=1, source_target_pairs={{0,8},{1,9},{2,3},{3,2},{4,12},{5,13},{6,7},{7,6},{8,0},{9,1},{10,... | collective-permute-start | bytes 884744 | tf_op jit(solution)/shard_map/ppermute | solution.py:107
  145.8 1.6 collective-permute-start.33
  147.3 3.4 %collective-permute-start.31 = (bf16[2,48,1152]{2,1,0:T(8,128)(2,1)S(1)}, bf16[2,48,1152]{2,1,0:T(8,128)(2,1)S(1)}, u32[]{:S(2)}, u32[]{:S(2)}) collective-permute-start(bf16[2,48,1152]{2,1,0:T(8,128)(2,1)S(1)} %add_convert_fusion.13), channel_id=1, source_target_pairs={{0,16},{1,17},{2,18},{3,19},{4,20},{5,21},{6,22},{7,23},{8,24},{9,... | collective-permute-start | bytes 663560 | tf_op jit(solution)/shard_map/ppermute | solution.py:107
  151.6 1.9 collective-permute-start.37
  153.5 2.4 %shard_map.166 = f32[384,768]{1,0:T(8,128)} custom-call(s32[10]{0:T(128)S(1)} %stack.37.s, f32[384,768]{1,0:T(8,128)S(1)} %get-tuple-element.504.own, bf16[384,768]{1,0:T(8,128)(2,1)S(1)} %collective-permute-done.17.far, bf16[384,768]{1,0:T(8,128)(2,1)S(1)} %bitcast.26, f32[384,768]{1,0:T(8,128)S(1)} %pad_maximum_fusion.pos, ...), custom_call_target="tpu_custom_call" | custom-call | flops 1 | bytes 1 | tf_op jit(solution)/shard_map/pallas_call | solution.py:51
  156.2 5.8 %collective-permute-start.36 = (bf16[8,64,768]{2,1,0:T(8,128)(2,1)S(1)}, bf16[8,64,768]{2,1,0:T(8,128)(2,1)S(1)}, u32[]{:S(2)}, u32[]{:S(2)}) collective-permute-start(bf16[8,64,768]{2,1,0:T(8,128)(2,1)S(1)} %constant_dynamic-update-slice_fusion.8.own), channel_id=1, source_target_pairs={{0,2},{1,3},{2,0},{3,1},{4,6},{5,7},{6,4},{7,5},{8,10},{9,11},{10,... | collective-permute-start | bytes 2359304 | tf_op jit(solution)/shard_map/ppermute | solution.py:107
  162.2 2.6 %shard_map.167 = (f32[2,768,128]{2,1,0:T(8,128)S(1)}, f32[3072,768]{1,0:T(8,128)}, f32[768,3072]{1,0:T(8,128)}) custom-call(s32[10]{0:T(128)S(1)} %stack.37.s, bf16[8,64,768]{2,1,0:T(8,128)(2,1)S(1)} %constant_dynamic-update-slice_fusion.2.own, bf16[8,64,768]{2,1,0:T(8,128)(2,1)S(1)} %collective-permute-done.32.other, ...), custom_call_target="tpu_custom_call", output_to_operand_aliasing={{0}: (4, {})} | custom-call | flops 1 | bytes 1 | tf_op jit(solution)/shard_map/pallas_call | solution.py:51
  164.8 2.3 %collective-permute-start.34 = (bf16[2,48,1152]{2,1,0:T(8,128)(2,1)S(1)}, bf16[2,48,1152]{2,1,0:T(8,128)(2,1)S(1)}, u32[]{:S(2)}, u32[]{:S(2)}) collective-permute-start(bf16[2,48,1152]{2,1,0:T(8,128)(2,1)S(1)} %add_convert_fusion.12), channel_id=1, source_target_pairs={{0,1},{1,0},{2,3},{3,2},{4,5},{5,4},{6,7},{7,6},{8,9},{9,8},{10,11... | collective-permute-start | bytes 663560 | tf_op jit(solution)/shard_map/ppermute | solution.py:107
  167.2 2.6 %shard_map.168 = (f32[2,768,128]{2,1,0:T(8,128)S(1)}, f32[3072,768]{1,0:T(8,128)}, f32[768,3072]{1,0:T(8,128)}) custom-call(s32[10]{0:T(128)S(1)} %stack.37.s, bf16[8,64,768]{2,1,0:T(8,128)(2,1)S(1)} %constant_dynamic-update-slice_fusion.8.own, ...), custom_call_target="tpu_custom_call", output_to_operand_aliasing={{0}: (4, {}), {1}: (5, {}), {2}: (6, {})} | custom-call | flops 1 | bytes 1 | tf_op jit(solution)/shard_map/pallas_call | solution.py:51
  169.7 2.6 %shard_map.169 = (f32[2,768,128]{2,1,0:T(8,128)S(1)}, f32[3072,768]{1,0:T(8,128)}, f32[768,3072]{1,0:T(8,128)}) custom-call(s32[10]{0:T(128)S(1)} %stack.37.s, bf16[8,64,768]{2,1,0:T(8,128)(2,1)S(1)} %collective-permute-done.27.own, ...), custom_call_target="tpu_custom_call", output_to_operand_aliasing={{0}: (4, {}), {1}: (5, {}), {2}: (6, {})} | custom-call | flops 1 | bytes 1 | tf_op jit(solution)/shard_map/pallas_call | solution.py:51
  174.5 11.8 %collective-permute-done.38 = bf16[2,48,2304]{2,1,0:T(8,128)(2,1)S(1)} collective-permute-done((bf16[2,48,2304]{2,1,0:T(8,128)(2,1)S(1)}, bf16[2,48,2304]{2,1,0:T(8,128)(2,1)S(1)}, u32[]{:S(2)}, u32[]{:S(2)}) %collective-permute-start.38) | collective-permute-done | bytes 442400 | tf_op jit(solution)/shard_map/ppermute | solution.py:107
  187.9 5.2 %collective-permute-done.44.own = bf16[8,96,768]{2,1,0:T(8,128)(2,1)S(1)} collective-permute-done((bf16[8,96,768]{2,1,0:T(8,128)(2,1)S(1)}, bf16[8,96,768]{2,1,0:T(8,128)(2,1)S(1)}, u32[]{:S(2)}, u32[]{:S(2)}) %collective-permute-start.44) | collective-permute-done | bytes 1179680 | tf_op jit(solution)/shard_map/ppermute | solution.py:107
  194.2 2.6 %shard_map.170 = (f32[2,768,128]{2,1,0:T(8,128)S(1)}, f32[3072,768]{1,0:T(8,128)}, f32[768,3072]{1,0:T(8,128)}) custom-call(s32[10]{0:T(128)S(1)} %stack.37.s, bf16[8,64,768]{2,1,0:T(8,128)(2,1)S(1)} %collective-permute-done.39.own, ...), custom_call_target="tpu_custom_call", output_to_operand_aliasing={{0}: (4, {}), {1}: (5, {}), {2}: (6, {})} | custom-call | flops 1 | bytes 1 | tf_op jit(solution)/shard_map/pallas_call | solution.py:51
  196.8 3.0 %shard_map.171 = (f32[2,768,128]{2,1,0:T(8,128)S(1)}, f32[3072,768]{1,0:T(8,128)}, f32[768,3072]{1,0:T(8,128)}, f32[768,768]{1,0:T(8,128)}) custom-call(s32[10]{0:T(128)S(1)} %stack.37.s, bf16[8,96,768]{2,1,0:T(8,128)(2,1)S(1)} %constant_dynamic-update-slice_fusion.10.own, ...), custom_call_target="tpu_custom_call", output_to_operand_aliasing={{0}: (4, {}), {1}: (5, {}), {2}: (6, {})} | custom-call | flops 1 | bytes 1 | tf_op jit(solution)/shard_map/pallas_call | solution.py:51
  199.8 2.6 %shard_map.172 = (f32[768,2304]{1,0:T(8,128)}, f32[768,128]{1,0:T(8,128)S(1)}) custom-call(s32[10]{0:T(128)S(1)} %stack.37.s, bf16[4,48,2304]{2,1,0:T(8,128)(2,1)S(1)} %constant_dynamic-update-slice_fusion.14.own, bf16[4,48,2304]{2,1,0:T(8,128)(2,1)S(1)} %collective-permute-done.41.other, bf16[768,2304]{1,0:T(8,128)(2,1)S(1)} %copy-done), custom_call_target="tpu_custom_call" | custom-call | flops 1 | bytes 1 | tf_op jit(solution)/shard_map/pallas_call | solution.py:51
  203.4 3.0 %shard_map.173 = (f32[2,768,128]{2,1,0:T(8,128)S(1)}, f32[3072,768]{1,0:T(8,128)}, f32[768,3072]{1,0:T(8,128)}, f32[768,768]{1,0:T(8,128)}) custom-call(s32[10]{0:T(128)S(1)} %stack.37.s, bf16[8,96,768]{2,1,0:T(8,128)(2,1)S(1)} %collective-permute-done.44.own, ...), custom_call_target="tpu_custom_call", output_to_operand_aliasing={{0}: (4, {}), {1}: (5, {}), {2}: (6, {}), {3}: (7, {})} | custom-call | flops 1 | bytes 1 | tf_op jit(solution)/shard_map/pallas_call | solution.py:51
  210.3 4.0 %shard_map.174 = (f32[768,2304]{1,0:T(8,128)}, f32[768,128]{1,0:T(8,128)S(1)}) custom-call(s32[10]{0:T(128)S(1)} %stack.37.s, bf16[4,48,2304]{2,1,0:T(8,128)(2,1)} %collective-permute-done.40.own, bf16[4,48,2304]{2,1,0:T(8,128)(2,1)} %collective-permute-done.45.other, bf16[768,2304]{1,0:T(8,128)(2,1)S(1)} %copy-done, ...), custom_call_target="tpu_custom_call", output_to_operand_aliasing={{0}: (4, {}), {1}: (5, {})} | custom-call | flops 1 | bytes 1 | tf_op jit(solution)/shard_map/pallas_call | solution.py:51
  (157 shorter events, 30.9 us)
Async XLA Ops:
  0.6 5.9 %collective-permute-start.1 = (s32[1,384]{1,0:T(1,128)}, s32[1,384]{1,0:T(1,128)S(1)}, u32[]{:S(2)}, u32[]{:S(2)}) collective-permute-start(s32[1,384]{1,0:T(1,128)} %param.10), channel_id=1, source_target_pairs={{0,1},{1,0},{2,3},{3,2},{4,5},{5,4},{6,7},{7,6},{8,9},{9,8},{10,11... | collective-permute-start | bytes 4616 | tf_op jit(solution)/shard_map/ppermute | solution.py:107
  3.7 15.1 %collective-permute-start = (bf16[384,768]{1,0:T(8,128)(2,1)}, bf16[384,768]{1,0:T(8,128)(2,1)}, u32[]{:S(2)}, u32[]{:S(2)}) collective-permute-start(bf16[384,768]{1,0:T(8,128)(2,1)} %bitcast.23), channel_id=1, source_target_pairs={{0,1},{1,0},{2,3},{3,2},{4,5},{5,4},{6,7},{7,6},{8,9},{9,8},{10,11... | collective-permute-start | bytes 1769480 | tf_op jit(solution)/shard_map/ppermute | solution.py:107
  18.8 12.8 %copy-start.3 = (bf16[768,768]{1,0:T(8,128)(2,1)S(1)}, bf16[768,768]{1,0:T(8,128)(2,1)}, u32[]{:S(2)}) copy-start(bf16[768,768]{1,0:T(8,128)(2,1)} %refs_5_) | copy-start | bytes 3538948
  37.5 5.6 %collective-permute-start.5 = (bf16[2,384,512]{2,1,0:T(8,128)(2,1)S(1)}, bf16[2,384,512]{2,1,0:T(8,128)(2,1)S(1)}, u32[]{:S(2)}, u32[]{:S(2)}) collective-permute-start(bf16[2,384,512]{2,1,0:T(8,128)(2,1)S(1)} %get-tuple-element.338), channel_id=1, source_target_pairs={{0,2},{1,3},{2,0},{3,1},{4,6},{5,7},{6,4},{7,5},{8,10},{9,11},{10,... | collective-permute-start | bytes 2359304 | tf_op jit(solution)/shard_map/ppermute | solution.py:107
  37.6 5.6 %collective-permute-start.2 = (bf16[384,768]{1,0:T(8,128)(2,1)S(1)}, bf16[384,768]{1,0:T(8,128)(2,1)S(1)}, u32[]{:S(2)}, u32[]{:S(2)}) collective-permute-start(bf16[384,768]{1,0:T(8,128)(2,1)S(1)} %bitcast.17), channel_id=1, source_target_pairs={{0,2},{1,3},{2,0},{3,1},{4,6},{5,7},{6,4},{7,5},{8,10},{9,11},{10,... | collective-permute-start | bytes 1769480 | tf_op jit(solution)/shard_map/ppermute | solution.py:107
  38.1 5.1 %collective-permute-start.3 = (bf16[768,384]{1,0:T(8,128)(2,1)S(1)}, bf16[768,384]{1,0:T(8,128)(2,1)S(1)}, u32[]{:S(2)}, u32[]{:S(2)}) collective-permute-start(bf16[768,384]{1,0:T(8,128)(2,1)S(1)} %get-tuple-element.399.nt), channel_id=1, source_target_pairs={{0,2},{1,3},{2,0},{3,1},{4,6},{5,7},{6,4},{7,5},{8,10},{9,11},{10,... | collective-permute-start | bytes 1769480 | tf_op jit(solution)/shard_map/ppermute | solution.py:107
  38.2 5.0 %collective-permute-start.4 = (bf16[384,384]{1,0:T(8,128)(2,1)S(1)}, bf16[384,384]{1,0:T(8,128)(2,1)S(1)}, u32[]{:S(2)}, u32[]{:S(2)}) collective-permute-start(bf16[384,384]{1,0:T(8,128)(2,1)S(1)} %get-tuple-element.336), channel_id=1, source_target_pairs={{0,2},{1,3},{2,0},{3,1},{4,6},{5,7},{6,4},{7,5},{8,10},{9,11},{10,... | collective-permute-start | bytes 884744 | tf_op jit(solution)/shard_map/ppermute | solution.py:107
  43.0 12.7 %collective-permute-start.6 = (bf16[2,384,512]{2,1,0:T(8,128)(2,1)S(1)}, bf16[2,384,512]{2,1,0:T(8,128)(2,1)S(1)}, u32[]{:S(2)}, u32[]{:S(2)}) collective-permute-start(bf16[2,384,512]{2,1,0:T(8,128)(2,1)S(1)} %get-tuple-element.355), channel_id=1, source_target_pairs={{0,2},{1,3},{2,0},{3,1},{4,6},{5,7},{6,4},{7,5},{8,10},{9,11},{10,... | collective-permute-start | bytes 2359304 | tf_op jit(solution)/shard_map/ppermute | solution.py:107
  52.4 18.4 %collective-permute-start.10 = (bf16[8,64,768]{2,1,0:T(8,128)(2,1)S(1)}, bf16[8,64,768]{2,1,0:T(8,128)(2,1)S(1)}, u32[]{:S(2)}, u32[]{:S(2)}) collective-permute-start(bf16[8,64,768]{2,1,0:T(8,128)(2,1)S(1)} %get-tuple-element.388), channel_id=1, source_target_pairs={{0,1},{1,0},{2,6},{3,7},{4,5},{5,4},{6,2},{7,3},{8,9},{9,8},{10,14... | collective-permute-start | bytes 2359304 | tf_op jit(solution)/shard_map/ppermute | solution.py:107
  52.9 2.9 %collective-permute-start.7 = (bf16[384,768]{1,0:T(8,128)(2,1)S(1)}, bf16[384,768]{1,0:T(8,128)(2,1)S(1)}, u32[]{:S(2)}, u32[]{:S(2)}) collective-permute-start(bf16[384,768]{1,0:T(8,128)(2,1)S(1)} %get-tuple-element.403.refs_2_), channel_id=1, source_target_pairs={{0,2},{1,3},{2,0},{3,1},{4,6},{5,7},{6,4},{7,5},{8,10},{9,11},{10,... | collective-permute-start | bytes 1769480 | tf_op jit(solution)/shard_map/ppermute | solution.py:107
  54.1 16.7 %collective-permute-start.8 = (bf16[384,384]{1,0:T(8,128)(2,1)S(1)}, bf16[384,384]{1,0:T(8,128)(2,1)S(1)}, u32[]{:S(2)}, u32[]{:S(2)}) collective-permute-start(bf16[384,384]{1,0:T(8,128)(2,1)S(1)} %get-tuple-element.381), channel_id=1, source_target_pairs={{0,1},{1,0},{2,3},{3,2},{4,5},{5,4},{6,7},{7,6},{8,9},{9,8},{10,11... | collective-permute-start | bytes 884744 | tf_op jit(solution)/shard_map/ppermute | solution.py:107
  54.7 19.5 %collective-permute-start.9 = (bf16[2,384,512]{2,1,0:T(8,128)(2,1)S(1)}, bf16[2,384,512]{2,1,0:T(8,128)(2,1)S(1)}, u32[]{:S(2)}, u32[]{:S(2)}) collective-permute-start(bf16[2,384,512]{2,1,0:T(8,128)(2,1)S(1)} %get-tuple-element.386), channel_id=1, source_target_pairs={{0,2},{1,3},{2,0},{3,1},{4,6},{5,7},{6,4},{7,5},{8,10},{9,11},{10,... | collective-permute-start | bytes 2359304 | tf_op jit(solution)/shard_map/ppermute | solution.py:107
  70.9 17.1 %collective-permute-start.12 = (bf16[4,64,768]{2,1,0:T(8,128)(2,1)S(1)}, bf16[4,64,768]{2,1,0:T(8,128)(2,1)S(1)}, u32[]{:S(2)}, u32[]{:S(2)}) collective-permute-start(bf16[4,64,768]{2,1,0:T(8,128)(2,1)S(1)} %add_convert_fusion.7), channel_id=1, source_target_pairs={{0,4},{1,5},{2,10},{3,11},{4,0},{5,1},{6,14},{7,15},{8,12},{9,13},... | collective-permute-start | bytes 1179656 | tf_op jit(solution)/shard_map/ppermute | solution.py:107
  72.5 20.3 %collective-permute-start.11 = (bf16[8,64,768]{2,1,0:T(8,128)(2,1)S(1)}, bf16[8,64,768]{2,1,0:T(8,128)(2,1)S(1)}, u32[]{:S(2)}, u32[]{:S(2)}) collective-permute-start(bf16[8,64,768]{2,1,0:T(8,128)(2,1)S(1)} %get-tuple-element.415), channel_id=1, source_target_pairs={{0,8},{1,9},{2,6},{3,7},{4,12},{5,13},{6,2},{7,3},{8,0},{9,1},{10,... | collective-permute-start | bytes 2359304 | tf_op jit(solution)/shard_map/ppermute | solution.py:107
  77.6 23.4 %collective-permute-start.15 = (bf16[8,96,768]{2,1,0:T(8,128)(2,1)S(1)}, bf16[8,96,768]{2,1,0:T(8,128)(2,1)S(1)}, u32[]{:S(2)}, u32[]{:S(2)}) collective-permute-start(bf16[8,96,768]{2,1,0:T(8,128)(2,1)S(1)} %get-tuple-element.436), channel_id=1, source_target_pairs={{0,4},{1,5},{2,10},{3,11},{4,0},{5,1},{6,14},{7,15},{8,12},{9,13},... | collective-permute-start | bytes 3538952 | tf_op jit(solution)/shard_map/ppermute | solution.py:107
  88.1 11.0 %collective-permute-start.16 = (bf16[2,64,768]{2,1,0:T(8,128)(2,1)S(1)}, bf16[2,64,768]{2,1,0:T(8,128)(2,1)S(1)}, u32[]{:S(2)}, u32[]{:S(2)}) collective-permute-start(bf16[2,64,768]{2,1,0:T(8,128)(2,1)S(1)} %add_convert_fusion.23), channel_id=1, source_target_pairs={{0,8},{1,9},{2,3},{3,2},{4,12},{5,13},{6,7},{7,6},{8,0},{9,1},{10,... | collective-permute-start | bytes 589832 | tf_op jit(solution)/shard_map/ppermute | solution.py:107
  92.9 8.9 %collective-permute-start.14 = (bf16[4,64,768]{2,1,0:T(8,128)(2,1)S(1)}, bf16[4,64,768]{2,1,0:T(8,128)(2,1)S(1)}, u32[]{:S(2)}, u32[]{:S(2)}) collective-permute-start(bf16[4,64,768]{2,1,0:T(8,128)(2,1)S(1)} %add_convert_fusion.5), channel_id=1, source_target_pairs={{0,4},{1,5},{2,3},{3,2},{4,0},{5,1},{6,7},{7,6},{8,12},{9,13},{10,... | collective-permute-start | bytes 1179656 | tf_op jit(solution)/shard_map/ppermute | solution.py:107
  99.1 8.8 %collective-permute-start.21 = (bf16[2,64,768]{2,1,0:T(8,128)(2,1)S(1)}, bf16[2,64,768]{2,1,0:T(8,128)(2,1)S(1)}, u32[]{:S(2)}, u32[]{:S(2)}) collective-permute-start(bf16[2,64,768]{2,1,0:T(8,128)(2,1)S(1)} %add_convert_fusion.21), channel_id=1, source_target_pairs={{0,16},{1,17},{2,18},{3,19},{4,20},{5,21},{6,22},{7,23},{8,24},{9,... | collective-permute-start | bytes 589832 | tf_op jit(solution)/shard_map/ppermute | solution.py:107
  101.0 3.1 %collective-permute-start.13 = (bf16[8,48,1152]{2,1,0:T(8,128)(2,1)S(1)}, bf16[8,48,1152]{2,1,0:T(8,128)(2,1)S(1)}, u32[]{:S(2)}, u32[]{:S(2)}) collective-permute-start(bf16[8,48,1152]{2,1,0:T(8,128)(2,1)S(1)} %get-tuple-element.433), channel_id=1, source_target_pairs={{0,2},{1,3},{2,0},{3,1},{4,6},{5,7},{6,4},{7,5},{8,10},{9,11},{10,... | collective-permute-start | bytes 2654216 | tf_op jit(solution)/shard_map/ppermute | solution.py:107
  101.9 6.1 %collective-permute-start.20 = (bf16[2,64,768]{2,1,0:T(8,128)(2,1)S(1)}, bf16[2,64,768]{2,1,0:T(8,128)(2,1)S(1)}, u32[]{:S(2)}, u32[]{:S(2)}) collective-permute-start(bf16[2,64,768]{2,1,0:T(8,128)(2,1)S(1)} %add_convert_fusion.20), channel_id=1, source_target_pairs={{0,1},{1,0},{2,10},{3,11},{4,5},{5,4},{6,14},{7,15},{8,9},{9,8},{1... | collective-permute-start | bytes 589832 | tf_op jit(solution)/shard_map/ppermute | solution.py:107
  102.5 13.2 %collective-permute-start.19 = (bf16[4,96,768]{2,1,0:T(8,128)(2,1)S(1)}, bf16[4,96,768]{2,1,0:T(8,128)(2,1)S(1)}, u32[]{:S(2)}, u32[]{:S(2)}) collective-permute-start(bf16[4,96,768]{2,1,0:T(8,128)(2,1)S(1)} %add_convert_fusion.1), channel_id=1, source_target_pairs={{0,1},{1,0},{2,6},{3,7},{4,5},{5,4},{6,2},{7,3},{8,9},{9,8},{10,14... | collective-permute-start | bytes 1769480 | tf_op jit(solution)/shard_map/ppermute | solution.py:107
  108.1 21.1 %collective-permute-start.26 = (bf16[2,64,768]{2,1,0:T(8,128)(2,1)S(1)}, bf16[2,64,768]{2,1,0:T(8,128)(2,1)S(1)}, u32[]{:S(2)}, u32[]{:S(2)}) collective-permute-start(bf16[2,64,768]{2,1,0:T(8,128)(2,1)S(1)} %add_convert_fusion.17), channel_id=1, source_target_pairs={{0,16},{1,17},{2,18},{3,19},{4,20},{5,21},{6,22},{7,23},{8,24},{9,... | collective-permute-start | bytes 589832 | tf_op jit(solution)/shard_map/ppermute | solution.py:107
  110.3 12.3 %collective-permute-start.23 = (bf16[2,64,768]{2,1,0:T(8,128)(2,1)S(1)}, bf16[2,64,768]{2,1,0:T(8,128)(2,1)S(1)}, u32[]{:S(2)}, u32[]{:S(2)}) collective-permute-start(bf16[2,64,768]{2,1,0:T(8,128)(2,1)S(1)} %add_convert_fusion.18), channel_id=1, source_target_pairs={{0,8},{1,9},{2,3},{3,2},{4,12},{5,13},{6,7},{7,6},{8,0},{9,1},{10,... | collective-permute-start | bytes 589832 | tf_op jit(solution)/shard_map/ppermute | solution.py:107
  113.1 16.0 %collective-permute-start.18 = (bf16[4,48,1152]{2,1,0:T(8,128)(2,1)S(1)}, bf16[4,48,1152]{2,1,0:T(8,128)(2,1)S(1)}, u32[]{:S(2)}, u32[]{:S(2)}) collective-permute-start(bf16[4,48,1152]{2,1,0:T(8,128)(2,1)S(1)} %add_convert_fusion.3), channel_id=1, source_target_pairs={{0,4},{1,5},{2,10},{3,11},{4,0},{5,1},{6,14},{7,15},{8,12},{9,13},... | collective-permute-start | bytes 1327112 | tf_op jit(solution)/shard_map/ppermute | solution.py:107
  113.1 28.2 %collective-permute-start.17 = (bf16[384,768]{1,0:T(8,128)(2,1)S(1)}, bf16[384,768]{1,0:T(8,128)(2,1)S(1)}, u32[]{:S(2)}, u32[]{:S(2)}) collective-permute-start(bf16[384,768]{1,0:T(8,128)(2,1)S(1)} %get-tuple-element.459), channel_id=1, source_target_pairs={{0,1},{1,0},{2,3},{3,2},{4,5},{5,4},{6,7},{7,6},{8,9},{9,8},{10,11... | collective-permute-start | bytes 1769480 | tf_op jit(solution)/shard_map/ppermute | solution.py:107
  115.7 13.2 %collective-permute-start.22 = (bf16[2,96,768]{2,1,0:T(8,128)(2,1)S(1)}, bf16[2,96,768]{2,1,0:T(8,128)(2,1)S(1)}, u32[]{:S(2)}, u32[]{:S(2)}) collective-permute-start(bf16[2,96,768]{2,1,0:T(8,128)(2,1)S(1)} %add_convert_fusion.11), channel_id=1, source_target_pairs={{0,8},{1,9},{2,3},{3,2},{4,12},{5,13},{6,7},{7,6},{8,0},{9,1},{10,... | collective-permute-start | bytes 884744 | tf_op jit(solution)/shard_map/ppermute | solution.py:107
  122.7 11.3 %collective-permute-start.25 = (bf16[4,64,768]{2,1,0:T(8,128)(2,1)S(1)}, bf16[4,64,768]{2,1,0:T(8,128)(2,1)S(1)}, u32[]{:S(2)}, u32[]{:S(2)}) collective-permute-start(bf16[4,64,768]{2,1,0:T(8,128)(2,1)S(1)} %constant_dynamic-update-slice_fusion), channel_id=1, source_target_pairs={{0,4},{1,5},{2,10},{3,11},{4,0},{5,1},{6,14},{7,15},{8,12},{9,13},... | collective-permute-start | bytes 1179656 | tf_op jit(solution)/shard_map/ppermute | solution.py:107
  129.2 12.1 %collective-permute-start.30 = (bf16[2,64,768]{2,1,0:T(8,128)(2,1)S(1)}, bf16[2,64,768]{2,1,0:T(8,128)(2,1)S(1)}, u32[]{:S(2)}, u32[]{:S(2)}) collective-permute-start(bf16[2,64,768]{2,1,0:T(8,128)(2,1)S(1)} %add_convert_fusion.16), channel_id=1, source_target_pairs={{0,1},{1,0},{2,10},{3,11},{4,5},{5,4},{6,14},{7,15},{8,9},{9,8},{1... | collective-permute-start | bytes 589832 | tf_op jit(solution)/shard_map/ppermute | solution.py:107
  129.3 8.5 %collective-permute-start.24 = (bf16[2,48,1152]{2,1,0:T(8,128)(2,1)S(1)}, bf16[2,48,1152]{2,1,0:T(8,128)(2,1)S(1)}, u32[]{:S(2)}, u32[]{:S(2)}) collective-permute-start(bf16[2,48,1152]{2,1,0:T(8,128)(2,1)S(1)} %add_convert_fusion.15), channel_id=1, source_target_pairs={{0,8},{1,9},{2,6},{3,7},{4,12},{5,13},{6,2},{7,3},{8,0},{9,1},{10,... | collective-permute-start | bytes 663560 | tf_op jit(solution)/shard_map/ppermute | solution.py:107
  129.5 11.7 %collective-permute-start.28 = (bf16[2,96,768]{2,1,0:T(8,128)(2,1)S(1)}, bf16[2,96,768]{2,1,0:T(8,128)(2,1)S(1)}, u32[]{:S(2)}, u32[]{:S(2)}) collective-permute-start(bf16[2,96,768]{2,1,0:T(8,128)(2,1)S(1)} %add_convert_fusion.9), channel_id=1, source_target_pairs={{0,16},{1,17},{2,18},{3,19},{4,20},{5,21},{6,22},{7,23},{8,24},{9,... | collective-permute-start | bytes 884744 | tf_op jit(solution)/shard_map/ppermute | solution.py:107
  134.1 28.0 %collective-permute-start.32 = (bf16[8,64,768]{2,1,0:T(8,128)(2,1)S(1)}, bf16[8,64,768]{2,1,0:T(8,128)(2,1)S(1)}, u32[]{:S(2)}, u32[]{:S(2)}) collective-permute-start(bf16[8,64,768]{2,1,0:T(8,128)(2,1)S(1)} %constant_dynamic-update-slice_fusion.2.own), channel_id=1, source_target_pairs={{0,2},{1,3},{2,0},{3,1},{4,6},{5,7},{6,4},{7,5},{8,10},{9,11},{10,... | collective-permute-start | bytes 2359304 | tf_op jit(solution)/shard_map/ppermute | solution.py:107
  137.8 15.6 %collective-permute-start.27 = (bf16[8,64,768]{2,1,0:T(8,128)(2,1)S(1)}, bf16[8,64,768]{2,1,0:T(8,128)(2,1)S(1)}, u32[]{:S(2)}, u32[]{:S(2)}) collective-permute-start(bf16[8,64,768]{2,1,0:T(8,128)(2,1)S(1)} %constant_dynamic-update-slice_fusion.2.own), channel_id=1, source_target_pairs={{0,1},{1,0},{2,6},{3,7},{4,5},{5,4},{6,2},{7,3},{8,9},{9,8},{10,14... | collective-permute-start | bytes 2359304 | tf_op jit(solution)/shard_map/ppermute | solution.py:107
  141.3 10.2 %collective-permute-start.29 = (bf16[2,96,768]{2,1,0:T(8,128)(2,1)S(1)}, bf16[2,96,768]{2,1,0:T(8,128)(2,1)S(1)}, u32[]{:S(2)}, u32[]{:S(2)}) collective-permute-start(bf16[2,96,768]{2,1,0:T(8,128)(2,1)S(1)} %add_convert_fusion.8), channel_id=1, source_target_pairs={{0,8},{1,9},{2,3},{3,2},{4,12},{5,13},{6,7},{7,6},{8,0},{9,1},{10,... | collective-permute-start | bytes 884744 | tf_op jit(solution)/shard_map/ppermute | solution.py:107
  145.8 10.3 %collective-permute-start.33 = (bf16[4,64,768]{2,1,0:T(8,128)(2,1)S(1)}, bf16[4,64,768]{2,1,0:T(8,128)(2,1)S(1)}, u32[]{:S(2)}, u32[]{:S(2)}) collective-permute-start(bf16[4,64,768]{2,1,0:T(8,128)(2,1)S(1)} %constant_dynamic-update-slice_fusion.4), channel_id=1, source_target_pairs={{0,4},{1,5},{2,3},{3,2},{4,0},{5,1},{6,7},{7,6},{8,12},{9,13},{10,... | collective-permute-start | bytes 1179656 | tf_op jit(solution)/shard_map/ppermute | solution.py:107
  147.3 17.4 %collective-permute-start.31 = (bf16[2,48,1152]{2,1,0:T(8,128)(2,1)S(1)}, bf16[2,48,1152]{2,1,0:T(8,128)(2,1)S(1)}, u32[]{:S(2)}, u32[]{:S(2)}) collective-permute-start(bf16[2,48,1152]{2,1,0:T(8,128)(2,1)S(1)} %add_convert_fusion.13), channel_id=1, source_target_pairs={{0,16},{1,17},{2,18},{3,19},{4,20},{5,21},{6,22},{7,23},{8,24},{9,... | collective-permute-start | bytes 663560 | tf_op jit(solution)/shard_map/ppermute | solution.py:107
  151.6 15.5 %collective-permute-start.37 = (bf16[4,96,768]{2,1,0:T(8,128)(2,1)S(1)}, bf16[4,96,768]{2,1,0:T(8,128)(2,1)S(1)}, u32[]{:S(2)}, u32[]{:S(2)}) collective-permute-start(bf16[4,96,768]{2,1,0:T(8,128)(2,1)S(1)} %constant_dynamic-update-slice_fusion.6), channel_id=1, source_target_pairs={{0,1},{1,0},{2,6},{3,7},{4,5},{5,4},{6,2},{7,3},{8,9},{9,8},{10,14... | collective-permute-start | bytes 1769480 | tf_op jit(solution)/shard_map/ppermute | solution.py:107
  156.2 11.0 %collective-permute-start.36 = (bf16[8,64,768]{2,1,0:T(8,128)(2,1)S(1)}, bf16[8,64,768]{2,1,0:T(8,128)(2,1)S(1)}, u32[]{:S(2)}, u32[]{:S(2)}) collective-permute-start(bf16[8,64,768]{2,1,0:T(8,128)(2,1)S(1)} %constant_dynamic-update-slice_fusion.8.own), channel_id=1, source_target_pairs={{0,2},{1,3},{2,0},{3,1},{4,6},{5,7},{6,4},{7,5},{8,10},{9,11},{10,... | collective-permute-start | bytes 2359304 | tf_op jit(solution)/shard_map/ppermute | solution.py:107
  162.0 7.7 %collective-permute-start.35 = (bf16[8,64,768]{2,1,0:T(8,128)(2,1)S(1)}, bf16[8,64,768]{2,1,0:T(8,128)(2,1)S(1)}, u32[]{:S(2)}, u32[]{:S(2)}) collective-permute-start(bf16[8,64,768]{2,1,0:T(8,128)(2,1)S(1)} %collective-permute-done.27.own), channel_id=1, source_target_pairs={{0,2},{1,3},{2,0},{3,1},{4,6},{5,7},{6,4},{7,5},{8,10},{9,11},{10,... | collective-permute-start | bytes 2359304 | tf_op jit(solution)/shard_map/ppermute | solution.py:107
  162.1 12.4 %collective-permute-start.39 = (bf16[8,64,768]{2,1,0:T(8,128)(2,1)S(1)}, bf16[8,64,768]{2,1,0:T(8,128)(2,1)S(1)}, u32[]{:S(2)}, u32[]{:S(2)}) collective-permute-start(bf16[8,64,768]{2,1,0:T(8,128)(2,1)S(1)} %constant_dynamic-update-slice_fusion.8.own), channel_id=1, source_target_pairs={{0,8},{1,9},{2,6},{3,7},{4,12},{5,13},{6,2},{7,3},{8,0},{9,1},{10,... | collective-permute-start | bytes 2359304 | tf_op jit(solution)/shard_map/ppermute | solution.py:107
  164.8 8.3 %collective-permute-start.34 = (bf16[2,48,1152]{2,1,0:T(8,128)(2,1)S(1)}, bf16[2,48,1152]{2,1,0:T(8,128)(2,1)S(1)}, u32[]{:S(2)}, u32[]{:S(2)}) collective-permute-start(bf16[2,48,1152]{2,1,0:T(8,128)(2,1)S(1)} %add_convert_fusion.12), channel_id=1, source_target_pairs={{0,1},{1,0},{2,3},{3,2},{4,5},{5,4},{6,7},{7,6},{8,9},{9,8},{10,11... | collective-permute-start | bytes 663560 | tf_op jit(solution)/shard_map/ppermute | solution.py:107
  173.1 13.1 %collective-permute-start.38 = (bf16[2,48,2304]{2,1,0:T(8,128)(2,1)S(1)}, bf16[2,48,2304]{2,1,0:T(8,128)(2,1)S(1)}, u32[]{:S(2)}, u32[]{:S(2)}) collective-permute-start(bf16[2,48,2304]{2,1,0:T(8,128)(2,1)S(1)} %constant_dynamic-update-slice_fusion.12), channel_id=1, source_target_pairs={{0,8},{1,9},{2,6},{3,7},{4,12},{5,13},{6,2},{7,3},{8,0},{9,1},{10,... | collective-permute-start | bytes 1327112 | tf_op jit(solution)/shard_map/ppermute | solution.py:107
  174.4 18.6 %collective-permute-start.44 = (bf16[8,96,768]{2,1,0:T(8,128)(2,1)S(1)}, bf16[8,96,768]{2,1,0:T(8,128)(2,1)S(1)}, u32[]{:S(2)}, u32[]{:S(2)}) collective-permute-start(bf16[8,96,768]{2,1,0:T(8,128)(2,1)S(1)} %constant_dynamic-update-slice_fusion.10.own), channel_id=1, source_target_pairs={{0,4},{1,5},{2,10},{3,11},{4,0},{5,1},{6,14},{7,15},{8,12},{9,13},... | collective-permute-start | bytes 3538952 | tf_op jit(solution)/shard_map/ppermute | solution.py:107
  174.4 22.3 %collective-permute-start.42 = (bf16[8,96,768]{2,1,0:T(8,128)(2,1)S(1)}, bf16[8,96,768]{2,1,0:T(8,128)(2,1)S(1)}, u32[]{:S(2)}, u32[]{:S(2)}) collective-permute-start(bf16[8,96,768]{2,1,0:T(8,128)(2,1)S(1)} %constant_dynamic-update-slice_fusion.10.own), channel_id=1, source_target_pairs={{0,2},{1,3},{2,0},{3,1},{4,6},{5,7},{6,4},{7,5},{8,10},{9,11},{10,... | collective-permute-start | bytes 3538952 | tf_op jit(solution)/shard_map/ppermute | solution.py:107
  186.3 13.5 %collective-permute-start.41 = (bf16[4,48,2304]{2,1,0:T(8,128)(2,1)S(1)}, bf16[4,48,2304]{2,1,0:T(8,128)(2,1)S(1)}, u32[]{:S(2)}, u32[]{:S(2)}) collective-permute-start(bf16[4,48,2304]{2,1,0:T(8,128)(2,1)S(1)} %constant_dynamic-update-slice_fusion.14.own), channel_id=1, source_target_pairs={{0,2},{1,3},{2,0},{3,1},{4,6},{5,7},{6,4},{7,5},{8,10},{9,11},{10,... | collective-permute-start | bytes 2654216 | tf_op jit(solution)/shard_map/ppermute | solution.py:107
  186.4 16.8 %collective-permute-start.40 = (bf16[4,48,2304]{2,1,0:T(8,128)(2,1)S(1)}, bf16[4,48,2304]{2,1,0:T(8,128)(2,1)}, u32[]{:S(2)}, u32[]{:S(2)}) collective-permute-start(bf16[4,48,2304]{2,1,0:T(8,128)(2,1)S(1)} %constant_dynamic-update-slice_fusion.14.own), channel_id=1, source_target_pairs={{0,4},{1,5},{2,10},{3,11},{4,0},{5,1},{6,14},{7,15},{8,12},{9,13},... | collective-permute-start | bytes 2654216 | tf_op jit(solution)/shard_map/ppermute | solution.py:107
  186.5 7.8 %collective-permute-start.43 = (bf16[8,64,768]{2,1,0:T(8,128)(2,1)S(1)}, bf16[8,64,768]{2,1,0:T(8,128)(2,1)S(1)}, u32[]{:S(2)}, u32[]{:S(2)}) collective-permute-start(bf16[8,64,768]{2,1,0:T(8,128)(2,1)S(1)} %collective-permute-done.39.own), channel_id=1, source_target_pairs={{0,2},{1,3},{2,0},{3,1},{4,6},{5,7},{6,4},{7,5},{8,10},{9,11},{10,... | collective-permute-start | bytes 2359304 | tf_op jit(solution)/shard_map/ppermute | solution.py:107
  193.0 10.4 %collective-permute-start.46 = (bf16[8,96,768]{2,1,0:T(8,128)(2,1)S(1)}, bf16[8,96,768]{2,1,0:T(8,128)(2,1)S(1)}, u32[]{:S(2)}, u32[]{:S(2)}) collective-permute-start(bf16[8,96,768]{2,1,0:T(8,128)(2,1)S(1)} %collective-permute-done.44.own), channel_id=1, source_target_pairs={{0,2},{1,3},{2,0},{3,1},{4,6},{5,7},{6,4},{7,5},{8,10},{9,11},{10,... | collective-permute-start | bytes 3538952 | tf_op jit(solution)/shard_map/ppermute | solution.py:107
  203.2 6.1 %collective-permute-start.45 = (bf16[4,48,2304]{2,1,0:T(8,128)(2,1)}, bf16[4,48,2304]{2,1,0:T(8,128)(2,1)}, u32[]{:S(2)}, u32[]{:S(2)}) collective-permute-start(bf16[4,48,2304]{2,1,0:T(8,128)(2,1)} %collective-permute-done.40.own), channel_id=1, source_target_pairs={{0,2},{1,3},{2,0},{3,1},{4,6},{5,7},{6,4},{7,5},{8,10},{9,11},{10,... | collective-permute-start | bytes 2654216 | tf_op jit(solution)/shard_map/ppermute | solution.py:107
  (15 other events, 73.3 us)

commit v4 on v3

--- a/solution.py
+++ b/solution.py
@@ -59,7 +59,7 @@
         ),
         out_shape=out_shape,
         input_output_aliases=aliases or {},
-        compiler_params=pltpu.CompilerParams(vmem_limit_bytes=28 * MIB),
+        compiler_params=pltpu.CompilerParams(vmem_limit_bytes=max(vmem, 28) * MIB),
         cost_estimate=pl.CostEstimate(flops=1, bytes_accessed=1, transcendentals=0),
     )(scalars, *args)
 
@@ -78,20 +78,21 @@
 
 
 FF_ORDERS = (
-    (("y", "x", "z0", "z1"), ("x", "z0", "y", "z1")),
-    (("z0", "x", "y", "z1"), ("x", "y", "z0", "z1")),
-    (("x", "y", "z0", "z1"), ("z0", "x", "y", "z1")),
+    (("x", "y", "z0", "z1"), ("y", "z0", "x", "z1")),
+    (("z0", "y", "x", "z1"), ("x", "y", "z1", "z0")),
+    (("y", "z0", "x", "z1"), ("x", "y", "z0", "z1")),
 )
-QKV_ORDER = (("x", "z0", "z1"), ("z0", "x", "z1"))
+QKV_ORDER = (("x", "z0", "z1"), ("z0", "z1", "x"))
 PLAN = (
-    ("ff", 0), ("ff", 1), ("wait", "e0"), ("wait", "early"), ("ff", 2), ("dw", 0),
-    ("wait", "branch_other"), ("wait", "e1"), ("dw", 1), ("own",), ("wait", "g"), ("go", 0),
-    ("wait", "e2"), ("dw", 2), ("far",), ("go", 0), ("go", 1), ("joint",), ("go", 0), ("go", 2),
-    ("go", 1), ("go", 3), ("back",), ("go", 0), ("go", 1), ("go", 2), ("go", 0), ("go", 2),
-    ("go", 3), ("go", 1), ("go", 0), ("go", 3), ("wait", "bf"), ("go", 2), ("go", 1), ("go", 2),
-    ("go", 0), ("tokens",), ("go", 1), ("unpack", 0, 0), ("go", 3), ("go", 2), ("unpack", 1, 0),
-    ("unpack", 0, 1), ("go", 3), ("go", 1), ("go", 3), ("go", 2), ("unpack", 1, 1),
-    ("unpack", 2, 0), ("unpack", 3, 0), ("go", 3), ("unpack", 2, 1), ("unpack", 3, 1),
+    ("ff", 0), ("ff", 1), ("wait", "early"), ("wait", "e0"), ("dw", 0), ("wait", "e2"),
+    ("wait", "e1"), ("wait", "branch_other"), ("own",), ("wait", "g"), ("dw", 2), ("dw", 1),
+    ("go", 0), ("far",), ("go", 2), ("joint",), ("go", 0), ("go", 1), ("go", 2), ("go", 0),
+    ("go", 3), ("back",), ("go", 2), ("go", 3), ("go", 1), ("go", 0), ("go", 2), ("go", 0),
+    ("go", 3), ("go", 2), ("wait", "bf"), ("go", 1), ("go", 3), ("go", 0), ("go", 3), ("go", 2),
+    ("tokens",), ("go", 1), ("wait", "n0"), ("go", 0), ("unpack", 0, 0), ("go", 3), ("go", 1),
+    ("wait", "f0"), ("unpack", 0, 1), ("go", 2), ("wait", "n2"), ("unpack", 2, 0), ("go", 1),
+    ("go", 3), ("wait", "f2"), ("wait", "n3"), ("unpack", 2, 1), ("wait", "f3"), ("unpack", 3, 0),
+    ("unpack", 3, 1), ("wait", "n1"), ("go", 1), ("unpack", 1, 0), ("wait", "f1"), ("unpack", 1, 1),
 )
 DP_BIT = {"c": 1, "x": 2, "z0": 4, "z1": 8}
 
@@ -174,70 +175,154 @@
     yield far, order.swap(far, "c")
 
 
-def ln_qkv_kernel(s, tok, pos, gain, w, normed, qkv):
+def sine_and_cosine(angle):
+    turns = jnp.floor(angle * (2.0 / math.pi) + 0.5)
+    rest = angle - turns * 1.5703125
+    rest = rest - turns * 4.837512969970703125e-4
+    rest = rest - turns * 7.54978995489188e-8
+    square = rest * rest
+    sine = rest + rest * square * (
+        -1.6666654611e-1 + square * (8.3321608736e-3 + square * -1.9515295891e-4)
+    )
+    cosine = (1.0 - 0.5 * square) + square * square * (
+        4.166664568298827e-2 + square * (-1.388731625493765e-3 + square * 2.443315711809948e-5)
+    )
+    quarter = turns.astype(jnp.int32)
+    odd = (quarter & 1) == 1
+    sin = jnp.where(odd, cosine, sine)
+    cos = jnp.where(odd, sine, cosine)
+    return (
+        jnp.where((quarter & 2) == 2, -sin, sin),
+        jnp.where(((quarter + 1) & 2) == 2, -cos, cos),
+    )
+
+
+def position_kernel(s, visible, freqs, out):
+    column = jnp.broadcast_to(visible[...].astype(f32), (8, visible.shape[1])).T[:, :1]
+    sin, cos = sine_and_cosine(column * freqs[...])
+    half = sin.shape[1]
+    out[:, :half] = sin
+    out[:, half:] = cos
+
+
+def positions(scalars, visible, freqs):
+    rows, width = visible.shape[1], 2 * freqs.shape[1]
+    out = shape((rows, width), f32)
+    return call(
+        position_kernel, (1,), [whole(visible), whole(freqs)], whole(out), out, (visible, freqs), scalars, 16
+    )
+
+
+def ln_qkv_kernel(s, tok, pos, gain, w, normed, qkv, *resid):
     @pl.when(pl.program_id(0) == 0)
     def _():
-        xhat, _ = normalize(tok[...].astype(f32) + pos[...])
+        value = tok[...].astype(f32) + pos[...]
+        if resid:
+            resid[0][...] = value
+        xhat, _ = normalize(value)
         normed[...] = (xhat * gain[...]).astype(bf16)
 
     qkv[...] = dot(normed[...], w[...]).astype(bf16)
 
 
-def ln_qkv(scalars, tok, pos, gain, w):
+def ln_qkv(scalars, far, tok, pos, gain, w):
     rows, width = tok.shape
+    full = spec((rows, width), lambda i, s: (0, 0))
+    parts = 2 if far else 3
+    out_shape = [shape((rows, width), bf16), shape((rows, parts * width), bf16)]
     return call(
         ln_qkv_kernel,
-        (3,),
-        [whole(tok), whole(pos), whole(gain), spec((width, width), lambda i, s: (0, i))],
-        [spec((rows, width), lambda i, s: (0, 0)), spec((rows, width), lambda i, s: (0, i))],
-        [shape((rows, width), bf16), shape((rows, 3 * width), bf16)],
+        (parts,),
+        [full, full, whole(gain), spec((width, width), lambda i, s: (0, i + far))],
+        [full, spec((rows, width), lambda i, s: (0, i))] + [full] * (not far),
+        out_shape + [shape((rows, width), f32)] * (not far),
         (tok, pos, gain, w),
         scalars,
         24,
     )
 
 
+def far_query_kernel(s, normed, w, out):
+    out[...] = dot(normed[...], w[...]).astype(bf16)
+
+
+def far_query(scalars, normed, w):
+    rows, width = normed.shape
+    out = shape((rows, width // 2), bf16)
+    return call(
+        far_query_kernel,
+        (1,),
+        [whole(normed), spec((width, width // 2), lambda i, s: (0, s[1]))],
+        whole(out),
+        out,
+        (normed, w),
+        scalars,
+        16,
+    )
+
+
 def head_masks(x):
     lane = lax.broadcasted_iota(jnp.int32, x.shape, 1)
     return jnp.where(lane < HD, x, 0.0).astype(bf16), jnp.where(lane >= HD, x, 0.0).astype(bf16)
 
 
-def attn_kernel(s, q, k_own, v_own, k_far, v_far, out):
+def attn_kernel(s, q, k, v, *refs):
     rows = q.shape[0]
-    k = jnp.concatenate([k_own[...], k_far[...]], 0)
-    vt = jnp.concatenate([v_own[...], v_far[...]], 0).T
-    parts = []
-    for h, qh in enumerate(head_masks(q[...].astype(f32) * HD**-0.5)):
-        scores = dot(k, qh, NT)
-        e = jnp.exp(scores - jnp.max(scores, 0, keepdims=True))
-        total = jnp.sum(e, 0, keepdims=True)
-        part = dot(vt[h * HD : (h + 1) * HD], e.astype(bf16))
-        parts.append(part * (1.0 / total))
+    qs = jnp.concatenate(head_masks(q[...].astype(f32) * HD**-0.5), 0)
+    scores = dot(k[...], qs, NT)
+    top = jnp.max(scores, 0, keepdims=True)
+    later = len(refs) == 3
+    if later:
+        acc_in, stat_in, out = refs
+        before = stat_in[0, 0:1]
+        top = jnp.maximum(top, before)
+    e = jnp.exp(scores - top)
+    total = jnp.sum(e, 0, keepdims=True)
+    vt = v[...].T
+    low = e.astype(bf16)
+    parts = [dot(vt[h * HD : (h + 1) * HD], low[:, h * rows : (h + 1) * rows]) for h in range(2)]
+    if not later:
+        acc, stat = refs
+        acc[0] = jnp.concatenate(parts, 0)
+        stat[0, 0:1] = top
+        stat[0, 1:2] = total
+        return
+    shrink = jnp.exp(before - top)
+    scale = 1.0 / (total + stat_in[0, 1:2] * shrink)
+    shrink = shrink * scale
+    for h in range(2):
+        at = slice(h * rows, (h + 1) * rows)
+        held = acc_in[0, h * HD : (h + 1) * HD]
+        parts[h] = parts[h] * scale[:, at] + held * shrink[:, at]
     out[...] = jnp.concatenate(parts, 0).T.astype(bf16)
 
 
-def attention(scalars, qkv, qkv_far):
+def attention(scalars, qkv, keys, *so_far):
     rows, width = qkv.shape[0], qkv.shape[1] // 3
     pairs = width // PAIR
 
     def column(part):
         return spec((rows, PAIR), lambda i, s: (0, part * pairs + i))
 
+    first = 0 if so_far else 1
+    acc = spec((1, PAIR, rows), lambda i, s: (i, 0, 0))
+    stat = spec((1, 8, 2 * rows), lambda i, s: (i, 0, 0))
+    sums = [shape((pairs, PAIR, rows), f32), shape((pairs, 8, 2 * rows), f32)]
     return call(
         attn_kernel,
         (pairs,),
-        [column(0), column(1), column(2), column(1), column(2)],
-        spec((rows, PAIR), lambda i, s: (0, i)),
-        shape((rows, width), bf16),
-        (qkv, qkv, qkv, qkv_far, qkv_far),
+        [column(0), column(first), column(first + 1)] + ([acc, stat] if so_far else []),
+        spec((rows, PAIR), lambda i, s: (0, i)) if so_far else [acc, stat],
+        shape((rows, width), bf16) if so_far else sums,
+        (qkv, keys, keys) + so_far,
         scalars,
-        32,
-    )
-
-
-def proj_kernel(s, att, att_half, w, tok, pos, gain, resid2, normed2, normed2_t, att_send):
+        28,
+    )
+
+
+def proj_kernel(s, att, att_half, w, resid, gain, resid2, normed2, normed2_t, att_send):
     att_send[...] = att_half[...]
-    value = tok[...].astype(f32) + pos[...] + dot(att[...], w[...])
+    value = resid[...] + dot(att[...], w[...])
     resid2[...] = value
     xhat, _ = normalize(value)
     low = (xhat * gain[...]).astype(bf16)
@@ -245,14 +330,14 @@
     normed2_t[...] = low.T
 
 
-def project(scalars, att, w, tok, pos, gain):
+def project(scalars, att, w, resid, gain):
     rows, width = att.shape
     full = spec((rows, width), lambda i, s: (0, 0))
     half = spec((rows, width // 2), lambda i, s: (0, 1 - s[0]))
     return call(
         proj_kernel,
         (1,),
-        [full, half, whole(w), full, full, whole(gain)],
+        [full, half, whole(w), full, whole(gain)],
         [
             full,
             full,
@@ -265,7 +350,7 @@
             shape((width, rows), bf16),
             shape((rows, width // 2), bf16),
         ],
-        (att, att, w, tok, pos, gain),
+        (att, att, w, resid, gain),
         scalars,
         24,
     )
@@ -280,15 +365,15 @@
     return act, slope
 
 
-def ff_kernel(first, last, s, normed, cot, up, down, *refs):
+def ff_kernel(count, s, normed, cot, up, down, *refs):
     step = pl.program_id(0)
-    if not first:
-        out_in, back_in, *refs = refs
-    if last:
-        resid2, gain, w_own, w_other, *refs = refs
-        keep, send, out_low, grad2, branch, g_own, g_other, out, back = refs
+    if count > 1:
+        out_in, back_in, resid2, gain, w_own, w_other, *refs = refs
+    pieces, refs = refs[: 2 * count], refs[2 * count :]
+    if count > 1:
+        out_low, grad2, branch, g_own, g_other, out, back = refs
     else:
-        keep, send, out, back = refs
+        out, back = refs
     hidden = dot(normed[...], up[...])
     act, slope = gelu_and_slope(hidden)
     act = act.astype(bf16)
@@ -298,18 +383,25 @@
 
     @pl.when(step == 0)
     def _():
-        send[0] = act
-        send[1] = grad
-        out[...] = out_part if first else out_in[...] + out_part
-        back[...] = back_part if first else back_in[...] + back_part
-
-    @pl.when(step == 1)
+        out[...] = out_in[...] + out_part if count > 1 else out_part
+        back[...] = back_in[...] + back_part if count > 1 else back_part
+
+    @pl.when(step > 0)
     def _():
-        keep[0] = act
-        keep[1] = grad
         out[...] += out_part
         back[...] += back_part
-        if last:
+
+    for at, piece in enumerate(pieces):
+
+        @pl.when(step == at)
+        def _(piece=piece):
+            piece[0] = act
+            piece[1] = grad
+
+    if count > 1:
+
+        @pl.when(step == 2 * count - 1)
+        def _():
             value = resid2[...]
             out_low[...] = (value + out[...]).astype(bf16)
             xhat, scale = normalize(value)
@@ -321,31 +413,29 @@
             g_own[...] = dot(low, w_own[...], NT).astype(bf16)
 
 
-def ff_chunk(scalars, chunk, last, normed, cot, up, down, *more):
+def ff_chunks(scalars, first, count, normed, cot, up, down, *more):
     rows, width = normed.shape
     half = width // 2
     wide = 512
-    first = chunk == 0
 
     def column(i, s):
-        return 2 * chunk + (s[0] ^ (1 - i))
+        return 2 * (first + i // 2) + (s[0] ^ (1 - (i & 1)))
 
     full = spec((rows, width), lambda i, s: (0, 0))
     part = spec((rows, half), lambda i, s: (0, 0))
-    piece = spec((2, rows, wide), lambda i, s: (0, 0, 0))
     in_specs = [
         whole(normed),
         whole(cot),
         spec((width, wide), lambda i, s: (0, column(i, s))),
         spec((wide, width), lambda i, s: (column(i, s), 0)),
     ]
-    out_specs = [piece, piece]
-    out_shape = [shape((2, rows, wide), bf16)] * 2
+    out_specs = [spec((2, rows, wide), lambda i, s: (0, 0, 0))] * (2 * count)
+    out_shape = [shape((2, rows, wide), bf16)] * (2 * count)
     scratch = []
-    if not first:
-        in_specs += [full, full]
-    if last:
+    if count > 1:
         in_specs += [
+            full,
+            full,
             full,
             spec((1, width), lambda i, s: (0, 0)),
             spec((half, width), lambda i, s: (s[1], 0)),
@@ -359,14 +449,14 @@
         out_specs += [full, full]
         out_shape += [shape((rows, width), f32)] * 2
     return call(
-        functools.partial(ff_kernel, first, last),
-        (2,),
+        functools.partial(ff_kernel, count),
+        (2 * count,),
         in_specs,
         out_specs,
         out_shape,
         (normed, cot, up, down) + more,
         scalars,
-        40,
+        28,
         scratch,
     )
 
@@ -439,7 +529,7 @@
         [shape((8, deep, width), bf16)] * 2,
         (mine, theirs, mine, theirs, cot, cot_other, normed_t, normed_t_other) + proj,
         scalars,
-        32,
+        28,
     )
 
 
@@ -449,26 +539,28 @@
     k = jnp.concatenate([k_o[...], k_f[...]], 0)
     v = jnp.concatenate([v_o[...], v_f[...]], 0)
     kt = (k.astype(f32) * HD**-0.5).astype(bf16).T
-    grad_q = []
-    grad_k, grad_v = (gk_in[...], gv_in[...]) if gk_in is not None else (0.0, 0.0)
-    q_heads = head_masks(q[...].astype(f32) * HD**-0.5)
-    g_heads = head_masks(g[...].astype(f32))
-    for h, (qh, gh) in enumerate(zip(q_heads, g_heads)):
-        scores = dot(k, qh, NT)
-        e = jnp.exp(scores - jnp.max(scores, 0, keepdims=True))
-        probs = e * (1.0 / jnp.sum(e, 0, keepdims=True))
-        grad_v = grad_v + dot(probs.astype(bf16), gh)
-        grad_p = dot(v, gh, NT)
-        row = jnp.sum(probs * grad_p, 0, keepdims=True)
-        grad_s = (probs * (grad_p - row)).astype(bf16)
-        grad_k = grad_k + dot(grad_s, qh)
-        grad_q.append(dot(kt[h * HD : (h + 1) * HD], grad_s))
+    rows = q.shape[0]
+    qs = jnp.concatenate(head_masks(q[...].astype(f32) * HD**-0.5), 0)
+    gs = jnp.concatenate(head_masks(g[...].astype(f32)), 0)
+    scores = dot(k, qs, NT)
+    e = jnp.exp(scores - jnp.max(scores, 0, keepdims=True))
+    probs = e * (1.0 / jnp.sum(e, 0, keepdims=True))
+    grad_v = dot(probs.astype(bf16), gs)
+    grad_p = dot(v, gs, NT)
+    row = jnp.sum(probs * grad_p, 0, keepdims=True)
+    grad_s = (probs * (grad_p - row)).astype(bf16)
+    grad_k = dot(grad_s, qs)
+    grad_q = [
+        dot(kt[h * HD : (h + 1) * HD], grad_s[:, h * rows : (h + 1) * rows]) for h in range(2)
+    ]
+    if gk_in is not None:
+        grad_k, grad_v = grad_k + gk_in[...], grad_v + gv_in[...]
     gq[...] = jnp.concatenate(grad_q, 0).T.astype(bf16)
     gk[...] = grad_k.astype(gk.dtype)
     gv[...] = grad_v.astype(gv.dtype)
 
 
-def attention_back(scalars, far, qkv, qkv_far, grad, *so_far):
+def attention_back(scalars, query, grad, qkv, kv_far, *so_far):
     rows, width = qkv.shape[0], qkv.shape[1] // 3
     pairs = width // PAIR
     mine = pairs // 2
@@ -482,12 +574,13 @@
     return call(
         attn_back_kernel,
         (mine,),
-        [column(0), block, column(1), column(1), column(2), column(2)] + [both] * len(so_far),
+        [block if so_far else column(0), block, column(1), column(0), column(2), column(1)]
+        + [both] * len(so_far),
         [block, both, both],
         [shape((rows, width // 2), bf16)] + [shape((2 * rows, width // 2), dtype)] * 2,
-        (qkv_far if far else qkv, grad, qkv, qkv_far, qkv, qkv_far) + so_far,
+        (query, grad, qkv, kv_far, qkv, kv_far) + so_far,
         scalars,
-        48,
+        28,
     )
 
 
@@ -529,7 +622,7 @@
         [shape((8, half // 8, cols), bf16)] * 2,
         (n_own, n_far, gq, gq_far, gk, gv),
         scalars,
-        32,
+        28,
     )
 
 
@@ -561,18 +654,18 @@
         [shape((rows, width), f32), shape((rows, width), bf16)],
         (gq, gq_far, gk, gv, w, w, w),
         scalars,
-        32,
-    )
-
-
-def last_kernel(s, own, far, tok, pos, gain, grad2, out):
-    xhat, scale = normalize(tok[...].astype(f32) + pos[...])
+        28,
+    )
+
+
+def last_kernel(s, own, far, resid, gain, grad2, out):
+    xhat, scale = normalize(resid[...])
     grad = own[...] + far[...].astype(f32)
     out[...] = grad2[...] + norm_backward(grad, gain[...], xhat, scale)
 
 
-def token_grad(scalars, own, far, tok, pos, gain, grad2):
-    args = (own, far, tok, pos, gain, grad2)
+def token_grad(scalars, own, far, resid, gain, grad2):
+    args = (own, far, resid, gain, grad2)
     return call(
         last_kernel,
         (1,),
@@ -585,8 +678,15 @@
     )
 
 
-def lane_sums(values):
-    return sum(values[:, at : at + 128] for at in range(0, values.shape[1], 128))
+def row_sums(values):
+    folded = sum(values[:, at : at + 128] for at in range(0, values.shape[1], 128))
+    return lax.dot_general(
+        jnp.ones((8, 128), f32),
+        folded,
+        (NT, ((), ())),
+        precision=lax.Precision.HIGHEST,
+        preferred_element_type=f32,
+    )
 
 
 def unpack_ff_kernel(at, last, s, own, other, w, gain_in, *refs):
@@ -615,8 +715,7 @@
     def _():
         unpack(other, s[at + 1])
 
-    sums = lane_sums(up[...] * w[...].astype(f32))
-    gain[...] = gain_in[...] + sums
+    gain[0, 0] = gain_in[0, 0] + row_sums(up[...] * w[...].astype(f32))
 
 
 def unpack_ff(scalars, chunk, far, own, other, w, so_far):
@@ -632,9 +731,9 @@
 
     any_spec = pl.BlockSpec(memory_space=pl.ANY)
     column = spec((width // 2, 512), lambda i, s: (side(i, s), half(i, s)))
-    gain = spec((None, width // 2, 128), lambda i, s: (i, side(i, s), 0))
+    gain = spec((1, 1, 8, width // 2), lambda i, s: (i, side(i, s), 0, 0))
     out_specs = [gain, spec((256, width), lambda i, s: (2 * half(i, s) + side(i, s), 0)), column]
-    out_shape = [shape((2, width, 128), f32), shape((hidden, width), f32), shape((width, hidden), f32)]
+    out_shape = [shape((2, 2, 8, width // 2), f32), shape((hidden, width), f32), shape((width, hidden), f32)]
     if last:
         out_specs.append(spec((width // 2, width // 2), lambda i, s: (s[0] ^ i, side(i, s))))
         out_shape.append(shape((width, width), f32))
@@ -648,7 +747,7 @@
         out_shape,
         (own, other, w) + tuple(so_far),
         scalars,
-        32,
+        28,
         aliases={4 + i: i for i in range(len(so_far))},
     )
 
@@ -660,41 +759,51 @@
 
     def unpack(source, code):
         half = source.shape[2] // 6
-        for block in range(4):
-            rows = pl.ds(pl.multiple_of((block ^ (code & 3)) * 48, 16), 48)
-            for part in range(3):
-                for side in range(2):
-                    column = pl.multiple_of(2 * half * part + half * (mine ^ side), 128)
-                    value = source[block, :, (3 * side + part) * half : (3 * side + part + 1) * half]
-                    joint[rows, pl.ds(column, half)] = value.astype(f32)
-
-    @pl.when(step == 0)
+
+        def place_columns(first):
+            for block in range(2):
+                rows = pl.ds(pl.multiple_of((block ^ (code & 1)) * 48, 16), 48)
+                for part in range(3):
+                    for side in range(2):
+                        column = 2 * half * part + half * (first ^ side)
+                        value = source[block, :, (3 * side + part) * half : (3 * side + part + 1) * half]
+                        joint[rows, column : column + half] = value.astype(f32)
+
+        for first in range(2):
+            pl.when(mine == first)(functools.partial(place_columns, first))
+
+    @pl.when(step < 2)
     def _():
         unpack(own, s[8])
 
-    @pl.when(step == 1)
+    @pl.when(step >= 2)
     def _():
         unpack(other, s[9])
 
-    gain[...] = lane_sums(joint[...] * w[...].astype(f32))
+    gain[0] = row_sums(joint[...] * w[...].astype(f32))
 
 
 def unpack_qkv(scalars, far, own, other, w, so_far):
     width = w.shape[0]
 
-    def rows(columns):
-        return spec((width // 4, columns), lambda i, s: (2 * (s[0] ^ i) + ((s[8 + i] // 4) ^ far), 0))
+    def row(i, s):
+        code = s[8 + i // 2]
+        return 4 * (s[0] ^ (i // 2)) + 2 * ((code // 4) ^ far) + ((i & 1) ^ ((code // 2) & 1))
+
+    def blocks(mine):
+        return spec((2,) + own.shape[1:], lambda i, s: (jnp.clip(i - 2 * mine, 0, 1), 0, 0))
 
     any_spec = pl.BlockSpec(memory_space=pl.ANY)
+    rows = spec((width // 8, 3 * width), lambda i, s: (row(i, s), 0))
     return call(
         unpack_qkv_kernel,
-        (2,),
-        [whole(own), whole(other), rows(3 * width)] + [any_spec] * len(so_far),
-        [rows(3 * width), rows(128)],
-        [shape((width, 3 * width), f32), shape((width, 128), f32)],
+        (4,),
+        [blocks(0), blocks(1), rows] + [any_spec] * len(so_far),
+        [rows, spec((1, 8, width // 8), lambda i, s: (row(i, s), 0, 0))],
+        [shape((width, 3 * width), f32), shape((8, 8, width // 8), f32)],
         (own, other, w) + tuple(so_far),
         scalars,
-        32,
+        28,
         aliases={4 + i: i for i in range(len(so_far))},
     )
 
@@ -710,37 +819,40 @@
 
     order = Order()
     run = order.run
-    vis_far = swap(visible, "y")[0]
+    vis_far = swap(visible, "y")
     tok_far = swap(tok, "y")
-    cot_other = swap(cot, "c")
-    pos = position_table(visible[0], width)
-    pos_far = position_table(vis_far, width)
-    normed1, qkv = run(functools.partial(ln_qkv, scalars), tok, pos, gain1, w_qkv)
-    normed1_far, qkv_far = run(functools.partial(ln_qkv, scalars), tok_far, pos_far, gain1, w_qkv)
-    attended = run(functools.partial(attention, scalars), qkv, qkv_far)
+    half = width // 2
+    freqs = jnp.exp(jnp.arange(half, dtype=f32) * (-math.log(10000.0) / half))[None]
+    pos = run(functools.partial(positions, scalars), visible, freqs)
+    normed1, qkv, resid = run(functools.partial(ln_qkv, scalars, False), tok, pos, gain1, w_qkv)
+    sums = run(functools.partial(attention, scalars), qkv, qkv)
+    pos_far = run(functools.partial(positions, scalars), vis_far, freqs)
+    normed1_far, kv_far = run(functools.partial(ln_qkv, scalars, True), tok_far, pos_far, gain1, w_qkv)
+    attended = run(functools.partial(attention, scalars), qkv, kv_far, *sums)
     resid2, normed2, normed2_t, att_half = run(
-        functools.partial(project, scalars), attended, w_proj, tok, pos, gain2
-    )
-    early = cot_other, order.swap(normed2_t, "c"), order.swap(att_half, "c")
+        functools.partial(project, scalars), attended, w_proj, resid, gain2
+    )
+    early = tuple(order.swap(array, "c") for array in (cot, normed2_t, att_half))
 
     streams, blocks, values = {}, {}, {"early": early}
-    ff, proj, joint = (jnp.zeros((2, width, 128), f32),), (), ()
-
-    def feed_forward(chunk):
-        more = values.pop("sums", ())
-        if chunk == 2:
-            more += (resid2, gain2, w_proj, w_proj)
-        keep, send, *rest = run(
-            functools.partial(ff_chunk, scalars, chunk, chunk == 2), normed2, cot, w_up, w_down, *more
+    ff, proj, joint = (jnp.zeros((2, 2, 8, width // 2), f32),), (), ()
+
+    def feed_forward(first):
+        if first == 0:
+            send, keep, *values["sums"] = run(
+                functools.partial(ff_chunks, scalars, 0, 1), normed2, cot, w_up, w_down
+            )
+            values["act", 0], values["e0"] = keep, order.swap(send, "c")
+            return
+        more = (*values["sums"], resid2, gain2, w_proj, w_proj)
+        send1, keep1, send2, keep2, out, grad2, branch, g_own, g_other = run(
+            functools.partial(ff_chunks, scalars, 1, 2), normed2, cot, w_up, w_down, *more
         )
-        values["act", chunk], values["e%d" % chunk] = keep, order.swap(send, "c")
-        if chunk == 2:
-            out, grad2, branch, g_own, g_other = rest
-            values["branch"], values["branch_other"] = branch, order.swap(branch, "c")
-            values["g"] = order.swap(g_other, "y")
-            values.update(out=out, grad2=grad2, own=g_own)
-        else:
-            values["sums"] = tuple(rest)
+        values["act", 1], values["e1"] = keep1, order.swap(send1, "c")
+        values["act", 2], values["e2"] = keep2, order.swap(send2, "c")
+        values["branch"], values["branch_other"] = branch, order.swap(branch, "c")
+        values["g"] = order.swap(g_other, "y")
+        values.update(out=out, grad2=grad2, own=g_own)
 
     def weight_grads(chunk):
         early = (*values["early"][:2], normed2_t)
@@ -760,15 +872,21 @@
             blocks.setdefault(chunk, []).append(pair)
 
     def wait(key):
+        if key[0] in "nf" and key[1:].isdigit():
+            chunk, far = int(key[1:]), int(key[0] == "f")
+            own, other = blocks[chunk][far]
+            blocks[chunk][far] = own, run(lambda value: value, other)
+            return
         value = values[key]
         values[key] = run(lambda *v: v if isinstance(value, tuple) else v[0], *(value if isinstance(value, tuple) else (value,)))
 
     def own_queries():
-        values["attn"] = run(functools.partial(attention_back, scalars, False), qkv, qkv_far, values["own"])
+        values["attn"] = run(functools.partial(attention_back, scalars), qkv, values["own"], qkv, kv_far)
 
     def far_queries():
         gq, *sums = values["attn"]
-        back = run(functools.partial(attention_back, scalars, True), qkv, qkv_far, values["g"], *sums)
+        values["q"] = run(functools.partial(far_query, scalars), normed1_far, w_qkv)
+        back = run(functools.partial(attention_back, scalars), values["q"], values["g"], qkv, kv_far, *sums)
         values["attn"] = (gq, *back)
 
     def joint_weights():
@@ -782,7 +900,7 @@
         values["norm"], values["bf"] = own, order.swap(far, "y")
 
     def finish_tokens():
-        args = (values["norm"], values["bf"], tok, pos, gain1, values["grad2"])
+        args = (values["norm"], values["bf"], resid, gain1, values["grad2"])
         values["tokens"] = run(functools.partial(token_grad, scalars), *args)
 
     def unpack(chunk, far):
@@ -792,11 +910,14 @@
             joint = run(lambda a, b, *f: unpack_qkv(scalars, far, a, b, w_qkv, f), own, other, *joint)
             return
         so_far = ff + proj if chunk == 2 else ff
+        weight = w_hbm if (chunk, far) == final else w_up
         result = tuple(
-            run(lambda a, b, *f: unpack_ff(scalars, chunk, far, a, b, w_up, f), own, other, *so_far)
+            run(lambda a, b, *f: unpack_ff(scalars, chunk, far, a, b, weight, f), own, other, *so_far)
         )
         ff, proj = result[:3], result[3:] or proj
 
+    w_hbm = pltpu.with_memory_space_constraint(w_up, pltpu.HBM)
+    final = [step[1:] for step in PLAN if step[0] == "unpack" and step[1] != 3][-1]
     steps = {
         "ff": feed_forward,
         "dw": weight_grads,
@@ -814,8 +935,8 @@
     sums2, d_down, d_up = ff
     d_qkv, sums1 = joint
     out, d_tokens, d_proj = values["out"], values["tokens"], proj[0]
-    d_gain1 = jnp.sum(sums1, 1) / ln1_gain
-    d_gain2 = jnp.sum(sums2, (0, 2)) / ln2_gain
+    d_gain1 = sums1[:, 0].reshape(-1) / ln1_gain
+    d_gain2 = (sums2[0, :, 0] + sums2[1, :, 0]).reshape(-1) / ln2_gain
     return out[None], d_tokens[None], d_gain1, d_qkv, d_proj, d_gain2, d_up, d_down
 
 

time: 222 us -> 206 us (0.928); the launches traced: 217 us -> 205 us
  starting transfers between devices: 57.1 us -> 38.1 us
  waiting for transfers between devices: 48.1 us -> 62.4 us
  other arithmetic: 11.9 us -> 3.1 us
  Pallas kernels: 92.1 us -> 95.6 us
    ppermute x47, starting transfers between devices: 57.1 us -> 38.1 us  [swap(): return lax.ppermute(array, AXES, pairs)]
    ppermute x47, waiting for transfers between devices: 48.1 us -> 62.4 us  [swap(): return lax.ppermute(array, AXES, pairs)]
    sin x1 -> x0, other arithmetic: 4.99 us -> none  [position_table(): return jnp.concatenate([jnp.sin(angles), jnp.cos(angles)], -1)]
    pallas_call x23 -> x26, Pallas kernels: 92.1 us -> 95.6 us  [call(): pl.pallas_call(kernel, grid_spec=pltpu.PrefetchScalarGridSpec(num_scalar_...]
    reduce_sum x2 -> x0, other arithmetic: 2.48 us -> none  [the longest x1 1.31 us: fast(): d_gain2 = jnp.sum(sums2, (0, 2)) / ln2_gain]
    unnamed x40 -> x52, local copies, waits for them, and re-layouts: 4.6 us -> 4.32 us
  transfers between devices with their start and end apart: 47 -> 47, of which waited for: 15 -> 18; matrix products, arithmetic and copies ran while one was open for 6% -> 1% of each run, Pallas kernels for 32% -> 40%
where the time goes in v4:
time: 206 us; the launch traced here: 205 us
  Pallas kernels  95.6 us (46%)
  waiting for transfers between devices  62.4 us (30%)
  starting transfers between devices  38.1 us (18%)
  local copies, waits for them, and re-layouts  4.73 us (2%)
  other arithmetic  3.1 us (2%)
    pallas_call x26, Pallas kernels, call(): pl.pallas_call(kernel, grid_spec=pltpu.PrefetchScalarGridSpec(num_scalar_...  95.6 us
    ppermute x47, waiting for transfers between devices, swap(): return lax.ppermute(array, AXES, pairs)  62.4 us
    ppermute x47, starting transfers between devices, swap(): return lax.ppermute(array, AXES, pairs)  38.1 us
    unnamed x52, local copies, waits for them, and re-layouts  4.32 us
  transfers between devices with their start and end apart: 47, of which 18 were waited for; matrix products, arithmetic and copies ran while one was open for 1% of the time, Pallas kernels for 40%

profile of v4, /device:TPU:0, one launch (start us, length us, event | category | flops | bytes accessed | tf_op | source)
XLA Modules:
  0.0 205.4 jit_solution(2365531196174949358)
XLA Ops:
  0.6 3.0 %collective-permute-start = (bf16[384,768]{1,0:T(8,128)(2,1)}, bf16[384,768]{1,0:T(8,128)(2,1)}, u32[]{:S(2)}, u32[]{:S(2)}) collective-permute-start(bf16[384,768]{1,0:T(8,128)(2,1)} %bitcast.22), channel_id=1, source_target_pairs={{0,1},{1,0},{2,3},{3,2},{4,5},{5,4},{6,7},{7,6},{8,9},{9,8},{10,11... | collective-permute-start | bytes 1769480 | tf_op jit(solution)/shard_map/ppermute | solution.py:108
  6.1 2.0 copy-done
  8.1 3.2 %shard_map.153 = (bf16[384,768]{1,0:T(8,128)(2,1)S(1)}, bf16[384,2304]{1,0:T(8,128)(2,1)S(1)}, f32[384,768]{1,0:T(8,128)S(1)}) custom-call(s32[10]{0:T(128)S(1)} %stack.37.s, bf16[384,768]{1,0:T(8,128)(2,1)S(1)} %bitcast.23, f32[384,768]{1,0:T(8,128)S(1)} %shard_map.152.pos, f32[1,768]{1,0:T(1,128)S(1)} %broadcast_in_dim.16.gain, bf16[768,2304]{1,0:T(8,128)(2,1)S(1)} %copy-done), custom_call_target="tpu_custom_call" | custom-call | flops 1 | bytes 1 | tf_op jit(solution)/shard_map/pallas_call | solution.py:51
  11.4 5.1 %shard_map.154 = (f32[6,128,384]{2,1,0:T(8,128)S(1)}, f32[6,8,768]{2,1,0:T(8,128)S(1)}) custom-call(s32[10]{0:T(128)S(1)} %stack.37.s, bf16[384,2304]{1,0:T(8,128)(2,1)S(1)} %get-tuple-element.432.q.k.v.k_o.v_o, bf16[384,2304]{1,0:T(8,128)(2,1)S(1)} %get-tuple-element.432.q.k.v.k_o.v_o, bf16[384,2304]{1,0:T(8,128)(2,1)S(1)} %get-tuple-element.432.q.k.v.k_o.v_o), custom_call_target="tpu_custom_call" | custom-call | flops 1 | bytes 1 | tf_op jit(solution)/shard_map/pallas_call | solution.py:51
  18.9 3.5 %shard_map.156 = (bf16[384,768]{1,0:T(8,128)(2,1)S(1)}, bf16[384,1536]{1,0:T(8,128)(2,1)S(1)}) custom-call(s32[10]{0:T(128)S(1)} %stack.37.s, bf16[384,768]{1,0:T(8,128)(2,1)} %collective-permute-done.tok, f32[384,768]{1,0:T(8,128)S(1)} %shard_map.155.pos, f32[1,768]{1,0:T(1,128)S(1)} %broadcast_in_dim.16.gain, bf16[768,2304]{1,0:T(8,128)(2,1)S(1)} %copy-done.1), custom_call_target="tpu_custom_call" | custom-call | flops 1 | bytes 1 | tf_op jit(solution)/shard_map/pallas_call | solution.py:51
  22.4 5.6 %shard_map.157.att.att_half.refs_0_ = bf16[384,768]{1,0:T(8,128)(2,1)S(1)} custom-call(s32[10]{0:T(128)S(1)} %stack.37.s, bf16[384,2304]{1,0:T(8,128)(2,1)S(1)} %get-tuple-element.432.q.k.v.k_o.v_o, bf16[384,1536]{1,0:T(8,128)(2,1)S(1)} %get-tuple-element.433.k.v.k_f.v_f, bf16[384,1536]{1,0:T(8,128)(2,1)S(1)} %get-tuple-element.433.k.v.k_f.v_f, ...), custom_call_target="tpu_custom_call" | custom-call | flops 1 | bytes 1 | tf_op jit(solution)/shard_map/pallas_call | solution.py:51
  28.0 1.6 shard_map.158
  30.3 4.5 %shard_map.159 = (bf16[2,384,512]{2,1,0:T(8,128)(2,1)S(1)}, bf16[2,384,512]{2,1,0:T(8,128)(2,1)S(1)}, f32[384,768]{1,0:T(8,128)S(1)}, f32[384,768]{1,0:T(8,128)S(1)}) custom-call(s32[10]{0:T(128)S(1)} %stack.37.s, bf16[384,768]{1,0:T(8,128)(2,1)S(1)} %get-tuple-element.353.normed, bf16[384,768]{1,0:T(8,128)(2,1)S(1)} %bitcast.16, ...), custom_call_target="tpu_custom_call" | custom-call | flops 1 | bytes 1 | tf_op jit(solution)/shard_map/pallas_call | solution.py:51
  35.4 10.9 %shard_map.160 = (bf16[2,384,512]{2,1,0:T(8,128)(2,1)S(1)}, bf16[2,384,512]{2,1,0:T(8,128)(2,1)S(1)}, bf16[2,384,512]{2,1,0:T(8,128)(2,1)S(1)}, bf16[2,384,512]{...) custom-call(s32[10]{0:T(128)S(1)} %stack.37.s, ...), custom_call_target="tpu_custom_call" | custom-call | flops 1 | bytes 1 | tf_op jit(solution)/shard_map/pallas_call | solution.py:51
  46.9 1.7 collective-permute-start.10
  48.6 2.5 %shard_map.161 = (bf16[8,64,768]{2,1,0:T(8,128)(2,1)S(1)}, bf16[8,64,768]{2,1,0:T(8,128)(2,1)S(1)}) custom-call(s32[10]{0:T(128)S(1)} %stack.37.s, bf16[2,384,512]{2,1,0:T(8,128)(2,1)S(1)} %get-tuple-element.381.act.grad, bf16[2,384,512]{2,1,0:T(8,128)(2,1)S(1)} %collective-permute-done.5.act_o.grad_o, bf16[2,384,512]{2,1,0:T(8,128)(2,1)S(1)} %get-tuple-element.381.act.grad, ...), custom_call_target="tpu_custom_call" | custom-call | flops 1 | bytes 1 | tf_op jit(solution)/shard_map/pallas_call | solution.py:51
  52.8 8.1 %shard_map.162 = (bf16[384,384]{1,0:T(8,128)(2,1)S(1)}, f32[768,384]{1,0:T(8,128)S(1)}, f32[768,384]{1,0:T(8,128)S(1)}) custom-call(s32[10]{0:T(128)S(1)} %stack.37.s, bf16[384,2304]{1,0:T(8,128)(2,1)S(1)} %get-tuple-element.432.q.k.v.k_o.v_o, bf16[384,384]{1,0:T(8,128)(2,1)S(1)} %get-tuple-element.392.g, ...), custom_call_target="tpu_custom_call" | custom-call | flops 1 | bytes 1 | tf_op jit(solution)/shard_map/pallas_call | solution.py:51
  60.9 3.4 %shard_map.163 = (bf16[8,96,768]{2,1,0:T(8,128)(2,1)S(1)}, bf16[8,96,768]{2,1,0:T(8,128)(2,1)S(1)}) custom-call(s32[10]{0:T(128)S(1)} %stack.37.s, bf16[2,384,512]{2,1,0:T(8,128)(2,1)S(1)} %get-tuple-element.404.act.grad, bf16[2,384,512]{2,1,0:T(8,128)(2,1)S(1)} %collective-permute-done.4.act_o.grad_o, bf16[2,384,512]{2,1,0:T(8,128)(2,1)S(1)} %get-tuple-element.404.act.grad, ...), custom_call_target="tpu_custom_call" | custom-call | flops 1 | bytes 1 | tf_op jit(solution)/shard_map/pallas_call | solution.py:51
  64.9 2.5 %shard_map.164 = (bf16[8,64,768]{2,1,0:T(8,128)(2,1)S(1)}, bf16[8,64,768]{2,1,0:T(8,128)(2,1)S(1)}) custom-call(s32[10]{0:T(128)S(1)} %stack.37.s, bf16[2,384,512]{2,1,0:T(8,128)(2,1)S(1)} %get-tuple-element.415.act.grad, bf16[2,384,512]{2,1,0:T(8,128)(2,1)S(1)} %collective-permute-done.3.act_o.grad_o, bf16[2,384,512]{2,1,0:T(8,128)(2,1)S(1)} %get-tuple-element.415.act.grad, ...), custom_call_target="tpu_custom_call" | custom-call | flops 1 | bytes 1 | tf_op jit(solution)/shard_map/pallas_call | solution.py:51
  67.5 1.6 collective-permute-start.16
  72.0 8.4 %shard_map.166 = (bf16[384,384]{1,0:T(8,128)(2,1)S(1)}, bf16[768,384]{1,0:T(8,128)(2,1)S(1)}, bf16[768,384]{1,0:T(8,128)(2,1)S(1)}) custom-call(s32[10]{0:T(128)S(1)} %stack.37.s, bf16[384,384]{1,0:T(8,128)(2,1)S(1)} %shard_map.165.q, bf16[384,384]{1,0:T(8,128)(2,1)S(1)} %collective-permute-done.10.g, ...), custom_call_target="tpu_custom_call" | custom-call | flops 1 | bytes 1 | tf_op jit(solution)/shard_map/pallas_call | solution.py:51
  81.0 3.4 %shard_map.167 = (bf16[8,48,1152]{2,1,0:T(8,128)(2,1)S(1)}, bf16[8,48,1152]{2,1,0:T(8,128)(2,1)S(1)}) custom-call(s32[10]{0:T(128)S(1)} %stack.37.s, bf16[384,768]{1,0:T(8,128)(2,1)S(1)} %get-tuple-element.445.n_own, bf16[384,768]{1,0:T(8,128)(2,1)S(1)} %copy-done.11, bf16[384,384]{1,0:T(8,128)(2,1)S(1)} %get-tuple-element.477.gq_o, ...), custom_call_target="tpu_custom_call" | custom-call | flops 1 | bytes 1 | tf_op jit(solution)/shard_map/pallas_call | solution.py:51
  84.9 1.6 collective-permute-start.15
  88.2 1.8 collective-permute-start.21
  90.1 4.9 %collective-permute-done.15 = bf16[4,96,768]{2,1,0:T(8,128)(2,1)S(1)} collective-permute-done((bf16[4,96,768]{2,1,0:T(8,128)(2,1)S(1)}, bf16[4,96,768]{2,1,0:T(8,128)(2,1)S(1)}, u32[]{:S(2)}, u32[]{:S(2)}) %collective-permute-start.15) | collective-permute-done | bytes 589856 | tf_op jit(solution)/shard_map/ppermute | solution.py:108
  95.2 6.2 %collective-permute-done.14 = bf16[2,64,768]{2,1,0:T(8,128)(2,1)S(1)} collective-permute-done((bf16[2,64,768]{2,1,0:T(8,128)(2,1)S(1)}, bf16[2,64,768]{2,1,0:T(8,128)(2,1)S(1)}, u32[]{:S(2)}, u32[]{:S(2)}) %collective-permute-start.14) | collective-permute-done | bytes 196640 | tf_op jit(solution)/shard_map/ppermute | solution.py:108
  101.4 2.0 collective-permute-start.20
  103.5 2.1 %collective-permute-start.22 = (bf16[4,48,1152]{2,1,0:T(8,128)(2,1)S(1)}, bf16[4,48,1152]{2,1,0:T(8,128)(2,1)S(1)}, u32[]{:S(2)}, u32[]{:S(2)}) collective-permute-start(bf16[4,48,1152]{2,1,0:T(8,128)(2,1)S(1)} %add_convert_fusion.3), channel_id=1, source_target_pairs={{0,4},{1,5},{2,10},{3,11},{4,0},{5,1},{6,14},{7,15},{8,12},{9,13},... | collective-permute-start | bytes 1327112 | tf_op jit(solution)/shard_map/ppermute | solution.py:108
  105.7 2.6 %shard_map.168 = (f32[384,768]{1,0:T(8,128)S(1)}, bf16[384,768]{1,0:T(8,128)(2,1)S(1)}) custom-call(s32[10]{0:T(128)S(1)} %stack.37.s, bf16[384,384]{1,0:T(8,128)(2,1)S(1)} %get-tuple-element.477.gq_o, bf16[384,384]{1,0:T(8,128)(2,1)S(1)} %get-tuple-element.478.gq_f, bf16[768,384]{1,0:T(8,128)(2,1)S(1)} %get-tuple-element.479.gk, ...), custom_call_target="tpu_custom_call" | custom-call | flops 1 | bytes 1 | tf_op jit(solution)/shard_map/pallas_call | solution.py:51
  108.4 1.7 collective-permute-start.19
  110.2 2.7 %collective-permute-done.22 = bf16[4,48,1152]{2,1,0:T(8,128)(2,1)S(1)} collective-permute-done((bf16[4,48,1152]{2,1,0:T(8,128)(2,1)S(1)}, bf16[4,48,1152]{2,1,0:T(8,128)(2,1)S(1)}, u32[]{:S(2)}, u32[]{:S(2)}) %collective-permute-start.22) | collective-permute-done | bytes 442400 | tf_op jit(solution)/shard_map/ppermute | solution.py:108
  113.1 5.6 %collective-permute-done.20 = bf16[2,64,768]{2,1,0:T(8,128)(2,1)S(1)} collective-permute-done((bf16[2,64,768]{2,1,0:T(8,128)(2,1)S(1)}, bf16[2,64,768]{2,1,0:T(8,128)(2,1)S(1)}, u32[]{:S(2)}, u32[]{:S(2)}) %collective-permute-start.20) | collective-permute-done | bytes 196640 | tf_op jit(solution)/shard_map/ppermute | solution.py:108
  118.7 3.9 %collective-permute-done.19 = bf16[2,96,768]{2,1,0:T(8,128)(2,1)S(1)} collective-permute-done((bf16[2,96,768]{2,1,0:T(8,128)(2,1)S(1)}, bf16[2,96,768]{2,1,0:T(8,128)(2,1)S(1)}, u32[]{:S(2)}, u32[]{:S(2)}) %collective-permute-start.19) | collective-permute-done | bytes 294944 | tf_op jit(solution)/shard_map/ppermute | solution.py:108
  122.6 3.7 %collective-permute-start.25 = (bf16[2,64,768]{2,1,0:T(8,128)(2,1)S(1)}, bf16[2,64,768]{2,1,0:T(8,128)(2,1)S(1)}, u32[]{:S(2)}, u32[]{:S(2)}) collective-permute-start(bf16[2,64,768]{2,1,0:T(8,128)(2,1)S(1)} %add_convert_fusion.18), channel_id=1, source_target_pairs={{0,8},{1,9},{2,6},{3,7},{4,12},{5,13},{6,2},{7,3},{8,0},{9,1},{10,... | collective-permute-start | bytes 589832 | tf_op jit(solution)/shard_map/ppermute | solution.py:108
  126.5 2.0 collective-permute-start.28
  128.5 6.6 %collective-permute-done.25 = bf16[2,64,768]{2,1,0:T(8,128)(2,1)S(1)} collective-permute-done((bf16[2,64,768]{2,1,0:T(8,128)(2,1)S(1)}, bf16[2,64,768]{2,1,0:T(8,128)(2,1)S(1)}, u32[]{:S(2)}, u32[]{:S(2)}) %collective-permute-start.25) | collective-permute-done | bytes 196640 | tf_op jit(solution)/shard_map/ppermute | solution.py:108
  135.2 4.6 %collective-permute-done.24 = bf16[2,48,1152]{2,1,0:T(8,128)(2,1)S(1)} collective-permute-done((bf16[2,48,1152]{2,1,0:T(8,128)(2,1)S(1)}, bf16[2,48,1152]{2,1,0:T(8,128)(2,1)S(1)}, u32[]{:S(2)}, u32[]{:S(2)}) %collective-permute-start.24) | collective-permute-done | bytes 221216 | tf_op jit(solution)/shard_map/ppermute | solution.py:108
  140.6 2.5 %collective-permute-start.26 = (bf16[4,96,768]{2,1,0:T(8,128)(2,1)S(1)}, bf16[4,96,768]{2,1,0:T(8,128)(2,1)S(1)}, u32[]{:S(2)}, u32[]{:S(2)}) collective-permute-start(bf16[4,96,768]{2,1,0:T(8,128)(2,1)S(1)} %constant_dynamic-update-slice_fusion.2), channel_id=1, source_target_pairs={{0,8},{1,9},{2,3},{3,2},{4,12},{5,13},{6,7},{7,6},{8,0},{9,1},{10,... | collective-permute-start | bytes 1769480 | tf_op jit(solution)/shard_map/ppermute | solution.py:108
  143.3 5.5 %collective-permute-done.27 = bf16[2,48,1152]{2,1,0:T(8,128)(2,1)S(1)} collective-permute-done((bf16[2,48,1152]{2,1,0:T(8,128)(2,1)S(1)}, bf16[2,48,1152]{2,1,0:T(8,128)(2,1)S(1)}, u32[]{:S(2)}, u32[]{:S(2)}) %collective-permute-start.27) | collective-permute-done | bytes 221216 | tf_op jit(solution)/shard_map/ppermute | solution.py:108
  150.2 7.1 %collective-permute-done.29 = bf16[2,48,1152]{2,1,0:T(8,128)(2,1)S(1)} collective-permute-done((bf16[2,48,1152]{2,1,0:T(8,128)(2,1)S(1)}, bf16[2,48,1152]{2,1,0:T(8,128)(2,1)S(1)}, u32[]{:S(2)}, u32[]{:S(2)}) %collective-permute-start.29) | collective-permute-done | bytes 221216 | tf_op jit(solution)/shard_map/ppermute | solution.py:108
  159.0 2.4 %shard_map.169 = f32[384,768]{1,0:T(8,128)} custom-call(s32[10]{0:T(128)S(1)} %stack.37.s, f32[384,768]{1,0:T(8,128)S(1)} %get-tuple-element.530.own, bf16[384,768]{1,0:T(8,128)(2,1)S(1)} %collective-permute-done.17.far, f32[384,768]{1,0:T(8,128)S(1)} %copy-done.9, f32[1,768]{1,0:T(1,128)S(1)} %broadcast_in_dim.16.gain, f32[384,768]{1,0:T(8,128)S(1)} %copy-done.13), custom_call_target="tpu_custom_call" | custom-call | flops 1 | bytes 1 | tf_op jit(solution)/shard_map/pallas_call | solution.py:51
  161.5 6.5 %collective-permute-done.34.own = bf16[8,64,768]{2,1,0:T(8,128)(2,1)S(1)} collective-permute-done((bf16[8,64,768]{2,1,0:T(8,128)(2,1)S(1)}, bf16[8,64,768]{2,1,0:T(8,128)(2,1)S(1)}, u32[]{:S(2)}, u32[]{:S(2)}) %collective-permute-start.34) | collective-permute-done | bytes 786464 | tf_op jit(solution)/shard_map/ppermute | solution.py:108
  168.0 2.6 %shard_map.170 = (f32[2,2,8,384]{3,2,1,0:T(8,128)S(1)}, f32[3072,768]{1,0:T(8,128)}, f32[768,3072]{1,0:T(8,128)}) custom-call(s32[10]{0:T(128)S(1)} %stack.37.s, bf16[8,64,768]{2,1,0:T(8,128)(2,1)S(1)} %constant_dynamic-update-slice_fusion.4.own, bf16[8,64,768]{2,1,0:T(8,128)(2,1)S(1)} %collective-permute-done.32.other, ...), custom_call_target="tpu_custom_call", output_to_operand_aliasing={{0}: (4, {})} | custom-call | flops 1 | bytes 1 | tf_op jit(solution)/shard_map/pallas_call | solution.py:51
  172.3 3.4 %collective-permute-start.37 = (bf16[4,64,768]{2,1,0:T(8,128)(2,1)S(1)}, bf16[4,64,768]{2,1,0:T(8,128)(2,1)S(1)}, u32[]{:S(2)}, u32[]{:S(2)}) collective-permute-start(bf16[4,64,768]{2,1,0:T(8,128)(2,1)S(1)} %constant_dynamic-update-slice_fusion.12), channel_id=1, source_target_pairs={{0,1},{1,0},{2,3},{3,2},{4,5},{5,4},{6,7},{7,6},{8,9},{9,8},{10,11... | collective-permute-start | bytes 1179656 | tf_op jit(solution)/shard_map/ppermute | solution.py:108
  175.7 2.6 %shard_map.171 = (f32[2,2,8,384]{3,2,1,0:T(8,128)S(1)}, f32[3072,768]{1,0:T(8,128)}, f32[768,3072]{1,0:T(8,128)}) custom-call(s32[10]{0:T(128)S(1)} %stack.37.s, bf16[8,64,768]{2,1,0:T(8,128)(2,1)S(1)} %collective-permute-done.34.own, ...), custom_call_target="tpu_custom_call", output_to_operand_aliasing={{0}: (4, {}), {1}: (5, {}), {2}: (6, {})} | custom-call | flops 1 | bytes 1 | tf_op jit(solution)/shard_map/pallas_call | solution.py:51
  178.8 3.1 %shard_map.172 = (f32[2,2,8,384]{3,2,1,0:T(8,128)S(1)}, f32[3072,768]{1,0:T(8,128)}, f32[768,3072]{1,0:T(8,128)}, f32[768,768]{1,0:T(8,128)}) custom-call(s32[10]{0:T(128)S(1)} %stack.37.s, bf16[8,96,768]{2,1,0:T(8,128)(2,1)S(1)} %constant_dynamic-update-slice_fusion.8.own, ...), custom_call_target="tpu_custom_call", output_to_operand_aliasing={{0}: (4, {}), {1}: (5, {}), {2}: (6, {})} | custom-call | flops 1 | bytes 1 | tf_op jit(solution)/shard_map/pallas_call | solution.py:51
  181.9 2.5 %collective-permute-done.37 = bf16[4,64,768]{2,1,0:T(8,128)(2,1)S(1)} collective-permute-done((bf16[4,64,768]{2,1,0:T(8,128)(2,1)S(1)}, bf16[4,64,768]{2,1,0:T(8,128)(2,1)S(1)}, u32[]{:S(2)}, u32[]{:S(2)}) %collective-permute-start.37) | collective-permute-done | bytes 393248 | tf_op jit(solution)/shard_map/ppermute | solution.py:108
  186.0 3.1 %shard_map.173 = (f32[2,2,8,384]{3,2,1,0:T(8,128)S(1)}, f32[3072,768]{1,0:T(8,128)}, f32[768,3072]{1,0:T(8,128)}, f32[768,768]{1,0:T(8,128)}) custom-call(s32[10]{0:T(128)S(1)} %stack.37.s, bf16[8,96,768]{2,1,0:T(8,128)(2,1)S(1)} %collective-permute-done.39.own, ...), custom_call_target="tpu_custom_call", output_to_operand_aliasing={{0}: (4, {}), {1}: (5, {}), {2}: (6, {}), {3}: (7, {})} | custom-call | flops 1 | bytes 1 | tf_op jit(solution)/shard_map/pallas_call | solution.py:51
  189.1 3.2 %shard_map.174 = (f32[768,2304]{1,0:T(8,128)}, f32[8,8,96]{2,1,0:T(8,128)S(1)}) custom-call(s32[10]{0:T(128)S(1)} %stack.37.s, bf16[4,48,2304]{2,1,0:T(8,128)(2,1)S(1)} %constant_dynamic-update-slice_fusion.10.own, bf16[4,48,2304]{2,1,0:T(8,128)(2,1)S(1)} %collective-permute-done.43.other, bf16[768,2304]{1,0:T(8,128)(2,1)S(1)} %copy-done.1), custom_call_target="tpu_custom_call" | custom-call | flops 1 | bytes 1 | tf_op jit(solution)/shard_map/pallas_call | solution.py:51
  192.3 3.2 %shard_map.175 = (f32[768,2304]{1,0:T(8,128)}, f32[8,8,96]{2,1,0:T(8,128)S(1)}) custom-call(s32[10]{0:T(128)S(1)} %stack.37.s, bf16[4,48,2304]{2,1,0:T(8,128)(2,1)S(1)} %collective-permute-done.35.own, bf16[4,48,2304]{2,1,0:T(8,128)(2,1)S(1)} %collective-permute-done.41.other, ...), custom_call_target="tpu_custom_call", output_to_operand_aliasing={{0}: (4, {}), {1}: (5, {})} | custom-call | flops 1 | bytes 1 | tf_op jit(solution)/shard_map/pallas_call | solution.py:51
  195.5 2.5 %collective-permute-done.44.own = bf16[8,64,768]{2,1,0:T(8,128)(2,1)S(1)} collective-permute-done((bf16[8,64,768]{2,1,0:T(8,128)(2,1)S(1)}, bf16[8,64,768]{2,1,0:T(8,128)(2,1)S(1)}, u32[]{:S(2)}, u32[]{:S(2)}) %collective-permute-start.44) | collective-permute-done | bytes 786464 | tf_op jit(solution)/shard_map/ppermute | solution.py:108
  197.9 2.6 %shard_map.176 = (f32[2,2,8,384]{3,2,1,0:T(8,128)S(1)}, f32[3072,768]{1,0:T(8,128)}, f32[768,3072]{1,0:T(8,128)}) custom-call(s32[10]{0:T(128)S(1)} %stack.37.s, bf16[8,64,768]{2,1,0:T(8,128)(2,1)S(1)} %constant_dynamic-update-slice_fusion.14.own, ...), custom_call_target="tpu_custom_call", output_to_operand_aliasing={{0}: (4, {}), {1}: (5, {}), {2}: (6, {})} | custom-call | flops 1 | bytes 1 | tf_op jit(solution)/shard_map/pallas_call | solution.py:51
  201.3 3.5 %shard_map.177 = (f32[2,2,8,384]{3,2,1,0:T(8,128)S(1)}, f32[3072,768]{1,0:T(8,128)}, f32[768,3072]{1,0:T(8,128)}) custom-call(s32[10]{0:T(128)S(1)} %stack.37.s, bf16[8,64,768]{2,1,0:T(8,128)(2,1)S(1)} %collective-permute-done.44.own, ...), custom_call_target="tpu_custom_call", output_to_operand_aliasing={{0}: (4, {}), {1}: (5, {}), {2}: (6, {})} | custom-call | flops 1 | bytes 1 | tf_op jit(solution)/shard_map/pallas_call | solution.py:51
  (169 shorter events, 24.6 us)
Async XLA Ops:
  0.6 18.2 %collective-permute-start = (bf16[384,768]{1,0:T(8,128)(2,1)}, bf16[384,768]{1,0:T(8,128)(2,1)}, u32[]{:S(2)}, u32[]{:S(2)}) collective-permute-start(bf16[384,768]{1,0:T(8,128)(2,1)} %bitcast.22), channel_id=1, source_target_pairs={{0,1},{1,0},{2,3},{3,2},{4,5},{5,4},{6,7},{7,6},{8,9},{9,8},{10,11... | collective-permute-start | bytes 1769480 | tf_op jit(solution)/shard_map/ppermute | solution.py:108
  3.7 13.7 %collective-permute-start.1 = (s32[1,384]{1,0:T(1,128)}, s32[1,384]{1,0:T(1,128)S(1)}, u32[]{:S(2)}, u32[]{:S(2)}) collective-permute-start(s32[1,384]{1,0:T(1,128)} %visible.1), channel_id=1, source_target_pairs={{0,1},{1,0},{2,3},{3,2},{4,5},{5,4},{6,7},{7,6},{8,9},{9,8},{10,11... | collective-permute-start | bytes 4616 | tf_op jit(solution)/shard_map/ppermute | solution.py:108
  29.7 19.0 %copy-start.4 = (bf16[768,384]{1,0:T(8,128)(2,1)}, bf16[768,384]{1,0:T(8,128)(2,1)S(1)}, u32[]{:S(2)}) copy-start(bf16[768,384]{1,0:T(8,128)(2,1)S(1)} %get-tuple-element.419.nt) | copy-start | bytes 1769476
  29.7 17.1 %collective-permute-start.7 = (bf16[768,384]{1,0:T(8,128)(2,1)S(1)}, bf16[768,384]{1,0:T(8,128)(2,1)S(1)}, u32[]{:S(2)}, u32[]{:S(2)}) collective-permute-start(bf16[768,384]{1,0:T(8,128)(2,1)S(1)} %get-tuple-element.419.nt), channel_id=1, source_target_pairs={{0,2},{1,3},{2,0},{3,1},{4,6},{5,7},{6,4},{7,5},{8,10},{9,11},{10,... | collective-permute-start | bytes 1769480 | tf_op jit(solution)/shard_map/ppermute | solution.py:108
  29.8 16.6 %collective-permute-start.8 = (bf16[384,384]{1,0:T(8,128)(2,1)S(1)}, bf16[384,384]{1,0:T(8,128)(2,1)S(1)}, u32[]{:S(2)}, u32[]{:S(2)}) collective-permute-start(bf16[384,384]{1,0:T(8,128)(2,1)S(1)} %get-tuple-element.377), channel_id=1, source_target_pairs={{0,2},{1,3},{2,0},{3,1},{4,6},{5,7},{6,4},{7,5},{8,10},{9,11},{10,... | collective-permute-start | bytes 884744 | tf_op jit(solution)/shard_map/ppermute | solution.py:108
  34.8 13.8 %collective-permute-start.5 = (bf16[2,384,512]{2,1,0:T(8,128)(2,1)S(1)}, bf16[2,384,512]{2,1,0:T(8,128)(2,1)S(1)}, u32[]{:S(2)}, u32[]{:S(2)}) collective-permute-start(bf16[2,384,512]{2,1,0:T(8,128)(2,1)S(1)} %get-tuple-element.372), channel_id=1, source_target_pairs={{0,2},{1,3},{2,0},{3,1},{4,6},{5,7},{6,4},{7,5},{8,10},{9,11},{10,... | collective-permute-start | bytes 2359304 | tf_op jit(solution)/shard_map/ppermute | solution.py:108
  35.0 11.9 %collective-permute-start.6 = (bf16[384,768]{1,0:T(8,128)(2,1)S(1)}, bf16[384,768]{1,0:T(8,128)(2,1)S(1)}, u32[]{:S(2)}, u32[]{:S(2)}) collective-permute-start(bf16[384,768]{1,0:T(8,128)(2,1)S(1)} %bitcast.17), channel_id=1, source_target_pairs={{0,2},{1,3},{2,0},{3,1},{4,6},{5,7},{6,4},{7,5},{8,10},{9,11},{10,... | collective-permute-start | bytes 1769480 | tf_op jit(solution)/shard_map/ppermute | solution.py:108
  46.3 6.5 %collective-permute-start.4 = (bf16[2,384,512]{2,1,0:T(8,128)(2,1)S(1)}, bf16[2,384,512]{2,1,0:T(8,128)(2,1)S(1)}, u32[]{:S(2)}, u32[]{:S(2)}) collective-permute-start(bf16[2,384,512]{2,1,0:T(8,128)(2,1)S(1)} %get-tuple-element.370), channel_id=1, source_target_pairs={{0,2},{1,3},{2,0},{3,1},{4,6},{5,7},{6,4},{7,5},{8,10},{9,11},{10,... | collective-permute-start | bytes 2359304 | tf_op jit(solution)/shard_map/ppermute | solution.py:108
  46.4 6.4 %collective-permute-start.3 = (bf16[2,384,512]{2,1,0:T(8,128)(2,1)S(1)}, bf16[2,384,512]{2,1,0:T(8,128)(2,1)S(1)}, u32[]{:S(2)}, u32[]{:S(2)}) collective-permute-start(bf16[2,384,512]{2,1,0:T(8,128)(2,1)S(1)} %get-tuple-element.368), channel_id=1, source_target_pairs={{0,2},{1,3},{2,0},{3,1},{4,6},{5,7},{6,4},{7,5},{8,10},{9,11},{10,... | collective-permute-start | bytes 2359304 | tf_op jit(solution)/shard_map/ppermute | solution.py:108
  46.8 5.9 %collective-permute-start.2 = (bf16[384,768]{1,0:T(8,128)(2,1)S(1)}, bf16[384,768]{1,0:T(8,128)(2,1)S(1)}, u32[]{:S(2)}, u32[]{:S(2)}) collective-permute-start(bf16[384,768]{1,0:T(8,128)(2,1)S(1)} %get-tuple-element.412.refs_2_), channel_id=1, source_target_pairs={{0,2},{1,3},{2,0},{3,1},{4,6},{5,7},{6,4},{7,5},{8,10},{9,11},{10,... | collective-permute-start | bytes 1769480 | tf_op jit(solution)/shard_map/ppermute | solution.py:108
  46.9 14.0 %collective-permute-start.10 = (bf16[384,384]{1,0:T(8,128)(2,1)S(1)}, bf16[384,384]{1,0:T(8,128)(2,1)S(1)}, u32[]{:S(2)}, u32[]{:S(2)}) collective-permute-start(bf16[384,384]{1,0:T(8,128)(2,1)S(1)} %get-tuple-element.402), channel_id=1, source_target_pairs={{0,1},{1,0},{2,3},{3,2},{4,5},{5,4},{6,7},{7,6},{8,9},{9,8},{10,11... | collective-permute-start | bytes 884744 | tf_op jit(solution)/shard_map/ppermute | solution.py:108
  51.2 18.0 %collective-permute-start.9 = (bf16[8,64,768]{2,1,0:T(8,128)(2,1)S(1)}, bf16[8,64,768]{2,1,0:T(8,128)(2,1)S(1)}, u32[]{:S(2)}, u32[]{:S(2)}) collective-permute-start(bf16[8,64,768]{2,1,0:T(8,128)(2,1)S(1)} %get-tuple-element.397), channel_id=1, source_target_pairs={{0,4},{1,5},{2,3},{3,2},{4,0},{5,1},{6,7},{7,6},{8,12},{9,13},{10,... | collective-permute-start | bytes 2359304 | tf_op jit(solution)/shard_map/ppermute | solution.py:108
  64.4 16.3 %collective-permute-start.11 = (bf16[8,96,768]{2,1,0:T(8,128)(2,1)S(1)}, bf16[8,96,768]{2,1,0:T(8,128)(2,1)S(1)}, u32[]{:S(2)}, u32[]{:S(2)}) collective-permute-start(bf16[8,96,768]{2,1,0:T(8,128)(2,1)S(1)} %get-tuple-element.440), channel_id=1, source_target_pairs={{0,1},{1,0},{2,6},{3,7},{4,5},{5,4},{6,2},{7,3},{8,9},{9,8},{10,14... | collective-permute-start | bytes 3538952 | tf_op jit(solution)/shard_map/ppermute | solution.py:108
  67.5 19.1 %collective-permute-start.16 = (bf16[8,64,768]{2,1,0:T(8,128)(2,1)S(1)}, bf16[8,64,768]{2,1,0:T(8,128)(2,1)S(1)}, u32[]{:S(2)}, u32[]{:S(2)}) collective-permute-start(bf16[8,64,768]{2,1,0:T(8,128)(2,1)S(1)} %get-tuple-element.462), channel_id=1, source_target_pairs={{0,8},{1,9},{2,6},{3,7},{4,12},{5,13},{6,2},{7,3},{8,0},{9,1},{10,... | collective-permute-start | bytes 2359304 | tf_op jit(solution)/shard_map/ppermute | solution.py:108
  70.4 14.5 %collective-permute-start.13 = (bf16[4,64,768]{2,1,0:T(8,128)(2,1)S(1)}, bf16[4,64,768]{2,1,0:T(8,128)(2,1)S(1)}, u32[]{:S(2)}, u32[]{:S(2)}) collective-permute-start(bf16[4,64,768]{2,1,0:T(8,128)(2,1)S(1)} %add_convert_fusion.7), channel_id=1, source_target_pairs={{0,1},{1,0},{2,10},{3,11},{4,5},{5,4},{6,14},{7,15},{8,9},{9,8},{1... | collective-permute-start | bytes 1179656 | tf_op jit(solution)/shard_map/ppermute | solution.py:108
  84.9 10.1 %collective-permute-start.15 = (bf16[4,96,768]{2,1,0:T(8,128)(2,1)S(1)}, bf16[4,96,768]{2,1,0:T(8,128)(2,1)S(1)}, u32[]{:S(2)}, u32[]{:S(2)}) collective-permute-start(bf16[4,96,768]{2,1,0:T(8,128)(2,1)S(1)} %add_convert_fusion.1), channel_id=1, source_target_pairs={{0,8},{1,9},{2,3},{3,2},{4,12},{5,13},{6,7},{7,6},{8,0},{9,1},{10,... | collective-permute-start | bytes 1769480 | tf_op jit(solution)/shard_map/ppermute | solution.py:108
  86.7 14.7 %collective-permute-start.14 = (bf16[2,64,768]{2,1,0:T(8,128)(2,1)S(1)}, bf16[2,64,768]{2,1,0:T(8,128)(2,1)S(1)}, u32[]{:S(2)}, u32[]{:S(2)}) collective-permute-start(bf16[2,64,768]{2,1,0:T(8,128)(2,1)S(1)} %add_convert_fusion.23), channel_id=1, source_target_pairs={{0,8},{1,9},{2,6},{3,7},{4,12},{5,13},{6,2},{7,3},{8,0},{9,1},{10,... | collective-permute-start | bytes 589832 | tf_op jit(solution)/shard_map/ppermute | solution.py:108
  87.3 16.2 %collective-permute-start.12 = (bf16[8,48,1152]{2,1,0:T(8,128)(2,1)S(1)}, bf16[8,48,1152]{2,1,0:T(8,128)(2,1)S(1)}, u32[]{:S(2)}, u32[]{:S(2)}) collective-permute-start(bf16[8,48,1152]{2,1,0:T(8,128)(2,1)S(1)} %get-tuple-element.453), channel_id=1, source_target_pairs={{0,2},{1,3},{2,0},{3,1},{4,6},{5,7},{6,4},{7,5},{8,10},{9,11},{10,... | collective-permute-start | bytes 2654216 | tf_op jit(solution)/shard_map/ppermute | solution.py:108
  88.2 24.8 %collective-permute-start.21 = (bf16[4,64,768]{2,1,0:T(8,128)(2,1)S(1)}, bf16[4,64,768]{2,1,0:T(8,128)(2,1)S(1)}, u32[]{:S(2)}, u32[]{:S(2)}) collective-permute-start(bf16[4,64,768]{2,1,0:T(8,128)(2,1)S(1)} %add_convert_fusion.5), channel_id=1, source_target_pairs={{0,1},{1,0},{2,3},{3,2},{4,5},{5,4},{6,7},{7,6},{8,9},{9,8},{10,11... | collective-permute-start | bytes 1179656 | tf_op jit(solution)/shard_map/ppermute | solution.py:108
  101.4 7.0 %collective-permute-start.18 = (bf16[2,96,768]{2,1,0:T(8,128)(2,1)S(1)}, bf16[2,96,768]{2,1,0:T(8,128)(2,1)S(1)}, u32[]{:S(2)}, u32[]{:S(2)}) collective-permute-start(bf16[2,96,768]{2,1,0:T(8,128)(2,1)S(1)} %add_convert_fusion.11), channel_id=1, source_target_pairs={{0,4},{1,5},{2,10},{3,11},{4,0},{5,1},{6,14},{7,15},{8,12},{9,13},... | collective-permute-start | bytes 884744 | tf_op jit(solution)/shard_map/ppermute | solution.py:108
  101.4 17.2 %collective-permute-start.20 = (bf16[2,64,768]{2,1,0:T(8,128)(2,1)S(1)}, bf16[2,64,768]{2,1,0:T(8,128)(2,1)S(1)}, u32[]{:S(2)}, u32[]{:S(2)}) collective-permute-start(bf16[2,64,768]{2,1,0:T(8,128)(2,1)S(1)} %add_convert_fusion.21), channel_id=1, source_target_pairs={{0,16},{1,17},{2,18},{3,19},{4,20},{5,21},{6,22},{7,23},{8,24},{9,... | collective-permute-start | bytes 589832 | tf_op jit(solution)/shard_map/ppermute | solution.py:108
  103.5 9.3 %collective-permute-start.22 = (bf16[4,48,1152]{2,1,0:T(8,128)(2,1)S(1)}, bf16[4,48,1152]{2,1,0:T(8,128)(2,1)S(1)}, u32[]{:S(2)}, u32[]{:S(2)}) collective-permute-start(bf16[4,48,1152]{2,1,0:T(8,128)(2,1)S(1)} %add_convert_fusion.3), channel_id=1, source_target_pairs={{0,4},{1,5},{2,10},{3,11},{4,0},{5,1},{6,14},{7,15},{8,12},{9,13},... | collective-permute-start | bytes 1327112 | tf_op jit(solution)/shard_map/ppermute | solution.py:108
  108.4 14.2 %collective-permute-start.19 = (bf16[2,96,768]{2,1,0:T(8,128)(2,1)S(1)}, bf16[2,96,768]{2,1,0:T(8,128)(2,1)S(1)}, u32[]{:S(2)}, u32[]{:S(2)}) collective-permute-start(bf16[2,96,768]{2,1,0:T(8,128)(2,1)S(1)} %add_convert_fusion.9), channel_id=1, source_target_pairs={{0,16},{1,17},{2,18},{3,19},{4,20},{5,21},{6,22},{7,23},{8,24},{9,... | collective-permute-start | bytes 884744 | tf_op jit(solution)/shard_map/ppermute | solution.py:108
  110.2 30.5 %collective-permute-start.17 = (bf16[384,768]{1,0:T(8,128)(2,1)S(1)}, bf16[384,768]{1,0:T(8,128)(2,1)S(1)}, u32[]{:S(2)}, u32[]{:S(2)}) collective-permute-start(bf16[384,768]{1,0:T(8,128)(2,1)S(1)} %get-tuple-element.484), channel_id=1, source_target_pairs={{0,1},{1,0},{2,3},{3,2},{4,5},{5,4},{6,7},{7,6},{8,9},{9,8},{10,11... | collective-permute-start | bytes 1769480 | tf_op jit(solution)/shard_map/ppermute | solution.py:108
  122.6 12.5 %collective-permute-start.25 = (bf16[2,64,768]{2,1,0:T(8,128)(2,1)S(1)}, bf16[2,64,768]{2,1,0:T(8,128)(2,1)S(1)}, u32[]{:S(2)}, u32[]{:S(2)}) collective-permute-start(bf16[2,64,768]{2,1,0:T(8,128)(2,1)S(1)} %add_convert_fusion.18), channel_id=1, source_target_pairs={{0,8},{1,9},{2,6},{3,7},{4,12},{5,13},{6,2},{7,3},{8,0},{9,1},{10,... | collective-permute-start | bytes 589832 | tf_op jit(solution)/shard_map/ppermute | solution.py:108
  126.3 13.5 %collective-permute-start.24 = (bf16[2,48,1152]{2,1,0:T(8,128)(2,1)S(1)}, bf16[2,48,1152]{2,1,0:T(8,128)(2,1)S(1)}, u32[]{:S(2)}, u32[]{:S(2)}) collective-permute-start(bf16[2,48,1152]{2,1,0:T(8,128)(2,1)S(1)} %add_convert_fusion.15), channel_id=1, source_target_pairs={{0,8},{1,9},{2,18},{3,19},{4,12},{5,13},{6,22},{7,23},{8,0},{9,1},... | collective-permute-start | bytes 663560 | tf_op jit(solution)/shard_map/ppermute | solution.py:108
  126.4 14.2 %collective-permute-start.23 = (bf16[2,96,768]{2,1,0:T(8,128)(2,1)S(1)}, bf16[2,96,768]{2,1,0:T(8,128)(2,1)S(1)}, u32[]{:S(2)}, u32[]{:S(2)}) collective-permute-start(bf16[2,96,768]{2,1,0:T(8,128)(2,1)S(1)} %add_convert_fusion.8), channel_id=1, source_target_pairs={{0,4},{1,5},{2,10},{3,11},{4,0},{5,1},{6,14},{7,15},{8,12},{9,13},... | collective-permute-start | bytes 884744 | tf_op jit(solution)/shard_map/ppermute | solution.py:108
  126.5 14.2 %collective-permute-start.28 = (bf16[2,64,768]{2,1,0:T(8,128)(2,1)S(1)}, bf16[2,64,768]{2,1,0:T(8,128)(2,1)S(1)}, u32[]{:S(2)}, u32[]{:S(2)}) collective-permute-start(bf16[2,64,768]{2,1,0:T(8,128)(2,1)S(1)} %add_convert_fusion.20), channel_id=1, source_target_pairs={{0,4},{1,5},{2,18},{3,19},{4,0},{5,1},{6,22},{7,23},{8,12},{9,13},... | collective-permute-start | bytes 589832 | tf_op jit(solution)/shard_map/ppermute | solution.py:108
  135.1 13.9 %collective-permute-start.30 = (bf16[4,64,768]{2,1,0:T(8,128)(2,1)S(1)}, bf16[4,64,768]{2,1,0:T(8,128)(2,1)S(1)}, u32[]{:S(2)}, u32[]{:S(2)}) collective-permute-start(bf16[4,64,768]{2,1,0:T(8,128)(2,1)S(1)} %constant_dynamic-update-slice_fusion), channel_id=1, source_target_pairs={{0,1},{1,0},{2,10},{3,11},{4,5},{5,4},{6,14},{7,15},{8,9},{9,8},{1... | collective-permute-start | bytes 1179656 | tf_op jit(solution)/shard_map/ppermute | solution.py:108
  139.9 9.0 %collective-permute-start.27 = (bf16[2,48,1152]{2,1,0:T(8,128)(2,1)S(1)}, bf16[2,48,1152]{2,1,0:T(8,128)(2,1)S(1)}, u32[]{:S(2)}, u32[]{:S(2)}) collective-permute-start(bf16[2,48,1152]{2,1,0:T(8,128)(2,1)S(1)} %add_convert_fusion.13), channel_id=1, source_target_pairs={{0,16},{1,17},{2,6},{3,7},{4,20},{5,21},{6,2},{7,3},{8,24},{9,25},... | collective-permute-start | bytes 663560 | tf_op jit(solution)/shard_map/ppermute | solution.py:108
  140.6 16.8 %collective-permute-start.26 = (bf16[4,96,768]{2,1,0:T(8,128)(2,1)S(1)}, bf16[4,96,768]{2,1,0:T(8,128)(2,1)S(1)}, u32[]{:S(2)}, u32[]{:S(2)}) collective-permute-start(bf16[4,96,768]{2,1,0:T(8,128)(2,1)S(1)} %constant_dynamic-update-slice_fusion.2), channel_id=1, source_target_pairs={{0,8},{1,9},{2,3},{3,2},{4,12},{5,13},{6,7},{7,6},{8,0},{9,1},{10,... | collective-permute-start | bytes 1769480 | tf_op jit(solution)/shard_map/ppermute | solution.py:108
  143.2 18.1 %collective-permute-start.33 = (bf16[2,64,768]{2,1,0:T(8,128)(2,1)S(1)}, bf16[2,64,768]{2,1,0:T(8,128)(2,1)S(1)}, u32[]{:S(2)}, u32[]{:S(2)}) collective-permute-start(bf16[2,64,768]{2,1,0:T(8,128)(2,1)S(1)} %add_convert_fusion.17), channel_id=1, source_target_pairs={{0,16},{1,17},{2,10},{3,11},{4,20},{5,21},{6,14},{7,15},{8,24},{9,... | collective-permute-start | bytes 589832 | tf_op jit(solution)/shard_map/ppermute | solution.py:108
  148.9 8.4 %collective-permute-start.29 = (bf16[2,48,1152]{2,1,0:T(8,128)(2,1)S(1)}, bf16[2,48,1152]{2,1,0:T(8,128)(2,1)S(1)}, u32[]{:S(2)}, u32[]{:S(2)}) collective-permute-start(bf16[2,48,1152]{2,1,0:T(8,128)(2,1)S(1)} %add_convert_fusion.12), channel_id=1, source_target_pairs={{0,1},{1,0},{2,3},{3,2},{4,5},{5,4},{6,7},{7,6},{8,9},{9,8},{10,11... | collective-permute-start | bytes 663560 | tf_op jit(solution)/shard_map/ppermute | solution.py:108
  149.1 12.3 %collective-permute-start.32 = (bf16[8,64,768]{2,1,0:T(8,128)(2,1)S(1)}, bf16[8,64,768]{2,1,0:T(8,128)(2,1)S(1)}, u32[]{:S(2)}, u32[]{:S(2)}) collective-permute-start(bf16[8,64,768]{2,1,0:T(8,128)(2,1)S(1)} %constant_dynamic-update-slice_fusion.4.own), channel_id=1, source_target_pairs={{0,2},{1,3},{2,0},{3,1},{4,6},{5,7},{6,4},{7,5},{8,10},{9,11},{10,... | collective-permute-start | bytes 2359304 | tf_op jit(solution)/shard_map/ppermute | solution.py:108
  149.2 18.9 %collective-permute-start.34 = (bf16[8,64,768]{2,1,0:T(8,128)(2,1)S(1)}, bf16[8,64,768]{2,1,0:T(8,128)(2,1)S(1)}, u32[]{:S(2)}, u32[]{:S(2)}) collective-permute-start(bf16[8,64,768]{2,1,0:T(8,128)(2,1)S(1)} %constant_dynamic-update-slice_fusion.4.own), channel_id=1, source_target_pairs={{0,4},{1,5},{2,3},{3,2},{4,0},{5,1},{6,7},{7,6},{8,12},{9,13},{10,... | collective-permute-start | bytes 2359304 | tf_op jit(solution)/shard_map/ppermute | solution.py:108
  157.4 13.8 %collective-permute-start.31 = (bf16[2,48,2304]{2,1,0:T(8,128)(2,1)S(1)}, bf16[2,48,2304]{2,1,0:T(8,128)(2,1)S(1)}, u32[]{:S(2)}, u32[]{:S(2)}) collective-permute-start(bf16[2,48,2304]{2,1,0:T(8,128)(2,1)S(1)} %constant_dynamic-update-slice_fusion.6), channel_id=1, source_target_pairs={{0,8},{1,9},{2,18},{3,19},{4,12},{5,13},{6,22},{7,23},{8,0},{9,1},... | collective-permute-start | bytes 1327112 | tf_op jit(solution)/shard_map/ppermute | solution.py:108
  157.5 20.8 %collective-permute-start.39 = (bf16[8,96,768]{2,1,0:T(8,128)(2,1)S(1)}, bf16[8,96,768]{2,1,0:T(8,128)(2,1)S(1)}, u32[]{:S(2)}, u32[]{:S(2)}) collective-permute-start(bf16[8,96,768]{2,1,0:T(8,128)(2,1)S(1)} %constant_dynamic-update-slice_fusion.8.own), channel_id=1, source_target_pairs={{0,1},{1,0},{2,6},{3,7},{4,5},{5,4},{6,2},{7,3},{8,9},{9,8},{10,14... | collective-permute-start | bytes 3538952 | tf_op jit(solution)/shard_map/ppermute | solution.py:108
  161.3 17.5 %collective-permute-start.38 = (bf16[8,96,768]{2,1,0:T(8,128)(2,1)S(1)}, bf16[8,96,768]{2,1,0:T(8,128)(2,1)S(1)}, u32[]{:S(2)}, u32[]{:S(2)}) collective-permute-start(bf16[8,96,768]{2,1,0:T(8,128)(2,1)S(1)} %constant_dynamic-update-slice_fusion.8.own), channel_id=1, source_target_pairs={{0,2},{1,3},{2,0},{3,1},{4,6},{5,7},{6,4},{7,5},{8,10},{9,11},{10,... | collective-permute-start | bytes 3538952 | tf_op jit(solution)/shard_map/ppermute | solution.py:108
  161.4 10.8 %collective-permute-start.36 = (bf16[2,64,768]{2,1,0:T(8,128)(2,1)S(1)}, bf16[2,64,768]{2,1,0:T(8,128)(2,1)S(1)}, u32[]{:S(2)}, u32[]{:S(2)}) collective-permute-start(bf16[2,64,768]{2,1,0:T(8,128)(2,1)S(1)} %add_convert_fusion.16), channel_id=1, source_target_pairs={{0,4},{1,5},{2,18},{3,19},{4,0},{5,1},{6,22},{7,23},{8,12},{9,13},... | collective-permute-start | bytes 589832 | tf_op jit(solution)/shard_map/ppermute | solution.py:108
  171.2 4.5 %collective-permute-start.40 = (bf16[8,64,768]{2,1,0:T(8,128)(2,1)S(1)}, bf16[8,64,768]{2,1,0:T(8,128)(2,1)S(1)}, u32[]{:S(2)}, u32[]{:S(2)}) collective-permute-start(bf16[8,64,768]{2,1,0:T(8,128)(2,1)S(1)} %collective-permute-done.34.own), channel_id=1, source_target_pairs={{0,2},{1,3},{2,0},{3,1},{4,6},{5,7},{6,4},{7,5},{8,10},{9,11},{10,... | collective-permute-start | bytes 2359304 | tf_op jit(solution)/shard_map/ppermute | solution.py:108
  171.3 14.2 %collective-permute-start.35 = (bf16[4,48,2304]{2,1,0:T(8,128)(2,1)S(1)}, bf16[4,48,2304]{2,1,0:T(8,128)(2,1)S(1)}, u32[]{:S(2)}, u32[]{:S(2)}) collective-permute-start(bf16[4,48,2304]{2,1,0:T(8,128)(2,1)S(1)} %constant_dynamic-update-slice_fusion.10.own), channel_id=1, source_target_pairs={{0,4},{1,5},{2,10},{3,11},{4,0},{5,1},{6,14},{7,15},{8,12},{9,13},... | collective-permute-start | bytes 2654216 | tf_op jit(solution)/shard_map/ppermute | solution.py:108
  172.3 12.1 %collective-permute-start.37 = (bf16[4,64,768]{2,1,0:T(8,128)(2,1)S(1)}, bf16[4,64,768]{2,1,0:T(8,128)(2,1)S(1)}, u32[]{:S(2)}, u32[]{:S(2)}) collective-permute-start(bf16[4,64,768]{2,1,0:T(8,128)(2,1)S(1)} %constant_dynamic-update-slice_fusion.12), channel_id=1, source_target_pairs={{0,1},{1,0},{2,3},{3,2},{4,5},{5,4},{6,7},{7,6},{8,9},{9,8},{10,11... | collective-permute-start | bytes 1179656 | tf_op jit(solution)/shard_map/ppermute | solution.py:108
  178.3 7.6 %collective-permute-start.42 = (bf16[8,96,768]{2,1,0:T(8,128)(2,1)S(1)}, bf16[8,96,768]{2,1,0:T(8,128)(2,1)S(1)}, u32[]{:S(2)}, u32[]{:S(2)}) collective-permute-start(bf16[8,96,768]{2,1,0:T(8,128)(2,1)S(1)} %collective-permute-done.39.own), channel_id=1, source_target_pairs={{0,2},{1,3},{2,0},{3,1},{4,6},{5,7},{6,4},{7,5},{8,10},{9,11},{10,... | collective-permute-start | bytes 3538952 | tf_op jit(solution)/shard_map/ppermute | solution.py:108
  178.3 7.6 %collective-permute-start.43 = (bf16[4,48,2304]{2,1,0:T(8,128)(2,1)S(1)}, bf16[4,48,2304]{2,1,0:T(8,128)(2,1)S(1)}, u32[]{:S(2)}, u32[]{:S(2)}) collective-permute-start(bf16[4,48,2304]{2,1,0:T(8,128)(2,1)S(1)} %constant_dynamic-update-slice_fusion.10.own), channel_id=1, source_target_pairs={{0,2},{1,3},{2,0},{3,1},{4,6},{5,7},{6,4},{7,5},{8,10},{9,11},{10,... | collective-permute-start | bytes 2654216 | tf_op jit(solution)/shard_map/ppermute | solution.py:108
  185.4 3.6 %collective-permute-start.41 = (bf16[4,48,2304]{2,1,0:T(8,128)(2,1)S(1)}, bf16[4,48,2304]{2,1,0:T(8,128)(2,1)S(1)}, u32[]{:S(2)}, u32[]{:S(2)}) collective-permute-start(bf16[4,48,2304]{2,1,0:T(8,128)(2,1)S(1)} %collective-permute-done.35.own), channel_id=1, source_target_pairs={{0,2},{1,3},{2,0},{3,1},{4,6},{5,7},{6,4},{7,5},{8,10},{9,11},{10,... | collective-permute-start | bytes 2654216 | tf_op jit(solution)/shard_map/ppermute | solution.py:108
  185.4 10.0 %collective-permute-start.45 = (bf16[8,64,768]{2,1,0:T(8,128)(2,1)S(1)}, bf16[8,64,768]{2,1,0:T(8,128)(2,1)S(1)}, u32[]{:S(2)}, u32[]{:S(2)}) collective-permute-start(bf16[8,64,768]{2,1,0:T(8,128)(2,1)S(1)} %constant_dynamic-update-slice_fusion.14.own), channel_id=1, source_target_pairs={{0,2},{1,3},{2,0},{3,1},{4,6},{5,7},{6,4},{7,5},{8,10},{9,11},{10,... | collective-permute-start | bytes 2359304 | tf_op jit(solution)/shard_map/ppermute | solution.py:108
  186.0 12.0 %collective-permute-start.44 = (bf16[8,64,768]{2,1,0:T(8,128)(2,1)S(1)}, bf16[8,64,768]{2,1,0:T(8,128)(2,1)S(1)}, u32[]{:S(2)}, u32[]{:S(2)}) collective-permute-start(bf16[8,64,768]{2,1,0:T(8,128)(2,1)S(1)} %constant_dynamic-update-slice_fusion.14.own), channel_id=1, source_target_pairs={{0,8},{1,9},{2,6},{3,7},{4,12},{5,13},{6,2},{7,3},{8,0},{9,1},{10,... | collective-permute-start | bytes 2359304 | tf_op jit(solution)/shard_map/ppermute | solution.py:108
  197.9 3.3 %collective-permute-start.46 = (bf16[8,64,768]{2,1,0:T(8,128)(2,1)S(1)}, bf16[8,64,768]{2,1,0:T(8,128)(2,1)S(1)}, u32[]{:S(2)}, u32[]{:S(2)}) collective-permute-start(bf16[8,64,768]{2,1,0:T(8,128)(2,1)S(1)} %collective-permute-done.44.own), channel_id=1, source_target_pairs={{0,2},{1,3},{2,0},{3,1},{4,6},{5,7},{6,4},{7,5},{8,10},{9,11},{10,... | collective-permute-start | bytes 2359304 | tf_op jit(solution)/shard_map/ppermute | solution.py:108
  (21 other events, 132.1 us)

commit v5 on v4

--- a/solution.py
+++ b/solution.py
@@ -84,15 +84,15 @@
 )
 QKV_ORDER = (("x", "z0", "z1"), ("z0", "z1", "x"))
 PLAN = (
-    ("ff", 0), ("ff", 1), ("wait", "early"), ("wait", "e0"), ("dw", 0), ("wait", "e2"),
-    ("wait", "e1"), ("wait", "branch_other"), ("own",), ("wait", "g"), ("dw", 2), ("dw", 1),
-    ("go", 0), ("far",), ("go", 2), ("joint",), ("go", 0), ("go", 1), ("go", 2), ("go", 0),
-    ("go", 3), ("back",), ("go", 2), ("go", 3), ("go", 1), ("go", 0), ("go", 2), ("go", 0),
-    ("go", 3), ("go", 2), ("wait", "bf"), ("go", 1), ("go", 3), ("go", 0), ("go", 3), ("go", 2),
-    ("tokens",), ("go", 1), ("wait", "n0"), ("go", 0), ("unpack", 0, 0), ("go", 3), ("go", 1),
-    ("wait", "f0"), ("unpack", 0, 1), ("go", 2), ("wait", "n2"), ("unpack", 2, 0), ("go", 1),
-    ("go", 3), ("wait", "f2"), ("wait", "n3"), ("unpack", 2, 1), ("wait", "f3"), ("unpack", 3, 0),
-    ("unpack", 3, 1), ("wait", "n1"), ("go", 1), ("unpack", 1, 0), ("wait", "f1"), ("unpack", 1, 1),
+    ("ff", 0), ("wait", "early"), ("ff", 1), ("wait", "e0"), ("dw", 0), ("own",),
+    ("wait", "branch_other"), ("wait", "e2"), ("wait", "g"), ("dw", 2), ("wait", "e1"), ("dw", 1),
+    ("go", 0), ("far",), ("go", 2), ("joint",), ("go", 0), ("go", 2), ("go", 1), ("go", 0),
+    ("go", 3), ("go", 2), ("back",), ("go", 3), ("go", 1), ("go", 0), ("wait", "bf"), ("go", 2),
+    ("go", 0), ("go", 3), ("go", 2), ("go", 1), ("go", 3), ("go", 0), ("go", 3), ("go", 2),
+    ("go", 1), ("wait", "n0"), ("go", 0), ("unpack", 0, 0), ("go", 3), ("go", 1), ("wait", "f0"),
+    ("tokens",), ("unpack", 0, 1), ("go", 2), ("wait", "n2"), ("unpack", 2, 0), ("go", 1),
+    ("go", 3), ("wait", "f2"), ("wait", "n3"), ("unpack", 2, 1), ("unpack", 3, 0), ("wait", "f3"),
+    ("unpack", 3, 1), ("go", 1), ("wait", "n1"), ("unpack", 1, 0), ("wait", "f1"), ("unpack", 1, 1),
 )
 DP_BIT = {"c": 1, "x": 2, "z0": 4, "z1": 8}
 

time: 206 us -> 195 us (0.947)
  waiting for transfers between devices: 62.4 us -> 48.1 us
  starting transfers between devices: 38.1 us -> 42.3 us
    ppermute x47, waiting for transfers between devices: 62.4 us -> 48.1 us  [swap(): return lax.ppermute(array, AXES, pairs)]
    ppermute x47, starting transfers between devices: 38.1 us -> 42.3 us  [swap(): return lax.ppermute(array, AXES, pairs)]
  transfers between devices with their start and end apart: 47 -> 47, of which waited for: 18 -> 16; matrix products, arithmetic and copies ran while one was open for 1% -> 2% of each run, Pallas kernels for 40% -> 42%
where the time goes in v5:
time: 195 us; the launch traced here: 194 us
  Pallas kernels  95.6 us (49%)
  waiting for transfers between devices  48.1 us (25%)
  starting transfers between devices  42.3 us (22%)
  local copies, waits for them, and re-layouts  3.39 us (2%)
  other arithmetic  3.07 us (2%)
    pallas_call x26, Pallas kernels, call(): pl.pallas_call(kernel, grid_spec=pltpu.PrefetchScalarGridSpec(num_scalar_...  95.6 us
    ppermute x47, waiting for transfers between devices, swap(): return lax.ppermute(array, AXES, pairs)  48.1 us
    ppermute x47, starting transfers between devices, swap(): return lax.ppermute(array, AXES, pairs)  42.3 us
  transfers between devices with their start and end apart: 47, of which 16 were waited for; matrix products, arithmetic and copies ran while one was open for 2% of the time, Pallas kernels for 42%

profile of v5, /device:TPU:0, one launch (start us, length us, event | category | flops | bytes accessed | tf_op | source)
XLA Modules:
  0.0 193.9 jit_solution(7397793334761653345)
XLA Ops:
  0.6 3.0 %collective-permute-start = (bf16[384,768]{1,0:T(8,128)(2,1)}, bf16[384,768]{1,0:T(8,128)(2,1)}, u32[]{:S(2)}, u32[]{:S(2)}) collective-permute-start(bf16[384,768]{1,0:T(8,128)(2,1)} %bitcast.22), channel_id=1, source_target_pairs={{0,1},{1,0},{2,3},{3,2},{4,5},{5,4},{6,7},{7,6},{8,9},{9,8},{10,11... | collective-permute-start | bytes 1769480 | tf_op jit(solution)/shard_map/ppermute | solution.py:108
  6.1 2.0 %copy-done = bf16[768,2304]{1,0:T(8,128)(2,1)S(1)} copy-done((bf16[768,2304]{1,0:T(8,128)(2,1)S(1)}, bf16[768,2304]{1,0:T(8,128)(2,1)}, u32[]{:S(2)}) %copy-start) | copy-done | bytes 3538968
  8.1 3.2 %shard_map.153 = (bf16[384,768]{1,0:T(8,128)(2,1)S(1)}, bf16[384,2304]{1,0:T(8,128)(2,1)S(1)}, f32[384,768]{1,0:T(8,128)S(1)}) custom-call(s32[10]{0:T(128)S(1)} %stack.37.s, bf16[384,768]{1,0:T(8,128)(2,1)S(1)} %bitcast.23, f32[384,768]{1,0:T(8,128)S(1)} %shard_map.152.pos, f32[1,768]{1,0:T(1,128)S(1)} %broadcast_in_dim.16.gain, bf16[768,2304]{1,0:T(8,128)(2,1)S(1)} %copy-done), custom_call_target="tpu_custom_call" | custom-call | flops 1 | bytes 1 | tf_op jit(solution)/shard_map/pallas_call | solution.py:51
  11.4 5.1 %shard_map.154 = (f32[6,128,384]{2,1,0:T(8,128)S(1)}, f32[6,8,768]{2,1,0:T(8,128)S(1)}) custom-call(s32[10]{0:T(128)S(1)} %stack.37.s, bf16[384,2304]{1,0:T(8,128)(2,1)S(1)} %get-tuple-element.432.q.k.v.k_o.v_o, bf16[384,2304]{1,0:T(8,128)(2,1)S(1)} %get-tuple-element.432.q.k.v.k_o.v_o, bf16[384,2304]{1,0:T(8,128)(2,1)S(1)} %get-tuple-element.432.q.k.v.k_o.v_o), custom_call_target="tpu_custom_call" | custom-call | flops 1 | bytes 1 | tf_op jit(solution)/shard_map/pallas_call | solution.py:51
  18.9 3.5 %shard_map.156 = (bf16[384,768]{1,0:T(8,128)(2,1)S(1)}, bf16[384,1536]{1,0:T(8,128)(2,1)S(1)}) custom-call(s32[10]{0:T(128)S(1)} %stack.37.s, bf16[384,768]{1,0:T(8,128)(2,1)} %collective-permute-done.tok, f32[384,768]{1,0:T(8,128)S(1)} %shard_map.155.pos, f32[1,768]{1,0:T(1,128)S(1)} %broadcast_in_dim.16.gain, bf16[768,2304]{1,0:T(8,128)(2,1)S(1)} %copy-done.1), custom_call_target="tpu_custom_call" | custom-call | flops 1 | bytes 1 | tf_op jit(solution)/shard_map/pallas_call | solution.py:51
  22.4 5.6 %shard_map.157.att.att_half.refs_0_ = bf16[384,768]{1,0:T(8,128)(2,1)S(1)} custom-call(s32[10]{0:T(128)S(1)} %stack.37.s, bf16[384,2304]{1,0:T(8,128)(2,1)S(1)} %get-tuple-element.432.q.k.v.k_o.v_o, bf16[384,1536]{1,0:T(8,128)(2,1)S(1)} %get-tuple-element.433.k.v.k_f.v_f, bf16[384,1536]{1,0:T(8,128)(2,1)S(1)} %get-tuple-element.433.k.v.k_f.v_f, ...), custom_call_target="tpu_custom_call" | custom-call | flops 1 | bytes 1 | tf_op jit(solution)/shard_map/pallas_call | solution.py:51
  28.0 1.6 shard_map.158
  30.4 4.5 %shard_map.159 = (bf16[2,384,512]{2,1,0:T(8,128)(2,1)S(1)}, bf16[2,384,512]{2,1,0:T(8,128)(2,1)S(1)}, f32[384,768]{1,0:T(8,128)S(1)}, f32[384,768]{1,0:T(8,128)S(1)}) custom-call(s32[10]{0:T(128)S(1)} %stack.37.s, bf16[384,768]{1,0:T(8,128)(2,1)S(1)} %get-tuple-element.359.normed, bf16[384,768]{1,0:T(8,128)(2,1)S(1)} %bitcast.17, ...), custom_call_target="tpu_custom_call" | custom-call | flops 1 | bytes 1 | tf_op jit(solution)/shard_map/pallas_call | solution.py:51
  35.4 10.9 %shard_map.160 = (bf16[2,384,512]{2,1,0:T(8,128)(2,1)S(1)}, bf16[2,384,512]{2,1,0:T(8,128)(2,1)S(1)}, bf16[2,384,512]{2,1,0:T(8,128)(2,1)S(1)}, bf16[2,384,512]{...) custom-call(s32[10]{0:T(128)S(1)} %stack.37.s, ...), custom_call_target="tpu_custom_call" | custom-call | flops 1 | bytes 1 | tf_op jit(solution)/shard_map/pallas_call | solution.py:51
  46.8 1.7 collective-permute-start.10
  48.6 2.5 %shard_map.161 = (bf16[8,64,768]{2,1,0:T(8,128)(2,1)S(1)}, bf16[8,64,768]{2,1,0:T(8,128)(2,1)S(1)}) custom-call(s32[10]{0:T(128)S(1)} %stack.37.s, bf16[2,384,512]{2,1,0:T(8,128)(2,1)S(1)} %get-tuple-element.376.act.grad, bf16[2,384,512]{2,1,0:T(8,128)(2,1)S(1)} %collective-permute-done.5.act_o.grad_o, bf16[2,384,512]{2,1,0:T(8,128)(2,1)S(1)} %get-tuple-element.376.act.grad, ...), custom_call_target="tpu_custom_call" | custom-call | flops 1 | bytes 1 | tf_op jit(solution)/shard_map/pallas_call | solution.py:51
  51.1 1.6 collective-permute-start.6
  52.7 8.1 %shard_map.162 = (bf16[384,384]{1,0:T(8,128)(2,1)S(1)}, f32[768,384]{1,0:T(8,128)S(1)}, f32[768,384]{1,0:T(8,128)S(1)}) custom-call(s32[10]{0:T(128)S(1)} %stack.37.s, bf16[384,2304]{1,0:T(8,128)(2,1)S(1)} %get-tuple-element.432.q.k.v.k_o.v_o, bf16[384,384]{1,0:T(8,128)(2,1)S(1)} %get-tuple-element.384.g, ...), custom_call_target="tpu_custom_call" | custom-call | flops 1 | bytes 1 | tf_op jit(solution)/shard_map/pallas_call | solution.py:51
  60.9 3.4 %shard_map.163 = (bf16[8,96,768]{2,1,0:T(8,128)(2,1)S(1)}, bf16[8,96,768]{2,1,0:T(8,128)(2,1)S(1)}) custom-call(s32[10]{0:T(128)S(1)} %stack.37.s, bf16[2,384,512]{2,1,0:T(8,128)(2,1)S(1)} %get-tuple-element.403.act.grad, bf16[2,384,512]{2,1,0:T(8,128)(2,1)S(1)} %collective-permute-done.8.act_o.grad_o, bf16[2,384,512]{2,1,0:T(8,128)(2,1)S(1)} %get-tuple-element.403.act.grad, ...), custom_call_target="tpu_custom_call" | custom-call | flops 1 | bytes 1 | tf_op jit(solution)/shard_map/pallas_call | solution.py:51
  64.9 2.5 %shard_map.164 = (bf16[8,64,768]{2,1,0:T(8,128)(2,1)S(1)}, bf16[8,64,768]{2,1,0:T(8,128)(2,1)S(1)}) custom-call(s32[10]{0:T(128)S(1)} %stack.37.s, bf16[2,384,512]{2,1,0:T(8,128)(2,1)S(1)} %get-tuple-element.415.act.grad, bf16[2,384,512]{2,1,0:T(8,128)(2,1)S(1)} %collective-permute-done.7.act_o.grad_o, bf16[2,384,512]{2,1,0:T(8,128)(2,1)S(1)} %get-tuple-element.415.act.grad, ...), custom_call_target="tpu_custom_call" | custom-call | flops 1 | bytes 1 | tf_op jit(solution)/shard_map/pallas_call | solution.py:51
  67.4 1.6 collective-permute-start.17
  70.3 1.6 collective-permute-start.13
  71.9 8.4 %shard_map.166 = (bf16[384,384]{1,0:T(8,128)(2,1)S(1)}, bf16[768,384]{1,0:T(8,128)(2,1)S(1)}, bf16[768,384]{1,0:T(8,128)(2,1)S(1)}) custom-call(s32[10]{0:T(128)S(1)} %stack.37.s, bf16[384,384]{1,0:T(8,128)(2,1)S(1)} %shard_map.165.q, bf16[384,384]{1,0:T(8,128)(2,1)S(1)} %collective-permute-done.10.g, ...), custom_call_target="tpu_custom_call" | custom-call | flops 1 | bytes 1 | tf_op jit(solution)/shard_map/pallas_call | solution.py:51
  80.7 1.6 collective-permute-start.12
  82.5 3.4 %shard_map.167 = (bf16[8,48,1152]{2,1,0:T(8,128)(2,1)S(1)}, bf16[8,48,1152]{2,1,0:T(8,128)(2,1)S(1)}) custom-call(s32[10]{0:T(128)S(1)} %stack.37.s, bf16[384,768]{1,0:T(8,128)(2,1)S(1)} %get-tuple-element.447.n_own, bf16[384,768]{1,0:T(8,128)(2,1)S(1)} %copy-done.13, bf16[384,384]{1,0:T(8,128)(2,1)S(1)} %get-tuple-element.480.gq_o, ...), custom_call_target="tpu_custom_call" | custom-call | flops 1 | bytes 1 | tf_op jit(solution)/shard_map/pallas_call | solution.py:51
  85.9 1.6 collective-permute-done.13
  87.5 1.9 collective-permute-start.16
  91.1 2.2 %collective-permute-done.16 = bf16[2,64,768]{2,1,0:T(8,128)(2,1)S(1)} collective-permute-done((bf16[2,64,768]{2,1,0:T(8,128)(2,1)S(1)}, bf16[2,64,768]{2,1,0:T(8,128)(2,1)S(1)}, u32[]{:S(2)}, u32[]{:S(2)}) %collective-permute-start.16) | collective-permute-done | bytes 196640 | tf_op jit(solution)/shard_map/ppermute | solution.py:108
  94.2 2.7 %collective-permute-start.19 = (bf16[2,64,768]{2,1,0:T(8,128)(2,1)S(1)}, bf16[2,64,768]{2,1,0:T(8,128)(2,1)S(1)}, u32[]{:S(2)}, u32[]{:S(2)}) collective-permute-start(bf16[2,64,768]{2,1,0:T(8,128)(2,1)S(1)} %add_convert_fusion.21), channel_id=1, source_target_pairs={{0,16},{1,17},{2,18},{3,19},{4,20},{5,21},{6,22},{7,23},{8,24},{9,... | collective-permute-start | bytes 589832 | tf_op jit(solution)/shard_map/ppermute | solution.py:108
  97.0 1.5 collective-permute-start.21
  100.1 2.6 %shard_map.168 = (f32[384,768]{1,0:T(8,128)S(1)}, bf16[384,768]{1,0:T(8,128)(2,1)S(1)}) custom-call(s32[10]{0:T(128)S(1)} %stack.37.s, bf16[384,384]{1,0:T(8,128)(2,1)S(1)} %get-tuple-element.480.gq_o, bf16[384,384]{1,0:T(8,128)(2,1)S(1)} %get-tuple-element.481.gq_f, bf16[768,384]{1,0:T(8,128)(2,1)S(1)} %get-tuple-element.482.gk, ...), custom_call_target="tpu_custom_call" | custom-call | flops 1 | bytes 1 | tf_op jit(solution)/shard_map/pallas_call | solution.py:51
  103.1 2.6 %collective-permute-start.23 = (bf16[2,96,768]{2,1,0:T(8,128)(2,1)S(1)}, bf16[2,96,768]{2,1,0:T(8,128)(2,1)S(1)}, u32[]{:S(2)}, u32[]{:S(2)}) collective-permute-start(bf16[2,96,768]{2,1,0:T(8,128)(2,1)S(1)} %add_convert_fusion.9), channel_id=1, source_target_pairs={{0,16},{1,17},{2,18},{3,19},{4,20},{5,21},{6,22},{7,23},{8,24},{9,... | collective-permute-start | bytes 884744 | tf_op jit(solution)/shard_map/ppermute | solution.py:108
  106.0 1.7 collective-permute-start.22
  109.3 8.4 %collective-permute-done.18.far = bf16[384,768]{1,0:T(8,128)(2,1)S(1)} collective-permute-done((bf16[384,768]{1,0:T(8,128)(2,1)S(1)}, bf16[384,768]{1,0:T(8,128)(2,1)S(1)}, u32[]{:S(2)}, u32[]{:S(2)}) %collective-permute-start.18) | collective-permute-done | bytes 589856 | tf_op jit(solution)/shard_map/ppermute | solution.py:108
  117.7 7.2 %collective-permute-done.23 = bf16[2,96,768]{2,1,0:T(8,128)(2,1)S(1)} collective-permute-done((bf16[2,96,768]{2,1,0:T(8,128)(2,1)S(1)}, bf16[2,96,768]{2,1,0:T(8,128)(2,1)S(1)}, u32[]{:S(2)}, u32[]{:S(2)}) %collective-permute-start.23) | collective-permute-done | bytes 294944 | tf_op jit(solution)/shard_map/ppermute | solution.py:108
  126.8 6.9 %collective-permute-done.28 = bf16[2,96,768]{2,1,0:T(8,128)(2,1)S(1)} collective-permute-done((bf16[2,96,768]{2,1,0:T(8,128)(2,1)S(1)}, bf16[2,96,768]{2,1,0:T(8,128)(2,1)S(1)}, u32[]{:S(2)}, u32[]{:S(2)}) %collective-permute-start.28) | collective-permute-done | bytes 294944 | tf_op jit(solution)/shard_map/ppermute | solution.py:108
  133.9 2.9 %collective-permute-start.31 = (bf16[2,64,768]{2,1,0:T(8,128)(2,1)S(1)}, bf16[2,64,768]{2,1,0:T(8,128)(2,1)S(1)}, u32[]{:S(2)}, u32[]{:S(2)}) collective-permute-start(bf16[2,64,768]{2,1,0:T(8,128)(2,1)S(1)} %add_convert_fusion.17), channel_id=1, source_target_pairs={{0,16},{1,17},{2,10},{3,11},{4,20},{5,21},{6,14},{7,15},{8,24},{9,... | collective-permute-start | bytes 589832 | tf_op jit(solution)/shard_map/ppermute | solution.py:108
  138.8 6.6 %collective-permute-done.33 = bf16[2,48,1152]{2,1,0:T(8,128)(2,1)S(1)} collective-permute-done((bf16[2,48,1152]{2,1,0:T(8,128)(2,1)S(1)}, bf16[2,48,1152]{2,1,0:T(8,128)(2,1)S(1)}, u32[]{:S(2)}, u32[]{:S(2)}) %collective-permute-start.33) | collective-permute-done | bytes 221216 | tf_op jit(solution)/shard_map/ppermute | solution.py:108
  145.5 2.4 %collective-permute-done.32 = bf16[4,96,768]{2,1,0:T(8,128)(2,1)S(1)} collective-permute-done((bf16[4,96,768]{2,1,0:T(8,128)(2,1)S(1)}, bf16[4,96,768]{2,1,0:T(8,128)(2,1)S(1)}, u32[]{:S(2)}, u32[]{:S(2)}) %collective-permute-start.32) | collective-permute-done | bytes 589856 | tf_op jit(solution)/shard_map/ppermute | solution.py:108
  148.0 1.7 collective-permute-start.40
  150.4 1.8 collective-permute-done.29.own
  152.2 2.6 %shard_map.169 = (f32[2,2,8,384]{3,2,1,0:T(8,128)S(1)}, f32[3072,768]{1,0:T(8,128)}, f32[768,3072]{1,0:T(8,128)}) custom-call(s32[10]{0:T(128)S(1)} %stack.37.s, bf16[8,64,768]{2,1,0:T(8,128)(2,1)S(1)} %constant_dynamic-update-slice_fusion.4.own, bf16[8,64,768]{2,1,0:T(8,128)(2,1)S(1)} %collective-permute-done.30.other, ...), custom_call_target="tpu_custom_call", output_to_operand_aliasing={{0}: (4, {})} | custom-call | flops 1 | bytes 1 | tf_op jit(solution)/shard_map/pallas_call | solution.py:51
  154.8 3.6 %collective-permute-done.36 = bf16[2,48,2304]{2,1,0:T(8,128)(2,1)S(1)} collective-permute-done((bf16[2,48,2304]{2,1,0:T(8,128)(2,1)S(1)}, bf16[2,48,2304]{2,1,0:T(8,128)(2,1)S(1)}, u32[]{:S(2)}, u32[]{:S(2)}) %collective-permute-start.36) | collective-permute-done | bytes 442400 | tf_op jit(solution)/shard_map/ppermute | solution.py:108
  159.6 3.2 %collective-permute-start.38 = (bf16[4,64,768]{2,1,0:T(8,128)(2,1)S(1)}, bf16[4,64,768]{2,1,0:T(8,128)(2,1)S(1)}, u32[]{:S(2)}, u32[]{:S(2)}) collective-permute-start(bf16[4,64,768]{2,1,0:T(8,128)(2,1)S(1)} %constant_dynamic-update-slice_fusion.12), channel_id=1, source_target_pairs={{0,1},{1,0},{2,3},{3,2},{4,5},{5,4},{6,7},{7,6},{8,9},{9,8},{10,11... | collective-permute-start | bytes 1179656 | tf_op jit(solution)/shard_map/ppermute | solution.py:108
  162.8 2.4 %shard_map.170 = f32[384,768]{1,0:T(8,128)} custom-call(s32[10]{0:T(128)S(1)} %stack.37.s, f32[384,768]{1,0:T(8,128)S(1)} %get-tuple-element.548.own, bf16[384,768]{1,0:T(8,128)(2,1)S(1)} %collective-permute-done.18.far, f32[384,768]{1,0:T(8,128)S(1)} %copy-done.11, f32[1,768]{1,0:T(1,128)S(1)} %broadcast_in_dim.16.gain, f32[384,768]{1,0:T(8,128)S(1)} %get-tuple-element.552.grad2), custom_call_target="tpu_custom_call" | custom-call | flops 1 | bytes 1 | tf_op jit(solution)/shard_map/pallas_call | solution.py:51
  165.2 2.6 %shard_map.171 = (f32[2,2,8,384]{3,2,1,0:T(8,128)S(1)}, f32[3072,768]{1,0:T(8,128)}, f32[768,3072]{1,0:T(8,128)}) custom-call(s32[10]{0:T(128)S(1)} %stack.37.s, bf16[8,64,768]{2,1,0:T(8,128)(2,1)S(1)} %collective-permute-done.29.own, ...), custom_call_target="tpu_custom_call", output_to_operand_aliasing={{0}: (4, {}), {1}: (5, {}), {2}: (6, {})} | custom-call | flops 1 | bytes 1 | tf_op jit(solution)/shard_map/pallas_call | solution.py:51
  168.7 3.1 %shard_map.172 = (f32[2,2,8,384]{3,2,1,0:T(8,128)S(1)}, f32[3072,768]{1,0:T(8,128)}, f32[768,3072]{1,0:T(8,128)}, f32[768,768]{1,0:T(8,128)}) custom-call(s32[10]{0:T(128)S(1)} %stack.37.s, bf16[8,96,768]{2,1,0:T(8,128)(2,1)S(1)} %constant_dynamic-update-slice_fusion.8.own, ...), custom_call_target="tpu_custom_call", output_to_operand_aliasing={{0}: (4, {}), {1}: (5, {}), {2}: (6, {})} | custom-call | flops 1 | bytes 1 | tf_op jit(solution)/shard_map/pallas_call | solution.py:51
  171.8 2.4 %collective-permute-done.38 = bf16[4,64,768]{2,1,0:T(8,128)(2,1)S(1)} collective-permute-done((bf16[4,64,768]{2,1,0:T(8,128)(2,1)S(1)}, bf16[4,64,768]{2,1,0:T(8,128)(2,1)S(1)}, u32[]{:S(2)}, u32[]{:S(2)}) %collective-permute-start.38) | collective-permute-done | bytes 393248 | tf_op jit(solution)/shard_map/ppermute | solution.py:108
  175.8 3.1 %shard_map.173 = (f32[2,2,8,384]{3,2,1,0:T(8,128)S(1)}, f32[3072,768]{1,0:T(8,128)}, f32[768,3072]{1,0:T(8,128)}, f32[768,768]{1,0:T(8,128)}) custom-call(s32[10]{0:T(128)S(1)} %stack.37.s, bf16[8,96,768]{2,1,0:T(8,128)(2,1)S(1)} %collective-permute-done.40.own, ...), custom_call_target="tpu_custom_call", output_to_operand_aliasing={{0}: (4, {}), {1}: (5, {}), {2}: (6, {}), {3}: (7, {})} | custom-call | flops 1 | bytes 1 | tf_op jit(solution)/shard_map/pallas_call | solution.py:51
  178.9 3.2 %shard_map.174 = (f32[768,2304]{1,0:T(8,128)}, f32[8,8,96]{2,1,0:T(8,128)S(1)}) custom-call(s32[10]{0:T(128)S(1)} %stack.37.s, bf16[4,48,2304]{2,1,0:T(8,128)(2,1)S(1)} %constant_dynamic-update-slice_fusion.10.own, bf16[4,48,2304]{2,1,0:T(8,128)(2,1)S(1)} %collective-permute-done.42.other, bf16[768,2304]{1,0:T(8,128)(2,1)S(1)} %copy-done.1), custom_call_target="tpu_custom_call" | custom-call | flops 1 | bytes 1 | tf_op jit(solution)/shard_map/pallas_call | solution.py:51
  182.1 3.2 %shard_map.175 = (f32[768,2304]{1,0:T(8,128)}, f32[8,8,96]{2,1,0:T(8,128)S(1)}) custom-call(s32[10]{0:T(128)S(1)} %stack.37.s, bf16[4,48,2304]{2,1,0:T(8,128)(2,1)S(1)} %collective-permute-done.37.own, bf16[4,48,2304]{2,1,0:T(8,128)(2,1)S(1)} %collective-permute-done.41.other, ...), custom_call_target="tpu_custom_call", output_to_operand_aliasing={{0}: (4, {}), {1}: (5, {})} | custom-call | flops 1 | bytes 1 | tf_op jit(solution)/shard_map/pallas_call | solution.py:51
  186.5 2.6 %shard_map.176 = (f32[2,2,8,384]{3,2,1,0:T(8,128)S(1)}, f32[3072,768]{1,0:T(8,128)}, f32[768,3072]{1,0:T(8,128)}) custom-call(s32[10]{0:T(128)S(1)} %stack.37.s, bf16[8,64,768]{2,1,0:T(8,128)(2,1)S(1)} %constant_dynamic-update-slice_fusion.14.own, ...), custom_call_target="tpu_custom_call", output_to_operand_aliasing={{0}: (4, {}), {1}: (5, {}), {2}: (6, {})} | custom-call | flops 1 | bytes 1 | tf_op jit(solution)/shard_map/pallas_call | solution.py:51
  189.8 3.5 %shard_map.177 = (f32[2,2,8,384]{3,2,1,0:T(8,128)S(1)}, f32[3072,768]{1,0:T(8,128)}, f32[768,3072]{1,0:T(8,128)}) custom-call(s32[10]{0:T(128)S(1)} %stack.37.s, bf16[8,64,768]{2,1,0:T(8,128)(2,1)S(1)} %collective-permute-done.44.own, ...), custom_call_target="tpu_custom_call", output_to_operand_aliasing={{0}: (4, {}), {1}: (5, {}), {2}: (6, {})} | custom-call | flops 1 | bytes 1 | tf_op jit(solution)/shard_map/pallas_call | solution.py:51
  (169 shorter events, 26.4 us)
Async XLA Ops:
  0.6 18.2 %collective-permute-start = (bf16[384,768]{1,0:T(8,128)(2,1)}, bf16[384,768]{1,0:T(8,128)(2,1)}, u32[]{:S(2)}, u32[]{:S(2)}) collective-permute-start(bf16[384,768]{1,0:T(8,128)(2,1)} %bitcast.22), channel_id=1, source_target_pairs={{0,1},{1,0},{2,3},{3,2},{4,5},{5,4},{6,7},{7,6},{8,9},{9,8},{10,11... | collective-permute-start | bytes 1769480 | tf_op jit(solution)/shard_map/ppermute | solution.py:108
  3.7 13.7 %collective-permute-start.1 = (s32[1,384]{1,0:T(1,128)}, s32[1,384]{1,0:T(1,128)S(1)}, u32[]{:S(2)}, u32[]{:S(2)}) collective-permute-start(s32[1,384]{1,0:T(1,128)} %visible.1), channel_id=1, source_target_pairs={{0,1},{1,0},{2,3},{3,2},{4,5},{5,4},{6,7},{7,6},{8,9},{9,8},{10,11... | collective-permute-start | bytes 4616 | tf_op jit(solution)/shard_map/ppermute | solution.py:108
  11.4 19.0 %slice-start.2 = ((s8[4718592]{0:T(1024)(128)(4,1)}), s8[4194304]{0:T(1024)(128)(4,1)S(1)}, s32[]{:S(2)}) async-start(s8[4718592]{0:T(1024)(128)(4,1)} %bitcast.14), calls=%async_computation.2 | async-start | bytes 8388608
  29.7 5.7 %collective-permute-start.3 = (bf16[768,384]{1,0:T(8,128)(2,1)S(1)}, bf16[768,384]{1,0:T(8,128)(2,1)S(1)}, u32[]{:S(2)}, u32[]{:S(2)}) collective-permute-start(bf16[768,384]{1,0:T(8,128)(2,1)S(1)} %get-tuple-element.419.nt), channel_id=1, source_target_pairs={{0,2},{1,3},{2,0},{3,1},{4,6},{5,7},{6,4},{7,5},{8,10},{9,11},{10,... | collective-permute-start | bytes 1769480 | tf_op jit(solution)/shard_map/ppermute | solution.py:108
  29.8 5.7 %collective-permute-start.2 = (bf16[384,768]{1,0:T(8,128)(2,1)S(1)}, bf16[384,768]{1,0:T(8,128)(2,1)S(1)}, u32[]{:S(2)}, u32[]{:S(2)}) collective-permute-start(bf16[384,768]{1,0:T(8,128)(2,1)S(1)} %bitcast.16), channel_id=1, source_target_pairs={{0,2},{1,3},{2,0},{3,1},{4,6},{5,7},{6,4},{7,5},{8,10},{9,11},{10,... | collective-permute-start | bytes 1769480 | tf_op jit(solution)/shard_map/ppermute | solution.py:108
  30.3 5.2 %collective-permute-start.4 = (bf16[384,384]{1,0:T(8,128)(2,1)S(1)}, bf16[384,384]{1,0:T(8,128)(2,1)S(1)}, u32[]{:S(2)}, u32[]{:S(2)}) collective-permute-start(bf16[384,384]{1,0:T(8,128)(2,1)S(1)} %get-tuple-element.356), channel_id=1, source_target_pairs={{0,2},{1,3},{2,0},{3,1},{4,6},{5,7},{6,4},{7,5},{8,10},{9,11},{10,... | collective-permute-start | bytes 884744 | tf_op jit(solution)/shard_map/ppermute | solution.py:108
  34.9 13.6 %collective-permute-start.5 = (bf16[2,384,512]{2,1,0:T(8,128)(2,1)S(1)}, bf16[2,384,512]{2,1,0:T(8,128)(2,1)S(1)}, u32[]{:S(2)}, u32[]{:S(2)}) collective-permute-start(bf16[2,384,512]{2,1,0:T(8,128)(2,1)S(1)} %get-tuple-element.372), channel_id=1, source_target_pairs={{0,2},{1,3},{2,0},{3,1},{4,6},{5,7},{6,4},{7,5},{8,10},{9,11},{10,... | collective-permute-start | bytes 2359304 | tf_op jit(solution)/shard_map/ppermute | solution.py:108
  46.3 14.5 %collective-permute-start.8 = (bf16[2,384,512]{2,1,0:T(8,128)(2,1)S(1)}, bf16[2,384,512]{2,1,0:T(8,128)(2,1)S(1)}, u32[]{:S(2)}, u32[]{:S(2)}) collective-permute-start(bf16[2,384,512]{2,1,0:T(8,128)(2,1)S(1)} %get-tuple-element.394), channel_id=1, source_target_pairs={{0,2},{1,3},{2,0},{3,1},{4,6},{5,7},{6,4},{7,5},{8,10},{9,11},{10,... | collective-permute-start | bytes 2359304 | tf_op jit(solution)/shard_map/ppermute | solution.py:108
  46.4 14.4 %collective-permute-start.9 = (bf16[384,768]{1,0:T(8,128)(2,1)S(1)}, bf16[384,768]{1,0:T(8,128)(2,1)S(1)}, u32[]{:S(2)}, u32[]{:S(2)}) collective-permute-start(bf16[384,768]{1,0:T(8,128)(2,1)S(1)} %get-tuple-element.411.refs_2_), channel_id=1, source_target_pairs={{0,2},{1,3},{2,0},{3,1},{4,6},{5,7},{6,4},{7,5},{8,10},{9,11},{10,... | collective-permute-start | bytes 1769480 | tf_op jit(solution)/shard_map/ppermute | solution.py:108
  46.8 14.0 %collective-permute-start.10 = (bf16[384,384]{1,0:T(8,128)(2,1)S(1)}, bf16[384,384]{1,0:T(8,128)(2,1)S(1)}, u32[]{:S(2)}, u32[]{:S(2)}) collective-permute-start(bf16[384,384]{1,0:T(8,128)(2,1)S(1)} %get-tuple-element.401), channel_id=1, source_target_pairs={{0,1},{1,0},{2,3},{3,2},{4,5},{5,4},{6,7},{7,6},{8,9},{9,8},{10,11... | collective-permute-start | bytes 884744 | tf_op jit(solution)/shard_map/ppermute | solution.py:108
  48.6 16.3 %collective-permute-start.7 = (bf16[2,384,512]{2,1,0:T(8,128)(2,1)S(1)}, bf16[2,384,512]{2,1,0:T(8,128)(2,1)S(1)}, u32[]{:S(2)}, u32[]{:S(2)}) collective-permute-start(bf16[2,384,512]{2,1,0:T(8,128)(2,1)S(1)} %get-tuple-element.391), channel_id=1, source_target_pairs={{0,2},{1,3},{2,0},{3,1},{4,6},{5,7},{6,4},{7,5},{8,10},{9,11},{10,... | collective-permute-start | bytes 2359304 | tf_op jit(solution)/shard_map/ppermute | solution.py:108
  51.1 18.0 %collective-permute-start.6 = (bf16[8,64,768]{2,1,0:T(8,128)(2,1)S(1)}, bf16[8,64,768]{2,1,0:T(8,128)(2,1)S(1)}, u32[]{:S(2)}, u32[]{:S(2)}) collective-permute-start(bf16[8,64,768]{2,1,0:T(8,128)(2,1)S(1)} %get-tuple-element.389), channel_id=1, source_target_pairs={{0,4},{1,5},{2,3},{3,2},{4,0},{5,1},{6,7},{7,6},{8,12},{9,13},{10,... | collective-permute-start | bytes 2359304 | tf_op jit(solution)/shard_map/ppermute | solution.py:108
  64.3 16.3 %collective-permute-start.11 = (bf16[8,96,768]{2,1,0:T(8,128)(2,1)S(1)}, bf16[8,96,768]{2,1,0:T(8,128)(2,1)S(1)}, u32[]{:S(2)}, u32[]{:S(2)}) collective-permute-start(bf16[8,96,768]{2,1,0:T(8,128)(2,1)S(1)} %get-tuple-element.440), channel_id=1, source_target_pairs={{0,1},{1,0},{2,6},{3,7},{4,5},{5,4},{6,2},{7,3},{8,9},{9,8},{10,14... | collective-permute-start | bytes 3538952 | tf_op jit(solution)/shard_map/ppermute | solution.py:108
  67.4 23.4 %collective-permute-start.17 = (bf16[8,64,768]{2,1,0:T(8,128)(2,1)S(1)}, bf16[8,64,768]{2,1,0:T(8,128)(2,1)S(1)}, u32[]{:S(2)}, u32[]{:S(2)}) collective-permute-start(bf16[8,64,768]{2,1,0:T(8,128)(2,1)S(1)} %get-tuple-element.467), channel_id=1, source_target_pairs={{0,8},{1,9},{2,6},{3,7},{4,12},{5,13},{6,2},{7,3},{8,0},{9,1},{10,... | collective-permute-start | bytes 2359304 | tf_op jit(solution)/shard_map/ppermute | solution.py:108
  70.3 17.2 %collective-permute-start.13 = (bf16[4,64,768]{2,1,0:T(8,128)(2,1)S(1)}, bf16[4,64,768]{2,1,0:T(8,128)(2,1)S(1)}, u32[]{:S(2)}, u32[]{:S(2)}) collective-permute-start(bf16[4,64,768]{2,1,0:T(8,128)(2,1)S(1)} %add_convert_fusion.7), channel_id=1, source_target_pairs={{0,1},{1,0},{2,10},{3,11},{4,5},{5,4},{6,14},{7,15},{8,9},{9,8},{1... | collective-permute-start | bytes 1179656 | tf_op jit(solution)/shard_map/ppermute | solution.py:108
  80.7 9.9 %collective-permute-start.12 = (bf16[4,96,768]{2,1,0:T(8,128)(2,1)S(1)}, bf16[4,96,768]{2,1,0:T(8,128)(2,1)S(1)}, u32[]{:S(2)}, u32[]{:S(2)}) collective-permute-start(bf16[4,96,768]{2,1,0:T(8,128)(2,1)S(1)} %add_convert_fusion.1), channel_id=1, source_target_pairs={{0,8},{1,9},{2,3},{3,2},{4,12},{5,13},{6,7},{7,6},{8,0},{9,1},{10,... | collective-permute-start | bytes 1769480 | tf_op jit(solution)/shard_map/ppermute | solution.py:108
  87.5 5.7 %collective-permute-start.16 = (bf16[2,64,768]{2,1,0:T(8,128)(2,1)S(1)}, bf16[2,64,768]{2,1,0:T(8,128)(2,1)S(1)}, u32[]{:S(2)}, u32[]{:S(2)}) collective-permute-start(bf16[2,64,768]{2,1,0:T(8,128)(2,1)S(1)} %add_convert_fusion.23), channel_id=1, source_target_pairs={{0,8},{1,9},{2,6},{3,7},{4,12},{5,13},{6,2},{7,3},{8,0},{9,1},{10,... | collective-permute-start | bytes 589832 | tf_op jit(solution)/shard_map/ppermute | solution.py:108
  89.4 7.5 %collective-permute-start.15 = (bf16[8,48,1152]{2,1,0:T(8,128)(2,1)S(1)}, bf16[8,48,1152]{2,1,0:T(8,128)(2,1)S(1)}, u32[]{:S(2)}, u32[]{:S(2)}) collective-permute-start(bf16[8,48,1152]{2,1,0:T(8,128)(2,1)S(1)} %get-tuple-element.464), channel_id=1, source_target_pairs={{0,2},{1,3},{2,0},{3,1},{4,6},{5,7},{6,4},{7,5},{8,10},{9,11},{10,... | collective-permute-start | bytes 2654216 | tf_op jit(solution)/shard_map/ppermute | solution.py:108
  93.3 6.7 %collective-permute-start.14 = (bf16[2,96,768]{2,1,0:T(8,128)(2,1)S(1)}, bf16[2,96,768]{2,1,0:T(8,128)(2,1)S(1)}, u32[]{:S(2)}, u32[]{:S(2)}) collective-permute-start(bf16[2,96,768]{2,1,0:T(8,128)(2,1)S(1)} %add_convert_fusion.11), channel_id=1, source_target_pairs={{0,4},{1,5},{2,10},{3,11},{4,0},{5,1},{6,14},{7,15},{8,12},{9,13},... | collective-permute-start | bytes 884744 | tf_op jit(solution)/shard_map/ppermute | solution.py:108
  93.3 12.5 %collective-permute-start.20 = (bf16[4,64,768]{2,1,0:T(8,128)(2,1)S(1)}, bf16[4,64,768]{2,1,0:T(8,128)(2,1)S(1)}, u32[]{:S(2)}, u32[]{:S(2)}) collective-permute-start(bf16[4,64,768]{2,1,0:T(8,128)(2,1)S(1)} %add_convert_fusion.5), channel_id=1, source_target_pairs={{0,1},{1,0},{2,3},{3,2},{4,5},{5,4},{6,7},{7,6},{8,9},{9,8},{10,11... | collective-permute-start | bytes 1179656 | tf_op jit(solution)/shard_map/ppermute | solution.py:108
  94.2 11.7 %collective-permute-start.19 = (bf16[2,64,768]{2,1,0:T(8,128)(2,1)S(1)}, bf16[2,64,768]{2,1,0:T(8,128)(2,1)S(1)}, u32[]{:S(2)}, u32[]{:S(2)}) collective-permute-start(bf16[2,64,768]{2,1,0:T(8,128)(2,1)S(1)} %add_convert_fusion.21), channel_id=1, source_target_pairs={{0,16},{1,17},{2,18},{3,19},{4,20},{5,21},{6,22},{7,23},{8,24},{9,... | collective-permute-start | bytes 589832 | tf_op jit(solution)/shard_map/ppermute | solution.py:108
  97.0 8.7 %collective-permute-start.21 = (bf16[4,48,1152]{2,1,0:T(8,128)(2,1)S(1)}, bf16[4,48,1152]{2,1,0:T(8,128)(2,1)S(1)}, u32[]{:S(2)}, u32[]{:S(2)}) collective-permute-start(bf16[4,48,1152]{2,1,0:T(8,128)(2,1)S(1)} %add_convert_fusion.3), channel_id=1, source_target_pairs={{0,4},{1,5},{2,10},{3,11},{4,0},{5,1},{6,14},{7,15},{8,12},{9,13},... | collective-permute-start | bytes 1327112 | tf_op jit(solution)/shard_map/ppermute | solution.py:108
  102.7 15.0 %collective-permute-start.18 = (bf16[384,768]{1,0:T(8,128)(2,1)S(1)}, bf16[384,768]{1,0:T(8,128)(2,1)S(1)}, u32[]{:S(2)}, u32[]{:S(2)}) collective-permute-start(bf16[384,768]{1,0:T(8,128)(2,1)S(1)} %get-tuple-element.487), channel_id=1, source_target_pairs={{0,1},{1,0},{2,3},{3,2},{4,5},{5,4},{6,7},{7,6},{8,9},{9,8},{10,11... | collective-permute-start | bytes 1769480 | tf_op jit(solution)/shard_map/ppermute | solution.py:108
  103.1 21.7 %collective-permute-start.23 = (bf16[2,96,768]{2,1,0:T(8,128)(2,1)S(1)}, bf16[2,96,768]{2,1,0:T(8,128)(2,1)S(1)}, u32[]{:S(2)}, u32[]{:S(2)}) collective-permute-start(bf16[2,96,768]{2,1,0:T(8,128)(2,1)S(1)} %add_convert_fusion.9), channel_id=1, source_target_pairs={{0,16},{1,17},{2,18},{3,19},{4,20},{5,21},{6,22},{7,23},{8,24},{9,... | collective-permute-start | bytes 884744 | tf_op jit(solution)/shard_map/ppermute | solution.py:108
  106.0 19.5 %collective-permute-start.22 = (bf16[2,64,768]{2,1,0:T(8,128)(2,1)S(1)}, bf16[2,64,768]{2,1,0:T(8,128)(2,1)S(1)}, u32[]{:S(2)}, u32[]{:S(2)}) collective-permute-start(bf16[2,64,768]{2,1,0:T(8,128)(2,1)S(1)} %add_convert_fusion.18), channel_id=1, source_target_pairs={{0,8},{1,9},{2,6},{3,7},{4,12},{5,13},{6,2},{7,3},{8,0},{9,1},{10,... | collective-permute-start | bytes 589832 | tf_op jit(solution)/shard_map/ppermute | solution.py:108
  107.7 19.0 %collective-permute-start.25 = (bf16[2,48,1152]{2,1,0:T(8,128)(2,1)S(1)}, bf16[2,48,1152]{2,1,0:T(8,128)(2,1)S(1)}, u32[]{:S(2)}, u32[]{:S(2)}) collective-permute-start(bf16[2,48,1152]{2,1,0:T(8,128)(2,1)S(1)} %add_convert_fusion.15), channel_id=1, source_target_pairs={{0,8},{1,9},{2,18},{3,19},{4,12},{5,13},{6,22},{7,23},{8,0},{9,1},... | collective-permute-start | bytes 663560 | tf_op jit(solution)/shard_map/ppermute | solution.py:108
  108.1 25.6 %collective-permute-start.27 = (bf16[2,64,768]{2,1,0:T(8,128)(2,1)S(1)}, bf16[2,64,768]{2,1,0:T(8,128)(2,1)S(1)}, u32[]{:S(2)}, u32[]{:S(2)}) collective-permute-start(bf16[2,64,768]{2,1,0:T(8,128)(2,1)S(1)} %add_convert_fusion.20), channel_id=1, source_target_pairs={{0,4},{1,5},{2,18},{3,19},{4,0},{5,1},{6,22},{7,23},{8,12},{9,13},... | collective-permute-start | bytes 589832 | tf_op jit(solution)/shard_map/ppermute | solution.py:108
  124.9 8.8 %collective-permute-start.28 = (bf16[2,96,768]{2,1,0:T(8,128)(2,1)S(1)}, bf16[2,96,768]{2,1,0:T(8,128)(2,1)S(1)}, u32[]{:S(2)}, u32[]{:S(2)}) collective-permute-start(bf16[2,96,768]{2,1,0:T(8,128)(2,1)S(1)} %add_convert_fusion.8), channel_id=1, source_target_pairs={{0,4},{1,5},{2,10},{3,11},{4,0},{5,1},{6,14},{7,15},{8,12},{9,13},... | collective-permute-start | bytes 884744 | tf_op jit(solution)/shard_map/ppermute | solution.py:108
  125.6 12.4 %collective-permute-start.24 = (bf16[4,64,768]{2,1,0:T(8,128)(2,1)S(1)}, bf16[4,64,768]{2,1,0:T(8,128)(2,1)S(1)}, u32[]{:S(2)}, u32[]{:S(2)}) collective-permute-start(bf16[4,64,768]{2,1,0:T(8,128)(2,1)S(1)} %constant_dynamic-update-slice_fusion), channel_id=1, source_target_pairs={{0,1},{1,0},{2,10},{3,11},{4,5},{5,4},{6,14},{7,15},{8,9},{9,8},{1... | collective-permute-start | bytes 1179656 | tf_op jit(solution)/shard_map/ppermute | solution.py:108
  126.7 10.1 %collective-permute-start.26 = (bf16[2,48,1152]{2,1,0:T(8,128)(2,1)S(1)}, bf16[2,48,1152]{2,1,0:T(8,128)(2,1)S(1)}, u32[]{:S(2)}, u32[]{:S(2)}) collective-permute-start(bf16[2,48,1152]{2,1,0:T(8,128)(2,1)S(1)} %add_convert_fusion.13), channel_id=1, source_target_pairs={{0,16},{1,17},{2,6},{3,7},{4,20},{5,21},{6,2},{7,3},{8,24},{9,25},... | collective-permute-start | bytes 663560 | tf_op jit(solution)/shard_map/ppermute | solution.py:108
  133.8 14.2 %collective-permute-start.32 = (bf16[4,96,768]{2,1,0:T(8,128)(2,1)S(1)}, bf16[4,96,768]{2,1,0:T(8,128)(2,1)S(1)}, u32[]{:S(2)}, u32[]{:S(2)}) collective-permute-start(bf16[4,96,768]{2,1,0:T(8,128)(2,1)S(1)} %constant_dynamic-update-slice_fusion.2), channel_id=1, source_target_pairs={{0,8},{1,9},{2,3},{3,2},{4,12},{5,13},{6,7},{7,6},{8,0},{9,1},{10,... | collective-permute-start | bytes 1769480 | tf_op jit(solution)/shard_map/ppermute | solution.py:108
  133.9 15.8 %collective-permute-start.31 = (bf16[2,64,768]{2,1,0:T(8,128)(2,1)S(1)}, bf16[2,64,768]{2,1,0:T(8,128)(2,1)S(1)}, u32[]{:S(2)}, u32[]{:S(2)}) collective-permute-start(bf16[2,64,768]{2,1,0:T(8,128)(2,1)S(1)} %add_convert_fusion.17), channel_id=1, source_target_pairs={{0,16},{1,17},{2,10},{3,11},{4,20},{5,21},{6,14},{7,15},{8,24},{9,... | collective-permute-start | bytes 589832 | tf_op jit(solution)/shard_map/ppermute | solution.py:108
  136.9 8.4 %collective-permute-start.33 = (bf16[2,48,1152]{2,1,0:T(8,128)(2,1)S(1)}, bf16[2,48,1152]{2,1,0:T(8,128)(2,1)S(1)}, u32[]{:S(2)}, u32[]{:S(2)}) collective-permute-start(bf16[2,48,1152]{2,1,0:T(8,128)(2,1)S(1)} %add_convert_fusion.12), channel_id=1, source_target_pairs={{0,1},{1,0},{2,3},{3,2},{4,5},{5,4},{6,7},{7,6},{8,9},{9,8},{10,11... | collective-permute-start | bytes 663560 | tf_op jit(solution)/shard_map/ppermute | solution.py:108
  138.1 11.7 %collective-permute-start.30 = (bf16[8,64,768]{2,1,0:T(8,128)(2,1)S(1)}, bf16[8,64,768]{2,1,0:T(8,128)(2,1)S(1)}, u32[]{:S(2)}, u32[]{:S(2)}) collective-permute-start(bf16[8,64,768]{2,1,0:T(8,128)(2,1)S(1)} %constant_dynamic-update-slice_fusion.4.own), channel_id=1, source_target_pairs={{0,2},{1,3},{2,0},{3,1},{4,6},{5,7},{6,4},{7,5},{8,10},{9,11},{10,... | collective-permute-start | bytes 2359304 | tf_op jit(solution)/shard_map/ppermute | solution.py:108
  138.2 14.0 %collective-permute-start.29 = (bf16[8,64,768]{2,1,0:T(8,128)(2,1)S(1)}, bf16[8,64,768]{2,1,0:T(8,128)(2,1)S(1)}, u32[]{:S(2)}, u32[]{:S(2)}) collective-permute-start(bf16[8,64,768]{2,1,0:T(8,128)(2,1)S(1)} %constant_dynamic-update-slice_fusion.4.own), channel_id=1, source_target_pairs={{0,4},{1,5},{2,3},{3,2},{4,0},{5,1},{6,7},{7,6},{8,12},{9,13},{10,... | collective-permute-start | bytes 2359304 | tf_op jit(solution)/shard_map/ppermute | solution.py:108
  145.4 12.9 %collective-permute-start.36 = (bf16[2,48,2304]{2,1,0:T(8,128)(2,1)S(1)}, bf16[2,48,2304]{2,1,0:T(8,128)(2,1)S(1)}, u32[]{:S(2)}, u32[]{:S(2)}) collective-permute-start(bf16[2,48,2304]{2,1,0:T(8,128)(2,1)S(1)} %constant_dynamic-update-slice_fusion.6), channel_id=1, source_target_pairs={{0,8},{1,9},{2,18},{3,19},{4,12},{5,13},{6,22},{7,23},{8,0},{9,1},... | collective-permute-start | bytes 1327112 | tf_op jit(solution)/shard_map/ppermute | solution.py:108
  148.0 19.8 %collective-permute-start.40 = (bf16[8,96,768]{2,1,0:T(8,128)(2,1)S(1)}, bf16[8,96,768]{2,1,0:T(8,128)(2,1)S(1)}, u32[]{:S(2)}, u32[]{:S(2)}) collective-permute-start(bf16[8,96,768]{2,1,0:T(8,128)(2,1)S(1)} %constant_dynamic-update-slice_fusion.8.own), channel_id=1, source_target_pairs={{0,1},{1,0},{2,6},{3,7},{4,5},{5,4},{6,2},{7,3},{8,9},{9,8},{10,14... | collective-permute-start | bytes 3538952 | tf_op jit(solution)/shard_map/ppermute | solution.py:108
  149.7 19.0 %collective-permute-start.39 = (bf16[8,96,768]{2,1,0:T(8,128)(2,1)S(1)}, bf16[8,96,768]{2,1,0:T(8,128)(2,1)S(1)}, u32[]{:S(2)}, u32[]{:S(2)}) collective-permute-start(bf16[8,96,768]{2,1,0:T(8,128)(2,1)S(1)} %constant_dynamic-update-slice_fusion.8.own), channel_id=1, source_target_pairs={{0,2},{1,3},{2,0},{3,1},{4,6},{5,7},{6,4},{7,5},{8,10},{9,11},{10,... | collective-permute-start | bytes 3538952 | tf_op jit(solution)/shard_map/ppermute | solution.py:108
  149.8 9.8 %collective-permute-start.35 = (bf16[2,64,768]{2,1,0:T(8,128)(2,1)S(1)}, bf16[2,64,768]{2,1,0:T(8,128)(2,1)S(1)}, u32[]{:S(2)}, u32[]{:S(2)}) collective-permute-start(bf16[2,64,768]{2,1,0:T(8,128)(2,1)S(1)} %add_convert_fusion.16), channel_id=1, source_target_pairs={{0,4},{1,5},{2,18},{3,19},{4,0},{5,1},{6,22},{7,23},{8,12},{9,13},... | collective-permute-start | bytes 589832 | tf_op jit(solution)/shard_map/ppermute | solution.py:108
  158.3 4.4 %collective-permute-start.34 = (bf16[8,64,768]{2,1,0:T(8,128)(2,1)S(1)}, bf16[8,64,768]{2,1,0:T(8,128)(2,1)S(1)}, u32[]{:S(2)}, u32[]{:S(2)}) collective-permute-start(bf16[8,64,768]{2,1,0:T(8,128)(2,1)S(1)} %collective-permute-done.29.own), channel_id=1, source_target_pairs={{0,2},{1,3},{2,0},{3,1},{4,6},{5,7},{6,4},{7,5},{8,10},{9,11},{10,... | collective-permute-start | bytes 2359304 | tf_op jit(solution)/shard_map/ppermute | solution.py:108
  158.4 16.0 %collective-permute-start.37 = (bf16[4,48,2304]{2,1,0:T(8,128)(2,1)S(1)}, bf16[4,48,2304]{2,1,0:T(8,128)(2,1)S(1)}, u32[]{:S(2)}, u32[]{:S(2)}) collective-permute-start(bf16[4,48,2304]{2,1,0:T(8,128)(2,1)S(1)} %constant_dynamic-update-slice_fusion.10.own), channel_id=1, source_target_pairs={{0,4},{1,5},{2,10},{3,11},{4,0},{5,1},{6,14},{7,15},{8,12},{9,13},... | collective-permute-start | bytes 2654216 | tf_op jit(solution)/shard_map/ppermute | solution.py:108
  159.6 14.7 %collective-permute-start.38 = (bf16[4,64,768]{2,1,0:T(8,128)(2,1)S(1)}, bf16[4,64,768]{2,1,0:T(8,128)(2,1)S(1)}, u32[]{:S(2)}, u32[]{:S(2)}) collective-permute-start(bf16[4,64,768]{2,1,0:T(8,128)(2,1)S(1)} %constant_dynamic-update-slice_fusion.12), channel_id=1, source_target_pairs={{0,1},{1,0},{2,3},{3,2},{4,5},{5,4},{6,7},{7,6},{8,9},{9,8},{10,11... | collective-permute-start | bytes 1179656 | tf_op jit(solution)/shard_map/ppermute | solution.py:108
  167.8 8.1 %collective-permute-start.43 = (bf16[8,96,768]{2,1,0:T(8,128)(2,1)S(1)}, bf16[8,96,768]{2,1,0:T(8,128)(2,1)S(1)}, u32[]{:S(2)}, u32[]{:S(2)}) collective-permute-start(bf16[8,96,768]{2,1,0:T(8,128)(2,1)S(1)} %collective-permute-done.40.own), channel_id=1, source_target_pairs={{0,2},{1,3},{2,0},{3,1},{4,6},{5,7},{6,4},{7,5},{8,10},{9,11},{10,... | collective-permute-start | bytes 3538952 | tf_op jit(solution)/shard_map/ppermute | solution.py:108
  168.7 7.2 %collective-permute-start.42 = (bf16[4,48,2304]{2,1,0:T(8,128)(2,1)S(1)}, bf16[4,48,2304]{2,1,0:T(8,128)(2,1)S(1)}, u32[]{:S(2)}, u32[]{:S(2)}) collective-permute-start(bf16[4,48,2304]{2,1,0:T(8,128)(2,1)S(1)} %constant_dynamic-update-slice_fusion.10.own), channel_id=1, source_target_pairs={{0,2},{1,3},{2,0},{3,1},{4,6},{5,7},{6,4},{7,5},{8,10},{9,11},{10,... | collective-permute-start | bytes 2654216 | tf_op jit(solution)/shard_map/ppermute | solution.py:108
  174.4 7.7 %collective-permute-start.41 = (bf16[4,48,2304]{2,1,0:T(8,128)(2,1)S(1)}, bf16[4,48,2304]{2,1,0:T(8,128)(2,1)S(1)}, u32[]{:S(2)}, u32[]{:S(2)}) collective-permute-start(bf16[4,48,2304]{2,1,0:T(8,128)(2,1)S(1)} %collective-permute-done.37.own), channel_id=1, source_target_pairs={{0,2},{1,3},{2,0},{3,1},{4,6},{5,7},{6,4},{7,5},{8,10},{9,11},{10,... | collective-permute-start | bytes 2654216 | tf_op jit(solution)/shard_map/ppermute | solution.py:108
  174.4 12.0 %collective-permute-start.44 = (bf16[8,64,768]{2,1,0:T(8,128)(2,1)S(1)}, bf16[8,64,768]{2,1,0:T(8,128)(2,1)S(1)}, u32[]{:S(2)}, u32[]{:S(2)}) collective-permute-start(bf16[8,64,768]{2,1,0:T(8,128)(2,1)S(1)} %constant_dynamic-update-slice_fusion.14.own), channel_id=1, source_target_pairs={{0,8},{1,9},{2,6},{3,7},{4,12},{5,13},{6,2},{7,3},{8,0},{9,1},{10,... | collective-permute-start | bytes 2359304 | tf_op jit(solution)/shard_map/ppermute | solution.py:108
  174.9 11.5 %collective-permute-start.46 = (bf16[8,64,768]{2,1,0:T(8,128)(2,1)S(1)}, bf16[8,64,768]{2,1,0:T(8,128)(2,1)S(1)}, u32[]{:S(2)}, u32[]{:S(2)}) collective-permute-start(bf16[8,64,768]{2,1,0:T(8,128)(2,1)S(1)} %constant_dynamic-update-slice_fusion.14.own), channel_id=1, source_target_pairs={{0,2},{1,3},{2,0},{3,1},{4,6},{5,7},{6,4},{7,5},{8,10},{9,11},{10,... | collective-permute-start | bytes 2359304 | tf_op jit(solution)/shard_map/ppermute | solution.py:108
  186.4 3.3 %collective-permute-start.45 = (bf16[8,64,768]{2,1,0:T(8,128)(2,1)S(1)}, bf16[8,64,768]{2,1,0:T(8,128)(2,1)S(1)}, u32[]{:S(2)}, u32[]{:S(2)}) collective-permute-start(bf16[8,64,768]{2,1,0:T(8,128)(2,1)S(1)} %collective-permute-done.44.own), channel_id=1, source_target_pairs={{0,2},{1,3},{2,0},{3,1},{4,6},{5,7},{6,4},{7,5},{8,10},{9,11},{10,... | collective-permute-start | bytes 2359304 | tf_op jit(solution)/shard_map/ppermute | solution.py:108
  (21 other events, 158.6 us)
